TPU v7x, 32 devices: a whole 2x2x4 slice. The times are simulated.
32 devices in a mesh: dp: 4 (over z), tensor: 8 (over y, x, core).
Axes of the slice: x: 2, y: 2, z: 4, core: 2. Of those that a mesh axis runs over, the one named last changes fastest.
Arguments:
- activations: bfloat16 [16384, 4096], P('dp', 'tensor'), may hold values from -6 to 6
- out_grads: bfloat16 [16384, 14336], P('dp', 'tensor'), may hold values from -6 to 6
- proj_in: bfloat16 [4096, 64], P('tensor'), may hold values from -0.09375 to 0.09375
- proj_out: bfloat16 [14336, 64], P('tensor'), may hold values from -0.046875 to 0.046875
- example_ids: int32 [4, 4096], P('dp'), may hold values from 0 to 511, never falling along the last dimension, each value on 1 to 16 neighbouring positions
- queries: float32 [1024, 4096], P('dp', 'tensor'), may hold values from -6 to 6
Outputs:
- preconditioned: float32 [4096, 1024], P('tensor')
- scores: float32 [1024, 2048], P('tensor', 'dp')
Inputs may be any that keep to these rules, and one draw needn't show every extreme that they name: `example_ids`: each row is non-decreasing; every number of 0 to 511 appears in each row, at most 2 * 8 times, and some number exactly that often.
All inputs are finite; a program needn't handle non-finite values.
Results may differ from a plain program's by a relative error of at most 0.0003.
Values sent between devices are 32-bit elements; how exact they have to be, the bound alone decides.
No kernel may reach another device: no remote copies, remote signals or barrier semaphores. Data moves between devices by JAX's collectives and lax.ppermute only.
A program may use at most 128 MiB of HBM per device.

v0:
```python
import jax
import jax.numpy as jnp
from jax import lax
from jax.sharding import PartitionSpec as P

ITERS = 4
EX_DEV = 512


def contract_first(left, right):
    return lax.dot_general(left, right, (((0,), (0,)), ((), ())), precision=lax.Precision.HIGHEST)


def per_device(activations, out_grads, proj_in, proj_out, example_ids, queries):
    high = lax.Precision.HIGHEST
    tok_rows = activations.shape[0]
    ranks_in = proj_in.shape[1]
    ranks_out = proj_out.shape[1]
    tensor_count = lax.axis_size("tensor")
    tensor_index = lax.axis_index("tensor")
    in_part = jnp.dot(activations, proj_in, preferred_element_type=jnp.float32)
    out_part = jnp.dot(out_grads, proj_out, preferred_element_type=jnp.float32)
    in_proj, out_proj = lax.psum((in_part, out_part), "tensor")
    rows_here = ranks_out // tensor_count
    out_slice = lax.dynamic_slice_in_dim(out_proj, tensor_index * rows_here, rows_here, 1)
    products = (out_slice[:, :, None] * in_proj[:, None, :]).reshape(tok_rows, rows_here * ranks_in)
    local_ids = example_ids[0]
    onehot = (jnp.arange(EX_DEV, dtype=jnp.int32)[:, None] == local_ids[None, :]).astype(
        jnp.float32
    )
    sketch = jnp.dot(onehot, products, precision=high)
    examples_all = EX_DEV * lax.axis_size("dp")
    comp = ranks_out * ranks_in
    total_sq = lax.psum(jnp.sum(sketch * sketch), ("dp", "tensor"))
    damping = 0.1 * total_sq / (examples_all * comp)
    gathered = lax.all_gather(queries, "dp", axis=0, tiled=True)
    residual = gathered.T

    def column_norm(values):
        return lax.psum(jnp.sum(values * values, axis=0), "tensor")

    direction = residual
    solution = jnp.zeros_like(residual)
    norm_now = column_norm(residual)
    for step in range(ITERS):
        inner = lax.psum(jnp.dot(sketch, direction, precision=high), "tensor")
        outer = lax.psum(contract_first(sketch, inner), "dp")
        image = outer / examples_all + damping * direction
        bend = lax.psum(jnp.sum(direction * image, axis=0), "tensor")
        alpha = norm_now / bend
        solution = solution + alpha * direction
        residual = residual - alpha * image
        norm_next = column_norm(residual)
        direction = residual + norm_next / norm_now * direction
        norm_now = norm_next
    scale = 1.0 / jnp.sqrt(jnp.float32(comp))
    scores = lax.psum_scatter(
        contract_first(solution, sketch.T) * scale, "tensor", scatter_dimension=0, tiled=True
    )
    return (solution, scores)


def solution(mesh):
    in_specs = (
        P("dp", "tensor"),
        P("dp", "tensor"),
        P("tensor", None),
        P("tensor", None),
        P("dp", None),
        P("dp", "tensor"),
    )
    out_specs = (P("tensor", None), P("tensor", "dp"))
    return jax.shard_map(
        per_device, mesh=mesh, in_specs=in_specs, out_specs=out_specs, check_vma=False
    )
```

profile of v0, /device:TPU:0, one launch (start us, length us, event | category | flops | bytes accessed | tf_op | source)
XLA Modules:
  0.0 907.6 jit_solution(7684742872334714678)
XLA Ops:
  8.0 0.0 all-reduce.28.cloned.1.call-start
  8.1 4.6 fusion.13
  12.7 10.6 %fusion.12 = f32[4096,64]{0,1:T(8,128)} fusion(bf16[4096,1792]{1,0:T(8,128)(2,1)} %param.7, bf16[1792,64]{0,1:T(8,128)(2,1)S(1)} %copy-done), kind=kOutput, calls=%fused_computation.34 | convolution fusion | flops 939524096 | bytes 15958016 | tf_op jit(solution)/shard_map/dot_general | solution.py:22
  23.3 0.0 all-reduce.28.cloned.1.call-update
  23.3 0.0 all-gather.2.cloned.1.call-start
  23.4 1.0 copy-done.5
  24.3 1.0 copy.11
  25.3 0.0 all-gather.2.cloned.1.call-update
  25.4 0.3 all-reduce.12.cloned.1.call-start
  25.7 62.0 %all-reduce.28.cloned.1.call-done = (f32[4096,64]{0,1:T(8,128)}, f32[4096,64]{0,1:T(8,128)}) async-done(((f32[4096,64]{0,1:T(8,128)}, f32[4096,64]{0,1:T(8,128)}), (f32[4096,64]{0,1:T(8,128)}, f32[4096,64]{0,1:T(8,128)})) %all-reduce.28.cloned.1.call-update) | async-done | bytes 2097168 | tf_op jit(solution)/shard_map/psum | solution.py:23
  87.7 0.9 constant_dynamic-slice_fusion
  88.6 2.2 broadcast_multiply_fusion
  90.9 8.2 multiply_reduce_fusion.6
  99.1 6.5 fusion.14
  105.6 0.0 all-reduce.12.cloned.1.call-update
  105.6 0.6 all-reduce.14.cloned.1.call-start
  106.2 60.2 %all-reduce.12.cloned.1.call-done = f32[512,1024]{1,0:T(8,128)} async-done(((f32[512,1024]{1,0:T(8,128)}), f32[512,1024]{1,0:T(8,128)}) %all-reduce.12.cloned.1.call-update) | async-done | bytes 2097168 | tf_op jit(solution)/shard_map/psum | solution.py:46
  166.4 6.4 fusion.15
  172.8 0.0 all-reduce.14.cloned.1.call-update
  172.8 0.0 all-reduce.16.cloned.1.call-start
  172.9 42.5 %psum.138 = f32[]{:T(128)} all-reduce(f32[]{:T(128)} %get-tuple-element.12), channel_id=1, replica_groups=mesh['dp'=4,'tensor'=8] {'dp','tensor'}, use_global_device_ids=true, to_apply=%region_7.0 | all-reduce | flops 1 | bytes 8 | tf_op jit(solution)/shard_map/psum | solution.py:34
  216.0 43.1 %all-reduce.14.cloned.1.call-done = f32[512,1024]{1,0:T(8,128)} async-done(((f32[512,1024]{1,0:T(8,128)}), f32[512,1024]{1,0:T(8,128)}) %all-reduce.14.cloned.1.call-update) | async-done | bytes 2097168 | tf_op jit(solution)/shard_map/psum | solution.py:47
  259.1 2.1 fusion.4
  261.2 13.6 %all-reduce = (f32[1024]{0:T(1024)S(1)}, f32[1024]{0:T(1024)S(1)}) all-reduce(f32[1024]{0:T(1024)S(1)} %get-tuple-element.3, f32[1024]{0:T(1024)S(1)} %get-tuple-element.2), channel_id=1, replica_groups=mesh['dp'=4,'tensor'=8] {'tensor'}, use_global_device_ids=true, to_apply=%region_1.0 | all-reduce | flops 2048 | bytes 16384 | tf_op jit(solution)/shard_map/psum | solution.py:40
  274.9 2.1 multiply_reduce_fusion.5
  277.0 11.8 %psum.140 = f32[1024]{0:T(1024)S(1)} all-reduce(f32[1024]{0:T(1024)S(1)} %multiply_reduce_fusion.5), channel_id=1, replica_groups=mesh['dp'=4,'tensor'=8] {'tensor'}, use_global_device_ids=true, to_apply=%region_11.0 | all-reduce | flops 1024 | bytes 8192 | tf_op jit(solution)/shard_map/psum | solution.py:40
  288.8 6.8 fusion.10
  295.5 0.0 all-reduce.16.cloned.1.call-update
  295.6 0.2 all-reduce.18.cloned.1.call-start
  295.8 58.9 %all-reduce.16.cloned.1.call-done = f32[512,1024]{1,0:T(8,128)} async-done(((f32[512,1024]{1,0:T(8,128)}), f32[512,1024]{1,0:T(8,128)}) %all-reduce.16.cloned.1.call-update) | async-done | bytes 2097168 | tf_op jit(solution)/shard_map/psum | solution.py:46
  354.7 6.4 fusion.16
  361.1 0.0 all-reduce.18.cloned.1.call-update
  361.1 0.0 all-reduce.20.cloned.1.call-start
  361.2 85.2 %all-reduce.18.cloned.1.call-done = f32[512,1024]{1,0:T(8,128)} async-done(((f32[512,1024]{1,0:T(8,128)}), f32[512,1024]{1,0:T(8,128)}) %all-reduce.18.cloned.1.call-update) | async-done | bytes 2097168 | tf_op jit(solution)/shard_map/psum | solution.py:47
  446.4 3.1 multiply_reduce_fusion.4
  449.4 13.4 %psum.143 = f32[1024]{0:T(1024)S(1)} all-reduce(f32[1024]{0:T(1024)S(1)} %multiply_reduce_fusion.4), channel_id=1, replica_groups=mesh['dp'=4,'tensor'=8] {'tensor'}, use_global_device_ids=true, to_apply=%region_15.0 | all-reduce | flops 1024 | bytes 8192 | tf_op jit(solution)/shard_map/psum | solution.py:49
  462.8 4.6 multiply_reduce_fusion.3
  467.4 11.8 %psum.144 = f32[1024]{0:T(1024)S(1)} all-reduce(f32[1024]{0:T(1024)S(1)} %get-tuple-element.10), channel_id=1, replica_groups=mesh['dp'=4,'tensor'=8] {'tensor'}, use_global_device_ids=true, to_apply=%region_17.0 | all-reduce | flops 1024 | bytes 8192 | tf_op jit(solution)/shard_map/psum | solution.py:40
  479.2 3.0 multiply_add_fusion.2
  482.2 1.3 copy-done.3
  483.5 4.9 fusion.17
  488.4 0.3 all-reduce.22.cloned.1.call-start
  488.7 58.9 %all-reduce.20.cloned.1.call-done = f32[512,1024]{1,0:T(8,128)} async-done(((f32[512,1024]{1,0:T(8,128)}), f32[512,1024]{1,0:T(8,128)}) %all-reduce.20.cloned.1.call-update) | async-done | bytes 2097168 | tf_op jit(solution)/shard_map/psum | solution.py:46
  547.6 6.4 fusion.18
  554.0 0.0 all-reduce.22.cloned.1.call-update
  554.0 0.0 all-reduce.24.cloned.1.call-start
  554.0 85.2 %all-reduce.22.cloned.1.call-done = f32[512,1024]{1,0:T(8,128)} async-done(((f32[512,1024]{1,0:T(8,128)}), f32[512,1024]{1,0:T(8,128)}) %all-reduce.22.cloned.1.call-update) | async-done | bytes 2097168 | tf_op jit(solution)/shard_map/psum | solution.py:47
  639.3 2.6 multiply_reduce_fusion.2
  641.9 13.4 %psum.147 = f32[1024]{0:T(1024)S(1)} all-reduce(f32[1024]{0:T(1024)S(1)} %multiply_reduce_fusion.2), channel_id=1, replica_groups=mesh['dp'=4,'tensor'=8] {'tensor'}, use_global_device_ids=true, to_apply=%region_21.0 | all-reduce | flops 1024 | bytes 8192 | tf_op jit(solution)/shard_map/psum | solution.py:49
  655.3 5.1 multiply_reduce_fusion.1
  660.4 11.8 %psum.148 = f32[1024]{0:T(1024)S(1)} all-reduce(f32[1024]{0:T(1024)S(1)} %get-tuple-element.8), channel_id=1, replica_groups=mesh['dp'=4,'tensor'=8] {'tensor'}, use_global_device_ids=true, to_apply=%region_23.0 | all-reduce | flops 1024 | bytes 8192 | tf_op jit(solution)/shard_map/psum | solution.py:40
  672.2 7.1 fusion.9
  679.3 0.0 all-reduce.26.cloned.1.call-start
  679.4 59.1 %all-reduce.24.cloned.1.call-done = f32[512,1024]{1,0:T(8,128)} async-done(((f32[512,1024]{1,0:T(8,128)}), f32[512,1024]{1,0:T(8,128)}) %all-reduce.24.cloned.1.call-update) | async-done | bytes 2097168 | tf_op jit(solution)/shard_map/psum | solution.py:46
  738.5 6.4 fusion.19
  744.9 0.0 all-reduce.26.cloned.1.call-update
  744.9 0.3 reduce-scatter.2.cloned.1.call-start
  745.2 85.0 %all-reduce.26.cloned.1.call-done = f32[512,1024]{1,0:T(8,128)} async-done(((f32[512,1024]{1,0:T(8,128)}), f32[512,1024]{1,0:T(8,128)}) %all-reduce.26.cloned.1.call-update) | async-done | bytes 2097168 | tf_op jit(solution)/shard_map/psum | solution.py:47
  830.2 3.6 multiply_reduce_fusion
  833.8 13.4 %psum.151 = f32[1024]{0:T(1024)S(1)} all-reduce(f32[1024]{0:T(1024)S(1)} %multiply_reduce_fusion), channel_id=1, replica_groups=mesh['dp'=4,'tensor'=8] {'tensor'}, use_global_device_ids=true, to_apply=%region_27.0 | all-reduce | flops 1024 | bytes 8192 | tf_op jit(solution)/shard_map/psum | solution.py:49
  847.2 4.0 fusion.7
  851.2 1.3 copy-done.4
  852.5 8.2 convolution_multiply_fusion
  860.8 39.0 %reduce-scatter.2.cloned.1.call-done = f32[128,512]{1,0:T(8,128)} async-done(((f32[1024,512]{1,0:T(8,128)}), f32[128,512]{1,0:T(8,128)}) %reduce-scatter.2.cloned.1.call-update) | async-done | bytes 262160 | tf_op jit(solution)/shard_map/reduce_scatter | solution.py:57
  (22 shorter events, 0.1 us)
Async XLA Ops:
  8.0 4.7 copy-start
  8.0 79.7 %all-reduce.28.cloned.1.call-start = ((), (), s32[]{:S(2)}) async-start(), calls=%async_computation.11 | async-start | bytes 4194304 | tf_op jit(solution)/shard_map/psum | solution.py:23
  23.3 1.0 copy-start.5
  23.3 75.8 %all-gather.2.cloned.1.call-start = ((), (), s32[]{:S(2)}) async-start(), calls=%async_computation.1 | async-start | bytes 2621440 | tf_op jit(solution)/shard_map/all_gather | solution.py:36
  25.4 141.0 %all-reduce.12.cloned.1.call-start = ((), (), s32[]{:S(2)}) async-start(), calls=%async_computation.2 | async-start | bytes 4194304 | tf_op jit(solution)/shard_map/psum | solution.py:46
  88.6 2.3 copy-start.6
  105.6 153.5 %all-reduce.14.cloned.1.call-start = ((), (), s32[]{:S(2)}) async-start(), calls=%async_computation.3 | async-start | bytes 4194304 | tf_op jit(solution)/shard_map/psum | solution.py:47
  172.8 86.3 %copy-start.2 = (f32[1024,512]{0,1:T(8,128)S(1)}, f32[1024,512]{0,1:T(8,128)}, u32[]{:S(2)}) copy-start(f32[1024,512]{0,1:T(8,128)} %all-gather.2.cloned.1.call-done) | copy-start | bytes 6291460
  172.8 181.9 %all-reduce.16.cloned.1.call-start = ((), (), s32[]{:S(2)}) async-start(), calls=%async_computation.4 | async-start | bytes 4194304 | tf_op jit(solution)/shard_map/psum | solution.py:46
  295.6 150.8 %all-reduce.18.cloned.1.call-start = ((), (), s32[]{:S(2)}) async-start(), calls=%async_computation.5 | async-start | bytes 4194304 | tf_op jit(solution)/shard_map/psum | solution.py:47
  361.1 186.4 %all-reduce.20.cloned.1.call-start = ((), (), s32[]{:S(2)}) async-start(), calls=%async_computation.6 | async-start | bytes 4194304 | tf_op jit(solution)/shard_map/psum | solution.py:46
  482.2 1.3 copy-start.3
  488.4 150.9 %all-reduce.22.cloned.1.call-start = ((), (), s32[]{:S(2)}) async-start(), calls=%async_computation.7 | async-start | bytes 4194304 | tf_op jit(solution)/shard_map/psum | solution.py:47
  554.0 184.5 %all-reduce.24.cloned.1.call-start = ((), (), s32[]{:S(2)}) async-start(), calls=%async_computation.8 | async-start | bytes 4194304 | tf_op jit(solution)/shard_map/psum | solution.py:46
  679.3 150.8 %all-reduce.26.cloned.1.call-start = ((), (), s32[]{:S(2)}) async-start(), calls=%async_computation.9 | async-start | bytes 4194304 | tf_op jit(solution)/shard_map/psum | solution.py:47
  744.9 154.8 %reduce-scatter.2.cloned.1.call-start = ((), (), s32[]{:S(2)}) async-start(), calls=%async_computation.10 | async-start | bytes 2359296 | tf_op jit(solution)/shard_map/reduce_scatter | solution.py:57
  851.2 1.3 copy-start.4
  852.5 47.2 %copy-start.1 = (bf16[1792,64]{0,1:T(8,128)(2,1)S(1)}, bf16[1792,64]{0,1:T(8,128)(2,1)}, u32[]{:S(2)}) copy-start(bf16[1792,64]{0,1:T(8,128)(2,1)} %param.9) | copy-start | bytes 688132
Sparse Core Ops, SparseCore 0:
  23.4 64.2 all-reduce.27
  105.7 60.6 all-reduce.11
  295.7 58.9 all-reduce.15
  488.5 58.9 all-reduce.19
  679.5 58.9 all-reduce.23
  860.9 38.7 reduce-scatter.1
Sparse Core Ops, SparseCore 1:
  25.5 48.2 all-gather.1
  172.9 86.2 all-reduce.13
  361.2 85.1 all-reduce.17
  554.1 85.1 all-reduce.21
  745.0 85.1 all-reduce.25
where the time goes:
time: 911 us; the launch traced here: 908 us
  waiting for transfers between devices  637 us (70%)
  blocking collectives  132 us (14%)
  matrix products  82.6 us (9%)
  other arithmetic  32.5 us (4%)
  between operations  16.8 us (2%)
    psum x4, waiting for transfers between devices, per_device(): outer = lax.psum(contract_first(sketch, inner), 'dp')  299 us
    psum x4, waiting for transfers between devices, per_device(): inner = lax.psum(jnp.dot(sketch, direction, precision=high), 'tensor')  237 us
    psum x1, waiting for transfers between devices, per_device(): in_proj, out_proj = lax.psum((in_part, out_part), 'tensor')  62 us
    psum x4, blocking collectives, column_norm(): return lax.psum(jnp.sum(values * values, axis=0), 'tensor')  49 us
    psum x1, blocking collectives, per_device(): total_sq = lax.psum(jnp.sum(sketch * sketch), ('dp', 'tensor'))  42.5 us
    psum x3, blocking collectives, per_device(): bend = lax.psum(jnp.sum(direction * image, axis=0), 'tensor')  40.1 us
    reduce_scatter x1, waiting for transfers between devices, per_device(): lax.psum_scatter(contract_first(solution, sketch.T) * scale, 'tensor', sc...  39 us
    dot_general x5, matrix products, contract_first(): lax.dot_general(left, right, (((0,), (0,)), ((), ())), precision=lax.Prec...  33.9 us
  transfers between devices with their start and end apart: 11, of which 10 were waited for; matrix products, arithmetic and copies ran while one was open for 1% of the time, Pallas kernels for 0%

commit v1 on v0

v1 whole, which is shorter than its diff:
```python
import functools

import jax
import jax.numpy as jnp
from jax import lax
from jax.experimental import pallas as pl
from jax.experimental.pallas import tpu as pltpu
from jax.sharding import PartitionSpec as P

ITERS = 4
EX_DEV = 512
MOST = 16
LANES = 128
WINDOW = 256
F32 = jnp.float32
BF16 = jnp.bfloat16
MIB = 1024 * 1024


def split2(values):
    high = values.astype(BF16)
    low = (values - high.astype(F32)).astype(BF16)
    return high, low


def dot_nn(left, right):
    return lax.dot_general(left, right, (((1,), (0,)), ((), ())), preferred_element_type=F32)


def dot_nt(left, right):
    return lax.dot_general(left, right, (((1,), (1,)), ((), ())), preferred_element_type=F32)


def project_kernel(order_ref, act_ref, grad_ref, wi_ref, wo_ref, out_ref):
    del order_ref
    out_ref[...] = dot_nn(act_ref[...], wi_ref[...]) + dot_nn(grad_ref[...], wo_ref[...])


def project(order, activations, out_grads, w_in, w_out, block):
    steps = order.shape[0]
    feats, hidden = activations.shape[1], out_grads.shape[1]
    lanes = w_in.shape[1]
    return pl.pallas_call(
        project_kernel,
        out_shape=jax.ShapeDtypeStruct((steps * block, lanes), F32),
        grid_spec=pltpu.PrefetchScalarGridSpec(
            num_scalar_prefetch=1,
            grid=(steps,),
            in_specs=[
                pl.BlockSpec((block, feats), lambda i, order: (order[i], 0)),
                pl.BlockSpec((block, hidden), lambda i, order: (order[i], 0)),
                pl.BlockSpec((feats, lanes), lambda i, order: (0, 0)),
                pl.BlockSpec((hidden, lanes), lambda i, order: (0, 0)),
            ],
            out_specs=pl.BlockSpec((block, lanes), lambda i, order: (i, 0)),
        ),
        compiler_params=pltpu.CompilerParams(vmem_limit_bytes=40 * MIB),
        cost_estimate=pl.CostEstimate(
            flops=2 * steps * block * (feats + hidden) * lanes,
            bytes_accessed=2 * steps * block * (feats + hidden),
            transcendentals=0,
        ),
    )(order, activations, out_grads, w_in, w_out)


def build_kernel(
    ranks, piece, ex_block,
    offs_ref, first_ref, near_ref, far_ref, ids_ref, pick_ref, b_ref,
    high_ref, low_ref, inner_ref, sq_ref,
    out_high, out_low, in_both, rows, sketch,
):
    step = pl.program_id(0)
    half_ranks = pick_ref.shape[0]
    pieces = near_ref.shape[0] // piece

    @pl.when(step == 0)
    def _():
        lane = lax.broadcasted_iota(jnp.int32, (piece, LANES), 1)
        for source, base in ((near_ref, 0), (far_ref, pieces)):
            for k in range(pieces):
                values = source[k * piece:(k + 1) * piece, :]
                at = pl.multiple_of(offs_ref[base + k], piece)
                high, low = split2(values)
                out_high[:, pl.ds(at, piece)] = dot_nt(pick_ref[...], high).astype(BF16)
                out_low[:, pl.ds(at, piece)] = dot_nt(pick_ref[...], low).astype(BF16)
                twice = jnp.where(lane < ranks, values, pltpu.roll(values, ranks, 1))
                high, low = split2(twice)
                in_both[pl.ds(at, piece), 0:LANES] = high
                in_both[pl.ds(at, piece), LANES:2 * LANES] = low
        sq_ref[...] = jnp.zeros_like(sq_ref)

    group = rows.shape[1] // half_ranks
    lane = lax.broadcasted_iota(jnp.int32, (group, LANES), 1)

    def one_group(g, slot):
        number = step * (ex_block // group) + g
        at = pl.multiple_of(first_ref[number] * LANES, LANES)
        ids = ids_ref[0:1, pl.ds(at, WINDOW)]
        oh = out_high[:, pl.ds(at, WINDOW)]
        ol = out_low[:, pl.ds(at, WINDOW)]
        zero = jnp.zeros_like(oh)
        masks = [
            jnp.broadcast_to((ids == number * group + e).astype(F32), oh.shape).astype(BF16)
            for e in range(group)
        ]
        del zero
        left = jnp.concatenate([oh * m for m in masks] + [ol * m for m in masks], axis=0)
        res = dot_nn(left, in_both[pl.ds(at, WINDOW), :])
        top = group * half_ranks
        rows[slot] = (
            (res[:top, :LANES] + res[top:, :LANES]) + (res[:top, LANES:] + res[top:, LANES:])
        )
        to = pl.multiple_of(g * group, group)
        for pair in range(half_ranks // 2):
            even = rows[slot, pl.ds(2 * pair, group, stride=half_ranks), :]
            odd = rows[slot, pl.ds(2 * pair + 1, group, stride=half_ranks), :]
            sketch[pl.ds(to, group), pair * LANES:(pair + 1) * LANES] = jnp.where(
                lane < ranks, even, odd
            )

    slots = rows.shape[0]

    @pl.loop(0, ex_block // group // slots)
    def _(turn):
        for slot in range(slots):
            one_group(turn * slots + slot, slot)

    values = sketch[...]
    high, low = split2(values)
    high_ref[...] = high
    low_ref[...] = low
    sq = jnp.sum((values * values).reshape(ex_block // 8, 8, -1), axis=0)
    total = sq[:, 0:LANES]
    for k in range(1, values.shape[1] // LANES):
        total = total + sq[:, k * LANES:(k + 1) * LANES]
    sq_ref[...] += total
    b_high, b_low = split2(b_ref[...])
    both = dot_nt(jnp.concatenate([b_high, b_low], axis=0), high)
    count = b_high.shape[0]
    inner_ref[...] = both[:count] + both[count:] + dot_nt(b_high, low)


def build(offs, first, near, far, ids, pick, b, ranks, piece):
    tokens = ids.shape[1]
    half_ranks = pick.shape[0]
    comps = b.shape[1]
    queries = b.shape[0]
    ex_block = 128
    group = 8
    whole = lambda i, *_: (0, 0)
    return pl.pallas_call(
        functools.partial(build_kernel, ranks, piece, ex_block),
        out_shape=(
            jax.ShapeDtypeStruct((EX_DEV, comps), BF16),
            jax.ShapeDtypeStruct((EX_DEV, comps), BF16),
            jax.ShapeDtypeStruct((queries, EX_DEV), F32),
            jax.ShapeDtypeStruct((8, LANES), F32),
        ),
        grid_spec=pltpu.PrefetchScalarGridSpec(
            num_scalar_prefetch=2,
            grid=(EX_DEV // ex_block,),
            in_specs=[
                pl.BlockSpec(near.shape, whole),
                pl.BlockSpec(far.shape, whole),
                pl.BlockSpec(ids.shape, whole),
                pl.BlockSpec(pick.shape, whole),
                pl.BlockSpec(b.shape, whole),
            ],
            out_specs=[
                pl.BlockSpec((ex_block, comps), lambda i, *_: (i, 0)),
                pl.BlockSpec((ex_block, comps), lambda i, *_: (i, 0)),
                pl.BlockSpec((queries, ex_block), lambda i, *_: (0, i)),
                pl.BlockSpec((8, LANES), whole),
            ],
            scratch_shapes=[
                pltpu.VMEM((half_ranks, tokens), BF16),
                pltpu.VMEM((half_ranks, tokens), BF16),
                pltpu.VMEM((tokens, 2 * LANES), BF16),
                pltpu.VMEM((2, group * half_ranks, LANES), F32),
                pltpu.VMEM((ex_block, comps), F32),
            ],
        ),
        compiler_params=pltpu.CompilerParams(vmem_limit_bytes=40 * MIB),
        cost_estimate=pl.CostEstimate(
            flops=2 * EX_DEV * half_ranks * 2 * WINDOW * 2 * LANES + 6 * EX_DEV * queries * comps,
            bytes_accessed=4 * EX_DEV * comps + 8 * near.shape[0] * LANES,
            transcendentals=0,
        ),
    )(offs, first, near, far, ids, pick, b)


def column(values, k):
    return values[:, k:k + 1]


def lanes_of(columns, shape):
    lane = lax.broadcasted_iota(jnp.int32, shape, 1)
    out = jnp.zeros(shape, F32)
    for k, one in enumerate(columns):
        out = jnp.where(lane == k, one, out)
    return out


def begin(first, examples, comps_all, mine, other, s_prev, state):
    total = mine + other
    inner, stats = total[:, :examples], total[:, examples:]
    norm = column(stats, 0)
    if first:
        damping = 0.1 * column(stats, 1) / (examples * comps_all)
        s, length, beta = inner, norm, None
    else:
        beta = norm / column(state, 0)
        s = inner + beta * s_prev
        length = norm + 2.0 * beta * column(stats, 1) + beta * beta * column(state, 1)
        damping = column(state, 2)
    bend = jnp.sum(s * s, axis=1, keepdims=True) / examples + damping * length
    return s, norm, length, damping, beta, norm / bend


def step_kernel(first, planes, examples, comps_all, *refs):
    refs = list(refs)
    take = lambda n: [refs.pop(0) for _ in range(n)]
    mine_ref, other_ref, r_ref = take(3)
    if not first:
        p_ref, x_ref, s_ref, y_ref, state_ref = take(5)
    highs, lows = take(planes), take(planes)
    msg_out, r_out, p_out, x_out, s_out, y_out, state_out = take(7)
    s_two, z_acc, stats_acc, scal = take(4)
    step = pl.program_id(0)
    count = mine_ref.shape[0]

    @pl.when(step == 0)
    def _():
        s, norm, length, damping, beta, alpha = begin(
            first, examples, comps_all, mine_ref[...], other_ref[...],
            None if first else s_ref[...], None if first else state_ref[...],
        )
        s_out[...] = s
        y_out[...] = alpha * s if first else y_ref[...] + alpha * s
        high, low = split2(s)
        s_two[0:count, :] = high
        s_two[count:2 * count, :] = low
        state_out[...] = lanes_of([norm, length, damping], state_out.shape)
        scal[...] = lanes_of([alpha, damping] + ([] if first else [beta]), scal.shape)
        z_acc[...] = jnp.zeros_like(z_acc)
        stats_acc[...] = jnp.zeros_like(stats_acc)

    alpha, damping = scal[:, 0:1], scal[:, 1:2]
    r = r_ref[...]
    if first:
        p = r
        x_out[...] = alpha * p
    else:
        p = r + scal[:, 2:3] * p_ref[...]
        x_out[...] = x_ref[...] + alpha * p
    p_out[...] = p
    q = jnp.zeros(r.shape, F32)
    for k in range(planes):
        part = slice(k * EX_DEV, (k + 1) * EX_DEV)
        both = dot_nn(s_two[:, part], highs[k][...])
        q = q + both[:count] + both[count:] + dot_nn(s_two[0:count, part], lows[k][...])
    r_new = r - alpha * (q / examples + damping * p)
    r_out[...] = r_new
    high, low = split2(r_new)
    stacked = jnp.concatenate([high, low], axis=0)
    for k in range(planes):
        part = slice(k * EX_DEV, (k + 1) * EX_DEV)
        both = dot_nt(stacked, highs[k][...])
        z_acc[:, part] += both[:count] + both[count:] + dot_nt(high, lows[k][...])
    stats_acc[...] += lanes_of(
        [
            jnp.sum(r_new * r_new, axis=1, keepdims=True),
            jnp.sum(r_new * p, axis=1, keepdims=True),
        ],
        stats_acc.shape,
    )

    @pl.when(step == pl.num_programs(0) - 1)
    def _():
        msg_out[:, 0:examples] = z_acc[...]
        msg_out[:, examples:] = stats_acc[...]


def one_step(first, examples, comps_all, mine, other, r, rest, highs, lows):
    planes = len(highs)
    count, comps = r.shape
    block = 256
    whole = lambda i: (0, 0)
    along = lambda i: (0, i)
    full = lambda a: pl.BlockSpec(a.shape, whole)
    piece = pl.BlockSpec((count, block), along)
    in_specs = [full(mine), full(other), piece]
    if not first:
        p, x, s, y, state = rest
        in_specs += [piece, piece, full(s), full(y), full(state)]
    in_specs += [pl.BlockSpec((EX_DEV, block), along)] * (2 * planes)
    wide = jax.ShapeDtypeStruct((count, examples), F32)
    long = jax.ShapeDtypeStruct((count, comps), F32)
    small = jax.ShapeDtypeStruct((count, LANES), F32)
    message = jax.ShapeDtypeStruct((count, examples + LANES), F32)
    return pl.pallas_call(
        functools.partial(step_kernel, first, planes, examples, comps_all),
        out_shape=(message, long, long, long, wide, wide, small),
        grid=(comps // block,),
        in_specs=in_specs,
        out_specs=[full(message), piece, piece, piece, full(wide), full(wide), full(small)],
        scratch_shapes=[
            pltpu.VMEM((2 * count, examples), BF16),
            pltpu.VMEM((count, examples), F32),
            pltpu.VMEM((count, LANES), F32),
            pltpu.VMEM((count, LANES), F32),
        ],
        compiler_params=pltpu.CompilerParams(vmem_limit_bytes=40 * MIB),
        cost_estimate=pl.CostEstimate(
            flops=12 * count * examples * comps,
            bytes_accessed=4 * examples * comps,
            transcendentals=0,
        ),
    )(mine, other, r, *rest, *highs, *lows)


def last_kernel(examples, comps_all, mine_ref, other_ref, r_ref, p_ref, x_ref, s_ref, y_ref, state_ref, x_out, y_out):
    s, _, _, _, beta, alpha = begin(
        False, examples, comps_all, mine_ref[...], other_ref[...], s_ref[...], state_ref[...]
    )
    scale = 1.0 / jnp.sqrt(F32(comps_all))
    y_out[...] = (y_ref[...] + alpha * s) * scale
    x_out[...] = x_ref[...] + alpha * (r_ref[...] + beta * p_ref[...])


def last_step(examples, comps_all, *arrays):
    x, y = arrays[4], arrays[6]
    return pl.pallas_call(
        functools.partial(last_kernel, examples, comps_all),
        out_shape=(jax.ShapeDtypeStruct(x.shape, F32), jax.ShapeDtypeStruct(y.shape, F32)),
        compiler_params=pltpu.CompilerParams(vmem_limit_bytes=40 * MIB),
    )(*arrays)


def per_device(n_dp, n_t, activations, out_grads, proj_in, proj_out, example_ids, queries):
    tokens = activations.shape[0]
    ranks = proj_in.shape[1]
    comps_all = proj_in.shape[1] * proj_out.shape[1]
    examples = EX_DEV * n_dp
    n_c = n_t // 2
    bits = n_c.bit_length() - 1
    j = lax.axis_index("tensor")
    i = lax.axis_index("dp")
    chip, core = j // 2, j % 2

    def swap(values, mask):
        return lax.ppermute(values, "tensor", [(a, a ^ mask) for a in range(n_t)])

    def shift(values, by):
        return lax.ppermute(values, "dp", [(a, (a + by) % n_dp) for a in range(n_dp)])

    near_chip = [chip ^ k for k in range(n_c)]

    q_chip = queries.shape[0] // n_c
    slots = [lax.dynamic_slice_in_dim(queries, near_chip[k] * q_chip, q_chip, 0) for k in range(n_c)]
    slots = [slots[0]] + [swap(slots[k], 2 * k) for k in range(1, n_c)]
    b = jnp.concatenate(slots, axis=1)

    ids_all = lax.all_gather(example_ids, "dp", axis=0, tiled=True)
    group = 8
    bounds = group * jnp.arange(EX_DEV // group, dtype=jnp.int32)
    starts = jnp.sum((ids_all[:, None, :] < bounds[None, :, None]).astype(jnp.int32), axis=-1)
    firsts = jnp.minimum(starts // LANES, (tokens - WINDOW) // LANES)

    w_in = jnp.pad(proj_in, ((0, 0), (0, ranks)))
    w_out = jnp.pad(proj_out, ((0, 0), (ranks, 0)))
    share = tokens // n_t
    blocks = jnp.stack(near_chip).astype(jnp.int32) * 2
    give = project(blocks + 1 - core, activations, out_grads, w_in, w_out, share)
    keep = project(blocks + core, activations, out_grads, w_in, w_out, share)
    kept = (keep + swap(give, 1)).reshape((n_c, share, LANES))
    half = share // 2
    own = []
    orders = (list(range(bits)), list(range(bits))[::-1])
    for part, order in enumerate(orders):
        held = {k: kept[k, part * half:(part + 1) * half] for k in range(n_c)}
        for bit in order:
            low = [k for k in held if not (k >> bit) & 1]
            came = swap(jnp.stack([held[k | (1 << bit)] for k in low]), 2 << bit)
            held = {k: held[k] + came[n] for n, k in enumerate(low)}
        own.append(held[0])

    rings = [jnp.concatenate(own, axis=0)]
    for _ in range(n_dp - 1):
        rings.append(shift(rings[-1], 1))
    slot_orders = []
    for order in orders:
        ks = [0]
        for bit in order[::-1]:
            ks = ks + [k | (1 << bit) for k in ks]
        slot_orders.append(ks)
    offs = jnp.stack(
        [
            (near_chip[k] * 2 + which) * share + part * half
            for which in (core, 1 - core)
            for part in range(2)
            for k in slot_orders[part]
        ]
    ).astype(jnp.int32)

    per = comps_all // ranks // n_t
    wanted = jnp.stack([(near_chip[k] * 2 + core) * per + a for k in range(n_c) for a in range(per)]) + ranks
    pick = (wanted[:, None] == jnp.arange(LANES)[None, :]).astype(BF16)

    highs, lows, inners, squares = [], [], [], []
    for away in range(n_dp):
        gathered = []
        for part, order in enumerate(orders):
            held = rings[away][part * half:(part + 1) * half]
            for bit in order[::-1]:
                held = jnp.concatenate([held, swap(held, 2 << bit)], axis=0)
            gathered.append(held)
        near = jnp.concatenate(gathered, axis=0)
        far = swap(near, 1)
        plane = (i - away) % n_dp
        ids = lax.dynamic_slice_in_dim(ids_all, plane, 1, 0)
        first = lax.dynamic_index_in_dim(firsts, plane, 0, keepdims=False)
        high, low, inner, square = build(offs, first, near, far, ids, pick, b, ranks, half)
        highs.append(high)
        lows.append(low)
        inners.append(inner)
        squares.append(square)

    square = jnp.sum(jnp.stack(squares))
    stats = jnp.concatenate(
        [
            jnp.sum(b * b, axis=1, keepdims=True),
            jnp.broadcast_to(square, (q_chip, 1)),
            jnp.zeros((q_chip, LANES - 2), F32),
        ],
        axis=1,
    )
    message = jnp.concatenate(inners + [stats], axis=1)
    r, rest = b, ()
    for step in range(ITERS - 1):
        other = swap(message, 1)
        message, r, p, x, s, y, state = one_step(
            step == 0, examples, comps_all, message, other, r, rest, highs, lows
        )
        rest = (p, x, s, y, state)
    other = swap(message, 1)
    x, y = last_step(examples, comps_all, message, other, r, *rest)

    per_slot = comps_all // n_t
    own_x = jnp.zeros((n_c * q_chip, per_slot), F32)
    for k in range(n_c):
        part = x[:, k * per_slot:(k + 1) * per_slot]
        if k:
            part = swap(part, 2 * k)
        own_x = lax.dynamic_update_slice_in_dim(own_x, part, near_chip[k] * q_chip, 0)
    q_plane = n_c * q_chip
    out = jnp.zeros((per_slot, n_dp * q_plane), F32)
    ring = own_x
    for away in range(n_dp):
        if away:
            ring = shift(ring, 1)
        out = lax.dynamic_update_slice_in_dim(out, ring.T, ((i - away) % n_dp) * q_plane, 1)

    part_q = q_chip // 2
    mine = lax.dynamic_slice_in_dim(y, core * part_q, part_q, 0)
    by_plane = jnp.zeros((n_dp, part_q, EX_DEV), F32)
    for away in range(n_dp):
        part = mine[:, away * EX_DEV:(away + 1) * EX_DEV]
        if away:
            part = shift(part, -away)
        by_plane = lax.dynamic_update_slice(by_plane, part[None], ((i + away) % n_dp, 0, 0))
    by_chip = jnp.zeros((n_c, part_q, EX_DEV), F32)
    for k in range(n_c):
        part = lax.dynamic_slice_in_dim(by_plane, near_chip[k], 1, 0)
        if k:
            part = swap(part, 2 * k)
        by_chip = lax.dynamic_update_slice(by_chip, part, (near_chip[k], 0, 0))
    n_half = n_c // 2
    give = lax.dynamic_slice_in_dim(by_chip, (1 - core) * n_half, n_half, 0)
    keep = lax.dynamic_slice_in_dim(by_chip, core * n_half, n_half, 0)
    came = swap(give, 1)
    scores = jnp.zeros((n_half, 2, part_q, EX_DEV), F32)
    scores = lax.dynamic_update_slice(scores, keep[:, None], (0, core, 0, 0))
    scores = lax.dynamic_update_slice(scores, came[:, None], (0, 1 - core, 0, 0))
    return (out, scores.reshape((n_half * q_chip, EX_DEV)))


def solution(mesh):
    in_specs = (
        P("dp", "tensor"),
        P("dp", "tensor"),
        P("tensor", None),
        P("tensor", None),
        P("dp", None),
        P("dp", "tensor"),
    )
    out_specs = (P("tensor", None), P("tensor", "dp"))
    body = functools.partial(per_device, mesh.shape["dp"], mesh.shape["tensor"])
    return jax.shard_map(body, mesh=mesh, in_specs=in_specs, out_specs=out_specs, check_vma=False)
```

time: 911 us -> 342 us (0.38)
  waiting for transfers between devices: 637 us -> 87 us
  Pallas kernels: 0 us -> 141 us
  blocking collectives: 132 us -> 13.4 us
  matrix products: 82.6 us -> 0 us
  local copies, waits for them, and re-layouts: 5.51 us -> 52.5 us
  starting transfers between devices: 1.92 us -> 38.6 us
  other arithmetic: 32.5 us -> 4.84 us
  between operations: 16.8 us -> 3.99 us
    psum x9 -> x0, waiting for transfers between devices: 598 us -> none  [the longest x4 299 us: per_device(): outer = lax.psum(contract_first(sketch, inner), 'dp')]
    pallas_call x0 -> x10, Pallas kernels: none -> 141 us  [the longest x4 79.1 us: build(): pl.pallas_call(functools.partial(build_kernel, ranks, piece, ex_block), o...]
    psum x8 -> x0, blocking collectives: 132 us -> none  [the longest x4 49 us: column_norm(): return lax.psum(jnp.sum(values * values, axis=0), 'tensor')]
    ppermute x0 -> x48, waiting for transfers between devices: none -> 87 us  [the longest x9 44.7 us: shift(): lax.ppermute(values, 'dp', [(a, (a + by) % n_dp) for a in range(n_dp)])]
    dot_general x12 -> x0, matrix products: 82.6 us -> none  [the longest x5 33.9 us: contract_first(): lax.dot_general(left, right, (((0,), (0,)), ((), ())), precision=lax.Prec...]
    reduce_scatter x1 -> x0, waiting for transfers between devices: 39 us -> none  [per_device(): lax.psum_scatter(contract_first(solution, sketch.T) * scale, 'tensor', sc...]
    ppermute x0 -> x48, starting transfers between devices: none -> 38.6 us  [the longest x39 33.2 us: swap(): return lax.ppermute(values, 'tensor', [(a, a ^ mask) for a in range(n_t)])]
    unnamed x15 -> x76, local copies, waits for them, and re-layouts: 4.6 us -> 36.8 us
  transfers between devices with their start and end apart: 11 -> 48, of which waited for: 10 -> 24; matrix products, arithmetic and copies ran while one was open for 1% -> 8% of each run, Pallas kernels for 0% -> 19%
where the time goes in v1:
time: 342 us; the launch traced here: 341 us
  Pallas kernels  141 us (41%)
  waiting for transfers between devices  87 us (25%)
  local copies, waits for them, and re-layouts  52.5 us (15%)
  starting transfers between devices  38.6 us (11%)
  blocking collectives  13.4 us (4%)
  other arithmetic  4.84 us (1%)
  between operations  3.99 us (1%)
    pallas_call x4, Pallas kernels, build(): pl.pallas_call(functools.partial(build_kernel, ranks, piece, ex_block), o...  79.1 us
    pallas_call x3, Pallas kernels, one_step(): pl.pallas_call(functools.partial(step_kernel, first, planes, examples, co...  48.7 us
    ppermute x9, waiting for transfers between devices, shift(): lax.ppermute(values, 'dp', [(a, (a + by) % n_dp) for a in range(n_dp)])  44.7 us
    ppermute x39, waiting for transfers between devices, swap(): return lax.ppermute(values, 'tensor', [(a, a ^ mask) for a in range(n_t)])  42.3 us
    unnamed x76, local copies, waits for them, and re-layouts  36.8 us
    ppermute x39, starting transfers between devices, swap(): return lax.ppermute(values, 'tensor', [(a, a ^ mask) for a in range(n_t)])  33.2 us
    all_gather x1, blocking collectives, per_device(): ids_all = lax.all_gather(example_ids, 'dp', axis=0, tiled=True)  13.4 us
    pallas_call x2, Pallas kernels, project(): pl.pallas_call(project_kernel, out_shape=jax.ShapeDtypeStruct((steps * bl...  12.3 us
  transfers between devices with their start and end apart: 48, of which 24 were waited for; matrix products, arithmetic and copies ran while one was open for 8% of the time, Pallas kernels for 19%

profile of v1, /device:TPU:0, one launch (start us, length us, event | category | flops | bytes accessed | tf_op | source)
XLA Modules:
  0.0 341.0 jit_solution(3670637364760094741)
XLA Ops:
  0.7 1.2 copy.25
  3.2 2.2 copy-done.10
  5.4 6.3 %shard_map.78 = f32[2048,128]{1,0:T(8,128)S(1)} custom-call(s32[4]{0:T(128)S(1)} %get-tuple-element.84.order_ref, bf16[4096,512]{1,0:T(8,128)(2,1)S(1)} %copy-done.10, bf16[4096,1792]{1,0:T(8,128)(2,1)} %grad_ref.3, bf16[512,128]{1,0:T(8,128)(2,1)S(1)} %pad.8.wi_ref, bf16[1792,128]{1,0:T(8,128)(2,1)S(1)} %pad.9.wo_ref), custom_call_target="tpu_custom_call" | custom-call | flops 1207959552 | bytes 9437184 | tf_op jit(solution)/shard_map/pallas_call | solution.py:43
  12.2 6.0 %shard_map.77 = f32[2048,128]{1,0:T(8,128)S(1)} custom-call(s32[4]{0:T(128)S(1)} %broadcast_add_fusion.1.order_ref, bf16[4096,512]{1,0:T(8,128)(2,1)S(1)} %copy-done.11, bf16[4096,1792]{1,0:T(8,128)(2,1)} %grad_ref.3, bf16[512,128]{1,0:T(8,128)(2,1)S(1)} %pad.8.wi_ref, bf16[1792,128]{1,0:T(8,128)(2,1)S(1)} %pad.9.wo_ref), custom_call_target="tpu_custom_call" | custom-call | flops 1207959552 | bytes 9437184 | tf_op jit(solution)/shard_map/pallas_call | solution.py:43
  18.5 2.6 collective-permute-start.1
  21.1 1.5 collective-permute-start.5
  24.1 2.7 collective-permute-start.12
  26.8 13.4 %all-gather = s32[4,1,4096]{2,1,0:T(1,128)S(1)} all-gather(s32[1,1,4096]{2,1,0:T(1,128)S(1)} %bitcast.112), channel_id=1, replica_groups=mesh['dp'=4,'tensor'=8] {'dp'}, dimensions={0}, use_global_device_ids=true | all-gather | bytes 81920 | tf_op jit(solution)/shard_map/all_gather | solution.py:364
  41.0 4.9 %collective-permute-done.2 = f32[1,256,128]{2,1,0:T(8,128)S(1)} collective-permute-done((f32[1,256,128]{2,1,0:T(8,128)S(1)}, f32[1,256,128]{2,1,0:T(8,128)S(1)}, u32[]{:S(2)}, u32[]{:S(2)}) %collective-permute-start.2) | collective-permute-done | bytes 131104 | tf_op jit(solution)/shard_map/ppermute | solution.py:352
  46.5 4.5 %collective-permute-done.3 = f32[256,128]{1,0:T(8,128)S(1)} collective-permute-done((f32[256,128]{1,0:T(8,128)S(1)}, f32[256,128]{1,0:T(8,128)S(1)}, u32[]{:S(2)}, u32[]{:S(2)}) %collective-permute-start.3) | collective-permute-done | bytes 131104 | tf_op jit(solution)/shard_map/ppermute | solution.py:352
  51.7 1.6 collective-permute-start.6
  53.2 5.5 %collective-permute-done.4 = f32[512,128]{1,0:T(8,128)S(1)} collective-permute-done((f32[512,128]{1,0:T(8,128)S(1)}, f32[512,128]{1,0:T(8,128)S(1)}, u32[]{:S(2)}, u32[]{:S(2)}) %collective-permute-start.4) | collective-permute-done | bytes 262176 | tf_op jit(solution)/shard_map/ppermute | solution.py:352
  58.8 1.4 collective-permute-done.6
  61.4 3.8 %collective-permute-done.7 = f32[256,128]{1,0:T(8,128)S(1)} collective-permute-done((f32[256,128]{1,0:T(8,128)S(1)}, f32[256,128]{1,0:T(8,128)S(1)}, u32[]{:S(2)}, u32[]{:S(2)}) %collective-permute-start.7) | collective-permute-done | bytes 131104 | tf_op jit(solution)/shard_map/ppermute | solution.py:352
  65.3 1.7 collective-permute-start.13
  67.1 1.2 multiply_reduce_fusion
  68.9 4.5 %collective-permute-done.13 = f32[512,128]{1,0:T(8,128)S(1)} collective-permute-done((f32[512,128]{1,0:T(8,128)S(1)}, f32[512,128]{1,0:T(8,128)S(1)}, u32[]{:S(2)}, u32[]{:S(2)}) %collective-permute-start.13) | collective-permute-done | bytes 262176 | tf_op jit(solution)/shard_map/ppermute | solution.py:355
  75.8 3.3 collective-permute-done.16
  80.7 1.8 collective-permute-start.15
  83.1 3.1 collective-permute-done.19
  86.9 1.2 collective-permute-start.20
  88.1 1.5 collective-permute-start.22
  93.2 5.5 %collective-permute-done.25 = f32[512,128]{1,0:T(8,128)S(1)} collective-permute-done((f32[512,128]{1,0:T(8,128)S(1)}, f32[512,128]{1,0:T(8,128)S(1)}, u32[]{:S(2)}, u32[]{:S(2)}) %collective-permute-start.25) | collective-permute-done | bytes 262176 | tf_op jit(solution)/shard_map/ppermute | solution.py:355
  99.9 1.6 collective-permute-start.23
  102.1 3.6 %collective-permute-done.26 = f32[256,128]{1,0:T(8,128)S(1)} collective-permute-done((f32[256,128]{1,0:T(8,128)S(1)}, f32[256,128]{1,0:T(8,128)S(1)}, u32[]{:S(2)}, u32[]{:S(2)}) %collective-permute-start.26) | collective-permute-done | bytes 131104 | tf_op jit(solution)/shard_map/ppermute | solution.py:352
  106.3 1.6 collective-permute-start.27
  112.0 1.6 collective-permute-done.27
  115.6 3.9 %collective-permute-done.29 = f32[512,128]{1,0:T(8,128)S(1)} collective-permute-done((f32[512,128]{1,0:T(8,128)S(1)}, f32[512,128]{1,0:T(8,128)S(1)}, u32[]{:S(2)}, u32[]{:S(2)}) %collective-permute-start.29) | collective-permute-done | bytes 262176 | tf_op jit(solution)/shard_map/ppermute | solution.py:352
  120.2 18.8 %shard_map.79 = (bf16[512,2048]{1,0:T(8,128)(2,1)S(1)}, bf16[512,2048]{1,0:T(8,128)(2,1)S(1)}, f32[64,512]{1,0:T(8,128)S(1)}, f32[8,128]{1,0:T(8,128)S(1)}) custom-call(s32[16]{0:T(128)S(1)} %stack.194.offs_ref, s32[64]{0:T(128)S(1)} %get-tuple-element.125.first_ref, f32[2048,128]{1,0:T(8,128)S(1)} %copy-done.24, ...), custom_call_target="tpu_custom_call" | custom-call | flops 4697620480 | bytes 6291456 | tf_op jit(solution)/shard_map/pallas_call | solution.py:151
  139.0 1.3 copy-done
  140.9 20.1 %shard_map.80 = (bf16[512,2048]{1,0:T(8,128)(2,1)S(1)}, bf16[512,2048]{1,0:T(8,128)(2,1)S(1)}, f32[64,512]{1,0:T(8,128)S(1)}, f32[8,128]{1,0:T(8,128)S(1)}) custom-call(s32[16]{0:T(128)S(1)} %stack.194.offs_ref, s32[64]{0:T(128)S(1)} %get-tuple-element.124.first_ref, f32[2048,128]{1,0:T(8,128)} %constant_dynamic-update-slice_fusion.6.near_ref, ...), custom_call_target="tpu_custom_call" | custom-call | flops 4697620480 | bytes 6291456 | tf_op jit(solution)/shard_map/pallas_call | solution.py:151
  161.0 1.3 copy-done.1
  162.3 1.4 copy-done.3
  165.6 20.1 %shard_map.81 = (bf16[512,2048]{1,0:T(8,128)(2,1)S(1)}, bf16[512,2048]{1,0:T(8,128)(2,1)S(1)}, f32[64,512]{1,0:T(8,128)S(1)}, f32[8,128]{1,0:T(8,128)S(1)}) custom-call(s32[16]{0:T(128)S(1)} %stack.194.offs_ref, s32[64]{0:T(128)S(1)} %get-tuple-element.123.first_ref, f32[2048,128]{1,0:T(8,128)} %constant_dynamic-update-slice_fusion.12.near_ref, ...), custom_call_target="tpu_custom_call" | custom-call | flops 4697620480 | bytes 6291456 | tf_op jit(solution)/shard_map/pallas_call | solution.py:151
  185.8 1.4 copy-done.4
  187.1 1.3 copy-done.6
  190.4 20.1 %shard_map.82 = (bf16[512,2048]{1,0:T(8,128)(2,1)S(1)}, bf16[512,2048]{1,0:T(8,128)(2,1)S(1)}, f32[64,512]{1,0:T(8,128)S(1)}, f32[8,128]{1,0:T(8,128)S(1)}) custom-call(s32[16]{0:T(128)S(1)} %stack.194.offs_ref, s32[64]{0:T(128)S(1)} %get-tuple-element.122.first_ref, f32[2048,128]{1,0:T(8,128)} %constant_dynamic-update-slice_fusion.18.near_ref, ...), custom_call_target="tpu_custom_call" | custom-call | flops 4697620480 | bytes 6291456 | tf_op jit(solution)/shard_map/pallas_call | solution.py:151
  210.5 1.3 copy-done.7
  211.8 1.4 copy-done.9
  215.2 1.1 concatenate.67.refs_0_
  216.8 1.6 collective-permute-done.31.refs_1_
  218.4 1.6 copy-done.2
  220.0 1.6 copy-done.5
  221.6 1.6 copy-done.8
  223.2 16.2 %shard_map.83 = (f32[64,2176]{1,0:T(8,128)S(1)}, f32[64,2048]{1,0:T(8,128)S(1)}, f32[64,2048]{1,0:T(8,128)S(1)}, f32[64,2048]{1,0:T(8,128)S(1)}, f32[64,2048]{1,...) custom-call(f32[64,2176]{1,0:T(8,128)S(1)} %concatenate.67.refs_0_, ...), custom_call_target="tpu_custom_call" | custom-call | flops 3221225472 | bytes 16777216 | tf_op jit(solution)/shard_map/pallas_call | solution.py:301
  239.9 1.6 collective-permute-done.32.refs_1_
  241.4 16.2 %shard_map.84 = (f32[64,2176]{1,0:T(8,128)S(1)}, f32[64,2048]{1,0:T(8,128)S(1)}, f32[64,2048]{1,0:T(8,128)S(1)}, f32[64,2048]{1,0:T(8,128)S(1)}, f32[64,2048]{1,...) custom-call(f32[64,2176]{1,0:T(8,128)S(1)} %get-tuple-element.57.refs_0_, ...), custom_call_target="tpu_custom_call" | custom-call | flops 3221225472 | bytes 16777216 | tf_op jit(solution)/shard_map/pallas_call | solution.py:301
  258.1 1.6 collective-permute-done.33.refs_1_
  259.7 16.2 %shard_map.85 = (f32[64,2176]{1,0:T(8,128)S(1)}, f32[64,2048]{1,0:T(8,128)S(1)}, f32[64,2048]{1,0:T(8,128)S(1)}, f32[64,2048]{1,0:T(8,128)S(1)}, f32[64,2048]{1,...) custom-call(f32[64,2176]{1,0:T(8,128)S(1)} %get-tuple-element.64.refs_0_, ...), custom_call_target="tpu_custom_call" | custom-call | flops 3221225472 | bytes 16777216 | tf_op jit(solution)/shard_map/pallas_call | solution.py:301
  279.6 1.6 collective-permute-done.34.other_ref
  286.0 2.0 collective-permute-start.43
  289.7 2.1 dynamic_update_slice.54
  292.7 1.7 collective-permute-start.37
  294.5 2.3 dynamic_update_slice.55
  297.0 1.1 dynamic_update_slice.56
  298.7 1.5 dynamic_update_slice.57
  300.2 1.6 collective-permute-start.38
  301.9 1.2 collective-permute-start.44
  303.0 1.5 collective-permute-start.45
  306.2 1.1 collective-permute-done.45
  307.3 7.0 %collective-permute-done.38 = f32[256,512]{0,1:T(8,128)S(1)} collective-permute-done((f32[256,512]{0,1:T(8,128)S(1)}, f32[256,512]{0,1:T(8,128)S(1)}, u32[]{:S(2)}, u32[]{:S(2)}) %collective-permute-start.38) | collective-permute-done | bytes 524320 | tf_op jit(solution)/shard_map/ppermute | solution.py:355
  314.8 12.6 %collective-permute-done.39 = f32[256,512]{0,1:T(8,128)S(1)} collective-permute-done((f32[256,512]{0,1:T(8,128)S(1)}, f32[256,512]{0,1:T(8,128)S(1)}, u32[]{:S(2)}, u32[]{:S(2)}) %collective-permute-start.39) | collective-permute-done | bytes 524320 | tf_op jit(solution)/shard_map/ppermute | solution.py:355
  327.6 12.0 %collective-permute-done.40 = f32[256,512]{0,1:T(8,128)S(1)} collective-permute-done((f32[256,512]{0,1:T(8,128)S(1)}, f32[256,512]{0,1:T(8,128)S(1)}, u32[]{:S(2)}, u32[]{:S(2)}) %collective-permute-start.40) | collective-permute-done | bytes 524320 | tf_op jit(solution)/shard_map/ppermute | solution.py:355
  339.7 1.3 copy-done.25
  (194 shorter events, 45.1 us)
Async XLA Ops:
  3.2 2.2 copy-start.10
  5.4 6.8 %copy-start.11 = (bf16[4096,512]{1,0:T(8,128)(2,1)S(1)}, bf16[4096,512]{1,0:T(8,128)(2,1)}, u32[]{:S(2)}) copy-start(bf16[4096,512]{1,0:T(8,128)(2,1)} %act_ref.3) | copy-start | bytes 12582916
  11.7 6.6 %collective-permute-start = (f32[2048,128]{1,0:T(8,128)S(1)}, f32[2048,128]{1,0:T(8,128)S(1)}, u32[]{:S(2)}, u32[]{:S(2)}) collective-permute-start(f32[2048,128]{1,0:T(8,128)S(1)} %shard_map.78), channel_id=1, source_target_pairs={{0,1},{1,0},{2,3},{3,2},{4,5},{5,4},{6,7},{7,6},{8,9},{9,8},{10,11... | collective-permute-start | bytes 3145736 | tf_op jit(solution)/shard_map/ppermute | solution.py:352
  18.2 4.3 %copy-start.26 = (f32[256,512]{1,0:T(8,128)S(1)}, f32[256,512]{1,0:T(8,128)}, u32[]{:S(2)}) copy-start(f32[256,512]{1,0:T(8,128)} %param.11) | copy-start | bytes 1572868
  18.4 8.4 %copy-start.28 = (s32[1,4096]{1,0:T(1,128)S(1)}, s32[1,4096]{1,0:T(1,128)}, u32[]{:S(2)}) copy-start(s32[1,4096]{1,0:T(1,128)} %param.10) | copy-start | bytes 49156
  18.5 21.8 %collective-permute-start.1 = (f32[2,256,128]{2,1,0:T(8,128)S(1)}, f32[2,256,128]{2,1,0:T(8,128)S(1)}, u32[]{:S(2)}, u32[]{:S(2)}) collective-permute-start(f32[2,256,128]{2,1,0:T(8,128)S(1)} %pad_maximum_fusion.3), channel_id=1, source_target_pairs={{0,2},{1,3},{2,0},{3,1},{4,6},{5,7},{6,4},{7,5},{8,10},{9,11},{10,... | collective-permute-start | bytes 786440 | tf_op jit(solution)/shard_map/ppermute | solution.py:352
  21.1 19.2 %collective-permute-start.5 = (f32[2,256,128]{2,1,0:T(8,128)S(1)}, f32[2,256,128]{2,1,0:T(8,128)S(1)}, u32[]{:S(2)}, u32[]{:S(2)}) collective-permute-start(f32[2,256,128]{2,1,0:T(8,128)S(1)} %stack.235), channel_id=1, source_target_pairs={{0,4},{1,5},{2,6},{3,7},{4,0},{5,1},{6,2},{7,3},{8,12},{9,13},{10,... | collective-permute-start | bytes 786440 | tf_op jit(solution)/shard_map/ppermute | solution.py:352
  23.3 43.7 %collective-permute-start.10 = (f32[64,512]{1,0:T(8,128)}, f32[64,512]{1,0:T(8,128)}, u32[]{:S(2)}, u32[]{:S(2)}) collective-permute-start(f32[64,512]{1,0:T(8,128)} %get-tuple-element.100), channel_id=1, source_target_pairs={{0,2},{1,3},{2,0},{3,1},{4,6},{5,7},{6,4},{7,5},{8,10},{9,11},{10,... | collective-permute-start | bytes 393224 | tf_op jit(solution)/shard_map/ppermute | solution.py:352
  23.9 43.2 %collective-permute-start.11 = (f32[64,512]{1,0:T(8,128)}, f32[64,512]{1,0:T(8,128)}, u32[]{:S(2)}, u32[]{:S(2)}) collective-permute-start(f32[64,512]{1,0:T(8,128)} %get-tuple-element.102), channel_id=1, source_target_pairs={{0,4},{1,5},{2,6},{3,7},{4,0},{5,1},{6,2},{7,3},{8,12},{9,13},{10,... | collective-permute-start | bytes 393224 | tf_op jit(solution)/shard_map/ppermute | solution.py:352
  24.1 43.0 %collective-permute-start.12 = (f32[64,512]{1,0:T(8,128)}, f32[64,512]{1,0:T(8,128)}, u32[]{:S(2)}, u32[]{:S(2)}) collective-permute-start(f32[64,512]{1,0:T(8,128)} %get-tuple-element.101), channel_id=1, source_target_pairs={{0,6},{1,7},{2,4},{3,5},{4,2},{5,3},{6,0},{7,1},{8,14},{9,15},{10,... | collective-permute-start | bytes 393224 | tf_op jit(solution)/shard_map/ppermute | solution.py:352
  40.3 5.6 %collective-permute-start.2 = (f32[1,256,128]{2,1,0:T(8,128)S(1)}, f32[1,256,128]{2,1,0:T(8,128)S(1)}, u32[]{:S(2)}, u32[]{:S(2)}) collective-permute-start(f32[1,256,128]{2,1,0:T(8,128)S(1)} %get-tuple-element.87), channel_id=1, source_target_pairs={{0,4},{1,5},{2,6},{3,7},{4,0},{5,1},{6,2},{7,3},{8,12},{9,13},{10,... | collective-permute-start | bytes 393224 | tf_op jit(solution)/shard_map/ppermute | solution.py:352
  45.9 5.0 %collective-permute-start.3 = (f32[256,128]{1,0:T(8,128)S(1)}, f32[256,128]{1,0:T(8,128)S(1)}, u32[]{:S(2)}, u32[]{:S(2)}) collective-permute-start(f32[256,128]{1,0:T(8,128)S(1)} %get-tuple-element.83), channel_id=1, source_target_pairs={{0,4},{1,5},{2,6},{3,7},{4,0},{5,1},{6,2},{7,3},{8,12},{9,13},{10,... | collective-permute-start | bytes 393224 | tf_op jit(solution)/shard_map/ppermute | solution.py:352
  50.9 7.8 %collective-permute-start.4 = (f32[512,128]{1,0:T(8,128)S(1)}, f32[512,128]{1,0:T(8,128)S(1)}, u32[]{:S(2)}, u32[]{:S(2)}) collective-permute-start(f32[512,128]{1,0:T(8,128)S(1)} %pad_maximum_fusion.2), channel_id=1, source_target_pairs={{0,2},{1,3},{2,0},{3,1},{4,6},{5,7},{6,4},{7,5},{8,10},{9,11},{10,... | collective-permute-start | bytes 786440 | tf_op jit(solution)/shard_map/ppermute | solution.py:352
  51.7 8.5 %collective-permute-start.6 = (f32[1,256,128]{2,1,0:T(8,128)S(1)}, f32[1,256,128]{2,1,0:T(8,128)S(1)}, u32[]{:S(2)}, u32[]{:S(2)}) collective-permute-start(f32[1,256,128]{2,1,0:T(8,128)S(1)} %get-tuple-element.86), channel_id=1, source_target_pairs={{0,2},{1,3},{2,0},{3,1},{4,6},{5,7},{6,4},{7,5},{8,10},{9,11},{10,... | collective-permute-start | bytes 393224 | tf_op jit(solution)/shard_map/ppermute | solution.py:352
  60.2 5.0 %collective-permute-start.7 = (f32[256,128]{1,0:T(8,128)S(1)}, f32[256,128]{1,0:T(8,128)S(1)}, u32[]{:S(2)}, u32[]{:S(2)}) collective-permute-start(f32[256,128]{1,0:T(8,128)S(1)} %get-tuple-element.81), channel_id=1, source_target_pairs={{0,2},{1,3},{2,0},{3,1},{4,6},{5,7},{6,4},{7,5},{8,10},{9,11},{10,... | collective-permute-start | bytes 393224 | tf_op jit(solution)/shard_map/ppermute | solution.py:352
  65.3 8.2 %collective-permute-start.13 = (f32[512,128]{1,0:T(8,128)S(1)}, f32[512,128]{1,0:T(8,128)S(1)}, u32[]{:S(2)}, u32[]{:S(2)}) collective-permute-start(f32[512,128]{1,0:T(8,128)S(1)} %get-tuple-element.116), channel_id=1, source_target_pairs={{0,8},{8,16},{16,24},{24,0},{1,9},{9,17},{17,25},{25,1},{2,10},{10... | collective-permute-start | bytes 786440 | tf_op jit(solution)/shard_map/ppermute | solution.py:355
  68.4 7.2 %collective-permute-start.8 = (f32[512,128]{1,0:T(8,128)S(1)}, f32[512,128]{1,0:T(8,128)S(1)}, u32[]{:S(2)}, u32[]{:S(2)}) collective-permute-start(f32[512,128]{1,0:T(8,128)S(1)} %get-tuple-element.117), channel_id=1, source_target_pairs={{0,4},{1,5},{2,6},{3,7},{4,0},{5,1},{6,2},{7,3},{8,12},{9,13},{10,... | collective-permute-start | bytes 786440 | tf_op jit(solution)/shard_map/ppermute | solution.py:352
  74.2 5.0 %collective-permute-start.16 = (f32[256,128]{1,0:T(8,128)S(1)}, f32[256,128]{1,0:T(8,128)S(1)}, u32[]{:S(2)}, u32[]{:S(2)}) collective-permute-start(f32[256,128]{1,0:T(8,128)S(1)} %get-tuple-element.113), channel_id=1, source_target_pairs={{0,2},{1,3},{2,0},{3,1},{4,6},{5,7},{6,4},{7,5},{8,10},{9,11},{10,... | collective-permute-start | bytes 393224 | tf_op jit(solution)/shard_map/ppermute | solution.py:352
  74.7 5.9 %collective-permute-start.14 = (f32[256,128]{1,0:T(8,128)S(1)}, f32[256,128]{1,0:T(8,128)S(1)}, u32[]{:S(2)}, u32[]{:S(2)}) collective-permute-start(f32[256,128]{1,0:T(8,128)S(1)} %get-tuple-element.115), channel_id=1, source_target_pairs={{0,4},{1,5},{2,6},{3,7},{4,0},{5,1},{6,2},{7,3},{8,12},{9,13},{10,... | collective-permute-start | bytes 393224 | tf_op jit(solution)/shard_map/ppermute | solution.py:352
  75.6 23.8 %copy-start.23 = (f32[2048,128]{1,0:T(8,128)}, f32[2048,128]{1,0:T(8,128)S(1)}, u32[]{:S(2)}) copy-start(f32[2048,128]{1,0:T(8,128)S(1)} %constant_dynamic-update-slice_fusion.near_ref) | copy-start | bytes 3145732
  75.6 44.6 %collective-permute-start.9 = (f32[2048,128]{1,0:T(8,128)S(1)}, f32[2048,128]{1,0:T(8,128)S(1)}, u32[]{:S(2)}, u32[]{:S(2)}) collective-permute-start(f32[2048,128]{1,0:T(8,128)S(1)} %constant_dynamic-update-slice_fusion.near_ref), channel_id=1, source_target_pairs={{0,1},{1,0},{2,3},{3,2},{4,5},{5,4},{6,7},{7,6},{8,9},{9,8},{10,11... | collective-permute-start | bytes 3145736 | tf_op jit(solution)/shard_map/ppermute | solution.py:352
  75.7 10.5 %collective-permute-start.19 = (f32[512,128]{1,0:T(8,128)S(1)}, f32[512,128]{1,0:T(8,128)S(1)}, u32[]{:S(2)}, u32[]{:S(2)}) collective-permute-start(f32[512,128]{1,0:T(8,128)S(1)} %collective-permute-done.13), channel_id=1, source_target_pairs={{0,8},{8,16},{16,24},{24,0},{1,9},{9,17},{17,25},{25,1},{2,10},{10... | collective-permute-start | bytes 786440 | tf_op jit(solution)/shard_map/ppermute | solution.py:355
  79.1 12.5 %collective-permute-start.17 = (f32[512,128]{1,0:T(8,128)S(1)}, f32[512,128]{1,0:T(8,128)S(1)}, u32[]{:S(2)}, u32[]{:S(2)}) collective-permute-start(f32[512,128]{1,0:T(8,128)S(1)} %pad_maximum_fusion.6), channel_id=1, source_target_pairs={{0,4},{1,5},{2,6},{3,7},{4,0},{5,1},{6,2},{7,3},{8,12},{9,13},{10,... | collective-permute-start | bytes 786440 | tf_op jit(solution)/shard_map/ppermute | solution.py:352
  80.7 8.9 %collective-permute-start.15 = (f32[512,128]{1,0:T(8,128)S(1)}, f32[512,128]{1,0:T(8,128)S(1)}, u32[]{:S(2)}, u32[]{:S(2)}) collective-permute-start(f32[512,128]{1,0:T(8,128)S(1)} %pad_maximum_fusion.5), channel_id=1, source_target_pairs={{0,2},{1,3},{2,0},{3,1},{4,6},{5,7},{6,4},{7,5},{8,10},{9,11},{10,... | collective-permute-start | bytes 786440 | tf_op jit(solution)/shard_map/ppermute | solution.py:352
  86.9 5.5 %collective-permute-start.20 = (f32[256,128]{1,0:T(8,128)S(1)}, f32[256,128]{1,0:T(8,128)S(1)}, u32[]{:S(2)}, u32[]{:S(2)}) collective-permute-start(f32[256,128]{1,0:T(8,128)S(1)} %get-tuple-element.112), channel_id=1, source_target_pairs={{0,4},{1,5},{2,6},{3,7},{4,0},{5,1},{6,2},{7,3},{8,12},{9,13},{10,... | collective-permute-start | bytes 393224 | tf_op jit(solution)/shard_map/ppermute | solution.py:352
  88.1 11.8 %collective-permute-start.22 = (f32[256,128]{1,0:T(8,128)S(1)}, f32[256,128]{1,0:T(8,128)S(1)}, u32[]{:S(2)}, u32[]{:S(2)}) collective-permute-start(f32[256,128]{1,0:T(8,128)S(1)} %get-tuple-element.110), channel_id=1, source_target_pairs={{0,2},{1,3},{2,0},{3,1},{4,6},{5,7},{6,4},{7,5},{8,10},{9,11},{10,... | collective-permute-start | bytes 393224 | tf_op jit(solution)/shard_map/ppermute | solution.py:352
  89.6 9.1 %collective-permute-start.25 = (f32[512,128]{1,0:T(8,128)S(1)}, f32[512,128]{1,0:T(8,128)S(1)}, u32[]{:S(2)}, u32[]{:S(2)}) collective-permute-start(f32[512,128]{1,0:T(8,128)S(1)} %collective-permute-done.19), channel_id=1, source_target_pairs={{0,8},{8,16},{16,24},{24,0},{1,9},{9,17},{17,25},{25,1},{2,10},{10... | collective-permute-start | bytes 786440 | tf_op jit(solution)/shard_map/ppermute | solution.py:355
  92.4 48.5 %collective-permute-start.18 = (f32[2048,128]{1,0:T(8,128)}, f32[2048,128]{1,0:T(8,128)}, u32[]{:S(2)}, u32[]{:S(2)}) collective-permute-start(f32[2048,128]{1,0:T(8,128)} %constant_dynamic-update-slice_fusion.6.near_ref), channel_id=1, source_target_pairs={{0,1},{1,0},{2,3},{3,2},{4,5},{5,4},{6,7},{7,6},{8,9},{9,8},{10,11... | collective-permute-start | bytes 3145736 | tf_op jit(solution)/shard_map/ppermute | solution.py:352
  92.4 13.9 %collective-permute-start.21 = (f32[512,128]{1,0:T(8,128)S(1)}, f32[512,128]{1,0:T(8,128)S(1)}, u32[]{:S(2)}, u32[]{:S(2)}) collective-permute-start(f32[512,128]{1,0:T(8,128)S(1)} %pad_maximum_fusion.7), channel_id=1, source_target_pairs={{0,2},{1,3},{2,0},{3,1},{4,6},{5,7},{6,4},{7,5},{8,10},{9,11},{10,... | collective-permute-start | bytes 786440 | tf_op jit(solution)/shard_map/ppermute | solution.py:352
  99.4 6.4 %collective-permute-start.26 = (f32[256,128]{1,0:T(8,128)S(1)}, f32[256,128]{1,0:T(8,128)S(1)}, u32[]{:S(2)}, u32[]{:S(2)}) collective-permute-start(f32[256,128]{1,0:T(8,128)S(1)} %get-tuple-element.109), channel_id=1, source_target_pairs={{0,4},{1,5},{2,6},{3,7},{4,0},{5,1},{6,2},{7,3},{8,12},{9,13},{10,... | collective-permute-start | bytes 393224 | tf_op jit(solution)/shard_map/ppermute | solution.py:352
  99.9 10.0 %collective-permute-start.23 = (f32[512,128]{1,0:T(8,128)S(1)}, f32[512,128]{1,0:T(8,128)S(1)}, u32[]{:S(2)}, u32[]{:S(2)}) collective-permute-start(f32[512,128]{1,0:T(8,128)S(1)} %pad_maximum_fusion.8), channel_id=1, source_target_pairs={{0,4},{1,5},{2,6},{3,7},{4,0},{5,1},{6,2},{7,3},{8,12},{9,13},{10,... | collective-permute-start | bytes 786440 | tf_op jit(solution)/shard_map/ppermute | solution.py:352
  105.8 5.0 %collective-permute-start.28 = (f32[256,128]{1,0:T(8,128)S(1)}, f32[256,128]{1,0:T(8,128)S(1)}, u32[]{:S(2)}, u32[]{:S(2)}) collective-permute-start(f32[256,128]{1,0:T(8,128)S(1)} %get-tuple-element.107), channel_id=1, source_target_pairs={{0,2},{1,3},{2,0},{3,1},{4,6},{5,7},{6,4},{7,5},{8,10},{9,11},{10,... | collective-permute-start | bytes 393224 | tf_op jit(solution)/shard_map/ppermute | solution.py:352
  106.3 13.9 %copy-start.24 = (f32[2048,128]{1,0:T(8,128)S(1)}, f32[2048,128]{1,0:T(8,128)}, u32[]{:S(2)}) copy-start(f32[2048,128]{1,0:T(8,128)} %copy-done.23) | copy-start | bytes 3145732
  106.3 7.2 %collective-permute-start.27 = (f32[512,128]{1,0:T(8,128)S(1)}, f32[512,128]{1,0:T(8,128)S(1)}, u32[]{:S(2)}, u32[]{:S(2)}) collective-permute-start(f32[512,128]{1,0:T(8,128)S(1)} %pad_maximum_fusion.9), channel_id=1, source_target_pairs={{0,2},{1,3},{2,0},{3,1},{4,6},{5,7},{6,4},{7,5},{8,10},{9,11},{10,... | collective-permute-start | bytes 786440 | tf_op jit(solution)/shard_map/ppermute | solution.py:352
  110.7 54.9 %collective-permute-start.24 = (f32[2048,128]{1,0:T(8,128)}, f32[2048,128]{1,0:T(8,128)}, u32[]{:S(2)}, u32[]{:S(2)}) collective-permute-start(f32[2048,128]{1,0:T(8,128)} %constant_dynamic-update-slice_fusion.12.near_ref), channel_id=1, source_target_pairs={{0,1},{1,0},{2,3},{3,2},{4,5},{5,4},{6,7},{7,6},{8,9},{9,8},{10,11... | collective-permute-start | bytes 3145736 | tf_op jit(solution)/shard_map/ppermute | solution.py:352
  110.8 8.7 %collective-permute-start.29 = (f32[512,128]{1,0:T(8,128)S(1)}, f32[512,128]{1,0:T(8,128)S(1)}, u32[]{:S(2)}, u32[]{:S(2)}) collective-permute-start(f32[512,128]{1,0:T(8,128)S(1)} %pad_maximum_fusion.10), channel_id=1, source_target_pairs={{0,4},{1,5},{2,6},{3,7},{4,0},{5,1},{6,2},{7,3},{8,12},{9,13},{10,... | collective-permute-start | bytes 786440 | tf_op jit(solution)/shard_map/ppermute | solution.py:352
  120.2 70.2 %collective-permute-start.30 = (f32[2048,128]{1,0:T(8,128)}, f32[2048,128]{1,0:T(8,128)}, u32[]{:S(2)}, u32[]{:S(2)}) collective-permute-start(f32[2048,128]{1,0:T(8,128)} %constant_dynamic-update-slice_fusion.18.near_ref), channel_id=1, source_target_pairs={{0,1},{1,0},{2,3},{3,2},{4,5},{5,4},{6,7},{7,6},{8,9},{9,8},{10,11... | collective-permute-start | bytes 3145736 | tf_op jit(solution)/shard_map/ppermute | solution.py:352
  162.3 1.4 copy-start.3
  185.7 1.4 copy-start.4
  187.1 1.3 copy-start.6
  211.8 1.4 copy-start.9
  216.3 2.1 collective-permute-start.31
  218.4 1.6 copy-start.2
  220.0 1.6 copy-start.5
  221.6 1.6 copy-start.8
  239.4 2.0 collective-permute-start.32
  257.7 2.0 collective-permute-start.33
  279.2 2.0 collective-permute-start.34
  285.8 2.2 copy-start.22
  285.9 6.8 %collective-permute-start.41 = (f32[32,512]{1,0:T(8,128)S(1)}, f32[32,512]{1,0:T(8,128)S(1)}, u32[]{:S(2)}, u32[]{:S(2)}) collective-permute-start(f32[32,512]{1,0:T(8,128)S(1)} %get-tuple-element.92), channel_id=1, source_target_pairs={{0,24},{8,0},{16,8},{24,16},{1,25},{9,1},{17,9},{25,17},{2,26},{10... | collective-permute-start | bytes 196616 | tf_op jit(solution)/shard_map/ppermute | solution.py:355
  285.9 8.4 %collective-permute-start.42 = (f32[32,512]{1,0:T(8,128)S(1)}, f32[32,512]{1,0:T(8,128)S(1)}, u32[]{:S(2)}, u32[]{:S(2)}) collective-permute-start(f32[32,512]{1,0:T(8,128)S(1)} %get-tuple-element.91), channel_id=1, source_target_pairs={{0,16},{8,24},{16,0},{24,8},{1,17},{9,25},{17,1},{25,9},{2,18},{10... | collective-permute-start | bytes 196616 | tf_op jit(solution)/shard_map/ppermute | solution.py:355
  286.0 15.8 %collective-permute-start.43 = (f32[32,512]{1,0:T(8,128)S(1)}, f32[32,512]{1,0:T(8,128)S(1)}, u32[]{:S(2)}, u32[]{:S(2)}) collective-permute-start(f32[32,512]{1,0:T(8,128)S(1)} %get-tuple-element.90), channel_id=1, source_target_pairs={{0,8},{8,16},{16,24},{24,0},{1,9},{9,17},{17,25},{25,1},{2,10},{10... | collective-permute-start | bytes 196616 | tf_op jit(solution)/shard_map/ppermute | solution.py:355
  288.1 6.3 %collective-permute-start.35 = (f32[64,512]{1,0:T(8,128)S(1)}, f32[64,512]{1,0:T(8,128)S(1)}, u32[]{:S(2)}, u32[]{:S(2)}) collective-permute-start(f32[64,512]{1,0:T(8,128)S(1)} %get-tuple-element.95), channel_id=1, source_target_pairs={{0,2},{1,3},{2,0},{3,1},{4,6},{5,7},{6,4},{7,5},{8,10},{9,11},{10,... | collective-permute-start | bytes 393224 | tf_op jit(solution)/shard_map/ppermute | solution.py:352
  288.7 8.1 %collective-permute-start.36 = (f32[64,512]{1,0:T(8,128)S(1)}, f32[64,512]{1,0:T(8,128)S(1)}, u32[]{:S(2)}, u32[]{:S(2)}) collective-permute-start(f32[64,512]{1,0:T(8,128)S(1)} %get-tuple-element.94), channel_id=1, source_target_pairs={{0,4},{1,5},{2,6},{3,7},{4,0},{5,1},{6,2},{7,3},{8,12},{9,13},{10,... | collective-permute-start | bytes 393224 | tf_op jit(solution)/shard_map/ppermute | solution.py:352
  292.7 5.9 %collective-permute-start.37 = (f32[64,512]{1,0:T(8,128)S(1)}, f32[64,512]{1,0:T(8,128)S(1)}, u32[]{:S(2)}, u32[]{:S(2)}) collective-permute-start(f32[64,512]{1,0:T(8,128)S(1)} %get-tuple-element.93), channel_id=1, source_target_pairs={{0,6},{1,7},{2,4},{3,5},{4,2},{5,3},{6,0},{7,1},{8,14},{9,15},{10,... | collective-permute-start | bytes 393224 | tf_op jit(solution)/shard_map/ppermute | solution.py:352
  300.2 14.1 %collective-permute-start.38 = (f32[256,512]{0,1:T(8,128)S(1)}, f32[256,512]{0,1:T(8,128)S(1)}, u32[]{:S(2)}, u32[]{:S(2)}) collective-permute-start(f32[256,512]{0,1:T(8,128)S(1)} %dynamic_update_slice.57), channel_id=1, source_target_pairs={{0,8},{8,16},{16,24},{24,0},{1,9},{9,17},{17,25},{25,1},{2,10},{10... | collective-permute-start | bytes 1572872 | tf_op jit(solution)/shard_map/ppermute | solution.py:355
  301.9 4.3 %collective-permute-start.44 = (f32[1,32,512]{2,1,0:T(8,128)S(1)}, f32[1,32,512]{2,1,0:T(8,128)S(1)}, u32[]{:S(2)}, u32[]{:S(2)}) collective-permute-start(f32[1,32,512]{2,1,0:T(8,128)S(1)} %get-tuple-element.105), channel_id=1, source_target_pairs={{0,2},{1,3},{2,0},{3,1},{4,6},{5,7},{6,4},{7,5},{8,10},{9,11},{10,... | collective-permute-start | bytes 196616 | tf_op jit(solution)/shard_map/ppermute | solution.py:352
  303.0 4.3 %collective-permute-start.45 = (f32[1,32,512]{2,1,0:T(8,128)S(1)}, f32[1,32,512]{2,1,0:T(8,128)S(1)}, u32[]{:S(2)}, u32[]{:S(2)}) collective-permute-start(f32[1,32,512]{2,1,0:T(8,128)S(1)} %get-tuple-element.104), channel_id=1, source_target_pairs={{0,4},{1,5},{2,6},{3,7},{4,0},{5,1},{6,2},{7,3},{8,12},{9,13},{10,... | collective-permute-start | bytes 196616 | tf_op jit(solution)/shard_map/ppermute | solution.py:352
  304.6 9.7 %collective-permute-start.46 = (f32[1,32,512]{2,1,0:T(8,128)S(1)}, f32[1,32,512]{2,1,0:T(8,128)S(1)}, u32[]{:S(2)}, u32[]{:S(2)}) collective-permute-start(f32[1,32,512]{2,1,0:T(8,128)S(1)} %get-tuple-element.103), channel_id=1, source_target_pairs={{0,6},{1,7},{2,4},{3,5},{4,2},{5,3},{6,0},{7,1},{8,14},{9,15},{10,... | collective-permute-start | bytes 196616 | tf_op jit(solution)/shard_map/ppermute | solution.py:352
  314.3 13.1 %collective-permute-start.39 = (f32[256,512]{0,1:T(8,128)S(1)}, f32[256,512]{0,1:T(8,128)S(1)}, u32[]{:S(2)}, u32[]{:S(2)}) collective-permute-start(f32[256,512]{0,1:T(8,128)S(1)} %collective-permute-done.38), channel_id=1, source_target_pairs={{0,8},{8,16},{16,24},{24,0},{1,9},{9,17},{17,25},{25,1},{2,10},{10... | collective-permute-start | bytes 1572872 | tf_op jit(solution)/shard_map/ppermute | solution.py:355
  314.4 13.1 %collective-permute-start.47 = (f32[2,32,512]{2,1,0:T(8,128)S(1)}, f32[2,32,512]{2,1,0:T(8,128)S(1)}, u32[]{:S(2)}, u32[]{:S(2)}) collective-permute-start(f32[2,32,512]{2,1,0:T(8,128)S(1)} %constant_dynamic-slice_fusion), channel_id=1, source_target_pairs={{0,1},{1,0},{2,3},{3,2},{4,5},{5,4},{6,7},{7,6},{8,9},{9,8},{10,11... | collective-permute-start | bytes 393224 | tf_op jit(solution)/shard_map/ppermute | solution.py:352
  327.4 12.2 %collective-permute-start.40 = (f32[256,512]{0,1:T(8,128)S(1)}, f32[256,512]{0,1:T(8,128)S(1)}, u32[]{:S(2)}, u32[]{:S(2)}) collective-permute-start(f32[256,512]{0,1:T(8,128)S(1)} %collective-permute-done.39), channel_id=1, source_target_pairs={{0,8},{8,16},{16,24},{24,0},{1,9},{9,17},{17,25},{25,1},{2,10},{10... | collective-permute-start | bytes 1572872 | tf_op jit(solution)/shard_map/ppermute | solution.py:355
  327.5 12.3 %copy-start.27 = (f32[2,2,32,512]{3,2,1,0:T(8,128)}, f32[2,2,32,512]{3,2,1,0:T(8,128)S(1)}, u32[]{:S(2)}) copy-start(f32[2,2,32,512]{3,2,1,0:T(8,128)S(1)} %bitcast_dynamic-update-slice_fusion.4) | copy-start | bytes 786436
  339.7 1.3 copy-start.25
  (13 other events, 12.6 us)

commit v2 on v1

--- a/solution.py
+++ b/solution.py
@@ -9,7 +9,6 @@
 
 ITERS = 4
 EX_DEV = 512
-MOST = 16
 LANES = 128
 WINDOW = 256
 F32 = jnp.float32
@@ -33,92 +32,106 @@
 
 def project_kernel(order_ref, act_ref, grad_ref, wi_ref, wo_ref, out_ref):
     del order_ref
-    out_ref[...] = dot_nn(act_ref[...], wi_ref[...]) + dot_nn(grad_ref[...], wo_ref[...])
+    out_ref[...] = jnp.concatenate(
+        [dot_nn(act_ref[...], wi_ref[...]), dot_nn(grad_ref[...], wo_ref[...])], axis=1
+    )
 
 
 def project(order, activations, out_grads, w_in, w_out, block):
     steps = order.shape[0]
     feats, hidden = activations.shape[1], out_grads.shape[1]
-    lanes = w_in.shape[1]
     return pl.pallas_call(
         project_kernel,
-        out_shape=jax.ShapeDtypeStruct((steps * block, lanes), F32),
+        out_shape=jax.ShapeDtypeStruct((steps * block, LANES), F32),
         grid_spec=pltpu.PrefetchScalarGridSpec(
             num_scalar_prefetch=1,
             grid=(steps,),
             in_specs=[
                 pl.BlockSpec((block, feats), lambda i, order: (order[i], 0)),
                 pl.BlockSpec((block, hidden), lambda i, order: (order[i], 0)),
-                pl.BlockSpec((feats, lanes), lambda i, order: (0, 0)),
-                pl.BlockSpec((hidden, lanes), lambda i, order: (0, 0)),
+                pl.BlockSpec(w_in.shape, lambda i, order: (0, 0)),
+                pl.BlockSpec(w_out.shape, lambda i, order: (0, 0)),
             ],
-            out_specs=pl.BlockSpec((block, lanes), lambda i, order: (i, 0)),
-        ),
-        compiler_params=pltpu.CompilerParams(vmem_limit_bytes=40 * MIB),
+            out_specs=pl.BlockSpec((block, LANES), lambda i, order: (i, 0)),
+        ),
+        compiler_params=pltpu.CompilerParams(vmem_limit_bytes=61 * MIB),
         cost_estimate=pl.CostEstimate(
-            flops=2 * steps * block * (feats + hidden) * lanes,
+            flops=2 * steps * block * (feats + hidden) * LANES,
             bytes_accessed=2 * steps * block * (feats + hidden),
             transcendentals=0,
         ),
     )(order, activations, out_grads, w_in, w_out)
 
 
-def build_kernel(
-    ranks, piece, ex_block,
-    offs_ref, first_ref, near_ref, far_ref, ids_ref, pick_ref, b_ref,
-    high_ref, low_ref, inner_ref, sq_ref,
-    out_high, out_low, in_both, rows, sketch,
-):
+def build_kernel(ranks, share, ex_block, n_sources, *refs):
+    offs_ref, start_ref = refs[:2]
+    sources = refs[2:2 + n_sources]
+    ids_ref, pick_ref, b_ref = refs[2 + n_sources:5 + n_sources]
+    high_ref, low_ref, inner_ref, sq_ref = refs[5 + n_sources:9 + n_sources]
+    out_t, in_twice, ids_wide, rows, sketch = refs[9 + n_sources:]
     step = pl.program_id(0)
     half_ranks = pick_ref.shape[0]
-    pieces = near_ref.shape[0] // piece
+    pairs = half_ranks // 2
+    tokens = ids_ref.shape[1]
 
     @pl.when(step == 0)
     def _():
-        lane = lax.broadcasted_iota(jnp.int32, (piece, LANES), 1)
-        for source, base in ((near_ref, 0), (far_ref, pieces)):
-            for k in range(pieces):
-                values = source[k * piece:(k + 1) * piece, :]
-                at = pl.multiple_of(offs_ref[base + k], piece)
+        lane = lax.broadcasted_iota(jnp.int32, (share, LANES), 1)
+        block = 0
+        for source in sources:
+            for k in range(source.shape[0] // share):
+                values = source[k * share:(k + 1) * share, :]
+                at = pl.multiple_of(offs_ref[block] * share, share)
+                block += 1
                 high, low = split2(values)
-                out_high[:, pl.ds(at, piece)] = dot_nt(pick_ref[...], high).astype(BF16)
-                out_low[:, pl.ds(at, piece)] = dot_nt(pick_ref[...], low).astype(BF16)
-                twice = jnp.where(lane < ranks, values, pltpu.roll(values, ranks, 1))
-                high, low = split2(twice)
-                in_both[pl.ds(at, piece), 0:LANES] = high
-                in_both[pl.ds(at, piece), LANES:2 * LANES] = low
+                out_t[:, pl.ds(at, share)] = dot_nt(pick_ref[...], high) + dot_nt(pick_ref[...], low)
+                in_twice[pl.ds(at, share), :] = jnp.where(
+                    lane < ranks, values, pltpu.roll(values, ranks, 1)
+                )
+        ids_wide[...] = jnp.broadcast_to(ids_ref[...], ids_wide.shape)
         sq_ref[...] = jnp.zeros_like(sq_ref)
 
-    group = rows.shape[1] // half_ranks
-    lane = lax.broadcasted_iota(jnp.int32, (group, LANES), 1)
+    slots = rows.shape[0]
+    group = rows.shape[1] // pairs
+    lane = lax.broadcasted_iota(jnp.int32, (LANES, LANES), 1)
+    left_lanes = (lane < ranks).astype(F32).astype(BF16)
+    right_lanes = (lane >= ranks).astype(F32).astype(BF16)
 
     def one_group(g, slot):
         number = step * (ex_block // group) + g
-        at = pl.multiple_of(first_ref[number] * LANES, LANES)
-        ids = ids_ref[0:1, pl.ds(at, WINDOW)]
-        oh = out_high[:, pl.ds(at, WINDOW)]
-        ol = out_low[:, pl.ds(at, WINDOW)]
-        zero = jnp.zeros_like(oh)
-        masks = [
-            jnp.broadcast_to((ids == number * group + e).astype(F32), oh.shape).astype(BF16)
-            for e in range(group)
-        ]
-        del zero
-        left = jnp.concatenate([oh * m for m in masks] + [ol * m for m in masks], axis=0)
-        res = dot_nn(left, in_both[pl.ds(at, WINDOW), :])
-        top = group * half_ranks
+        start = start_ref[number]
+        at = jnp.minimum(lax.div(start, LANES) * LANES, tokens - WINDOW)
+        turn = lax.rem(WINDOW - (start - at), WINDOW)
+        at = pl.multiple_of(at, LANES)
+        out_win = pltpu.roll(out_t[:, pl.ds(at, WINDOW)], turn, 1)[:, :LANES]
+        ids_win = pltpu.roll(ids_wide[:, pl.ds(at, WINDOW)], turn, 1)[:, :LANES]
+        base = (number * group).astype(F32)
+        lefts = ([], [])
+        terms = split2(out_win)
+        for e in range(group):
+            mask = (ids_win == base + float(e)).astype(F32)
+            mask = jnp.concatenate([mask] * (pairs // 8), axis=0).astype(BF16)
+            for left, term in zip(lefts, terms):
+                left.append(jnp.concatenate([term[:pairs] * mask, term[pairs:] * mask], axis=1))
+        left = jnp.concatenate(lefts[0] + lefts[1], axis=0)
+        high, low = split2(in_twice[pl.ds(start, LANES), :])
+        right = jnp.concatenate(
+            [
+                jnp.concatenate([high * lanes, low * lanes], axis=1)
+                for lanes in (left_lanes, right_lanes)
+            ],
+            axis=0,
+        )
+        res = dot_nn(left, right)
+        top = group * pairs
         rows[slot] = (
             (res[:top, :LANES] + res[top:, :LANES]) + (res[:top, LANES:] + res[top:, LANES:])
         )
         to = pl.multiple_of(g * group, group)
-        for pair in range(half_ranks // 2):
-            even = rows[slot, pl.ds(2 * pair, group, stride=half_ranks), :]
-            odd = rows[slot, pl.ds(2 * pair + 1, group, stride=half_ranks), :]
-            sketch[pl.ds(to, group), pair * LANES:(pair + 1) * LANES] = jnp.where(
-                lane < ranks, even, odd
-            )
-
-    slots = rows.shape[0]
+        for pair in range(pairs):
+            sketch[pl.ds(to, group), pair * LANES:(pair + 1) * LANES] = rows[
+                slot, pl.ds(pair, group, stride=pairs), :
+            ]
 
     @pl.loop(0, ex_block // group // slots)
     def _(turn):
@@ -140,16 +153,15 @@
     inner_ref[...] = both[:count] + both[count:] + dot_nt(b_high, low)
 
 
-def build(offs, first, near, far, ids, pick, b, ranks, piece):
+def build(offs, starts, sources, ids, pick, b, ranks, share):
     tokens = ids.shape[1]
     half_ranks = pick.shape[0]
-    comps = b.shape[1]
-    queries = b.shape[0]
-    ex_block = 128
+    queries, comps = b.shape
+    ex_block = 256
     group = 8
     whole = lambda i, *_: (0, 0)
     return pl.pallas_call(
-        functools.partial(build_kernel, ranks, piece, ex_block),
+        functools.partial(build_kernel, ranks, share, ex_block, len(sources)),
         out_shape=(
             jax.ShapeDtypeStruct((EX_DEV, comps), BF16),
             jax.ShapeDtypeStruct((EX_DEV, comps), BF16),
@@ -159,13 +171,7 @@
         grid_spec=pltpu.PrefetchScalarGridSpec(
             num_scalar_prefetch=2,
             grid=(EX_DEV // ex_block,),
-            in_specs=[
-                pl.BlockSpec(near.shape, whole),
-                pl.BlockSpec(far.shape, whole),
-                pl.BlockSpec(ids.shape, whole),
-                pl.BlockSpec(pick.shape, whole),
-                pl.BlockSpec(b.shape, whole),
-            ],
+            in_specs=[pl.BlockSpec(a.shape, whole) for a in (*sources, ids, pick, b)],
             out_specs=[
                 pl.BlockSpec((ex_block, comps), lambda i, *_: (i, 0)),
                 pl.BlockSpec((ex_block, comps), lambda i, *_: (i, 0)),
@@ -173,20 +179,20 @@
                 pl.BlockSpec((8, LANES), whole),
             ],
             scratch_shapes=[
-                pltpu.VMEM((half_ranks, tokens), BF16),
-                pltpu.VMEM((half_ranks, tokens), BF16),
-                pltpu.VMEM((tokens, 2 * LANES), BF16),
-                pltpu.VMEM((2, group * half_ranks, LANES), F32),
+                pltpu.VMEM((half_ranks, tokens), F32),
+                pltpu.VMEM((tokens, LANES), F32),
+                pltpu.VMEM((8, tokens), F32),
+                pltpu.VMEM((4, group * half_ranks // 2, LANES), F32),
                 pltpu.VMEM((ex_block, comps), F32),
             ],
         ),
-        compiler_params=pltpu.CompilerParams(vmem_limit_bytes=40 * MIB),
+        compiler_params=pltpu.CompilerParams(vmem_limit_bytes=53 * MIB),
         cost_estimate=pl.CostEstimate(
-            flops=2 * EX_DEV * half_ranks * 2 * WINDOW * 2 * LANES + 6 * EX_DEV * queries * comps,
-            bytes_accessed=4 * EX_DEV * comps + 8 * near.shape[0] * LANES,
+            flops=12 * EX_DEV * half_ranks * WINDOW * 2 * LANES,
+            bytes_accessed=4 * EX_DEV * comps + 4 * tokens * LANES,
             transcendentals=0,
         ),
-    )(offs, first, near, far, ids, pick, b)
+    )(offs, starts, *sources, ids, pick, b)
 
 
 def column(values, k):
@@ -284,7 +290,7 @@
 def one_step(first, examples, comps_all, mine, other, r, rest, highs, lows):
     planes = len(highs)
     count, comps = r.shape
-    block = 256
+    block = 512
     whole = lambda i: (0, 0)
     along = lambda i: (0, i)
     full = lambda a: pl.BlockSpec(a.shape, whole)
@@ -310,7 +316,7 @@
             pltpu.VMEM((count, LANES), F32),
             pltpu.VMEM((count, LANES), F32),
         ],
-        compiler_params=pltpu.CompilerParams(vmem_limit_bytes=40 * MIB),
+        compiler_params=pltpu.CompilerParams(vmem_limit_bytes=56 * MIB),
         cost_estimate=pl.CostEstimate(
             flops=12 * count * examples * comps,
             bytes_accessed=4 * examples * comps,
@@ -333,8 +339,43 @@
     return pl.pallas_call(
         functools.partial(last_kernel, examples, comps_all),
         out_shape=(jax.ShapeDtypeStruct(x.shape, F32), jax.ShapeDtypeStruct(y.shape, F32)),
-        compiler_params=pltpu.CompilerParams(vmem_limit_bytes=40 * MIB),
+        compiler_params=pltpu.CompilerParams(vmem_limit_bytes=24 * MIB),
     )(*arrays)
+
+
+def place_kernel(where_ref, *refs):
+    parts, out_ref, held = refs[:-2], refs[-2], refs[-1]
+    parts = parts[:2]
+    rows = parts[0].shape[0]
+    slot = 0
+    for part in parts:
+        for k in range(part.shape[0] // rows):
+            at = pl.multiple_of(where_ref[1 + slot] * rows, rows)
+            held[pl.ds(at, rows), :] = part[k * rows:(k + 1) * rows, :]
+            slot += 1
+    out_ref[...] = held[...].T
+
+
+def place(where, own, others, out, shape):
+    rows = own.shape[0] + others.shape[0]
+    whole = lambda i, where: (0, 0)
+    operands = [own, others] + ([] if out is None else [out])
+    in_specs = [pl.BlockSpec(own.shape, whole), pl.BlockSpec(others.shape, whole)]
+    if out is not None:
+        in_specs.append(pl.BlockSpec(memory_space=pl.ANY))
+    return pl.pallas_call(
+        place_kernel,
+        out_shape=jax.ShapeDtypeStruct(shape, F32),
+        grid_spec=pltpu.PrefetchScalarGridSpec(
+            num_scalar_prefetch=1,
+            grid=(1,),
+            in_specs=in_specs,
+            out_specs=pl.BlockSpec((shape[0], rows), lambda i, where: (0, where[0])),
+            scratch_shapes=[pltpu.VMEM((rows, own.shape[1]), F32)],
+        ),
+        input_output_aliases={} if out is None else {3: 0},
+        compiler_params=pltpu.CompilerParams(vmem_limit_bytes=24 * MIB),
+    )(where, *operands)
 
 
 def per_device(n_dp, n_t, activations, out_grads, proj_in, proj_out, example_ids, queries):
@@ -361,66 +402,55 @@
     slots = [slots[0]] + [swap(slots[k], 2 * k) for k in range(1, n_c)]
     b = jnp.concatenate(slots, axis=1)
 
-    ids_all = lax.all_gather(example_ids, "dp", axis=0, tiled=True)
     group = 8
     bounds = group * jnp.arange(EX_DEV // group, dtype=jnp.int32)
-    starts = jnp.sum((ids_all[:, None, :] < bounds[None, :, None]).astype(jnp.int32), axis=-1)
-    firsts = jnp.minimum(starts // LANES, (tokens - WINDOW) // LANES)
-
-    w_in = jnp.pad(proj_in, ((0, 0), (0, ranks)))
-    w_out = jnp.pad(proj_out, ((0, 0), (ranks, 0)))
+    starts = jnp.sum((example_ids[0][None, :] < bounds[:, None]).astype(F32), axis=1)
+    starts = jnp.minimum(starts, F32(tokens - LANES))
+    id_rows = tokens // LANES
+    extra = jnp.concatenate(
+        [
+            example_ids.astype(F32).reshape((id_rows, LANES)),
+            jnp.pad(starts[None, :], ((0, 7), (0, LANES - EX_DEV // group))),
+        ],
+        axis=0,
+    )
+
     share = tokens // n_t
     blocks = jnp.stack(near_chip).astype(jnp.int32) * 2
-    give = project(blocks + 1 - core, activations, out_grads, w_in, w_out, share)
-    keep = project(blocks + core, activations, out_grads, w_in, w_out, share)
+    give = project(blocks + 1 - core, activations, out_grads, proj_in, proj_out, share)
+    keep = project(blocks + core, activations, out_grads, proj_in, proj_out, share)
     kept = (keep + swap(give, 1)).reshape((n_c, share, LANES))
-    half = share // 2
-    own = []
-    orders = (list(range(bits)), list(range(bits))[::-1])
-    for part, order in enumerate(orders):
-        held = {k: kept[k, part * half:(part + 1) * half] for k in range(n_c)}
-        for bit in order:
-            low = [k for k in held if not (k >> bit) & 1]
-            came = swap(jnp.stack([held[k | (1 << bit)] for k in low]), 2 << bit)
-            held = {k: held[k] + came[n] for n, k in enumerate(low)}
-        own.append(held[0])
-
-    rings = [jnp.concatenate(own, axis=0)]
+    own = kept[0]
+    for k in range(1, n_c):
+        own = own + swap(kept[k], 2 * k)
+
+    rings = [jnp.concatenate([own, extra], axis=0)]
     for _ in range(n_dp - 1):
         rings.append(shift(rings[-1], 1))
-    slot_orders = []
-    for order in orders:
-        ks = [0]
-        for bit in order[::-1]:
-            ks = ks + [k | (1 << bit) for k in ks]
-        slot_orders.append(ks)
-    offs = jnp.stack(
-        [
-            (near_chip[k] * 2 + which) * share + part * half
-            for which in (core, 1 - core)
-            for part in range(2)
-            for k in slot_orders[part]
-        ]
-    ).astype(jnp.int32)
 
     per = comps_all // ranks // n_t
-    wanted = jnp.stack([(near_chip[k] * 2 + core) * per + a for k in range(n_c) for a in range(per)]) + ranks
+    wanted = [(near_chip[k] * 2 + core) * per + a + ranks for k in range(n_c) for a in range(per)]
+    wanted = jnp.stack(wanted[0::2] + wanted[1::2])
     pick = (wanted[:, None] == jnp.arange(LANES)[None, :]).astype(BF16)
 
     highs, lows, inners, squares = [], [], [], []
     for away in range(n_dp):
-        gathered = []
-        for part, order in enumerate(orders):
-            held = rings[away][part * half:(part + 1) * half]
-            for bit in order[::-1]:
-                held = jnp.concatenate([held, swap(held, 2 << bit)], axis=0)
-            gathered.append(held)
-        near = jnp.concatenate(gathered, axis=0)
-        far = swap(near, 1)
-        plane = (i - away) % n_dp
-        ids = lax.dynamic_slice_in_dim(ids_all, plane, 1, 0)
-        first = lax.dynamic_index_in_dim(firsts, plane, 0, keepdims=False)
-        high, low, inner, square = build(offs, first, near, far, ids, pick, b, ranks, half)
+        order = list(range(bits))
+        if away % 2:
+            order = order[::-1]
+        held, ks = rings[away][:share], [0]
+        for bit in order[:-1]:
+            held = jnp.concatenate([held, swap(held, 2 << bit)], axis=0)
+            ks = ks + [k | (1 << bit) for k in ks]
+        came = swap(held, 2 << order[-1])
+        ks = ks + [k | (1 << order[-1]) for k in ks]
+        sources = [held, came, swap(held, 1), swap(came, 1)]
+        offs = jnp.stack(
+            [near_chip[k] * 2 + which for which in (core, 1 - core) for k in ks]
+        ).astype(jnp.int32)
+        ids = rings[away][share:share + id_rows].reshape((1, tokens))
+        first = rings[away][share + id_rows, :EX_DEV // group].astype(jnp.int32)
+        high, low, inner, square = build(offs, first, sources, ids, pick, b, ranks, share)
         highs.append(high)
         lows.append(low)
         inners.append(inner)
@@ -447,19 +477,16 @@
     x, y = last_step(examples, comps_all, message, other, r, *rest)
 
     per_slot = comps_all // n_t
-    own_x = jnp.zeros((n_c * q_chip, per_slot), F32)
-    for k in range(n_c):
-        part = x[:, k * per_slot:(k + 1) * per_slot]
-        if k:
-            part = swap(part, 2 * k)
-        own_x = lax.dynamic_update_slice_in_dim(own_x, part, near_chip[k] * q_chip, 0)
-    q_plane = n_c * q_chip
-    out = jnp.zeros((per_slot, n_dp * q_plane), F32)
-    ring = own_x
+    own_x = x[:, :per_slot]
+    others_x = jnp.concatenate(
+        [swap(x[:, k * per_slot:(k + 1) * per_slot], 2 * k) for k in range(1, n_c)], axis=0
+    )
+    out = None
     for away in range(n_dp):
         if away:
-            ring = shift(ring, 1)
-        out = lax.dynamic_update_slice_in_dim(out, ring.T, ((i - away) % n_dp) * q_plane, 1)
+            own_x, others_x = shift(own_x, 1), shift(others_x, 1)
+        where = jnp.stack([(i - away) % n_dp] + near_chip).astype(jnp.int32)
+        out = place(where, own_x, others_x, out, (per_slot, n_dp * n_c * q_chip))
 
     part_q = q_chip // 2
     mine = lax.dynamic_slice_in_dim(y, core * part_q, part_q, 0)

time: 342 us -> 251 us (0.73)
  local copies, waits for them, and re-layouts: 52.5 us -> 15.5 us
  Pallas kernels: 141 us -> 113 us
  waiting for transfers between devices: 87 us -> 69 us
  blocking collectives: 13.4 us -> 0 us
  starting transfers between devices: 38.6 us -> 42.4 us
    pallas_call x4 -> x8, Pallas kernels: 79.1 us -> 53.9 us  [the longest x4 47.6 us: build(): pl.pallas_call(functools.partial(build_kernel, ranks, share, ex_block, le...]
    unnamed x76 -> x42, local copies, waits for them, and re-layouts: 36.8 us -> 14.3 us
    ppermute x9 -> x12, waiting for transfers between devices: 44.7 us -> 30.5 us  [shift(): lax.ppermute(values, 'dp', [(a, (a + by) % n_dp) for a in range(n_dp)])]
    all_gather x1 -> x0, blocking collectives: 13.4 us -> none  [per_device(): ids_all = lax.all_gather(example_ids, 'dp', axis=0, tiled=True)]
    dynamic_update_slice x8 -> x0, local copies, waits for them, and re-layouts: 7.23 us -> none  [the longest x4 6.98 us: per_device(): lax.dynamic_update_slice_in_dim(own_x, part, near_chip[k] * q_chip, 0)]
    ppermute x9 -> x12, starting transfers between devices: 5.39 us -> 12.3 us  [shift(): lax.ppermute(values, 'dp', [(a, (a + by) % n_dp) for a in range(n_dp)])]
    pallas_call x3, Pallas kernels: 48.7 us -> 43.6 us  [one_step(): pl.pallas_call(functools.partial(step_kernel, first, planes, examples, co...]
    ppermute x39 -> x34, waiting for transfers between devices: 42.3 us -> 38.6 us  [swap(): return lax.ppermute(values, 'tensor', [(a, a ^ mask) for a in range(n_t)])]
  transfers between devices with their start and end apart: 48 -> 46, of which waited for: 24 -> 19; matrix products, arithmetic and copies ran while one was open for 8% -> 2% of each run, Pallas kernels for 19% -> 19%
where the time goes in v2:
time: 251 us; the launch traced here: 250 us
  Pallas kernels  113 us (45%)
  waiting for transfers between devices  69 us (27%)
  starting transfers between devices  42.4 us (17%)
  local copies, waits for them, and re-layouts  15.5 us (6%)
  other arithmetic  6.44 us (3%)
  between operations  3.75 us (1%)
    pallas_call x4, Pallas kernels, build(): pl.pallas_call(functools.partial(build_kernel, ranks, share, ex_block, le...  47.6 us
    pallas_call x3, Pallas kernels, one_step(): pl.pallas_call(functools.partial(step_kernel, first, planes, examples, co...  43.6 us
    ppermute x34, waiting for transfers between devices, swap(): return lax.ppermute(values, 'tensor', [(a, a ^ mask) for a in range(n_t)])  38.6 us
    ppermute x12, waiting for transfers between devices, shift(): lax.ppermute(values, 'dp', [(a, (a + by) % n_dp) for a in range(n_dp)])  30.5 us
    ppermute x34, starting transfers between devices, swap(): return lax.ppermute(values, 'tensor', [(a, a ^ mask) for a in range(n_t)])  30.1 us
    pallas_call x2, Pallas kernels, project(): pl.pallas_call(project_kernel, out_shape=jax.ShapeDtypeStruct((steps * bl...  15.4 us
    unnamed x42, local copies, waits for them, and re-layouts  14.3 us
    ppermute x12, starting transfers between devices, shift(): lax.ppermute(values, 'dp', [(a, (a + by) % n_dp) for a in range(n_dp)])  12.3 us
  transfers between devices with their start and end apart: 46, of which 19 were waited for; matrix products, arithmetic and copies ran while one was open for 2% of the time, Pallas kernels for 19%

profile of v2, /device:TPU:0, one launch (start us, length us, event | category | flops | bytes accessed | tf_op | source)
XLA Modules:
  0.0 250.5 jit_solution(7830661831550409852)
XLA Ops:
  0.7 1.9 copy.18.wo_ref
  2.6 1.6 copy.17.wi_ref
  4.8 7.7 %shard_map.78 = f32[2048,128]{1,0:T(8,128)} custom-call(s32[4]{0:T(128)} %get-tuple-element.80.order_ref, bf16[4096,512]{1,0:T(8,128)(2,1)} %act_ref.3, bf16[4096,1792]{1,0:T(8,128)(2,1)} %grad_ref.3, bf16[512,64]{1,0:T(8,128)(2,1)} %copy.17.wi_ref, bf16[1792,64]{1,0:T(8,128)(2,1)} %copy.18.wo_ref), custom_call_target="tpu_custom_call" | custom-call | flops 1207959552 | bytes 9437184 | tf_op jit(solution)/shard_map/pallas_call | solution.py:43
  13.5 7.7 %shard_map.77 = f32[2048,128]{1,0:T(8,128)} custom-call(s32[4]{0:T(128)} %broadcast_add_fusion.order_ref, bf16[4096,512]{1,0:T(8,128)(2,1)} %act_ref.3, bf16[4096,1792]{1,0:T(8,128)(2,1)} %grad_ref.3, bf16[512,64]{1,0:T(8,128)(2,1)} %copy.17.wi_ref, bf16[1792,64]{1,0:T(8,128)(2,1)} %copy.18.wo_ref), custom_call_target="tpu_custom_call" | custom-call | flops 1207959552 | bytes 9437184 | tf_op jit(solution)/shard_map/pallas_call | solution.py:43
  21.2 1.4 add.391
  22.6 2.6 %collective-permute-start.1 = (f32[512,128]{1,0:T(8,128)S(1)}, f32[512,128]{1,0:T(8,128)S(1)}, u32[]{:S(2)}, u32[]{:S(2)}) collective-permute-start(f32[512,128]{1,0:T(8,128)S(1)} %get-tuple-element.82), channel_id=1, source_target_pairs={{0,2},{1,3},{2,0},{3,1},{4,6},{5,7},{6,4},{7,5},{8,10},{9,11},{10,... | collective-permute-start | bytes 786440 | tf_op jit(solution)/shard_map/ppermute | solution.py:393
  25.2 1.5 collective-permute-start.2
  26.8 3.0 %collective-permute-start.10 = (f32[64,512]{1,0:T(8,128)S(1)}, f32[64,512]{1,0:T(8,128)S(1)}, u32[]{:S(2)}, u32[]{:S(2)}) collective-permute-start(f32[64,512]{1,0:T(8,128)S(1)} %get-tuple-element.96), channel_id=1, source_target_pairs={{0,6},{1,7},{2,4},{3,5},{4,2},{5,3},{6,0},{7,1},{8,14},{9,15},{10,... | collective-permute-start | bytes 393224 | tf_op jit(solution)/shard_map/ppermute | solution.py:393
  30.7 1.6 collective-permute-done.1
  32.4 2.0 collective-permute-start.9
  34.3 7.7 %collective-permute-done.2 = f32[512,128]{1,0:T(8,128)S(1)} collective-permute-done((f32[512,128]{1,0:T(8,128)S(1)}, f32[512,128]{1,0:T(8,128)S(1)}, u32[]{:S(2)}, u32[]{:S(2)}) %collective-permute-start.2) | collective-permute-done | bytes 262176 | tf_op jit(solution)/shard_map/ppermute | solution.py:393
  42.2 1.6 collective-permute-start.11
  43.9 5.2 %collective-permute-done.4 = f32[512,128]{1,0:T(8,128)S(1)} collective-permute-done((f32[512,128]{1,0:T(8,128)S(1)}, f32[512,128]{1,0:T(8,128)S(1)}, u32[]{:S(2)}, u32[]{:S(2)}) %collective-permute-start.4) | collective-permute-done | bytes 262176 | tf_op jit(solution)/shard_map/ppermute | solution.py:393
  49.1 2.3 collective-permute-start.5
  51.7 2.1 collective-permute-start.12
  53.8 0.9 multiply_reduce_fusion
  54.9 7.3 %collective-permute-done.16 = f32[552,128]{1,0:T(8,128)S(1)} collective-permute-done((f32[552,128]{1,0:T(8,128)S(1)}, f32[552,128]{1,0:T(8,128)S(1)}, u32[]{:S(2)}, u32[]{:S(2)}) %collective-permute-start.16) | collective-permute-done | bytes 282656 | tf_op jit(solution)/shard_map/ppermute | solution.py:396
  62.2 1.8 collective-permute-start.17
  64.0 3.4 %collective-permute-done.12 = f32[512,128]{1,0:T(8,128)S(1)} collective-permute-done((f32[512,128]{1,0:T(8,128)S(1)}, f32[512,128]{1,0:T(8,128)S(1)}, u32[]{:S(2)}, u32[]{:S(2)}) %collective-permute-start.12) | collective-permute-done | bytes 262176 | tf_op jit(solution)/shard_map/ppermute | solution.py:393
  67.4 2.5 %collective-permute-start.13 = (f32[1024,128]{1,0:T(8,128)S(1)}, f32[1024,128]{1,0:T(8,128)S(1)}, u32[]{:S(2)}, u32[]{:S(2)}) collective-permute-start(f32[1024,128]{1,0:T(8,128)S(1)} %pad_maximum_fusion.2.refs_2_), channel_id=1, source_target_pairs={{0,2},{1,3},{2,0},{3,1},{4,6},{5,7},{6,4},{7,5},{8,10},{9,11},{10,... | collective-permute-start | bytes 1572872 | tf_op jit(solution)/shard_map/ppermute | solution.py:393
  70.0 2.4 collective-permute-done.21
  72.6 8.6 %collective-permute-done.22 = f32[512,128]{1,0:T(8,128)S(1)} collective-permute-done((f32[512,128]{1,0:T(8,128)S(1)}, f32[512,128]{1,0:T(8,128)S(1)}, u32[]{:S(2)}, u32[]{:S(2)}) %collective-permute-start.22) | collective-permute-done | bytes 262176 | tf_op jit(solution)/shard_map/ppermute | solution.py:393
  83.0 11.9 %shard_map.79 = (bf16[512,2048]{1,0:T(8,128)(2,1)}, bf16[512,2048]{1,0:T(8,128)(2,1)}, f32[64,512]{1,0:T(8,128)S(1)}, f32[8,128]{1,0:T(8,128)S(1)}) custom-call(s32[8]{0:T(128)S(1)} %stack.229.refs_0_, s32[64]{0:T(128)S(1)} %get-tuple-element.103.refs_1_, f32[1024,128]{1,0:T(8,128)S(1)} %pad_maximum_fusion.refs_2_, ...), custom_call_target="tpu_custom_call" | custom-call | flops 12884901888 | bytes 6291456 | tf_op jit(solution)/shard_map/pallas_call | solution.py:163
  96.0 11.9 %shard_map.80 = (bf16[512,2048]{1,0:T(8,128)(2,1)}, bf16[512,2048]{1,0:T(8,128)(2,1)}, f32[64,512]{1,0:T(8,128)S(1)}, f32[8,128]{1,0:T(8,128)S(1)}) custom-call(s32[8]{0:T(128)S(1)} %stack.264.refs_0_, s32[64]{0:T(128)S(1)} %fusion.6.refs_1_, f32[1024,128]{1,0:T(8,128)S(1)} %pad_maximum_fusion.2.refs_2_, f32[1024,128]{1,0:T(8,128)} %copy-done.14, ...), custom_call_target="tpu_custom_call" | custom-call | flops 12884901888 | bytes 6291456 | tf_op jit(solution)/shard_map/pallas_call | solution.py:163
  109.9 11.9 %shard_map.81 = (bf16[512,2048]{1,0:T(8,128)(2,1)}, bf16[512,2048]{1,0:T(8,128)(2,1)}, f32[64,512]{1,0:T(8,128)S(1)}, f32[8,128]{1,0:T(8,128)S(1)}) custom-call(s32[8]{0:T(128)S(1)} %stack.229.refs_0_, s32[64]{0:T(128)S(1)} %fusion.5.refs_1_, f32[1024,128]{1,0:T(8,128)S(1)} %pad_maximum_fusion.3.refs_2_, f32[1024,128]{1,0:T(8,128)} %copy-done.16, ...), custom_call_target="tpu_custom_call" | custom-call | flops 12884901888 | bytes 6291456 | tf_op jit(solution)/shard_map/pallas_call | solution.py:163
  123.1 0.8 copy-done.18
  123.9 11.9 %shard_map.82 = (bf16[512,2048]{1,0:T(8,128)(2,1)}, bf16[512,2048]{1,0:T(8,128)(2,1)}, f32[64,512]{1,0:T(8,128)S(1)}, f32[8,128]{1,0:T(8,128)S(1)}) custom-call(s32[8]{0:T(128)S(1)} %stack.264.refs_0_, s32[64]{0:T(128)S(1)} %fusion.4.refs_1_, f32[1024,128]{1,0:T(8,128)S(1)} %pad_maximum_fusion.4.refs_2_, f32[1024,128]{1,0:T(8,128)} %collective-permute-done.23.refs_3_, ...), custom_call_target="tpu_custom_call" | custom-call | flops 12884901888 | bytes 6291456 | tf_op jit(solution)/shard_map/pallas_call | solution.py:163
  137.6 1.6 collective-permute-done.26.refs_1_
  139.2 0.8 copy-done.10
  140.0 14.0 %shard_map.83 = (f32[64,2176]{1,0:T(8,128)}, f32[64,2048]{1,0:T(8,128)}, f32[64,2048]{1,0:T(8,128)}, f32[64,2048]{1,0:T(8,128)}, f32[64,2048]{1,0:T(8,128)}, /*index=5*/f32[64,2048]{1,0:T(8,128)}, f32[64,128]{1,0:T(8,128)}) custom-call(f32[64,2176]{1,0:T(8,128)} %copy-done.7, f32[64,2176]{1,0:T(8,128)} %copy-done.10, ...), custom_call_target="tpu_custom_call" | custom-call | flops 3221225472 | bytes 16777216 | tf_op jit(solution)/shard_map/pallas_call | solution.py:307
  154.4 1.8 collective-permute-done.27.refs_1_
  156.2 0.8 copy-done.9
  157.1 14.7 %shard_map.84 = (f32[64,2176]{1,0:T(8,128)}, f32[64,2048]{1,0:T(8,128)}, f32[64,2048]{1,0:T(8,128)}, f32[64,2048]{1,0:T(8,128)}, f32[64,2048]{1,0:T(8,128)}, /*index=5*/f32[64,2048]{1,0:T(8,128)}, f32[64,128]{1,0:T(8,128)}) custom-call(f32[64,2176]{1,0:T(8,128)} %get-tuple-element.57.refs_0_, f32[64,2176]{1,0:T(8,128)} %copy-done.9, ...), custom_call_target="tpu_custom_call" | custom-call | flops 3221225472 | bytes 16777216 | tf_op jit(solution)/shard_map/pallas_call | solution.py:307
  172.2 1.8 collective-permute-done.28.refs_1_
  174.0 0.8 copy-done.8
  174.8 14.9 %shard_map.85 = (f32[64,2176]{1,0:T(8,128)}, f32[64,2048]{1,0:T(8,128)}, f32[64,2048]{1,0:T(8,128)}, f32[64,2048]{1,0:T(8,128)}, f32[64,2048]{1,0:T(8,128)}, /*index=5*/f32[64,2048]{1,0:T(8,128)}, f32[64,128]{1,0:T(8,128)}) custom-call(f32[64,2176]{1,0:T(8,128)} %get-tuple-element.64.refs_0_, f32[64,2176]{1,0:T(8,128)} %copy-done.8, ...), custom_call_target="tpu_custom_call" | custom-call | flops 3221225472 | bytes 16777216 | tf_op jit(solution)/shard_map/pallas_call | solution.py:307
  190.2 1.8 collective-permute-done.29.other_ref
  192.0 1.1 copy-done
  193.0 1.0 copy-done.1
  194.1 1.0 copy-done.2
  195.1 1.0 copy-done.3
  196.1 1.0 copy-done.4
  197.2 1.0 copy-done.5
  198.2 0.8 copy-done.6
  199.5 3.1 %collective-permute-start.39 = (f32[32,512]{1,0:T(8,128)S(1)}, f32[32,512]{1,0:T(8,128)S(1)}, u32[]{:S(2)}, u32[]{:S(2)}) collective-permute-start(f32[32,512]{1,0:T(8,128)S(1)} %get-tuple-element.87), channel_id=1, source_target_pairs={{0,24},{8,0},{16,8},{24,16},{1,25},{9,1},{17,9},{25,17},{2,26},{10... | collective-permute-start | bytes 196616 | tf_op jit(solution)/shard_map/ppermute | solution.py:396
  202.7 1.0 collective-permute-start.41
  203.7 1.1 collective-permute-start.33
  205.1 2.3 collective-permute-start.35
  207.4 2.4 collective-permute-done.33
  209.8 2.5 collective-permute-start.30
  212.3 2.4 collective-permute-start.36
  214.8 1.2 collective-permute-start.42
  216.0 8.2 %collective-permute-done.36.refs_1_ = f32[192,512]{1,0:T(8,128)S(1)} collective-permute-done((f32[192,512]{1,0:T(8,128)S(1)}, f32[192,512]{1,0:T(8,128)S(1)}, u32[]{:S(2)}, u32[]{:S(2)}) %collective-permute-start.36) | collective-permute-done | bytes 393248 | tf_op jit(solution)/shard_map/ppermute | solution.py:396
  224.1 0.7 collective-permute-start.37
  224.9 0.7 collective-permute-start.43
  225.6 1.9 collective-permute-start.44
  228.1 1.0 collective-permute-done.43
  229.1 1.6 collective-permute-done.44
  230.8 5.5 %collective-permute-done.37.refs_1_ = f32[192,512]{1,0:T(8,128)S(1)} collective-permute-done((f32[192,512]{1,0:T(8,128)S(1)}, f32[192,512]{1,0:T(8,128)S(1)}, u32[]{:S(2)}, u32[]{:S(2)}) %collective-permute-start.37) | collective-permute-done | bytes 393248 | tf_op jit(solution)/shard_map/ppermute | solution.py:396
  236.8 1.6 shard_map.87.refs_2_
  239.4 1.6 shard_map.88.refs_2_
  241.0 1.6 shard_map.89.refs_2_
  242.6 6.3 %collective-permute-done.32.refs_0_ = f32[64,512]{1,0:T(8,128)S(1)} collective-permute-done((f32[64,512]{1,0:T(8,128)S(1)}, f32[64,512]{1,0:T(8,128)S(1)}, u32[]{:S(2)}, u32[]{:S(2)}) %collective-permute-start.32) | collective-permute-done | bytes 131104 | tf_op jit(solution)/shard_map/ppermute | solution.py:396
  248.9 1.6 shard_map.90
  (142 shorter events, 13.2 us)
Async XLA Ops:
  12.5 8.7 %collective-permute-start = (f32[2048,128]{1,0:T(8,128)}, f32[2048,128]{1,0:T(8,128)S(1)}, u32[]{:S(2)}, u32[]{:S(2)}) collective-permute-start(f32[2048,128]{1,0:T(8,128)} %shard_map.78), channel_id=1, source_target_pairs={{0,1},{1,0},{2,3},{3,2},{4,5},{5,4},{6,7},{7,6},{8,9},{9,8},{10,11... | collective-permute-start | bytes 3145736 | tf_op jit(solution)/shard_map/ppermute | solution.py:393
  21.2 5.6 %copy-start.11 = (f32[256,512]{1,0:T(8,128)S(1)}, f32[256,512]{1,0:T(8,128)}, u32[]{:S(2)}) copy-start(f32[256,512]{1,0:T(8,128)} %param.11) | copy-start | bytes 1572868
  22.6 7.7 %copy-start.13 = (s32[1,4096]{1,0:T(1,128)S(1)}, s32[1,4096]{1,0:T(1,128)}, u32[]{:S(2)}) copy-start(s32[1,4096]{1,0:T(1,128)} %param.10) | copy-start | bytes 49156
  22.6 9.7 %collective-permute-start.1 = (f32[512,128]{1,0:T(8,128)S(1)}, f32[512,128]{1,0:T(8,128)S(1)}, u32[]{:S(2)}, u32[]{:S(2)}) collective-permute-start(f32[512,128]{1,0:T(8,128)S(1)} %get-tuple-element.82), channel_id=1, source_target_pairs={{0,2},{1,3},{2,0},{3,1},{4,6},{5,7},{6,4},{7,5},{8,10},{9,11},{10,... | collective-permute-start | bytes 786440 | tf_op jit(solution)/shard_map/ppermute | solution.py:393
  25.2 16.9 %collective-permute-start.2 = (f32[512,128]{1,0:T(8,128)S(1)}, f32[512,128]{1,0:T(8,128)S(1)}, u32[]{:S(2)}, u32[]{:S(2)}) collective-permute-start(f32[512,128]{1,0:T(8,128)S(1)} %get-tuple-element.84), channel_id=1, source_target_pairs={{0,4},{1,5},{2,6},{3,7},{4,0},{5,1},{6,2},{7,3},{8,12},{9,13},{10,... | collective-permute-start | bytes 786440 | tf_op jit(solution)/shard_map/ppermute | solution.py:393
  26.7 15.3 %collective-permute-start.3 = (f32[512,128]{1,0:T(8,128)S(1)}, f32[512,128]{1,0:T(8,128)S(1)}, u32[]{:S(2)}, u32[]{:S(2)}) collective-permute-start(f32[512,128]{1,0:T(8,128)S(1)} %get-tuple-element.83), channel_id=1, source_target_pairs={{0,6},{1,7},{2,4},{3,5},{4,2},{5,3},{6,0},{7,1},{8,14},{9,15},{10,... | collective-permute-start | bytes 786440 | tf_op jit(solution)/shard_map/ppermute | solution.py:393
  26.8 27.0 %collective-permute-start.10 = (f32[64,512]{1,0:T(8,128)S(1)}, f32[64,512]{1,0:T(8,128)S(1)}, u32[]{:S(2)}, u32[]{:S(2)}) collective-permute-start(f32[64,512]{1,0:T(8,128)S(1)} %get-tuple-element.96), channel_id=1, source_target_pairs={{0,6},{1,7},{2,4},{3,5},{4,2},{5,3},{6,0},{7,1},{8,14},{9,15},{10,... | collective-permute-start | bytes 393224 | tf_op jit(solution)/shard_map/ppermute | solution.py:393
  29.8 24.1 %collective-permute-start.8 = (f32[64,512]{1,0:T(8,128)S(1)}, f32[64,512]{1,0:T(8,128)S(1)}, u32[]{:S(2)}, u32[]{:S(2)}) collective-permute-start(f32[64,512]{1,0:T(8,128)S(1)} %get-tuple-element.95), channel_id=1, source_target_pairs={{0,2},{1,3},{2,0},{3,1},{4,6},{5,7},{6,4},{7,5},{8,10},{9,11},{10,... | collective-permute-start | bytes 393224 | tf_op jit(solution)/shard_map/ppermute | solution.py:393
  32.4 21.5 %collective-permute-start.9 = (f32[64,512]{1,0:T(8,128)S(1)}, f32[64,512]{1,0:T(8,128)S(1)}, u32[]{:S(2)}, u32[]{:S(2)}) collective-permute-start(f32[64,512]{1,0:T(8,128)S(1)} %get-tuple-element.97), channel_id=1, source_target_pairs={{0,4},{1,5},{2,6},{3,7},{4,0},{5,1},{6,2},{7,3},{8,12},{9,13},{10,... | collective-permute-start | bytes 393224 | tf_op jit(solution)/shard_map/ppermute | solution.py:393
  42.1 7.0 %collective-permute-start.4 = (f32[512,128]{1,0:T(8,128)S(1)}, f32[512,128]{1,0:T(8,128)S(1)}, u32[]{:S(2)}, u32[]{:S(2)}) collective-permute-start(f32[512,128]{1,0:T(8,128)S(1)} %fusion.1), channel_id=1, source_target_pairs={{0,2},{1,3},{2,0},{3,1},{4,6},{5,7},{6,4},{7,5},{8,10},{9,11},{10,... | collective-permute-start | bytes 786440 | tf_op jit(solution)/shard_map/ppermute | solution.py:393
  42.2 9.4 %collective-permute-start.11 = (f32[552,128]{1,0:T(8,128)S(1)}, f32[552,128]{1,0:T(8,128)S(1)}, u32[]{:S(2)}, u32[]{:S(2)}) collective-permute-start(f32[552,128]{1,0:T(8,128)S(1)} %select_maximum_fusion), channel_id=1, source_target_pairs={{0,8},{8,16},{16,24},{24,0},{1,9},{9,17},{17,25},{25,1},{2,10},{10... | collective-permute-start | bytes 847880 | tf_op jit(solution)/shard_map/ppermute | solution.py:396
  49.1 20.9 %collective-permute-start.5 = (f32[1024,128]{1,0:T(8,128)S(1)}, f32[1024,128]{1,0:T(8,128)}, u32[]{:S(2)}, u32[]{:S(2)}) collective-permute-start(f32[1024,128]{1,0:T(8,128)S(1)} %pad_maximum_fusion.refs_2_), channel_id=1, source_target_pairs={{0,4},{1,5},{2,6},{3,7},{4,0},{5,1},{6,2},{7,3},{8,12},{9,13},{10,... | collective-permute-start | bytes 1572872 | tf_op jit(solution)/shard_map/ppermute | solution.py:393
  51.7 15.7 %collective-permute-start.12 = (f32[512,128]{1,0:T(8,128)S(1)}, f32[512,128]{1,0:T(8,128)S(1)}, u32[]{:S(2)}, u32[]{:S(2)}) collective-permute-start(f32[512,128]{1,0:T(8,128)S(1)} %slice.94), channel_id=1, source_target_pairs={{0,4},{1,5},{2,6},{3,7},{4,0},{5,1},{6,2},{7,3},{8,12},{9,13},{10,... | collective-permute-start | bytes 786440 | tf_op jit(solution)/shard_map/ppermute | solution.py:393
  53.8 8.4 %collective-permute-start.16 = (f32[552,128]{1,0:T(8,128)S(1)}, f32[552,128]{1,0:T(8,128)S(1)}, u32[]{:S(2)}, u32[]{:S(2)}) collective-permute-start(f32[552,128]{1,0:T(8,128)S(1)} %collective-permute-done.11), channel_id=1, source_target_pairs={{0,8},{8,16},{16,24},{24,0},{1,9},{9,17},{17,25},{25,1},{2,10},{10... | collective-permute-start | bytes 847880 | tf_op jit(solution)/shard_map/ppermute | solution.py:396
  54.9 26.7 %collective-permute-start.6 = (f32[1024,128]{1,0:T(8,128)S(1)}, f32[1024,128]{1,0:T(8,128)S(1)}, u32[]{:S(2)}, u32[]{:S(2)}) collective-permute-start(f32[1024,128]{1,0:T(8,128)S(1)} %pad_maximum_fusion.refs_2_), channel_id=1, source_target_pairs={{0,1},{1,0},{2,3},{3,2},{4,5},{5,4},{6,7},{7,6},{8,9},{9,8},{10,11... | collective-permute-start | bytes 1572872 | tf_op jit(solution)/shard_map/ppermute | solution.py:393
  62.2 10.2 %collective-permute-start.17 = (f32[512,128]{1,0:T(8,128)S(1)}, f32[512,128]{1,0:T(8,128)S(1)}, u32[]{:S(2)}, u32[]{:S(2)}) collective-permute-start(f32[512,128]{1,0:T(8,128)S(1)} %slice.97), channel_id=1, source_target_pairs={{0,2},{1,3},{2,0},{3,1},{4,6},{5,7},{6,4},{7,5},{8,10},{9,11},{10,... | collective-permute-start | bytes 786440 | tf_op jit(solution)/shard_map/ppermute | solution.py:393
  64.0 8.4 %collective-permute-start.21 = (f32[552,128]{1,0:T(8,128)S(1)}, f32[552,128]{1,0:T(8,128)S(1)}, u32[]{:S(2)}, u32[]{:S(2)}) collective-permute-start(f32[552,128]{1,0:T(8,128)S(1)} %collective-permute-done.16), channel_id=1, source_target_pairs={{0,8},{8,16},{16,24},{24,0},{1,9},{9,17},{17,25},{25,1},{2,10},{10... | collective-permute-start | bytes 847880 | tf_op jit(solution)/shard_map/ppermute | solution.py:396
  67.4 14.2 %collective-permute-start.13 = (f32[1024,128]{1,0:T(8,128)S(1)}, f32[1024,128]{1,0:T(8,128)S(1)}, u32[]{:S(2)}, u32[]{:S(2)}) collective-permute-start(f32[1024,128]{1,0:T(8,128)S(1)} %pad_maximum_fusion.2.refs_2_), channel_id=1, source_target_pairs={{0,2},{1,3},{2,0},{3,1},{4,6},{5,7},{6,4},{7,5},{8,10},{9,11},{10,... | collective-permute-start | bytes 1572872 | tf_op jit(solution)/shard_map/ppermute | solution.py:393
  70.0 12.2 %collective-permute-start.7 = (f32[1024,128]{1,0:T(8,128)}, f32[1024,128]{1,0:T(8,128)S(1)}, u32[]{:S(2)}, u32[]{:S(2)}) collective-permute-start(f32[1024,128]{1,0:T(8,128)} %collective-permute-done.5.refs_3_), channel_id=1, source_target_pairs={{0,1},{1,0},{2,3},{3,2},{4,5},{5,4},{6,7},{7,6},{8,9},{9,8},{10,11... | collective-permute-start | bytes 1572872 | tf_op jit(solution)/shard_map/ppermute | solution.py:393
  72.4 23.0 %collective-permute-start.14 = (f32[1024,128]{1,0:T(8,128)S(1)}, f32[1024,128]{1,0:T(8,128)}, u32[]{:S(2)}, u32[]{:S(2)}) collective-permute-start(f32[1024,128]{1,0:T(8,128)S(1)} %pad_maximum_fusion.2.refs_2_), channel_id=1, source_target_pairs={{0,1},{1,0},{2,3},{3,2},{4,5},{5,4},{6,7},{7,6},{8,9},{9,8},{10,11... | collective-permute-start | bytes 1572872 | tf_op jit(solution)/shard_map/ppermute | solution.py:393
  72.4 8.8 %collective-permute-start.22 = (f32[512,128]{1,0:T(8,128)S(1)}, f32[512,128]{1,0:T(8,128)S(1)}, u32[]{:S(2)}, u32[]{:S(2)}) collective-permute-start(f32[512,128]{1,0:T(8,128)S(1)} %slice.100), channel_id=1, source_target_pairs={{0,4},{1,5},{2,6},{3,7},{4,0},{5,1},{6,2},{7,3},{8,12},{9,13},{10,... | collective-permute-start | bytes 786440 | tf_op jit(solution)/shard_map/ppermute | solution.py:393
  81.2 14.4 %collective-permute-start.18 = (f32[1024,128]{1,0:T(8,128)S(1)}, f32[1024,128]{1,0:T(8,128)S(1)}, u32[]{:S(2)}, u32[]{:S(2)}) collective-permute-start(f32[1024,128]{1,0:T(8,128)S(1)} %pad_maximum_fusion.3.refs_2_), channel_id=1, source_target_pairs={{0,4},{1,5},{2,6},{3,7},{4,0},{5,1},{6,2},{7,3},{8,12},{9,13},{10,... | collective-permute-start | bytes 1572872 | tf_op jit(solution)/shard_map/ppermute | solution.py:393
  81.6 0.9 copy-start.15
  81.6 28.3 %collective-permute-start.19 = (f32[1024,128]{1,0:T(8,128)S(1)}, f32[1024,128]{1,0:T(8,128)}, u32[]{:S(2)}, u32[]{:S(2)}) collective-permute-start(f32[1024,128]{1,0:T(8,128)S(1)} %pad_maximum_fusion.3.refs_2_), channel_id=1, source_target_pairs={{0,1},{1,0},{2,3},{3,2},{4,5},{5,4},{6,7},{7,6},{8,9},{9,8},{10,11... | collective-permute-start | bytes 1572872 | tf_op jit(solution)/shard_map/ppermute | solution.py:393
  81.7 13.2 %copy-start.14 = (f32[1024,128]{1,0:T(8,128)}, f32[1024,128]{1,0:T(8,128)S(1)}, u32[]{:S(2)}) copy-start(f32[1024,128]{1,0:T(8,128)S(1)} %collective-permute-done.13.refs_3_) | copy-start | bytes 1572868
  81.7 14.3 %collective-permute-start.15 = (f32[1024,128]{1,0:T(8,128)S(1)}, f32[1024,128]{1,0:T(8,128)}, u32[]{:S(2)}, u32[]{:S(2)}) collective-permute-start(f32[1024,128]{1,0:T(8,128)S(1)} %collective-permute-done.13.refs_3_), channel_id=1, source_target_pairs={{0,1},{1,0},{2,3},{3,2},{4,5},{5,4},{6,7},{7,6},{8,9},{9,8},{10,11... | collective-permute-start | bytes 1572872 | tf_op jit(solution)/shard_map/ppermute | solution.py:393
  82.2 0.8 copy-start.17
  82.2 27.5 %collective-permute-start.23 = (f32[1024,128]{1,0:T(8,128)S(1)}, f32[1024,128]{1,0:T(8,128)}, u32[]{:S(2)}, u32[]{:S(2)}) collective-permute-start(f32[1024,128]{1,0:T(8,128)S(1)} %pad_maximum_fusion.4.refs_2_), channel_id=1, source_target_pairs={{0,2},{1,3},{2,0},{3,1},{4,6},{5,7},{6,4},{7,5},{8,10},{9,11},{10,... | collective-permute-start | bytes 1572872 | tf_op jit(solution)/shard_map/ppermute | solution.py:393
  95.5 27.6 %collective-permute-start.24 = (f32[1024,128]{1,0:T(8,128)S(1)}, f32[1024,128]{1,0:T(8,128)}, u32[]{:S(2)}, u32[]{:S(2)}) collective-permute-start(f32[1024,128]{1,0:T(8,128)S(1)} %pad_maximum_fusion.4.refs_2_), channel_id=1, source_target_pairs={{0,1},{1,0},{2,3},{3,2},{4,5},{5,4},{6,7},{7,6},{8,9},{9,8},{10,11... | collective-permute-start | bytes 1572872 | tf_op jit(solution)/shard_map/ppermute | solution.py:393
  95.6 12.3 %copy-start.16 = (f32[1024,128]{1,0:T(8,128)}, f32[1024,128]{1,0:T(8,128)S(1)}, u32[]{:S(2)}) copy-start(f32[1024,128]{1,0:T(8,128)S(1)} %collective-permute-done.18.refs_3_) | copy-start | bytes 1572868
  95.6 14.3 %collective-permute-start.20 = (f32[1024,128]{1,0:T(8,128)S(1)}, f32[1024,128]{1,0:T(8,128)}, u32[]{:S(2)}, u32[]{:S(2)}) collective-permute-start(f32[1024,128]{1,0:T(8,128)S(1)} %collective-permute-done.18.refs_3_), channel_id=1, source_target_pairs={{0,1},{1,0},{2,3},{3,2},{4,5},{5,4},{6,7},{7,6},{8,9},{9,8},{10,11... | collective-permute-start | bytes 1572872 | tf_op jit(solution)/shard_map/ppermute | solution.py:393
  109.7 13.4 %collective-permute-start.25 = (f32[1024,128]{1,0:T(8,128)}, f32[1024,128]{1,0:T(8,128)S(1)}, u32[]{:S(2)}, u32[]{:S(2)}) collective-permute-start(f32[1024,128]{1,0:T(8,128)} %collective-permute-done.23.refs_3_), channel_id=1, source_target_pairs={{0,1},{1,0},{2,3},{3,2},{4,5},{5,4},{6,7},{7,6},{8,9},{9,8},{10,11... | collective-permute-start | bytes 1572872 | tf_op jit(solution)/shard_map/ppermute | solution.py:393
  123.1 0.8 copy-start.18
  137.2 2.0 copy-start.7
  137.2 2.0 collective-permute-start.26
  139.2 0.8 copy-start.10
  154.0 2.2 collective-permute-start.27
  156.2 0.8 copy-start.9
  171.7 2.2 collective-permute-start.28
  174.0 0.8 copy-start.8
  189.7 2.2 collective-permute-start.29
  192.0 1.1 copy-start
  193.0 1.0 copy-start.1
  194.1 1.0 copy-start.2
  195.1 1.0 copy-start.3
  196.1 1.0 copy-start.4
  197.2 1.0 copy-start.5
  199.5 5.6 %collective-permute-start.39 = (f32[32,512]{1,0:T(8,128)S(1)}, f32[32,512]{1,0:T(8,128)S(1)}, u32[]{:S(2)}, u32[]{:S(2)}) collective-permute-start(f32[32,512]{1,0:T(8,128)S(1)} %get-tuple-element.87), channel_id=1, source_target_pairs={{0,24},{8,0},{16,8},{24,16},{1,25},{9,1},{17,9},{25,17},{2,26},{10... | collective-permute-start | bytes 196616 | tf_op jit(solution)/shard_map/ppermute | solution.py:396
  202.6 12.1 %collective-permute-start.40 = (f32[32,512]{1,0:T(8,128)S(1)}, f32[32,512]{1,0:T(8,128)S(1)}, u32[]{:S(2)}, u32[]{:S(2)}) collective-permute-start(f32[32,512]{1,0:T(8,128)S(1)} %get-tuple-element.86), channel_id=1, source_target_pairs={{0,16},{8,24},{16,0},{24,8},{1,17},{9,25},{17,1},{25,9},{2,18},{10... | collective-permute-start | bytes 196616 | tf_op jit(solution)/shard_map/ppermute | solution.py:396
  202.7 12.1 %collective-permute-start.41 = (f32[32,512]{1,0:T(8,128)S(1)}, f32[32,512]{1,0:T(8,128)S(1)}, u32[]{:S(2)}, u32[]{:S(2)}) collective-permute-start(f32[32,512]{1,0:T(8,128)S(1)} %get-tuple-element.85), channel_id=1, source_target_pairs={{0,8},{8,16},{16,24},{24,0},{1,9},{9,17},{17,25},{25,1},{2,10},{10... | collective-permute-start | bytes 196616 | tf_op jit(solution)/shard_map/ppermute | solution.py:396
  203.7 6.1 %collective-permute-start.33 = (f32[64,512]{1,0:T(8,128)S(1)}, f32[64,512]{1,0:T(8,128)S(1)}, u32[]{:S(2)}, u32[]{:S(2)}) collective-permute-start(f32[64,512]{1,0:T(8,128)S(1)} %get-tuple-element.90), channel_id=1, source_target_pairs={{0,2},{1,3},{2,0},{3,1},{4,6},{5,7},{6,4},{7,5},{8,10},{9,11},{10,... | collective-permute-start | bytes 393224 | tf_op jit(solution)/shard_map/ppermute | solution.py:393
  204.8 7.4 %collective-permute-start.34 = (f32[64,512]{1,0:T(8,128)S(1)}, f32[64,512]{1,0:T(8,128)S(1)}, u32[]{:S(2)}, u32[]{:S(2)}) collective-permute-start(f32[64,512]{1,0:T(8,128)S(1)} %get-tuple-element.89), channel_id=1, source_target_pairs={{0,4},{1,5},{2,6},{3,7},{4,0},{5,1},{6,2},{7,3},{8,12},{9,13},{10,... | collective-permute-start | bytes 393224 | tf_op jit(solution)/shard_map/ppermute | solution.py:393
  205.1 7.2 %collective-permute-start.35 = (f32[64,512]{1,0:T(8,128)S(1)}, f32[64,512]{1,0:T(8,128)S(1)}, u32[]{:S(2)}, u32[]{:S(2)}) collective-permute-start(f32[64,512]{1,0:T(8,128)S(1)} %get-tuple-element.88), channel_id=1, source_target_pairs={{0,6},{1,7},{2,4},{3,5},{4,2},{5,3},{6,0},{7,1},{8,14},{9,15},{10,... | collective-permute-start | bytes 393224 | tf_op jit(solution)/shard_map/ppermute | solution.py:393
  209.8 17.7 %collective-permute-start.30 = (f32[64,512]{1,0:T(8,128)S(1)}, f32[64,512]{1,0:T(8,128)S(1)}, u32[]{:S(2)}, u32[]{:S(2)}) collective-permute-start(f32[64,512]{1,0:T(8,128)S(1)} %get-tuple-element.91.refs_0_), channel_id=1, source_target_pairs={{0,8},{8,16},{16,24},{24,0},{1,9},{9,17},{17,25},{25,1},{2,10},{10... | collective-permute-start | bytes 393224 | tf_op jit(solution)/shard_map/ppermute | solution.py:396
  212.3 11.8 %collective-permute-start.36 = (f32[192,512]{1,0:T(8,128)S(1)}, f32[192,512]{1,0:T(8,128)S(1)}, u32[]{:S(2)}, u32[]{:S(2)}) collective-permute-start(f32[192,512]{1,0:T(8,128)S(1)} %constant_dynamic-update-slice_fusion.refs_1_), channel_id=1, source_target_pairs={{0,8},{8,16},{16,24},{24,0},{1,9},{9,17},{17,25},{25,1},{2,10},{10... | collective-permute-start | bytes 1179656 | tf_op jit(solution)/shard_map/ppermute | solution.py:396
  214.8 13.3 %collective-permute-start.42 = (f32[1,32,512]{2,1,0:T(8,128)S(1)}, f32[1,32,512]{2,1,0:T(8,128)S(1)}, u32[]{:S(2)}, u32[]{:S(2)}) collective-permute-start(f32[1,32,512]{2,1,0:T(8,128)S(1)} %get-tuple-element.100), channel_id=1, source_target_pairs={{0,2},{1,3},{2,0},{3,1},{4,6},{5,7},{6,4},{7,5},{8,10},{9,11},{10,... | collective-permute-start | bytes 196616 | tf_op jit(solution)/shard_map/ppermute | solution.py:393
  224.1 12.1 %collective-permute-start.37 = (f32[192,512]{1,0:T(8,128)S(1)}, f32[192,512]{1,0:T(8,128)S(1)}, u32[]{:S(2)}, u32[]{:S(2)}) collective-permute-start(f32[192,512]{1,0:T(8,128)S(1)} %collective-permute-done.36.refs_1_), channel_id=1, source_target_pairs={{0,8},{8,16},{16,24},{24,0},{1,9},{9,17},{17,25},{25,1},{2,10},{10... | collective-permute-start | bytes 1179656 | tf_op jit(solution)/shard_map/ppermute | solution.py:396
  224.9 4.3 %collective-permute-start.43 = (f32[1,32,512]{2,1,0:T(8,128)S(1)}, f32[1,32,512]{2,1,0:T(8,128)S(1)}, u32[]{:S(2)}, u32[]{:S(2)}) collective-permute-start(f32[1,32,512]{2,1,0:T(8,128)S(1)} %get-tuple-element.99), channel_id=1, source_target_pairs={{0,4},{1,5},{2,6},{3,7},{4,0},{5,1},{6,2},{7,3},{8,12},{9,13},{10,... | collective-permute-start | bytes 196616 | tf_op jit(solution)/shard_map/ppermute | solution.py:393
  225.6 5.2 %collective-permute-start.44 = (f32[1,32,512]{2,1,0:T(8,128)S(1)}, f32[1,32,512]{2,1,0:T(8,128)S(1)}, u32[]{:S(2)}, u32[]{:S(2)}) collective-permute-start(f32[1,32,512]{2,1,0:T(8,128)S(1)} %get-tuple-element.98), channel_id=1, source_target_pairs={{0,6},{1,7},{2,4},{3,5},{4,2},{5,3},{6,0},{7,1},{8,14},{9,15},{10,... | collective-permute-start | bytes 196616 | tf_op jit(solution)/shard_map/ppermute | solution.py:393
  227.5 11.5 %collective-permute-start.31 = (f32[64,512]{1,0:T(8,128)S(1)}, f32[64,512]{1,0:T(8,128)S(1)}, u32[]{:S(2)}, u32[]{:S(2)}) collective-permute-start(f32[64,512]{1,0:T(8,128)S(1)} %collective-permute-done.30.refs_0_), channel_id=1, source_target_pairs={{0,8},{8,16},{16,24},{24,0},{1,9},{9,17},{17,25},{25,1},{2,10},{10... | collective-permute-start | bytes 393224 | tf_op jit(solution)/shard_map/ppermute | solution.py:396
  236.3 12.6 %collective-permute-start.38 = (f32[192,512]{1,0:T(8,128)S(1)}, f32[192,512]{1,0:T(8,128)S(1)}, u32[]{:S(2)}, u32[]{:S(2)}) collective-permute-start(f32[192,512]{1,0:T(8,128)S(1)} %collective-permute-done.37.refs_1_), channel_id=1, source_target_pairs={{0,8},{8,16},{16,24},{24,0},{1,9},{9,17},{17,25},{25,1},{2,10},{10... | collective-permute-start | bytes 1179656 | tf_op jit(solution)/shard_map/ppermute | solution.py:396
  236.3 3.1 %collective-permute-start.45 = (f32[2,32,512]{2,1,0:T(8,128)S(1)}, f32[2,32,512]{2,1,0:T(8,128)S(1)}, u32[]{:S(2)}, u32[]{:S(2)}) collective-permute-start(f32[2,32,512]{2,1,0:T(8,128)S(1)} %constant_dynamic-slice_fusion), channel_id=1, source_target_pairs={{0,1},{1,0},{2,3},{3,2},{4,5},{5,4},{6,7},{7,6},{8,9},{9,8},{10,11... | collective-permute-start | bytes 393224 | tf_op jit(solution)/shard_map/ppermute | solution.py:393
  239.0 9.9 %collective-permute-start.32 = (f32[64,512]{1,0:T(8,128)S(1)}, f32[64,512]{1,0:T(8,128)S(1)}, u32[]{:S(2)}, u32[]{:S(2)}) collective-permute-start(f32[64,512]{1,0:T(8,128)S(1)} %collective-permute-done.31.refs_0_), channel_id=1, source_target_pairs={{0,8},{8,16},{16,24},{24,0},{1,9},{9,17},{17,25},{25,1},{2,10},{10... | collective-permute-start | bytes 393224 | tf_op jit(solution)/shard_map/ppermute | solution.py:396
  239.4 1.6 copy-start.12
  (1 other events, 0.8 us)

commit v3 on v2

--- a/solution.py
+++ b/solution.py
@@ -33,7 +33,7 @@
 def project_kernel(order_ref, act_ref, grad_ref, wi_ref, wo_ref, out_ref):
     del order_ref
     out_ref[...] = jnp.concatenate(
-        [dot_nn(act_ref[...], wi_ref[...]), dot_nn(grad_ref[...], wo_ref[...])], axis=1
+        [dot_nt(act_ref[...], wi_ref[...]), dot_nt(grad_ref[...], wo_ref[...])], axis=1
     )
 
 
@@ -56,7 +56,7 @@
         ),
         compiler_params=pltpu.CompilerParams(vmem_limit_bytes=61 * MIB),
         cost_estimate=pl.CostEstimate(
-            flops=2 * steps * block * (feats + hidden) * LANES,
+            flops=2 * steps * block * (feats + hidden) * 4 * WINDOW,
             bytes_accessed=2 * steps * block * (feats + hidden),
             transcendentals=0,
         ),
@@ -147,10 +147,10 @@
     for k in range(1, values.shape[1] // LANES):
         total = total + sq[:, k * LANES:(k + 1) * LANES]
     sq_ref[...] += total
-    b_high, b_low = split2(b_ref[...])
-    both = dot_nt(jnp.concatenate([b_high, b_low], axis=0), high)
-    count = b_high.shape[0]
-    inner_ref[...] = both[:count] + both[count:] + dot_nt(b_high, low)
+    b_both = jnp.concatenate(split2(b_ref[...]), axis=0)
+    count = b_ref.shape[0]
+    both = (dot_nt(high, b_both) + dot_nt(low, b_both)).T
+    inner_ref[...] = both[:count] + both[count:]
 
 
 def build(offs, starts, sources, ids, pick, b, ranks, share):
@@ -186,7 +186,7 @@
                 pltpu.VMEM((ex_block, comps), F32),
             ],
         ),
-        compiler_params=pltpu.CompilerParams(vmem_limit_bytes=53 * MIB),
+        compiler_params=pltpu.CompilerParams(vmem_limit_bytes=50 * MIB),
         cost_estimate=pl.CostEstimate(
             flops=12 * EX_DEV * half_ranks * WINDOW * 2 * LANES,
             bytes_accessed=4 * EX_DEV * comps + 4 * tokens * LANES,
@@ -267,12 +267,10 @@
         q = q + both[:count] + both[count:] + dot_nn(s_two[0:count, part], lows[k][...])
     r_new = r - alpha * (q / examples + damping * p)
     r_out[...] = r_new
-    high, low = split2(r_new)
-    stacked = jnp.concatenate([high, low], axis=0)
+    stacked = jnp.concatenate(split2(r_new), axis=0)
     for k in range(planes):
         part = slice(k * EX_DEV, (k + 1) * EX_DEV)
-        both = dot_nt(stacked, highs[k][...])
-        z_acc[:, part] += both[:count] + both[count:] + dot_nt(high, lows[k][...])
+        z_acc[part, :] += dot_nt(highs[k][...], stacked) + dot_nt(lows[k][...], stacked)
     stats_acc[...] += lanes_of(
         [
             jnp.sum(r_new * r_new, axis=1, keepdims=True),
@@ -283,7 +281,8 @@
 
     @pl.when(step == pl.num_programs(0) - 1)
     def _():
-        msg_out[:, 0:examples] = z_acc[...]
+        both = z_acc[...].T
+        msg_out[:, 0:examples] = both[:count] + both[count:]
         msg_out[:, examples:] = stats_acc[...]
 
 
@@ -312,7 +311,7 @@
         out_specs=[full(message), piece, piece, piece, full(wide), full(wide), full(small)],
         scratch_shapes=[
             pltpu.VMEM((2 * count, examples), BF16),
-            pltpu.VMEM((count, examples), F32),
+            pltpu.VMEM((examples, 2 * count), F32),
             pltpu.VMEM((count, LANES), F32),
             pltpu.VMEM((count, LANES), F32),
         ],
@@ -336,10 +335,14 @@
 
 def last_step(examples, comps_all, *arrays):
     x, y = arrays[4], arrays[6]
+    full = lambda a: pl.BlockSpec(a.shape, lambda i: (0, 0))
     return pl.pallas_call(
         functools.partial(last_kernel, examples, comps_all),
         out_shape=(jax.ShapeDtypeStruct(x.shape, F32), jax.ShapeDtypeStruct(y.shape, F32)),
-        compiler_params=pltpu.CompilerParams(vmem_limit_bytes=24 * MIB),
+        grid=(1,),
+        in_specs=[full(a) for a in arrays],
+        out_specs=(full(x), full(y)),
+        compiler_params=pltpu.CompilerParams(vmem_limit_bytes=60 * MIB),
     )(*arrays)
 
 
@@ -395,6 +398,9 @@
     def shift(values, by):
         return lax.ppermute(values, "dp", [(a, (a + by) % n_dp) for a in range(n_dp)])
 
+    def tie(values, token):
+        return lax.optimization_barrier((values, token))[0]
+
     near_chip = [chip ^ k for k in range(n_c)]
 
     q_chip = queries.shape[0] // n_c
@@ -417,8 +423,9 @@
 
     share = tokens // n_t
     blocks = jnp.stack(near_chip).astype(jnp.int32) * 2
-    give = project(blocks + 1 - core, activations, out_grads, proj_in, proj_out, share)
-    keep = project(blocks + core, activations, out_grads, proj_in, proj_out, share)
+    w_in, w_out = proj_in.T, proj_out.T
+    give = project(blocks + 1 - core, activations, out_grads, w_in, w_out, share)
+    keep = project(tie(blocks + core, slots), activations, out_grads, w_in, w_out, share)
     kept = (keep + swap(give, 1)).reshape((n_c, share, LANES))
     own = kept[0]
     for k in range(1, n_c):
@@ -438,11 +445,14 @@
         order = list(range(bits))
         if away % 2:
             order = order[::-1]
-        held, ks = rings[away][:share], [0]
-        for bit in order[:-1]:
-            held = jnp.concatenate([held, swap(held, 2 << bit)], axis=0)
+        after = lambda values, stage: (
+            tie(values, squares[away - bits - 1 + stage]) if away > bits - stage else values
+        )
+        held, ks = after(rings[away][:share], 0), [0]
+        for stage, bit in enumerate(order[:-1]):
+            held = jnp.concatenate([held, after(swap(held, 2 << bit), stage + 1)], axis=0)
             ks = ks + [k | (1 << bit) for k in ks]
-        came = swap(held, 2 << order[-1])
+        came = after(swap(held, 2 << order[-1]), bits)
         ks = ks + [k | (1 << order[-1]) for k in ks]
         sources = [held, came, swap(held, 1), swap(came, 1)]
         offs = jnp.stack(
@@ -481,12 +491,16 @@
     others_x = jnp.concatenate(
         [swap(x[:, k * per_slot:(k + 1) * per_slot], 2 * k) for k in range(1, n_c)], axis=0
     )
+    y, others_x = lax.optimization_barrier((y, others_x))
+    own_parts = [own_x] + [shift(own_x, away) for away in range(1, n_dp)]
     out = None
     for away in range(n_dp):
+        if away == 2:
+            others_x = tie(others_x, own_parts)
         if away:
-            own_x, others_x = shift(own_x, 1), shift(others_x, 1)
+            others_x = shift(others_x, 1)
         where = jnp.stack([(i - away) % n_dp] + near_chip).astype(jnp.int32)
-        out = place(where, own_x, others_x, out, (per_slot, n_dp * n_c * q_chip))
+        out = place(where, own_parts[away], others_x, out, (per_slot, n_dp * n_c * q_chip))
 
     part_q = q_chip // 2
     mine = lax.dynamic_slice_in_dim(y, core * part_q, part_q, 0)

time: 251 us -> 271 us (1.080)
  waiting for transfers between devices: 69 us -> 86.8 us
  starting transfers between devices: 42.4 us -> 49.5 us
  local copies, waits for them, and re-layouts: 15.5 us -> 10.2 us
    ppermute x34, waiting for transfers between devices: 38.6 us -> 62.9 us  [swap(): return lax.ppermute(values, 'tensor', [(a, a ^ mask) for a in range(n_t)])]
    unnamed x42 -> x27, local copies, waits for them, and re-layouts: 14.3 us -> 3.99 us
    ppermute x12, starting transfers between devices: 12.3 us -> 22.4 us  [shift(): lax.ppermute(values, 'dp', [(a, (a + by) % n_dp) for a in range(n_dp)])]
    ppermute x12, waiting for transfers between devices: 30.5 us -> 23.8 us  [shift(): lax.ppermute(values, 'dp', [(a, (a + by) % n_dp) for a in range(n_dp)])]
    pallas_call x4, Pallas kernels: 47.6 us -> 43.1 us  [build(): pl.pallas_call(functools.partial(build_kernel, ranks, share, ex_block, le...]
    ppermute x34, starting transfers between devices: 30.1 us -> 27 us  [swap(): return lax.ppermute(values, 'tensor', [(a, a ^ mask) for a in range(n_t)])]
    pallas_call x1, Pallas kernels: 0.48 us -> 3.48 us  [last_step(): pl.pallas_call(functools.partial(last_kernel, examples, comps_all), out_s...]
  transfers between devices with their start and end apart: 46 -> 46, of which waited for: 19 -> 25; matrix products, arithmetic and copies ran while one was open for 2% -> 4% of each run, Pallas kernels for 19% -> 17%
where the time goes in v3:
time: 271 us
  Pallas kernels  112 us (41%)
  waiting for transfers between devices  86.8 us (32%)
  starting transfers between devices  49.5 us (18%)
  local copies, waits for them, and re-layouts  10.2 us (4%)
  other arithmetic  8.75 us (3%)
  between operations  3.6 us (1%)
    ppermute x34, waiting for transfers between devices, swap(): return lax.ppermute(values, 'tensor', [(a, a ^ mask) for a in range(n_t)])  62.9 us
    pallas_call x3, Pallas kernels, one_step(): pl.pallas_call(functools.partial(step_kernel, first, planes, examples, co...  43.8 us
    pallas_call x4, Pallas kernels, build(): pl.pallas_call(functools.partial(build_kernel, ranks, share, ex_block, le...  43.1 us
    ppermute x34, starting transfers between devices, swap(): return lax.ppermute(values, 'tensor', [(a, a ^ mask) for a in range(n_t)])  27 us
    ppermute x12, waiting for transfers between devices, shift(): lax.ppermute(values, 'dp', [(a, (a + by) % n_dp) for a in range(n_dp)])  23.8 us
    ppermute x12, starting transfers between devices, shift(): lax.ppermute(values, 'dp', [(a, (a + by) % n_dp) for a in range(n_dp)])  22.4 us
    pallas_call x2, Pallas kernels, project(): pl.pallas_call(project_kernel, out_shape=jax.ShapeDtypeStruct((steps * bl...  15.2 us
    pallas_call x4, Pallas kernels, place(): pl.pallas_call(place_kernel, out_shape=jax.ShapeDtypeStruct(shape, F32),...  6.31 us
  transfers between devices with their start and end apart: 46, of which 25 were waited for; matrix products, arithmetic and copies ran while one was open for 4% of the time, Pallas kernels for 17%

profile of v3, /device:TPU:0, one launch (start us, length us, event | category | flops | bytes accessed | tf_op | source)
XLA Modules:
  0.0 270.5 jit_solution(5166854034992052518)
XLA Ops:
  1.2 7.7 %shard_map.78 = f32[2048,128]{1,0:T(8,128)} custom-call(s32[4]{0:T(128)} %get-tuple-element.100.order_ref, bf16[4096,512]{1,0:T(8,128)(2,1)} %act_ref.3, bf16[4096,1792]{1,0:T(8,128)(2,1)} %grad_ref.3, bf16[64,512]{1,0:T(8,128)(2,1)} %bitcast.90, bf16[64,1792]{1,0:T(8,128)(2,1)} %bitcast.88), custom_call_target="tpu_custom_call" | custom-call | flops 9663676416 | bytes 9437184 | tf_op jit(solution)/shard_map/pallas_call | solution.py:43
  10.1 2.5 collective-permute-start
  12.6 1.5 collective-permute-start.1
  14.7 2.2 collective-permute-done
  16.9 4.2 %collective-permute-done.1 = f32[64,512]{1,0:T(8,128)} collective-permute-done((f32[64,512]{1,0:T(8,128)S(1)}, f32[64,512]{1,0:T(8,128)}, u32[]{:S(2)}, u32[]{:S(2)}) %collective-permute-start.1) | collective-permute-done | bytes 131104 | tf_op jit(solution)/shard_map/ppermute | solution.py:396
  21.1 7.5 %shard_map.77 = f32[2048,128]{1,0:T(8,128)} custom-call(s32[4]{0:T(128)} %broadcast_add_fusion.order_ref, bf16[4096,512]{1,0:T(8,128)(2,1)} %act_ref.3, bf16[4096,1792]{1,0:T(8,128)(2,1)} %grad_ref.3, bf16[64,512]{1,0:T(8,128)(2,1)} %bitcast.91, bf16[64,1792]{1,0:T(8,128)(2,1)} %bitcast.89), custom_call_target="tpu_custom_call" | custom-call | flops 9663676416 | bytes 9437184 | tf_op jit(solution)/shard_map/pallas_call | solution.py:43
  28.6 1.3 add.395
  30.1 1.3 collective-permute-start.4
  31.4 0.8 collective-permute-start.5
  32.2 1.4 collective-permute-start.6
  33.6 5.8 %collective-permute-done.4 = f32[512,128]{1,0:T(8,128)S(1)} collective-permute-done((f32[512,128]{1,0:T(8,128)S(1)}, f32[512,128]{1,0:T(8,128)S(1)}, u32[]{:S(2)}, u32[]{:S(2)}) %collective-permute-start.4) | collective-permute-done | bytes 262176 | tf_op jit(solution)/shard_map/ppermute | solution.py:396
  39.4 5.3 %collective-permute-done.5 = f32[512,128]{1,0:T(8,128)S(1)} collective-permute-done((f32[512,128]{1,0:T(8,128)S(1)}, f32[512,128]{1,0:T(8,128)S(1)}, u32[]{:S(2)}, u32[]{:S(2)}) %collective-permute-start.5) | collective-permute-done | bytes 262176 | tf_op jit(solution)/shard_map/ppermute | solution.py:396
  45.4 5.8 %collective-permute-done.7 = f32[512,128]{1,0:T(8,128)S(1)} collective-permute-done((f32[512,128]{1,0:T(8,128)S(1)}, f32[512,128]{1,0:T(8,128)S(1)}, u32[]{:S(2)}, u32[]{:S(2)}) %collective-permute-start.7) | collective-permute-done | bytes 262176 | tf_op jit(solution)/shard_map/ppermute | solution.py:396
  52.0 1.6 collective-permute-start.11
  53.6 8.5 %collective-permute-done.8.refs_3_ = f32[1024,128]{1,0:T(8,128)S(1)} collective-permute-done((f32[1024,128]{1,0:T(8,128)S(1)}, f32[1024,128]{1,0:T(8,128)S(1)}, u32[]{:S(2)}, u32[]{:S(2)}) %collective-permute-start.8) | collective-permute-done | bytes 524320 | tf_op jit(solution)/shard_map/ppermute | solution.py:396
  62.3 1.0 slice.94
  63.3 1.1 collective-permute-start.12
  64.5 1.2 multiply_reduce_fusion
  65.7 1.6 collective-permute-start.16
  67.3 4.8 %collective-permute-done.12 = f32[512,128]{1,0:T(8,128)S(1)} collective-permute-done((f32[512,128]{1,0:T(8,128)S(1)}, f32[512,128]{1,0:T(8,128)S(1)}, u32[]{:S(2)}, u32[]{:S(2)}) %collective-permute-start.12) | collective-permute-done | bytes 262176 | tf_op jit(solution)/shard_map/ppermute | solution.py:396
  72.1 1.4 collective-permute-start.13
  73.6 10.4 %shard_map.79 = (bf16[512,2048]{1,0:T(8,128)(2,1)}, bf16[512,2048]{1,0:T(8,128)(2,1)}, f32[64,512]{1,0:T(8,128)S(1)}, f32[8,128]{1,0:T(8,128)S(1)}) custom-call(s32[8]{0:T(128)S(1)} %stack.229.refs_0_, s32[64]{0:T(128)S(1)} %get-tuple-element.123.refs_1_, f32[1024,128]{1,0:T(8,128)S(1)} %pad_maximum_fusion.refs_2_, ...), custom_call_target="tpu_custom_call" | custom-call | flops 12884901888 | bytes 6291456 | tf_op jit(solution)/shard_map/pallas_call | solution.py:163
  84.0 1.9 collective-permute-done.13.refs_3_
  86.6 1.3 collective-permute-start.17
  89.5 1.6 collective-permute-start.21
  91.1 4.3 %collective-permute-done.17 = f32[512,128]{1,0:T(8,128)S(1)} collective-permute-done((f32[512,128]{1,0:T(8,128)S(1)}, f32[512,128]{1,0:T(8,128)S(1)}, u32[]{:S(2)}, u32[]{:S(2)}) %collective-permute-start.17) | collective-permute-done | bytes 262176 | tf_op jit(solution)/shard_map/ppermute | solution.py:396
  95.4 1.4 collective-permute-start.18
  96.8 11.6 %shard_map.80 = (bf16[512,2048]{1,0:T(8,128)(2,1)}, bf16[512,2048]{1,0:T(8,128)(2,1)}, f32[64,512]{1,0:T(8,128)S(1)}, f32[8,128]{1,0:T(8,128)S(1)}) custom-call(s32[8]{0:T(128)S(1)} %stack.264.refs_0_, s32[64]{0:T(128)S(1)} %fusion.6.refs_1_, f32[1024,128]{1,0:T(8,128)S(1)} %pad_maximum_fusion.2.refs_2_, f32[1024,128]{1,0:T(8,128)} %collective-permute-done.13.refs_3_, ...), custom_call_target="tpu_custom_call" | custom-call | flops 12884901888 | bytes 6291456 | tf_op jit(solution)/shard_map/pallas_call | solution.py:163
  109.8 1.4 collective-permute-start.22
  111.9 6.7 %collective-permute-done.22 = f32[512,128]{1,0:T(8,128)S(1)} collective-permute-done((f32[512,128]{1,0:T(8,128)S(1)}, f32[512,128]{1,0:T(8,128)S(1)}, u32[]{:S(2)}, u32[]{:S(2)}) %collective-permute-start.22) | collective-permute-done | bytes 262176 | tf_op jit(solution)/shard_map/ppermute | solution.py:396
  118.6 1.4 collective-permute-start.23
  120.0 10.5 %shard_map.81 = (bf16[512,2048]{1,0:T(8,128)(2,1)}, bf16[512,2048]{1,0:T(8,128)(2,1)}, f32[64,512]{1,0:T(8,128)S(1)}, f32[8,128]{1,0:T(8,128)S(1)}) custom-call(s32[8]{0:T(128)S(1)} %stack.229.refs_0_, s32[64]{0:T(128)S(1)} %fusion.5.refs_1_, f32[1024,128]{1,0:T(8,128)S(1)} %pad_maximum_fusion.3.refs_2_, f32[1024,128]{1,0:T(8,128)S(1)} %collective-permute-done.18.refs_3_, ...), custom_call_target="tpu_custom_call" | custom-call | flops 12884901888 | bytes 6291456 | tf_op jit(solution)/shard_map/pallas_call | solution.py:163
  130.5 1.7 collective-permute-done.23.refs_3_
  137.4 10.5 %shard_map.82 = (bf16[512,2048]{1,0:T(8,128)(2,1)}, bf16[512,2048]{1,0:T(8,128)(2,1)}, f32[64,512]{1,0:T(8,128)S(1)}, f32[8,128]{1,0:T(8,128)S(1)}) custom-call(s32[8]{0:T(128)S(1)} %stack.264.refs_0_, s32[64]{0:T(128)S(1)} %fusion.4.refs_1_, f32[1024,128]{1,0:T(8,128)S(1)} %constant_dynamic-update-slice_fusion.refs_2_, ...), custom_call_target="tpu_custom_call" | custom-call | flops 12884901888 | bytes 6291456 | tf_op jit(solution)/shard_map/pallas_call | solution.py:163
  149.8 1.6 collective-permute-done.26.refs_1_
  152.2 14.1 %shard_map.83 = (f32[64,2176]{1,0:T(8,128)}, f32[64,2048]{1,0:T(8,128)}, f32[64,2048]{1,0:T(8,128)}, f32[64,2048]{1,0:T(8,128)}, f32[64,2048]{1,0:T(8,128)}, /*index=5*/f32[64,2048]{1,0:T(8,128)}, f32[64,128]{1,0:T(8,128)}) custom-call(f32[64,2176]{1,0:T(8,128)} %copy-done.1, f32[64,2176]{1,0:T(8,128)} %copy-done.4, f32[64,2048]{1,0:T(8,128)} %copy-done, ...), custom_call_target="tpu_custom_call" | custom-call | flops 3221225472 | bytes 16777216 | tf_op jit(solution)/shard_map/pallas_call | solution.py:306
  166.8 1.8 collective-permute-done.27.refs_1_
  169.4 14.7 %shard_map.84 = (f32[64,2176]{1,0:T(8,128)}, f32[64,2048]{1,0:T(8,128)}, f32[64,2048]{1,0:T(8,128)}, f32[64,2048]{1,0:T(8,128)}, f32[64,2048]{1,0:T(8,128)}, /*index=5*/f32[64,2048]{1,0:T(8,128)}, f32[64,128]{1,0:T(8,128)}) custom-call(f32[64,2176]{1,0:T(8,128)} %get-tuple-element.74.refs_0_, f32[64,2176]{1,0:T(8,128)} %copy-done.3, ...), custom_call_target="tpu_custom_call" | custom-call | flops 3221225472 | bytes 16777216 | tf_op jit(solution)/shard_map/pallas_call | solution.py:306
  184.5 1.8 collective-permute-done.28.refs_1_
  187.1 15.0 %shard_map.85 = (f32[64,2176]{1,0:T(8,128)}, f32[64,2048]{1,0:T(8,128)}, f32[64,2048]{1,0:T(8,128)}, f32[64,2048]{1,0:T(8,128)}, f32[64,2048]{1,0:T(8,128)}, /*index=5*/f32[64,2048]{1,0:T(8,128)}, f32[64,128]{1,0:T(8,128)}) custom-call(f32[64,2176]{1,0:T(8,128)} %get-tuple-element.81.refs_0_, f32[64,2176]{1,0:T(8,128)} %copy-done.2, ...), custom_call_target="tpu_custom_call" | custom-call | flops 3221225472 | bytes 16777216 | tf_op jit(solution)/shard_map/pallas_call | solution.py:306
  202.5 1.8 collective-permute-done.29.other_ref
  205.1 3.5 %shard_map.86 = (f32[64,2048]{1,0:T(8,128)}, f32[64,2048]{1,0:T(8,128)}) custom-call(f32[64,2176]{1,0:T(8,128)} %get-tuple-element.88.mine_ref, f32[64,2176]{1,0:T(8,128)} %copy-done.5, f32[64,2048]{1,0:T(8,128)} %get-tuple-element.89.r_ref, f32[64,2048]{1,0:T(8,128)} %get-tuple-element.90.p_ref, f32[64,2048]{1,0:T(8,128)} %get-tuple-element.91.x_ref, ...), custom_call_target="tpu_custom_call" | custom-call | tf_op jit(solution)/shard_map/pallas_call | solution.py:339
  208.6 1.2 fusion.9
  209.8 1.1 collective-permute-start.31
  210.8 2.1 collective-permute-start.32
  213.3 1.6 collective-permute-start.35
  214.9 2.2 collective-permute-start.30
  217.2 1.5 collective-permute-start.36
  219.6 3.7 %collective-permute-start.39 = (f32[32,512]{1,0:T(8,128)S(1)}, f32[32,512]{1,0:T(8,128)S(1)}, u32[]{:S(2)}, u32[]{:S(2)}) collective-permute-start(f32[32,512]{1,0:T(8,128)S(1)} %get-tuple-element.107), channel_id=1, source_target_pairs={{0,24},{8,0},{16,8},{24,16},{1,25},{9,1},{17,9},{25,17},{2,26},{10... | collective-permute-start | bytes 196616 | tf_op jit(solution)/shard_map/ppermute | solution.py:399
  223.3 1.9 collective-permute-done.39
  225.1 8.6 %collective-permute-start.41 = (f32[32,512]{1,0:T(8,128)S(1)}, f32[32,512]{1,0:T(8,128)S(1)}, u32[]{:S(2)}, u32[]{:S(2)}) collective-permute-start(f32[32,512]{1,0:T(8,128)S(1)} %get-tuple-element.105), channel_id=1, source_target_pairs={{0,8},{8,16},{16,24},{24,0},{1,9},{9,17},{17,25},{25,1},{2,10},{10... | collective-permute-start | bytes 196616 | tf_op jit(solution)/shard_map/ppermute | solution.py:399
  234.2 2.0 collective-permute-done.41
  236.2 1.1 collective-permute-start.42
  237.4 9.3 %collective-permute-done.34.refs_1_ = f32[192,512]{1,0:T(8,128)S(1)} collective-permute-done((f32[192,512]{1,0:T(8,128)S(1)}, f32[192,512]{1,0:T(8,128)S(1)}, u32[]{:S(2)}, u32[]{:S(2)}) %collective-permute-start.34) | collective-permute-done | bytes 393248 | tf_op jit(solution)/shard_map/ppermute | solution.py:399
  246.7 1.5 collective-permute-start.43
  248.2 1.6 collective-permute-start.44
  249.8 1.8 collective-permute-done.43
  251.6 1.7 collective-permute-done.44
  253.4 4.9 %collective-permute-done.37.refs_1_ = f32[192,512]{1,0:T(8,128)S(1)} collective-permute-done((f32[192,512]{1,0:T(8,128)S(1)}, f32[192,512]{1,0:T(8,128)S(1)}, u32[]{:S(2)}, u32[]{:S(2)}) %collective-permute-start.37) | collective-permute-done | bytes 393248 | tf_op jit(solution)/shard_map/ppermute | solution.py:399
  258.8 1.6 shard_map.87.refs_2_
  260.4 1.6 shard_map.88.refs_2_
  262.0 1.6 shard_map.89.refs_2_
  263.6 5.4 %collective-permute-done.38.refs_1_ = f32[192,512]{1,0:T(8,128)S(1)} collective-permute-done((f32[192,512]{1,0:T(8,128)S(1)}, f32[192,512]{1,0:T(8,128)S(1)}, u32[]{:S(2)}, u32[]{:S(2)}) %collective-permute-start.38) | collective-permute-done | bytes 393248 | tf_op jit(solution)/shard_map/ppermute | solution.py:399
  269.0 1.6 shard_map.90
  (127 shorter events, 20.1 us)
Async XLA Ops:
  1.2 8.1 %copy-start.6 = (f32[256,512]{1,0:T(8,128)S(1)}, f32[256,512]{1,0:T(8,128)}, u32[]{:S(2)}) copy-start(f32[256,512]{1,0:T(8,128)} %param.11) | copy-start | bytes 1572868
  8.9 19.7 %collective-permute-start.3 = (f32[2048,128]{1,0:T(8,128)}, f32[2048,128]{1,0:T(8,128)S(1)}, u32[]{:S(2)}, u32[]{:S(2)}) collective-permute-start(f32[2048,128]{1,0:T(8,128)} %shard_map.78), channel_id=1, source_target_pairs={{0,1},{1,0},{2,3},{3,2},{4,5},{5,4},{6,7},{7,6},{8,9},{9,8},{10,11... | collective-permute-start | bytes 3145736 | tf_op jit(solution)/shard_map/ppermute | solution.py:396
  10.1 6.9 %collective-permute-start = (f32[64,512]{1,0:T(8,128)S(1)}, f32[64,512]{1,0:T(8,128)}, u32[]{:S(2)}, u32[]{:S(2)}) collective-permute-start(f32[64,512]{1,0:T(8,128)S(1)} %get-tuple-element.115), channel_id=1, source_target_pairs={{0,2},{1,3},{2,0},{3,1},{4,6},{5,7},{6,4},{7,5},{8,10},{9,11},{10,... | collective-permute-start | bytes 393224 | tf_op jit(solution)/shard_map/ppermute | solution.py:396
  12.6 8.5 %collective-permute-start.1 = (f32[64,512]{1,0:T(8,128)S(1)}, f32[64,512]{1,0:T(8,128)}, u32[]{:S(2)}, u32[]{:S(2)}) collective-permute-start(f32[64,512]{1,0:T(8,128)S(1)} %get-tuple-element.117), channel_id=1, source_target_pairs={{0,4},{1,5},{2,6},{3,7},{4,0},{5,1},{6,2},{7,3},{8,12},{9,13},{10,... | collective-permute-start | bytes 393224 | tf_op jit(solution)/shard_map/ppermute | solution.py:396
  14.1 7.0 %collective-permute-start.2 = (f32[64,512]{1,0:T(8,128)S(1)}, f32[64,512]{1,0:T(8,128)}, u32[]{:S(2)}, u32[]{:S(2)}) collective-permute-start(f32[64,512]{1,0:T(8,128)S(1)} %get-tuple-element.114), channel_id=1, source_target_pairs={{0,6},{1,7},{2,4},{3,5},{4,2},{5,3},{6,0},{7,1},{8,14},{9,15},{10,... | collective-permute-start | bytes 393224 | tf_op jit(solution)/shard_map/ppermute | solution.py:396
  30.0 15.2 %copy-start.12 = (s32[1,4096]{1,0:T(1,128)S(1)}, s32[1,4096]{1,0:T(1,128)}, u32[]{:S(2)}) copy-start(s32[1,4096]{1,0:T(1,128)} %param.10) | copy-start | bytes 49156
  30.0 34.5 %copy-start.7 = (f32[64,512]{1,0:T(8,128)S(1)}, f32[64,512]{1,0:T(8,128)}, u32[]{:S(2)}) copy-start(f32[64,512]{1,0:T(8,128)} %get-tuple-element.116) | copy-start | bytes 393220
  30.1 9.3 %collective-permute-start.4 = (f32[512,128]{1,0:T(8,128)S(1)}, f32[512,128]{1,0:T(8,128)S(1)}, u32[]{:S(2)}, u32[]{:S(2)}) collective-permute-start(f32[512,128]{1,0:T(8,128)S(1)} %get-tuple-element.102), channel_id=1, source_target_pairs={{0,2},{1,3},{2,0},{3,1},{4,6},{5,7},{6,4},{7,5},{8,10},{9,11},{10,... | collective-permute-start | bytes 786440 | tf_op jit(solution)/shard_map/ppermute | solution.py:396
  31.4 13.3 %collective-permute-start.5 = (f32[512,128]{1,0:T(8,128)S(1)}, f32[512,128]{1,0:T(8,128)S(1)}, u32[]{:S(2)}, u32[]{:S(2)}) collective-permute-start(f32[512,128]{1,0:T(8,128)S(1)} %get-tuple-element.104), channel_id=1, source_target_pairs={{0,4},{1,5},{2,6},{3,7},{4,0},{5,1},{6,2},{7,3},{8,12},{9,13},{10,... | collective-permute-start | bytes 786440 | tf_op jit(solution)/shard_map/ppermute | solution.py:396
  32.2 12.4 %collective-permute-start.6 = (f32[512,128]{1,0:T(8,128)S(1)}, f32[512,128]{1,0:T(8,128)S(1)}, u32[]{:S(2)}, u32[]{:S(2)}) collective-permute-start(f32[512,128]{1,0:T(8,128)S(1)} %get-tuple-element.103), channel_id=1, source_target_pairs={{0,6},{1,7},{2,4},{3,5},{4,2},{5,3},{6,0},{7,1},{8,14},{9,15},{10,... | collective-permute-start | bytes 786440 | tf_op jit(solution)/shard_map/ppermute | solution.py:396
  44.7 6.5 %collective-permute-start.7 = (f32[512,128]{1,0:T(8,128)S(1)}, f32[512,128]{1,0:T(8,128)S(1)}, u32[]{:S(2)}, u32[]{:S(2)}) collective-permute-start(f32[512,128]{1,0:T(8,128)S(1)} %fusion.1), channel_id=1, source_target_pairs={{0,2},{1,3},{2,0},{3,1},{4,6},{5,7},{6,4},{7,5},{8,10},{9,11},{10,... | collective-permute-start | bytes 786440 | tf_op jit(solution)/shard_map/ppermute | solution.py:396
  51.2 10.9 %collective-permute-start.8 = (f32[1024,128]{1,0:T(8,128)S(1)}, f32[1024,128]{1,0:T(8,128)S(1)}, u32[]{:S(2)}, u32[]{:S(2)}) collective-permute-start(f32[1024,128]{1,0:T(8,128)S(1)} %pad_maximum_fusion.refs_2_), channel_id=1, source_target_pairs={{0,4},{1,5},{2,6},{3,7},{4,0},{5,1},{6,2},{7,3},{8,12},{9,13},{10,... | collective-permute-start | bytes 1572872 | tf_op jit(solution)/shard_map/ppermute | solution.py:396
  52.0 10.4 %collective-permute-start.11 = (f32[552,128]{1,0:T(8,128)S(1)}, f32[552,128]{1,0:T(8,128)}, u32[]{:S(2)}, u32[]{:S(2)}) collective-permute-start(f32[552,128]{1,0:T(8,128)S(1)} %select_maximum_fusion), channel_id=1, source_target_pairs={{0,8},{8,16},{16,24},{24,0},{1,9},{9,17},{17,25},{25,1},{2,10},{10... | collective-permute-start | bytes 847880 | tf_op jit(solution)/shard_map/ppermute | solution.py:399
  53.6 19.9 %collective-permute-start.9 = (f32[1024,128]{1,0:T(8,128)S(1)}, f32[1024,128]{1,0:T(8,128)S(1)}, u32[]{:S(2)}, u32[]{:S(2)}) collective-permute-start(f32[1024,128]{1,0:T(8,128)S(1)} %pad_maximum_fusion.refs_2_), channel_id=1, source_target_pairs={{0,1},{1,0},{2,3},{3,2},{4,5},{5,4},{6,7},{7,6},{8,9},{9,8},{10,11... | collective-permute-start | bytes 1572872 | tf_op jit(solution)/shard_map/ppermute | solution.py:396
  62.1 11.4 %collective-permute-start.10 = (f32[1024,128]{1,0:T(8,128)S(1)}, f32[1024,128]{1,0:T(8,128)S(1)}, u32[]{:S(2)}, u32[]{:S(2)}) collective-permute-start(f32[1024,128]{1,0:T(8,128)S(1)} %collective-permute-done.8.refs_3_), channel_id=1, source_target_pairs={{0,1},{1,0},{2,3},{3,2},{4,5},{5,4},{6,7},{7,6},{8,9},{9,8},{10,11... | collective-permute-start | bytes 1572872 | tf_op jit(solution)/shard_map/ppermute | solution.py:396
  63.3 8.8 %collective-permute-start.12 = (f32[512,128]{1,0:T(8,128)S(1)}, f32[512,128]{1,0:T(8,128)S(1)}, u32[]{:S(2)}, u32[]{:S(2)}) collective-permute-start(f32[512,128]{1,0:T(8,128)S(1)} %slice.94), channel_id=1, source_target_pairs={{0,4},{1,5},{2,6},{3,7},{4,0},{5,1},{6,2},{7,3},{8,12},{9,13},{10,... | collective-permute-start | bytes 786440 | tf_op jit(solution)/shard_map/ppermute | solution.py:396
  65.7 71.7 %copy-start = (f32[64,2048]{1,0:T(8,128)}, f32[64,2048]{1,0:T(8,128)S(1)}, u32[]{:S(2)}) copy-start(f32[64,2048]{1,0:T(8,128)S(1)} %get-tuple-element.113.refs_8_.refs_2_) | copy-start | bytes 1572868
  65.7 20.2 %collective-permute-start.16 = (f32[552,128]{1,0:T(8,128)}, f32[552,128]{1,0:T(8,128)S(1)}, u32[]{:S(2)}, u32[]{:S(2)}) collective-permute-start(f32[552,128]{1,0:T(8,128)} %collective-permute-done.11), channel_id=1, source_target_pairs={{0,8},{8,16},{16,24},{24,0},{1,9},{9,17},{17,25},{25,1},{2,10},{10... | collective-permute-start | bytes 847880 | tf_op jit(solution)/shard_map/ppermute | solution.py:399
  72.1 13.7 %collective-permute-start.13 = (f32[1024,128]{1,0:T(8,128)S(1)}, f32[1024,128]{1,0:T(8,128)}, u32[]{:S(2)}, u32[]{:S(2)}) collective-permute-start(f32[1024,128]{1,0:T(8,128)S(1)} %pad_maximum_fusion.2.refs_2_), channel_id=1, source_target_pairs={{0,2},{1,3},{2,0},{3,1},{4,6},{5,7},{6,4},{7,5},{8,10},{9,11},{10,... | collective-permute-start | bytes 1572872 | tf_op jit(solution)/shard_map/ppermute | solution.py:396
  73.6 23.3 %collective-permute-start.14 = (f32[1024,128]{1,0:T(8,128)S(1)}, f32[1024,128]{1,0:T(8,128)}, u32[]{:S(2)}, u32[]{:S(2)}) collective-permute-start(f32[1024,128]{1,0:T(8,128)S(1)} %pad_maximum_fusion.2.refs_2_), channel_id=1, source_target_pairs={{0,1},{1,0},{2,3},{3,2},{4,5},{5,4},{6,7},{7,6},{8,9},{9,8},{10,11... | collective-permute-start | bytes 1572872 | tf_op jit(solution)/shard_map/ppermute | solution.py:396
  85.9 10.9 %collective-permute-start.15 = (f32[1024,128]{1,0:T(8,128)}, f32[1024,128]{1,0:T(8,128)S(1)}, u32[]{:S(2)}, u32[]{:S(2)}) collective-permute-start(f32[1024,128]{1,0:T(8,128)} %collective-permute-done.13.refs_3_), channel_id=1, source_target_pairs={{0,1},{1,0},{2,3},{3,2},{4,5},{5,4},{6,7},{7,6},{8,9},{9,8},{10,11... | collective-permute-start | bytes 1572872 | tf_op jit(solution)/shard_map/ppermute | solution.py:396
  85.9 0.8 copy-start.8
  86.6 8.7 %collective-permute-start.17 = (f32[512,128]{1,0:T(8,128)S(1)}, f32[512,128]{1,0:T(8,128)S(1)}, u32[]{:S(2)}, u32[]{:S(2)}) collective-permute-start(f32[512,128]{1,0:T(8,128)S(1)} %slice.97), channel_id=1, source_target_pairs={{0,2},{1,3},{2,0},{3,1},{4,6},{5,7},{6,4},{7,5},{8,10},{9,11},{10,... | collective-permute-start | bytes 786440 | tf_op jit(solution)/shard_map/ppermute | solution.py:396
  89.5 20.3 %collective-permute-start.21 = (f32[552,128]{1,0:T(8,128)}, f32[552,128]{1,0:T(8,128)S(1)}, u32[]{:S(2)}, u32[]{:S(2)}) collective-permute-start(f32[552,128]{1,0:T(8,128)} %copy-done.8), channel_id=1, source_target_pairs={{0,8},{8,16},{16,24},{24,0},{1,9},{9,17},{17,25},{25,1},{2,10},{10... | collective-permute-start | bytes 847880 | tf_op jit(solution)/shard_map/ppermute | solution.py:399
  95.4 13.6 %collective-permute-start.18 = (f32[1024,128]{1,0:T(8,128)S(1)}, f32[1024,128]{1,0:T(8,128)S(1)}, u32[]{:S(2)}, u32[]{:S(2)}) collective-permute-start(f32[1024,128]{1,0:T(8,128)S(1)} %pad_maximum_fusion.3.refs_2_), channel_id=1, source_target_pairs={{0,4},{1,5},{2,6},{3,7},{4,0},{5,1},{6,2},{7,3},{8,12},{9,13},{10,... | collective-permute-start | bytes 1572872 | tf_op jit(solution)/shard_map/ppermute | solution.py:396
  96.8 23.2 %collective-permute-start.19 = (f32[1024,128]{1,0:T(8,128)S(1)}, f32[1024,128]{1,0:T(8,128)S(1)}, u32[]{:S(2)}, u32[]{:S(2)}) collective-permute-start(f32[1024,128]{1,0:T(8,128)S(1)} %pad_maximum_fusion.3.refs_2_), channel_id=1, source_target_pairs={{0,1},{1,0},{2,3},{3,2},{4,5},{5,4},{6,7},{7,6},{8,9},{9,8},{10,11... | collective-permute-start | bytes 1572872 | tf_op jit(solution)/shard_map/ppermute | solution.py:396
  109.0 11.0 %collective-permute-start.20 = (f32[1024,128]{1,0:T(8,128)S(1)}, f32[1024,128]{1,0:T(8,128)S(1)}, u32[]{:S(2)}, u32[]{:S(2)}) collective-permute-start(f32[1024,128]{1,0:T(8,128)S(1)} %collective-permute-done.18.refs_3_), channel_id=1, source_target_pairs={{0,1},{1,0},{2,3},{3,2},{4,5},{5,4},{6,7},{7,6},{8,9},{9,8},{10,11... | collective-permute-start | bytes 1572872 | tf_op jit(solution)/shard_map/ppermute | solution.py:396
  109.7 20.8 %copy-start.9 = (f32[552,128]{1,0:T(8,128)}, f32[552,128]{1,0:T(8,128)S(1)}, u32[]{:S(2)}) copy-start(f32[552,128]{1,0:T(8,128)S(1)} %collective-permute-done.21) | copy-start | bytes 847876
  109.8 8.8 %collective-permute-start.22 = (f32[512,128]{1,0:T(8,128)S(1)}, f32[512,128]{1,0:T(8,128)S(1)}, u32[]{:S(2)}, u32[]{:S(2)}) collective-permute-start(f32[512,128]{1,0:T(8,128)S(1)} %slice.100), channel_id=1, source_target_pairs={{0,4},{1,5},{2,6},{3,7},{4,0},{5,1},{6,2},{7,3},{8,12},{9,13},{10,... | collective-permute-start | bytes 786440 | tf_op jit(solution)/shard_map/ppermute | solution.py:396
  118.6 13.6 %collective-permute-start.23 = (f32[1024,128]{1,0:T(8,128)S(1)}, f32[1024,128]{1,0:T(8,128)S(1)}, u32[]{:S(2)}, u32[]{:S(2)}) collective-permute-start(f32[1024,128]{1,0:T(8,128)S(1)} %constant_dynamic-update-slice_fusion.refs_2_), channel_id=1, source_target_pairs={{0,2},{1,3},{2,0},{3,1},{4,6},{5,7},{6,4},{7,5},{8,10},{9,11},{10,... | collective-permute-start | bytes 1572872 | tf_op jit(solution)/shard_map/ppermute | solution.py:396
  120.0 17.4 %collective-permute-start.24 = (f32[1024,128]{1,0:T(8,128)S(1)}, f32[1024,128]{1,0:T(8,128)S(1)}, u32[]{:S(2)}, u32[]{:S(2)}) collective-permute-start(f32[1024,128]{1,0:T(8,128)S(1)} %constant_dynamic-update-slice_fusion.refs_2_), channel_id=1, source_target_pairs={{0,1},{1,0},{2,3},{3,2},{4,5},{5,4},{6,7},{7,6},{8,9},{9,8},{10,11... | collective-permute-start | bytes 1572872 | tf_op jit(solution)/shard_map/ppermute | solution.py:396
  132.2 5.2 %collective-permute-start.25 = (f32[1024,128]{1,0:T(8,128)S(1)}, f32[1024,128]{1,0:T(8,128)S(1)}, u32[]{:S(2)}, u32[]{:S(2)}) collective-permute-start(f32[1024,128]{1,0:T(8,128)S(1)} %collective-permute-done.23.refs_3_), channel_id=1, source_target_pairs={{0,1},{1,0},{2,3},{3,2},{4,5},{5,4},{6,7},{7,6},{8,9},{9,8},{10,11... | collective-permute-start | bytes 1572872 | tf_op jit(solution)/shard_map/ppermute | solution.py:396
  149.3 2.2 copy-start.1
  149.3 2.2 collective-permute-start.26
  151.4 0.8 copy-start.4
  166.3 2.2 collective-permute-start.27
  168.6 0.8 copy-start.3
  184.0 2.2 collective-permute-start.28
  186.3 0.8 copy-start.2
  202.1 2.2 collective-permute-start.29
  204.3 0.8 copy-start.5
  208.6 10.9 %copy-start.11 = (f32[64,2048]{1,0:T(8,128)S(1)}, f32[64,2048]{1,0:T(8,128)}, u32[]{:S(2)}) copy-start(f32[64,2048]{1,0:T(8,128)} %get-tuple-element.99) | copy-start | bytes 1572868
  209.8 7.4 %collective-permute-start.31 = (f32[64,512]{1,0:T(8,128)S(1)}, f32[64,512]{1,0:T(8,128)S(1)}, u32[]{:S(2)}, u32[]{:S(2)}) collective-permute-start(f32[64,512]{1,0:T(8,128)S(1)} %get-tuple-element.108), channel_id=1, source_target_pairs={{0,2},{1,3},{2,0},{3,1},{4,6},{5,7},{6,4},{7,5},{8,10},{9,11},{10,... | collective-permute-start | bytes 393224 | tf_op jit(solution)/shard_map/ppermute | solution.py:396
  210.8 8.7 %collective-permute-start.32 = (f32[64,512]{1,0:T(8,128)S(1)}, f32[64,512]{1,0:T(8,128)S(1)}, u32[]{:S(2)}, u32[]{:S(2)}) collective-permute-start(f32[64,512]{1,0:T(8,128)S(1)} %get-tuple-element.110), channel_id=1, source_target_pairs={{0,4},{1,5},{2,6},{3,7},{4,0},{5,1},{6,2},{7,3},{8,12},{9,13},{10,... | collective-permute-start | bytes 393224 | tf_op jit(solution)/shard_map/ppermute | solution.py:396
  212.9 6.5 %collective-permute-start.33 = (f32[64,512]{1,0:T(8,128)S(1)}, f32[64,512]{1,0:T(8,128)S(1)}, u32[]{:S(2)}, u32[]{:S(2)}) collective-permute-start(f32[64,512]{1,0:T(8,128)S(1)} %get-tuple-element.109), channel_id=1, source_target_pairs={{0,6},{1,7},{2,4},{3,5},{4,2},{5,3},{6,0},{7,1},{8,14},{9,15},{10,... | collective-permute-start | bytes 393224 | tf_op jit(solution)/shard_map/ppermute | solution.py:396
  213.3 24.0 %collective-permute-start.35 = (f32[64,512]{1,0:T(8,128)S(1)}, f32[64,512]{1,0:T(8,128)S(1)}, u32[]{:S(2)}, u32[]{:S(2)}) collective-permute-start(f32[64,512]{1,0:T(8,128)S(1)} %get-tuple-element.111.refs_0_), channel_id=1, source_target_pairs={{0,8},{8,16},{16,24},{24,0},{1,9},{9,17},{17,25},{25,1},{2,10},{10... | collective-permute-start | bytes 393224 | tf_op jit(solution)/shard_map/ppermute | solution.py:399
  214.9 22.4 %collective-permute-start.30 = (f32[64,512]{1,0:T(8,128)S(1)}, f32[64,512]{1,0:T(8,128)S(1)}, u32[]{:S(2)}, u32[]{:S(2)}) collective-permute-start(f32[64,512]{1,0:T(8,128)S(1)} %get-tuple-element.111.refs_0_), channel_id=1, source_target_pairs={{0,24},{8,0},{16,8},{24,16},{1,25},{9,1},{17,9},{25,17},{2,26},{10... | collective-permute-start | bytes 393224 | tf_op jit(solution)/shard_map/ppermute | solution.py:399
  217.2 20.2 %collective-permute-start.36 = (f32[64,512]{1,0:T(8,128)S(1)}, f32[64,512]{1,0:T(8,128)S(1)}, u32[]{:S(2)}, u32[]{:S(2)}) collective-permute-start(f32[64,512]{1,0:T(8,128)S(1)} %get-tuple-element.111.refs_0_), channel_id=1, source_target_pairs={{0,16},{8,24},{16,0},{24,8},{1,17},{9,25},{17,1},{25,9},{2,18},{10... | collective-permute-start | bytes 393224 | tf_op jit(solution)/shard_map/ppermute | solution.py:399
  219.6 5.6 %collective-permute-start.39 = (f32[32,512]{1,0:T(8,128)S(1)}, f32[32,512]{1,0:T(8,128)S(1)}, u32[]{:S(2)}, u32[]{:S(2)}) collective-permute-start(f32[32,512]{1,0:T(8,128)S(1)} %get-tuple-element.107), channel_id=1, source_target_pairs={{0,24},{8,0},{16,8},{24,16},{1,25},{9,1},{17,9},{25,17},{2,26},{10... | collective-permute-start | bytes 196616 | tf_op jit(solution)/shard_map/ppermute | solution.py:399
  223.2 10.9 %collective-permute-start.40 = (f32[32,512]{1,0:T(8,128)S(1)}, f32[32,512]{1,0:T(8,128)S(1)}, u32[]{:S(2)}, u32[]{:S(2)}) collective-permute-start(f32[32,512]{1,0:T(8,128)S(1)} %get-tuple-element.106), channel_id=1, source_target_pairs={{0,16},{8,24},{16,0},{24,8},{1,17},{9,25},{17,1},{25,9},{2,18},{10... | collective-permute-start | bytes 196616 | tf_op jit(solution)/shard_map/ppermute | solution.py:399
  225.1 11.0 %collective-permute-start.41 = (f32[32,512]{1,0:T(8,128)S(1)}, f32[32,512]{1,0:T(8,128)S(1)}, u32[]{:S(2)}, u32[]{:S(2)}) collective-permute-start(f32[32,512]{1,0:T(8,128)S(1)} %get-tuple-element.105), channel_id=1, source_target_pairs={{0,8},{8,16},{16,24},{24,0},{1,9},{9,17},{17,25},{25,1},{2,10},{10... | collective-permute-start | bytes 196616 | tf_op jit(solution)/shard_map/ppermute | solution.py:399
  234.2 12.5 %collective-permute-start.34 = (f32[192,512]{1,0:T(8,128)S(1)}, f32[192,512]{1,0:T(8,128)S(1)}, u32[]{:S(2)}, u32[]{:S(2)}) collective-permute-start(f32[192,512]{1,0:T(8,128)S(1)} %pad_maximum_fusion.4.refs_1_), channel_id=1, source_target_pairs={{0,8},{8,16},{16,24},{24,0},{1,9},{9,17},{17,25},{25,1},{2,10},{10... | collective-permute-start | bytes 1179656 | tf_op jit(solution)/shard_map/ppermute | solution.py:399
  236.2 13.6 %collective-permute-start.42 = (f32[1,32,512]{2,1,0:T(8,128)S(1)}, f32[1,32,512]{2,1,0:T(8,128)S(1)}, u32[]{:S(2)}, u32[]{:S(2)}) collective-permute-start(f32[1,32,512]{2,1,0:T(8,128)S(1)} %get-tuple-element.120), channel_id=1, source_target_pairs={{0,2},{1,3},{2,0},{3,1},{4,6},{5,7},{6,4},{7,5},{8,10},{9,11},{10,... | collective-permute-start | bytes 196616 | tf_op jit(solution)/shard_map/ppermute | solution.py:396
  246.7 11.6 %collective-permute-start.37 = (f32[192,512]{1,0:T(8,128)S(1)}, f32[192,512]{1,0:T(8,128)S(1)}, u32[]{:S(2)}, u32[]{:S(2)}) collective-permute-start(f32[192,512]{1,0:T(8,128)S(1)} %collective-permute-done.34.refs_1_), channel_id=1, source_target_pairs={{0,8},{8,16},{16,24},{24,0},{1,9},{9,17},{17,25},{25,1},{2,10},{10... | collective-permute-start | bytes 1179656 | tf_op jit(solution)/shard_map/ppermute | solution.py:399
  246.7 5.0 %collective-permute-start.43 = (f32[1,32,512]{2,1,0:T(8,128)S(1)}, f32[1,32,512]{2,1,0:T(8,128)S(1)}, u32[]{:S(2)}, u32[]{:S(2)}) collective-permute-start(f32[1,32,512]{2,1,0:T(8,128)S(1)} %get-tuple-element.119), channel_id=1, source_target_pairs={{0,4},{1,5},{2,6},{3,7},{4,0},{5,1},{6,2},{7,3},{8,12},{9,13},{10,... | collective-permute-start | bytes 196616 | tf_op jit(solution)/shard_map/ppermute | solution.py:396
  248.2 5.2 %collective-permute-start.44 = (f32[1,32,512]{2,1,0:T(8,128)S(1)}, f32[1,32,512]{2,1,0:T(8,128)S(1)}, u32[]{:S(2)}, u32[]{:S(2)}) collective-permute-start(f32[1,32,512]{2,1,0:T(8,128)S(1)} %get-tuple-element.118), channel_id=1, source_target_pairs={{0,6},{1,7},{2,4},{3,5},{4,2},{5,3},{6,0},{7,1},{8,14},{9,15},{10,... | collective-permute-start | bytes 196616 | tf_op jit(solution)/shard_map/ppermute | solution.py:396
  258.3 10.7 %collective-permute-start.38 = (f32[192,512]{1,0:T(8,128)S(1)}, f32[192,512]{1,0:T(8,128)S(1)}, u32[]{:S(2)}, u32[]{:S(2)}) collective-permute-start(f32[192,512]{1,0:T(8,128)S(1)} %collective-permute-done.37.refs_1_), channel_id=1, source_target_pairs={{0,8},{8,16},{16,24},{24,0},{1,9},{9,17},{17,25},{25,1},{2,10},{10... | collective-permute-start | bytes 1179656 | tf_op jit(solution)/shard_map/ppermute | solution.py:399
  258.3 2.1 collective-permute-start.45
  260.4 1.6 copy-start.10

commit v4 on v3

--- a/solution.py
+++ b/solution.py
@@ -14,6 +14,8 @@
 F32 = jnp.float32
 BF16 = jnp.bfloat16
 MIB = 1024 * 1024
+BUILD = 24
+STEP = 24
 
 
 def split2(values):
@@ -186,7 +188,7 @@
                 pltpu.VMEM((ex_block, comps), F32),
             ],
         ),
-        compiler_params=pltpu.CompilerParams(vmem_limit_bytes=50 * MIB),
+        compiler_params=pltpu.CompilerParams(vmem_limit_bytes=BUILD * MIB),
         cost_estimate=pl.CostEstimate(
             flops=12 * EX_DEV * half_ranks * WINDOW * 2 * LANES,
             bytes_accessed=4 * EX_DEV * comps + 4 * tokens * LANES,
@@ -232,73 +234,61 @@
     highs, lows = take(planes), take(planes)
     msg_out, r_out, p_out, x_out, s_out, y_out, state_out = take(7)
     s_two, z_acc, stats_acc, scal = take(4)
-    step = pl.program_id(0)
-    count = mine_ref.shape[0]
-
-    @pl.when(step == 0)
-    def _():
-        s, norm, length, damping, beta, alpha = begin(
-            first, examples, comps_all, mine_ref[...], other_ref[...],
-            None if first else s_ref[...], None if first else state_ref[...],
+    count, comps = r_ref.shape
+    s, norm, length, damping, beta, alpha = begin(
+        first, examples, comps_all, mine_ref[...], other_ref[...],
+        None if first else s_ref[...], None if first else state_ref[...],
+    )
+    s_out[...] = s
+    y_out[...] = alpha * s if first else y_ref[...] + alpha * s
+    high, low = split2(s)
+    s_two[0:count, :] = high
+    s_two[count:2 * count, :] = low
+    state_out[...] = lanes_of([norm, length, damping], state_out.shape)
+    scal[...] = lanes_of([alpha, damping] + ([] if first else [beta]), scal.shape)
+    z_acc[...] = jnp.zeros_like(z_acc)
+    stats_acc[...] = jnp.zeros_like(stats_acc)
+    block = 512
+
+    @pl.loop(0, comps // block)
+    def _(turn):
+        at = pl.ds(pl.multiple_of(turn * block, block), block)
+        alpha, damping = scal[:, 0:1], scal[:, 1:2]
+        r = r_ref[:, at]
+        if first:
+            p = r
+            x_out[:, at] = alpha * p
+        else:
+            p = r + scal[:, 2:3] * p_ref[:, at]
+            x_out[:, at] = x_ref[:, at] + alpha * p
+        p_out[:, at] = p
+        q = jnp.zeros(r.shape, F32)
+        for k in range(planes):
+            part = slice(k * EX_DEV, (k + 1) * EX_DEV)
+            both = dot_nn(s_two[:, part], highs[k][:, at])
+            q = q + both[:count] + both[count:] + dot_nn(s_two[0:count, part], lows[k][:, at])
+        r_new = r - alpha * (q / examples + damping * p)
+        r_out[:, at] = r_new
+        stacked = jnp.concatenate(split2(r_new), axis=0)
+        for k in range(planes):
+            part = slice(k * EX_DEV, (k + 1) * EX_DEV)
+            z_acc[part, :] += dot_nt(highs[k][:, at], stacked) + dot_nt(lows[k][:, at], stacked)
+        stats_acc[...] += lanes_of(
+            [
+                jnp.sum(r_new * r_new, axis=1, keepdims=True),
+                jnp.sum(r_new * p, axis=1, keepdims=True),
+            ],
+            stats_acc.shape,
         )
-        s_out[...] = s
-        y_out[...] = alpha * s if first else y_ref[...] + alpha * s
-        high, low = split2(s)
-        s_two[0:count, :] = high
-        s_two[count:2 * count, :] = low
-        state_out[...] = lanes_of([norm, length, damping], state_out.shape)
-        scal[...] = lanes_of([alpha, damping] + ([] if first else [beta]), scal.shape)
-        z_acc[...] = jnp.zeros_like(z_acc)
-        stats_acc[...] = jnp.zeros_like(stats_acc)
-
-    alpha, damping = scal[:, 0:1], scal[:, 1:2]
-    r = r_ref[...]
-    if first:
-        p = r
-        x_out[...] = alpha * p
-    else:
-        p = r + scal[:, 2:3] * p_ref[...]
-        x_out[...] = x_ref[...] + alpha * p
-    p_out[...] = p
-    q = jnp.zeros(r.shape, F32)
-    for k in range(planes):
-        part = slice(k * EX_DEV, (k + 1) * EX_DEV)
-        both = dot_nn(s_two[:, part], highs[k][...])
-        q = q + both[:count] + both[count:] + dot_nn(s_two[0:count, part], lows[k][...])
-    r_new = r - alpha * (q / examples + damping * p)
-    r_out[...] = r_new
-    stacked = jnp.concatenate(split2(r_new), axis=0)
-    for k in range(planes):
-        part = slice(k * EX_DEV, (k + 1) * EX_DEV)
-        z_acc[part, :] += dot_nt(highs[k][...], stacked) + dot_nt(lows[k][...], stacked)
-    stats_acc[...] += lanes_of(
-        [
-            jnp.sum(r_new * r_new, axis=1, keepdims=True),
-            jnp.sum(r_new * p, axis=1, keepdims=True),
-        ],
-        stats_acc.shape,
-    )
-
-    @pl.when(step == pl.num_programs(0) - 1)
-    def _():
-        both = z_acc[...].T
-        msg_out[:, 0:examples] = both[:count] + both[count:]
-        msg_out[:, examples:] = stats_acc[...]
+
+    both = z_acc[...].T
+    msg_out[:, 0:examples] = both[:count] + both[count:]
+    msg_out[:, examples:] = stats_acc[...]
 
 
 def one_step(first, examples, comps_all, mine, other, r, rest, highs, lows):
     planes = len(highs)
     count, comps = r.shape
-    block = 512
-    whole = lambda i: (0, 0)
-    along = lambda i: (0, i)
-    full = lambda a: pl.BlockSpec(a.shape, whole)
-    piece = pl.BlockSpec((count, block), along)
-    in_specs = [full(mine), full(other), piece]
-    if not first:
-        p, x, s, y, state = rest
-        in_specs += [piece, piece, full(s), full(y), full(state)]
-    in_specs += [pl.BlockSpec((EX_DEV, block), along)] * (2 * planes)
     wide = jax.ShapeDtypeStruct((count, examples), F32)
     long = jax.ShapeDtypeStruct((count, comps), F32)
     small = jax.ShapeDtypeStruct((count, LANES), F32)
@@ -306,16 +296,13 @@
     return pl.pallas_call(
         functools.partial(step_kernel, first, planes, examples, comps_all),
         out_shape=(message, long, long, long, wide, wide, small),
-        grid=(comps // block,),
-        in_specs=in_specs,
-        out_specs=[full(message), piece, piece, piece, full(wide), full(wide), full(small)],
         scratch_shapes=[
             pltpu.VMEM((2 * count, examples), BF16),
             pltpu.VMEM((examples, 2 * count), F32),
             pltpu.VMEM((count, LANES), F32),
             pltpu.VMEM((count, LANES), F32),
         ],
-        compiler_params=pltpu.CompilerParams(vmem_limit_bytes=56 * MIB),
+        compiler_params=pltpu.CompilerParams(vmem_limit_bytes=STEP * MIB),
         cost_estimate=pl.CostEstimate(
             flops=12 * count * examples * comps,
             bytes_accessed=4 * examples * comps,
@@ -335,14 +322,10 @@
 
 def last_step(examples, comps_all, *arrays):
     x, y = arrays[4], arrays[6]
-    full = lambda a: pl.BlockSpec(a.shape, lambda i: (0, 0))
     return pl.pallas_call(
         functools.partial(last_kernel, examples, comps_all),
         out_shape=(jax.ShapeDtypeStruct(x.shape, F32), jax.ShapeDtypeStruct(y.shape, F32)),
-        grid=(1,),
-        in_specs=[full(a) for a in arrays],
-        out_specs=(full(x), full(y)),
-        compiler_params=pltpu.CompilerParams(vmem_limit_bytes=60 * MIB),
+        compiler_params=pltpu.CompilerParams(vmem_limit_bytes=STEP * MIB),
     )(*arrays)
 
 
@@ -387,7 +370,6 @@
     comps_all = proj_in.shape[1] * proj_out.shape[1]
     examples = EX_DEV * n_dp
     n_c = n_t // 2
-    bits = n_c.bit_length() - 1
     j = lax.axis_index("tensor")
     i = lax.axis_index("dp")
     chip, core = j // 2, j % 2
@@ -442,21 +424,13 @@
 
     highs, lows, inners, squares = [], [], [], []
     for away in range(n_dp):
-        order = list(range(bits))
-        if away % 2:
-            order = order[::-1]
-        after = lambda values, stage: (
-            tie(values, squares[away - bits - 1 + stage]) if away > bits - stage else values
-        )
-        held, ks = after(rings[away][:share], 0), [0]
-        for stage, bit in enumerate(order[:-1]):
-            held = jnp.concatenate([held, after(swap(held, 2 << bit), stage + 1)], axis=0)
-            ks = ks + [k | (1 << bit) for k in ks]
-        came = after(swap(held, 2 << order[-1]), bits)
-        ks = ks + [k | (1 << order[-1]) for k in ks]
-        sources = [held, came, swap(held, 1), swap(came, 1)]
+        piece = rings[away][:share]
+        near = [piece] + [swap(piece, 2 * k) for k in range(1, n_c)]
+        sources = near + [
+            swap(part, 1) for part in (tie(near, squares[-1]) if squares else near)
+        ]
         offs = jnp.stack(
-            [near_chip[k] * 2 + which for which in (core, 1 - core) for k in ks]
+            [near_chip[k] * 2 + which for which in (core, 1 - core) for k in range(n_c)]
         ).astype(jnp.int32)
         ids = rings[away][share:share + id_rows].reshape((1, tokens))
         first = rings[away][share + id_rows, :EX_DEV // group].astype(jnp.int32)
@@ -491,16 +465,16 @@
     others_x = jnp.concatenate(
         [swap(x[:, k * per_slot:(k + 1) * per_slot], 2 * k) for k in range(1, n_c)], axis=0
     )
-    y, others_x = lax.optimization_barrier((y, others_x))
-    own_parts = [own_x] + [shift(own_x, away) for away in range(1, n_dp)]
     out = None
     for away in range(n_dp):
-        if away == 2:
-            others_x = tie(others_x, own_parts)
         if away:
+            own_x = shift(own_x, 1)
+            others_x = tie(others_x, own_x)
+            if away == 2:
+                y = tie(y, others_x)
             others_x = shift(others_x, 1)
         where = jnp.stack([(i - away) % n_dp] + near_chip).astype(jnp.int32)
-        out = place(where, own_parts[away], others_x, out, (per_slot, n_dp * n_c * q_chip))
+        out = place(where, own_x, others_x, out, (per_slot, n_dp * n_c * q_chip))
 
     part_q = q_chip // 2
     mine = lax.dynamic_slice_in_dim(y, core * part_q, part_q, 0)

time: 271 us -> 238 us (0.88)
  Pallas kernels: 112 us -> 89.2 us
  waiting for transfers between devices: 86.8 us -> 69.3 us
  local copies, waits for them, and re-layouts: 10.2 us -> 25.4 us
  starting transfers between devices: 49.5 us -> 43.3 us
    ppermute x34 -> x46, waiting for transfers between devices: 62.9 us -> 39.8 us  [swap(): return lax.ppermute(values, 'tensor', [(a, a ^ mask) for a in range(n_t)])]
    unnamed x27 -> x46, local copies, waits for them, and re-layouts: 3.99 us -> 22 us
    pallas_call x3, Pallas kernels: 43.8 us -> 27.9 us  [one_step(): pl.pallas_call(functools.partial(step_kernel, first, planes, examples, co...]
    ppermute x12, starting transfers between devices: 22.4 us -> 9.08 us  [shift(): lax.ppermute(values, 'dp', [(a, (a + by) % n_dp) for a in range(n_dp)])]
    ppermute x34 -> x46, starting transfers between devices: 27 us -> 34.2 us  [swap(): return lax.ppermute(values, 'tensor', [(a, a ^ mask) for a in range(n_t)])]
    ppermute x12, waiting for transfers between devices: 23.8 us -> 29.5 us  [shift(): lax.ppermute(values, 'dp', [(a, (a + by) % n_dp) for a in range(n_dp)])]
    pallas_call x4, Pallas kernels: 43.1 us -> 39.3 us  [build(): pl.pallas_call(functools.partial(build_kernel, ranks, share, ex_block, le...]
    pallas_call x1, Pallas kernels: 3.48 us -> 0.48 us  [last_step(): pl.pallas_call(functools.partial(last_kernel, examples, comps_all), out_s...]
  transfers between devices with their start and end apart: 46 -> 58, of which waited for: 25 -> 22; matrix products, arithmetic and copies ran while one was open for 4% -> 2% of each run, Pallas kernels for 17% -> 17%
where the time goes in v4:
time: 238 us
  Pallas kernels  89.2 us (37%)
  waiting for transfers between devices  69.3 us (29%)
  starting transfers between devices  43.3 us (18%)
  local copies, waits for them, and re-layouts  25.4 us (11%)
  other arithmetic  6.36 us (3%)
  between operations  3.87 us (2%)
    ppermute x46, waiting for transfers between devices, swap(): return lax.ppermute(values, 'tensor', [(a, a ^ mask) for a in range(n_t)])  39.8 us
    pallas_call x4, Pallas kernels, build(): pl.pallas_call(functools.partial(build_kernel, ranks, share, ex_block, le...  39.3 us
    ppermute x46, starting transfers between devices, swap(): return lax.ppermute(values, 'tensor', [(a, a ^ mask) for a in range(n_t)])  34.2 us
    ppermute x12, waiting for transfers between devices, shift(): lax.ppermute(values, 'dp', [(a, (a + by) % n_dp) for a in range(n_dp)])  29.5 us
    pallas_call x3, Pallas kernels, one_step(): pl.pallas_call(functools.partial(step_kernel, first, planes, examples, co...  27.9 us
    unnamed x46, local copies, waits for them, and re-layouts  22 us
    pallas_call x2, Pallas kernels, project(): pl.pallas_call(project_kernel, out_shape=jax.ShapeDtypeStruct((steps * bl...  15.2 us
    ppermute x12, starting transfers between devices, shift(): lax.ppermute(values, 'dp', [(a, (a + by) % n_dp) for a in range(n_dp)])  9.08 us
  transfers between devices with their start and end apart: 58, of which 22 were waited for; matrix products, arithmetic and copies ran while one was open for 2% of the time, Pallas kernels for 17%

profile of v4, /device:TPU:0, one launch (start us, length us, event | category | flops | bytes accessed | tf_op | source)
XLA Modules:
  0.0 237.5 jit_solution(10143279950759042748)
XLA Ops:
  1.2 7.7 %shard_map.78 = f32[2048,128]{1,0:T(8,128)} custom-call(s32[4]{0:T(128)} %get-tuple-element.114.order_ref, bf16[4096,512]{1,0:T(8,128)(2,1)} %act_ref.3, bf16[4096,1792]{1,0:T(8,128)(2,1)} %grad_ref.3, bf16[64,512]{1,0:T(8,128)(2,1)} %bitcast.90, bf16[64,1792]{1,0:T(8,128)(2,1)} %bitcast.88), custom_call_target="tpu_custom_call" | custom-call | flops 9663676416 | bytes 9437184 | tf_op jit(solution)/shard_map/pallas_call | solution.py:45
  9.4 2.6 %collective-permute-start = (f32[64,512]{1,0:T(8,128)S(1)}, f32[64,512]{1,0:T(8,128)S(1)}, u32[]{:S(2)}, u32[]{:S(2)}) collective-permute-start(f32[64,512]{1,0:T(8,128)S(1)} %get-tuple-element.129), channel_id=1, source_target_pairs={{0,2},{1,3},{2,0},{3,1},{4,6},{5,7},{6,4},{7,5},{8,10},{9,11},{10,... | collective-permute-start | bytes 393224 | tf_op jit(solution)/shard_map/ppermute | solution.py:378
  12.0 1.5 collective-permute-start.1
  14.1 2.2 collective-permute-done
  16.3 4.2 %collective-permute-done.1 = f32[64,512]{1,0:T(8,128)S(1)} collective-permute-done((f32[64,512]{1,0:T(8,128)S(1)}, f32[64,512]{1,0:T(8,128)S(1)}, u32[]{:S(2)}, u32[]{:S(2)}) %collective-permute-start.1) | collective-permute-done | bytes 131104 | tf_op jit(solution)/shard_map/ppermute | solution.py:378
  20.4 7.5 %shard_map.77 = f32[2048,128]{1,0:T(8,128)} custom-call(s32[4]{0:T(128)} %broadcast_add_fusion.order_ref, bf16[4096,512]{1,0:T(8,128)(2,1)} %act_ref.3, bf16[4096,1792]{1,0:T(8,128)(2,1)} %grad_ref.3, bf16[64,512]{1,0:T(8,128)(2,1)} %bitcast.91, bf16[64,1792]{1,0:T(8,128)(2,1)} %bitcast.89), custom_call_target="tpu_custom_call" | custom-call | flops 9663676416 | bytes 9437184 | tf_op jit(solution)/shard_map/pallas_call | solution.py:45
  28.0 1.3 add.395
  31.5 1.4 collective-permute-start.6
  33.5 5.2 %collective-permute-done.4 = f32[512,128]{1,0:T(8,128)S(1)} collective-permute-done((f32[512,128]{1,0:T(8,128)S(1)}, f32[512,128]{1,0:T(8,128)S(1)}, u32[]{:S(2)}, u32[]{:S(2)}) %collective-permute-start.4) | collective-permute-done | bytes 262176 | tf_op jit(solution)/shard_map/ppermute | solution.py:378
  38.7 5.2 %collective-permute-done.5 = f32[512,128]{1,0:T(8,128)S(1)} collective-permute-done((f32[512,128]{1,0:T(8,128)S(1)}, f32[512,128]{1,0:T(8,128)S(1)}, u32[]{:S(2)}, u32[]{:S(2)}) %collective-permute-start.5) | collective-permute-done | bytes 262176 | tf_op jit(solution)/shard_map/ppermute | solution.py:378
  44.4 1.6 collective-permute-start.8
  46.1 1.5 collective-permute-start.9
  47.6 1.6 collective-permute-start.14
  49.2 4.1 %collective-permute-done.7.refs_3_ = f32[512,128]{1,0:T(8,128)S(1)} collective-permute-done((f32[512,128]{1,0:T(8,128)S(1)}, f32[512,128]{1,0:T(8,128)S(1)}, u32[]{:S(2)}, u32[]{:S(2)}) %collective-permute-start.7) | collective-permute-done | bytes 262176 | tf_op jit(solution)/shard_map/ppermute | solution.py:378
  53.3 3.2 %collective-permute-done.8.refs_4_ = f32[512,128]{1,0:T(8,128)S(1)} collective-permute-done((f32[512,128]{1,0:T(8,128)S(1)}, f32[512,128]{1,0:T(8,128)S(1)}, u32[]{:S(2)}, u32[]{:S(2)}) %collective-permute-start.8) | collective-permute-done | bytes 262176 | tf_op jit(solution)/shard_map/ppermute | solution.py:378
  57.2 1.4 collective-permute-done.14
  59.1 1.6 collective-permute-start.16
  60.8 1.5 collective-permute-start.17
  62.4 9.4 %shard_map.79 = (bf16[512,2048]{1,0:T(8,128)(2,1)S(1)}, bf16[512,2048]{1,0:T(8,128)(2,1)S(1)}, f32[64,512]{1,0:T(8,128)S(1)}, f32[8,128]{1,0:T(8,128)S(1)}) custom-call(s32[8]{0:T(128)S(1)} %stack.227.refs_0_, s32[64]{0:T(128)S(1)} %get-tuple-element.137.refs_1_, f32[512,128]{1,0:T(8,128)S(1)} %fusion.1.refs_2_, ...), custom_call_target="tpu_custom_call" | custom-call | flops 12884901888 | bytes 6291456 | tf_op jit(solution)/shard_map/pallas_call | solution.py:165
  74.3 1.7 collective-permute-start.23
  76.5 1.3 collective-permute-start.25
  77.9 1.6 collective-permute-start.30
  79.4 9.6 %shard_map.80 = (bf16[512,2048]{1,0:T(8,128)(2,1)S(1)}, bf16[512,2048]{1,0:T(8,128)(2,1)S(1)}, f32[64,512]{1,0:T(8,128)S(1)}, f32[8,128]{1,0:T(8,128)S(1)}) custom-call(s32[8]{0:T(128)S(1)} %stack.227.refs_0_, s32[64]{0:T(128)S(1)} %fusion.6.refs_1_, f32[512,128]{1,0:T(8,128)S(1)} %slice.94.refs_2_, f32[512,128]{1,0:T(8,128)S(1)} %collective-permute-done.15.refs_3_, ...), custom_call_target="tpu_custom_call" | custom-call | flops 12884901888 | bytes 6291456 | tf_op jit(solution)/shard_map/pallas_call | solution.py:165
  89.1 1.3 copy-done.2
  90.4 1.4 copy-done.4
  92.9 1.7 collective-permute-start.31
  95.1 1.3 collective-permute-start.33
  96.5 9.4 %shard_map.81 = (bf16[512,2048]{1,0:T(8,128)(2,1)S(1)}, bf16[512,2048]{1,0:T(8,128)(2,1)S(1)}, f32[64,512]{1,0:T(8,128)S(1)}, f32[8,128]{1,0:T(8,128)S(1)}) custom-call(s32[8]{0:T(128)S(1)} %stack.227.refs_0_, s32[64]{0:T(128)S(1)} %fusion.5.refs_1_, f32[512,128]{1,0:T(8,128)S(1)} %slice.97.refs_2_, f32[512,128]{1,0:T(8,128)S(1)} %collective-permute-done.23.refs_3_, ...), custom_call_target="tpu_custom_call" | custom-call | flops 12884901888 | bytes 6291456 | tf_op jit(solution)/shard_map/pallas_call | solution.py:165
  106.0 1.4 copy-done.6
  107.3 1.4 copy-done.8
  115.9 10.8 %shard_map.82 = (bf16[512,2048]{1,0:T(8,128)(2,1)S(1)}, bf16[512,2048]{1,0:T(8,128)(2,1)S(1)}, f32[64,512]{1,0:T(8,128)S(1)}, f32[8,128]{1,0:T(8,128)S(1)}) custom-call(s32[8]{0:T(128)S(1)} %stack.227.refs_0_, s32[64]{0:T(128)S(1)} %fusion.4.refs_1_, f32[512,128]{1,0:T(8,128)S(1)} %slice.100.refs_2_, f32[512,128]{1,0:T(8,128)S(1)} %collective-permute-done.31.refs_3_, ...), custom_call_target="tpu_custom_call" | custom-call | flops 12884901888 | bytes 6291456 | tf_op jit(solution)/shard_map/pallas_call | solution.py:165
  126.7 1.3 copy-done.10
  128.0 1.5 copy-done.12
  133.4 1.9 collective-permute-done.38.refs_1_
  135.2 1.6 copy-done.1
  136.8 1.6 copy-done.3
  138.4 1.6 copy-done.5
  140.0 1.6 copy-done.7
  141.6 1.6 copy-done.9
  143.2 1.6 copy-done.11
  144.8 1.6 copy-done.13
  146.4 9.2 %shard_map.83 = (f32[64,2176]{1,0:T(8,128)S(1)}, f32[64,2048]{1,0:T(8,128)S(1)}, f32[64,2048]{1,0:T(8,128)S(1)}, f32[64,2048]{1,0:T(8,128)S(1)}, f32[64,2048]{1,...) custom-call(f32[64,2176]{1,0:T(8,128)S(1)} %concatenate.14.refs_0_, ...), custom_call_target="tpu_custom_call" | custom-call | flops 3221225472 | bytes 16777216 | tf_op jit(solution)/shard_map/pallas_call | solution.py:296
  155.8 1.8 collective-permute-done.39.refs_1_
  157.6 9.2 %shard_map.84 = (f32[64,2176]{1,0:T(8,128)S(1)}, f32[64,2048]{1,0:T(8,128)S(1)}, f32[64,2048]{1,0:T(8,128)S(1)}, f32[64,2048]{1,0:T(8,128)S(1)}, f32[64,2048]{1,...) custom-call(f32[64,2176]{1,0:T(8,128)S(1)} %get-tuple-element.87.refs_0_, ...), custom_call_target="tpu_custom_call" | custom-call | flops 3221225472 | bytes 16777216 | tf_op jit(solution)/shard_map/pallas_call | solution.py:296
  167.1 1.8 collective-permute-done.40.refs_1_
  168.9 9.5 %shard_map.85 = (f32[64,2176]{1,0:T(8,128)S(1)}, f32[64,2048]{1,0:T(8,128)S(1)}, f32[64,2048]{1,0:T(8,128)S(1)}, f32[64,2048]{1,0:T(8,128)S(1)}, f32[64,2048]{1,...) custom-call(f32[64,2176]{1,0:T(8,128)S(1)} %get-tuple-element.94.refs_0_, ...), custom_call_target="tpu_custom_call" | custom-call | flops 3221225472 | bytes 16777216 | tf_op jit(solution)/shard_map/pallas_call | solution.py:296
  178.5 1.8 collective-permute-done.41.other_ref
  180.9 1.7 collective-permute-start.45
  183.1 1.3 collective-permute-start.47
  184.5 1.6 collective-permute-start.42
  186.7 3.9 %collective-permute-done.46 = f32[64,512]{1,0:T(8,128)S(1)} collective-permute-done((f32[64,512]{1,0:T(8,128)S(1)}, f32[64,512]{1,0:T(8,128)S(1)}, u32[]{:S(2)}, u32[]{:S(2)}) %collective-permute-start.46) | collective-permute-done | bytes 131104 | tf_op jit(solution)/shard_map/ppermute | solution.py:378
  192.8 13.0 %collective-permute-done.43.refs_0_ = f32[64,512]{1,0:T(8,128)S(1)} collective-permute-done((f32[64,512]{1,0:T(8,128)S(1)}, f32[64,512]{1,0:T(8,128)S(1)}, u32[]{:S(2)}, u32[]{:S(2)}) %collective-permute-start.43) | collective-permute-done | bytes 131104 | tf_op jit(solution)/shard_map/ppermute | solution.py:381
  207.9 3.6 %collective-permute-done.51 = f32[32,512]{1,0:T(8,128)S(1)} collective-permute-done((f32[32,512]{1,0:T(8,128)S(1)}, f32[32,512]{1,0:T(8,128)S(1)}, u32[]{:S(2)}, u32[]{:S(2)}) %collective-permute-start.51) | collective-permute-done | bytes 65568 | tf_op jit(solution)/shard_map/ppermute | solution.py:381
  211.6 1.6 collective-permute-done.53
  214.8 1.4 collective-permute-start.55
  216.1 1.4 collective-permute-start.56
  217.6 1.4 collective-permute-done.55
  219.0 2.2 collective-permute-done.56
  221.3 5.0 %collective-permute-done.44.refs_0_ = f32[64,512]{1,0:T(8,128)S(1)} collective-permute-done((f32[64,512]{1,0:T(8,128)S(1)}, f32[64,512]{1,0:T(8,128)S(1)}, u32[]{:S(2)}, u32[]{:S(2)}) %collective-permute-start.44) | collective-permute-done | bytes 131104 | tf_op jit(solution)/shard_map/ppermute | solution.py:381
  226.8 1.6 shard_map.87.refs_2_
  228.4 1.6 shard_map.88.refs_2_
  230.1 1.6 shard_map.89.refs_2_
  231.7 4.2 %collective-permute-done.50.refs_1_ = f32[192,512]{1,0:T(8,128)S(1)} collective-permute-done((f32[192,512]{1,0:T(8,128)S(1)}, f32[192,512]{1,0:T(8,128)S(1)}, u32[]{:S(2)}, u32[]{:S(2)}) %collective-permute-start.50) | collective-permute-done | bytes 393248 | tf_op jit(solution)/shard_map/ppermute | solution.py:381
  235.9 1.6 shard_map.90
  (165 shorter events, 27.9 us)
Async XLA Ops:
  1.2 8.1 %copy-start.16 = (f32[256,512]{1,0:T(8,128)S(1)}, f32[256,512]{1,0:T(8,128)}, u32[]{:S(2)}) copy-start(f32[256,512]{1,0:T(8,128)} %param.11) | copy-start | bytes 1572868
  8.9 19.0 %collective-permute-start.3 = (f32[2048,128]{1,0:T(8,128)}, f32[2048,128]{1,0:T(8,128)S(1)}, u32[]{:S(2)}, u32[]{:S(2)}) collective-permute-start(f32[2048,128]{1,0:T(8,128)} %shard_map.78), channel_id=1, source_target_pairs={{0,1},{1,0},{2,3},{3,2},{4,5},{5,4},{6,7},{7,6},{8,9},{9,8},{10,11... | collective-permute-start | bytes 3145736 | tf_op jit(solution)/shard_map/ppermute | solution.py:378
  9.4 6.8 %collective-permute-start = (f32[64,512]{1,0:T(8,128)S(1)}, f32[64,512]{1,0:T(8,128)S(1)}, u32[]{:S(2)}, u32[]{:S(2)}) collective-permute-start(f32[64,512]{1,0:T(8,128)S(1)} %get-tuple-element.129), channel_id=1, source_target_pairs={{0,2},{1,3},{2,0},{3,1},{4,6},{5,7},{6,4},{7,5},{8,10},{9,11},{10,... | collective-permute-start | bytes 393224 | tf_op jit(solution)/shard_map/ppermute | solution.py:378
  12.0 8.4 %collective-permute-start.1 = (f32[64,512]{1,0:T(8,128)S(1)}, f32[64,512]{1,0:T(8,128)S(1)}, u32[]{:S(2)}, u32[]{:S(2)}) collective-permute-start(f32[64,512]{1,0:T(8,128)S(1)} %get-tuple-element.131), channel_id=1, source_target_pairs={{0,4},{1,5},{2,6},{3,7},{4,0},{5,1},{6,2},{7,3},{8,12},{9,13},{10,... | collective-permute-start | bytes 393224 | tf_op jit(solution)/shard_map/ppermute | solution.py:378
  13.5 6.9 %collective-permute-start.2 = (f32[64,512]{1,0:T(8,128)S(1)}, f32[64,512]{1,0:T(8,128)S(1)}, u32[]{:S(2)}, u32[]{:S(2)}) collective-permute-start(f32[64,512]{1,0:T(8,128)S(1)} %get-tuple-element.128), channel_id=1, source_target_pairs={{0,6},{1,7},{2,4},{3,5},{4,2},{5,3},{6,0},{7,1},{8,14},{9,15},{10,... | collective-permute-start | bytes 393224 | tf_op jit(solution)/shard_map/ppermute | solution.py:378
  20.4 7.5 %copy-start.19 = (f32[64,512]{1,0:T(8,128)}, f32[64,512]{1,0:T(8,128)S(1)}, u32[]{:S(2)}) copy-start(f32[64,512]{1,0:T(8,128)S(1)} %collective-permute-done.2) | copy-start | bytes 393220
  28.0 5.0 %copy-start.21 = (s32[1,4096]{1,0:T(1,128)S(1)}, s32[1,4096]{1,0:T(1,128)}, u32[]{:S(2)}) copy-start(s32[1,4096]{1,0:T(1,128)} %param.10) | copy-start | bytes 49156
  29.3 27.8 %copy-start.20 = (f32[64,512]{1,0:T(8,128)S(1)}, f32[64,512]{1,0:T(8,128)}, u32[]{:S(2)}) copy-start(f32[64,512]{1,0:T(8,128)} %copy-done.19) | copy-start | bytes 393220
  29.4 9.3 %collective-permute-start.4 = (f32[512,128]{1,0:T(8,128)S(1)}, f32[512,128]{1,0:T(8,128)S(1)}, u32[]{:S(2)}, u32[]{:S(2)}) collective-permute-start(f32[512,128]{1,0:T(8,128)S(1)} %get-tuple-element.116), channel_id=1, source_target_pairs={{0,2},{1,3},{2,0},{3,1},{4,6},{5,7},{6,4},{7,5},{8,10},{9,11},{10,... | collective-permute-start | bytes 786440 | tf_op jit(solution)/shard_map/ppermute | solution.py:378
  30.7 13.3 %collective-permute-start.5 = (f32[512,128]{1,0:T(8,128)S(1)}, f32[512,128]{1,0:T(8,128)S(1)}, u32[]{:S(2)}, u32[]{:S(2)}) collective-permute-start(f32[512,128]{1,0:T(8,128)S(1)} %get-tuple-element.118), channel_id=1, source_target_pairs={{0,4},{1,5},{2,6},{3,7},{4,0},{5,1},{6,2},{7,3},{8,12},{9,13},{10,... | collective-permute-start | bytes 786440 | tf_op jit(solution)/shard_map/ppermute | solution.py:378
  31.5 12.4 %collective-permute-start.6 = (f32[512,128]{1,0:T(8,128)S(1)}, f32[512,128]{1,0:T(8,128)S(1)}, u32[]{:S(2)}, u32[]{:S(2)}) collective-permute-start(f32[512,128]{1,0:T(8,128)S(1)} %get-tuple-element.117), channel_id=1, source_target_pairs={{0,6},{1,7},{2,4},{3,5},{4,2},{5,3},{6,0},{7,1},{8,14},{9,15},{10,... | collective-permute-start | bytes 786440 | tf_op jit(solution)/shard_map/ppermute | solution.py:378
  44.0 9.3 %collective-permute-start.7 = (f32[512,128]{1,0:T(8,128)S(1)}, f32[512,128]{1,0:T(8,128)S(1)}, u32[]{:S(2)}, u32[]{:S(2)}) collective-permute-start(f32[512,128]{1,0:T(8,128)S(1)} %fusion.1.refs_2_), channel_id=1, source_target_pairs={{0,2},{1,3},{2,0},{3,1},{4,6},{5,7},{6,4},{7,5},{8,10},{9,11},{10,... | collective-permute-start | bytes 786440 | tf_op jit(solution)/shard_map/ppermute | solution.py:378
  44.4 12.1 %collective-permute-start.8 = (f32[512,128]{1,0:T(8,128)S(1)}, f32[512,128]{1,0:T(8,128)S(1)}, u32[]{:S(2)}, u32[]{:S(2)}) collective-permute-start(f32[512,128]{1,0:T(8,128)S(1)} %fusion.1.refs_2_), channel_id=1, source_target_pairs={{0,4},{1,5},{2,6},{3,7},{4,0},{5,1},{6,2},{7,3},{8,12},{9,13},{10,... | collective-permute-start | bytes 786440 | tf_op jit(solution)/shard_map/ppermute | solution.py:378
  46.1 10.4 %collective-permute-start.9 = (f32[512,128]{1,0:T(8,128)S(1)}, f32[512,128]{1,0:T(8,128)S(1)}, u32[]{:S(2)}, u32[]{:S(2)}) collective-permute-start(f32[512,128]{1,0:T(8,128)S(1)} %fusion.1.refs_2_), channel_id=1, source_target_pairs={{0,6},{1,7},{2,4},{3,5},{4,2},{5,3},{6,0},{7,1},{8,14},{9,15},{10,... | collective-permute-start | bytes 786440 | tf_op jit(solution)/shard_map/ppermute | solution.py:378
  47.6 11.5 %collective-permute-start.10 = (f32[512,128]{1,0:T(8,128)S(1)}, f32[512,128]{1,0:T(8,128)S(1)}, u32[]{:S(2)}, u32[]{:S(2)}) collective-permute-start(f32[512,128]{1,0:T(8,128)S(1)} %fusion.1.refs_2_), channel_id=1, source_target_pairs={{0,1},{1,0},{2,3},{3,2},{4,5},{5,4},{6,7},{7,6},{8,9},{9,8},{10,11... | collective-permute-start | bytes 786440 | tf_op jit(solution)/shard_map/ppermute | solution.py:378
  47.6 11.1 %collective-permute-start.14 = (f32[552,128]{1,0:T(8,128)S(1)}, f32[552,128]{1,0:T(8,128)S(1)}, u32[]{:S(2)}, u32[]{:S(2)}) collective-permute-start(f32[552,128]{1,0:T(8,128)S(1)} %select_maximum_fusion), channel_id=1, source_target_pairs={{0,8},{8,16},{16,24},{24,0},{1,9},{9,17},{17,25},{25,1},{2,10},{10... | collective-permute-start | bytes 847880 | tf_op jit(solution)/shard_map/ppermute | solution.py:381
  53.3 7.5 %collective-permute-start.11 = (f32[512,128]{1,0:T(8,128)S(1)}, f32[512,128]{1,0:T(8,128)S(1)}, u32[]{:S(2)}, u32[]{:S(2)}) collective-permute-start(f32[512,128]{1,0:T(8,128)S(1)} %collective-permute-done.7.refs_3_), channel_id=1, source_target_pairs={{0,1},{1,0},{2,3},{3,2},{4,5},{5,4},{6,7},{7,6},{8,9},{9,8},{10,11... | collective-permute-start | bytes 786440 | tf_op jit(solution)/shard_map/ppermute | solution.py:378
  56.5 5.8 %collective-permute-start.12 = (f32[512,128]{1,0:T(8,128)S(1)}, f32[512,128]{1,0:T(8,128)S(1)}, u32[]{:S(2)}, u32[]{:S(2)}) collective-permute-start(f32[512,128]{1,0:T(8,128)S(1)} %collective-permute-done.8.refs_4_), channel_id=1, source_target_pairs={{0,1},{1,0},{2,3},{3,2},{4,5},{5,4},{6,7},{7,6},{8,9},{9,8},{10,11... | collective-permute-start | bytes 786440 | tf_op jit(solution)/shard_map/ppermute | solution.py:378
  56.5 5.9 %collective-permute-start.13 = (f32[512,128]{1,0:T(8,128)S(1)}, f32[512,128]{1,0:T(8,128)S(1)}, u32[]{:S(2)}, u32[]{:S(2)}) collective-permute-start(f32[512,128]{1,0:T(8,128)S(1)} %collective-permute-done.9.refs_5_), channel_id=1, source_target_pairs={{0,1},{1,0},{2,3},{3,2},{4,5},{5,4},{6,7},{7,6},{8,9},{9,8},{10,11... | collective-permute-start | bytes 786440 | tf_op jit(solution)/shard_map/ppermute | solution.py:378
  58.7 14.5 %collective-permute-start.15 = (f32[512,128]{1,0:T(8,128)S(1)}, f32[512,128]{1,0:T(8,128)S(1)}, u32[]{:S(2)}, u32[]{:S(2)}) collective-permute-start(f32[512,128]{1,0:T(8,128)S(1)} %slice.94.refs_2_), channel_id=1, source_target_pairs={{0,2},{1,3},{2,0},{3,1},{4,6},{5,7},{6,4},{7,5},{8,10},{9,11},{10,... | collective-permute-start | bytes 786440 | tf_op jit(solution)/shard_map/ppermute | solution.py:378
  59.1 14.0 %collective-permute-start.16 = (f32[512,128]{1,0:T(8,128)S(1)}, f32[512,128]{1,0:T(8,128)S(1)}, u32[]{:S(2)}, u32[]{:S(2)}) collective-permute-start(f32[512,128]{1,0:T(8,128)S(1)} %slice.94.refs_2_), channel_id=1, source_target_pairs={{0,4},{1,5},{2,6},{3,7},{4,0},{5,1},{6,2},{7,3},{8,12},{9,13},{10,... | collective-permute-start | bytes 786440 | tf_op jit(solution)/shard_map/ppermute | solution.py:378
  60.8 12.4 %collective-permute-start.17 = (f32[512,128]{1,0:T(8,128)S(1)}, f32[512,128]{1,0:T(8,128)S(1)}, u32[]{:S(2)}, u32[]{:S(2)}) collective-permute-start(f32[512,128]{1,0:T(8,128)S(1)} %slice.94.refs_2_), channel_id=1, source_target_pairs={{0,6},{1,7},{2,4},{3,5},{4,2},{5,3},{6,0},{7,1},{8,14},{9,15},{10,... | collective-permute-start | bytes 786440 | tf_op jit(solution)/shard_map/ppermute | solution.py:378
  62.3 12.0 %collective-permute-start.22 = (f32[552,128]{1,0:T(8,128)S(1)}, f32[552,128]{1,0:T(8,128)S(1)}, u32[]{:S(2)}, u32[]{:S(2)}) collective-permute-start(f32[552,128]{1,0:T(8,128)S(1)} %collective-permute-done.14), channel_id=1, source_target_pairs={{0,8},{8,16},{16,24},{24,0},{1,9},{9,17},{17,25},{25,1},{2,10},{10... | collective-permute-start | bytes 847880 | tf_op jit(solution)/shard_map/ppermute | solution.py:381
  73.2 2.8 %collective-permute-start.18 = (f32[512,128]{1,0:T(8,128)S(1)}, f32[512,128]{1,0:T(8,128)S(1)}, u32[]{:S(2)}, u32[]{:S(2)}) collective-permute-start(f32[512,128]{1,0:T(8,128)S(1)} %slice.94.refs_2_), channel_id=1, source_target_pairs={{0,1},{1,0},{2,3},{3,2},{4,5},{5,4},{6,7},{7,6},{8,9},{9,8},{10,11... | collective-permute-start | bytes 786440 | tf_op jit(solution)/shard_map/ppermute | solution.py:378
  73.2 3.3 %collective-permute-start.19 = (f32[512,128]{1,0:T(8,128)S(1)}, f32[512,128]{1,0:T(8,128)S(1)}, u32[]{:S(2)}, u32[]{:S(2)}) collective-permute-start(f32[512,128]{1,0:T(8,128)S(1)} %collective-permute-done.15.refs_3_), channel_id=1, source_target_pairs={{0,1},{1,0},{2,3},{3,2},{4,5},{5,4},{6,7},{7,6},{8,9},{9,8},{10,11... | collective-permute-start | bytes 786440 | tf_op jit(solution)/shard_map/ppermute | solution.py:378
  73.7 4.1 %collective-permute-start.20 = (f32[512,128]{1,0:T(8,128)S(1)}, f32[512,128]{1,0:T(8,128)S(1)}, u32[]{:S(2)}, u32[]{:S(2)}) collective-permute-start(f32[512,128]{1,0:T(8,128)S(1)} %collective-permute-done.16.refs_4_), channel_id=1, source_target_pairs={{0,1},{1,0},{2,3},{3,2},{4,5},{5,4},{6,7},{7,6},{8,9},{9,8},{10,11... | collective-permute-start | bytes 786440 | tf_op jit(solution)/shard_map/ppermute | solution.py:378
  73.8 5.6 %collective-permute-start.21 = (f32[512,128]{1,0:T(8,128)S(1)}, f32[512,128]{1,0:T(8,128)S(1)}, u32[]{:S(2)}, u32[]{:S(2)}) collective-permute-start(f32[512,128]{1,0:T(8,128)S(1)} %collective-permute-done.17.refs_5_), channel_id=1, source_target_pairs={{0,1},{1,0},{2,3},{3,2},{4,5},{5,4},{6,7},{7,6},{8,9},{9,8},{10,11... | collective-permute-start | bytes 786440 | tf_op jit(solution)/shard_map/ppermute | solution.py:378
  74.3 17.5 %collective-permute-start.23 = (f32[512,128]{1,0:T(8,128)S(1)}, f32[512,128]{1,0:T(8,128)S(1)}, u32[]{:S(2)}, u32[]{:S(2)}) collective-permute-start(f32[512,128]{1,0:T(8,128)S(1)} %slice.97.refs_2_), channel_id=1, source_target_pairs={{0,2},{1,3},{2,0},{3,1},{4,6},{5,7},{6,4},{7,5},{8,10},{9,11},{10,... | collective-permute-start | bytes 786440 | tf_op jit(solution)/shard_map/ppermute | solution.py:378
  76.0 15.8 %collective-permute-start.24 = (f32[512,128]{1,0:T(8,128)S(1)}, f32[512,128]{1,0:T(8,128)S(1)}, u32[]{:S(2)}, u32[]{:S(2)}) collective-permute-start(f32[512,128]{1,0:T(8,128)S(1)} %slice.97.refs_2_), channel_id=1, source_target_pairs={{0,4},{1,5},{2,6},{3,7},{4,0},{5,1},{6,2},{7,3},{8,12},{9,13},{10,... | collective-permute-start | bytes 786440 | tf_op jit(solution)/shard_map/ppermute | solution.py:378
  76.5 15.3 %collective-permute-start.25 = (f32[512,128]{1,0:T(8,128)S(1)}, f32[512,128]{1,0:T(8,128)S(1)}, u32[]{:S(2)}, u32[]{:S(2)}) collective-permute-start(f32[512,128]{1,0:T(8,128)S(1)} %slice.97.refs_2_), channel_id=1, source_target_pairs={{0,6},{1,7},{2,4},{3,5},{4,2},{5,3},{6,0},{7,1},{8,14},{9,15},{10,... | collective-permute-start | bytes 786440 | tf_op jit(solution)/shard_map/ppermute | solution.py:378
  77.9 15.0 %collective-permute-start.30 = (f32[552,128]{1,0:T(8,128)S(1)}, f32[552,128]{1,0:T(8,128)S(1)}, u32[]{:S(2)}, u32[]{:S(2)}) collective-permute-start(f32[552,128]{1,0:T(8,128)S(1)} %collective-permute-done.22), channel_id=1, source_target_pairs={{0,8},{8,16},{16,24},{24,0},{1,9},{9,17},{17,25},{25,1},{2,10},{10... | collective-permute-start | bytes 847880 | tf_op jit(solution)/shard_map/ppermute | solution.py:381
  91.8 2.8 %collective-permute-start.26 = (f32[512,128]{1,0:T(8,128)S(1)}, f32[512,128]{1,0:T(8,128)S(1)}, u32[]{:S(2)}, u32[]{:S(2)}) collective-permute-start(f32[512,128]{1,0:T(8,128)S(1)} %slice.97.refs_2_), channel_id=1, source_target_pairs={{0,1},{1,0},{2,3},{3,2},{4,5},{5,4},{6,7},{7,6},{8,9},{9,8},{10,11... | collective-permute-start | bytes 786440 | tf_op jit(solution)/shard_map/ppermute | solution.py:378
  91.9 3.3 %collective-permute-start.27 = (f32[512,128]{1,0:T(8,128)S(1)}, f32[512,128]{1,0:T(8,128)S(1)}, u32[]{:S(2)}, u32[]{:S(2)}) collective-permute-start(f32[512,128]{1,0:T(8,128)S(1)} %collective-permute-done.23.refs_3_), channel_id=1, source_target_pairs={{0,1},{1,0},{2,3},{3,2},{4,5},{5,4},{6,7},{7,6},{8,9},{9,8},{10,11... | collective-permute-start | bytes 786440 | tf_op jit(solution)/shard_map/ppermute | solution.py:378
  92.4 4.1 %collective-permute-start.28 = (f32[512,128]{1,0:T(8,128)S(1)}, f32[512,128]{1,0:T(8,128)S(1)}, u32[]{:S(2)}, u32[]{:S(2)}) collective-permute-start(f32[512,128]{1,0:T(8,128)S(1)} %collective-permute-done.24.refs_4_), channel_id=1, source_target_pairs={{0,1},{1,0},{2,3},{3,2},{4,5},{5,4},{6,7},{7,6},{8,9},{9,8},{10,11... | collective-permute-start | bytes 786440 | tf_op jit(solution)/shard_map/ppermute | solution.py:378
  92.4 4.0 %collective-permute-start.29 = (f32[512,128]{1,0:T(8,128)S(1)}, f32[512,128]{1,0:T(8,128)S(1)}, u32[]{:S(2)}, u32[]{:S(2)}) collective-permute-start(f32[512,128]{1,0:T(8,128)S(1)} %collective-permute-done.25.refs_5_), channel_id=1, source_target_pairs={{0,1},{1,0},{2,3},{3,2},{4,5},{5,4},{6,7},{7,6},{8,9},{9,8},{10,11... | collective-permute-start | bytes 786440 | tf_op jit(solution)/shard_map/ppermute | solution.py:378
  92.9 13.1 %copy-start.17 = (f32[552,128]{1,0:T(8,128)}, f32[552,128]{1,0:T(8,128)S(1)}, u32[]{:S(2)}) copy-start(f32[552,128]{1,0:T(8,128)S(1)} %collective-permute-done.30) | copy-start | bytes 847876
  92.9 16.5 %collective-permute-start.31 = (f32[512,128]{1,0:T(8,128)S(1)}, f32[512,128]{1,0:T(8,128)S(1)}, u32[]{:S(2)}, u32[]{:S(2)}) collective-permute-start(f32[512,128]{1,0:T(8,128)S(1)} %slice.100.refs_2_), channel_id=1, source_target_pairs={{0,2},{1,3},{2,0},{3,1},{4,6},{5,7},{6,4},{7,5},{8,10},{9,11},{10,... | collective-permute-start | bytes 786440 | tf_op jit(solution)/shard_map/ppermute | solution.py:378
  94.6 14.8 %collective-permute-start.32 = (f32[512,128]{1,0:T(8,128)S(1)}, f32[512,128]{1,0:T(8,128)}, u32[]{:S(2)}, u32[]{:S(2)}) collective-permute-start(f32[512,128]{1,0:T(8,128)S(1)} %slice.100.refs_2_), channel_id=1, source_target_pairs={{0,4},{1,5},{2,6},{3,7},{4,0},{5,1},{6,2},{7,3},{8,12},{9,13},{10,... | collective-permute-start | bytes 786440 | tf_op jit(solution)/shard_map/ppermute | solution.py:378
  95.1 14.2 %collective-permute-start.33 = (f32[512,128]{1,0:T(8,128)S(1)}, f32[512,128]{1,0:T(8,128)}, u32[]{:S(2)}, u32[]{:S(2)}) collective-permute-start(f32[512,128]{1,0:T(8,128)S(1)} %slice.100.refs_2_), channel_id=1, source_target_pairs={{0,6},{1,7},{2,4},{3,5},{4,2},{5,3},{6,0},{7,1},{8,14},{9,15},{10,... | collective-permute-start | bytes 786440 | tf_op jit(solution)/shard_map/ppermute | solution.py:378
  109.4 6.5 %collective-permute-start.34 = (f32[512,128]{1,0:T(8,128)S(1)}, f32[512,128]{1,0:T(8,128)}, u32[]{:S(2)}, u32[]{:S(2)}) collective-permute-start(f32[512,128]{1,0:T(8,128)S(1)} %slice.100.refs_2_), channel_id=1, source_target_pairs={{0,1},{1,0},{2,3},{3,2},{4,5},{5,4},{6,7},{7,6},{8,9},{9,8},{10,11... | collective-permute-start | bytes 786440 | tf_op jit(solution)/shard_map/ppermute | solution.py:378
  109.5 6.4 %collective-permute-start.35 = (f32[512,128]{1,0:T(8,128)S(1)}, f32[512,128]{1,0:T(8,128)}, u32[]{:S(2)}, u32[]{:S(2)}) collective-permute-start(f32[512,128]{1,0:T(8,128)S(1)} %collective-permute-done.31.refs_3_), channel_id=1, source_target_pairs={{0,1},{1,0},{2,3},{3,2},{4,5},{5,4},{6,7},{7,6},{8,9},{9,8},{10,11... | collective-permute-start | bytes 786440 | tf_op jit(solution)/shard_map/ppermute | solution.py:378
  110.0 5.9 %collective-permute-start.36 = (f32[512,128]{1,0:T(8,128)}, f32[512,128]{1,0:T(8,128)}, u32[]{:S(2)}, u32[]{:S(2)}) collective-permute-start(f32[512,128]{1,0:T(8,128)} %collective-permute-done.32.refs_4_), channel_id=1, source_target_pairs={{0,1},{1,0},{2,3},{3,2},{4,5},{5,4},{6,7},{7,6},{8,9},{9,8},{10,11... | collective-permute-start | bytes 786440 | tf_op jit(solution)/shard_map/ppermute | solution.py:378
  110.0 5.8 %collective-permute-start.37 = (f32[512,128]{1,0:T(8,128)}, f32[512,128]{1,0:T(8,128)}, u32[]{:S(2)}, u32[]{:S(2)}) collective-permute-start(f32[512,128]{1,0:T(8,128)} %collective-permute-done.33.refs_5_), channel_id=1, source_target_pairs={{0,1},{1,0},{2,3},{3,2},{4,5},{5,4},{6,7},{7,6},{8,9},{9,8},{10,11... | collective-permute-start | bytes 786440 | tf_op jit(solution)/shard_map/ppermute | solution.py:378
  133.2 2.0 collective-permute-start.38
  155.6 2.0 collective-permute-start.39
  166.8 2.0 collective-permute-start.40
  178.3 2.0 collective-permute-start.41
  180.9 5.8 %collective-permute-start.45 = (f32[64,512]{1,0:T(8,128)S(1)}, f32[64,512]{1,0:T(8,128)S(1)}, u32[]{:S(2)}, u32[]{:S(2)}) collective-permute-start(f32[64,512]{1,0:T(8,128)S(1)} %get-tuple-element.124), channel_id=1, source_target_pairs={{0,2},{1,3},{2,0},{3,1},{4,6},{5,7},{6,4},{7,5},{8,10},{9,11},{10,... | collective-permute-start | bytes 393224 | tf_op jit(solution)/shard_map/ppermute | solution.py:378
  182.6 8.1 %collective-permute-start.46 = (f32[64,512]{1,0:T(8,128)S(1)}, f32[64,512]{1,0:T(8,128)S(1)}, u32[]{:S(2)}, u32[]{:S(2)}) collective-permute-start(f32[64,512]{1,0:T(8,128)S(1)} %get-tuple-element.123), channel_id=1, source_target_pairs={{0,4},{1,5},{2,6},{3,7},{4,0},{5,1},{6,2},{7,3},{8,12},{9,13},{10,... | collective-permute-start | bytes 393224 | tf_op jit(solution)/shard_map/ppermute | solution.py:378
  183.1 7.5 %collective-permute-start.47 = (f32[64,512]{1,0:T(8,128)S(1)}, f32[64,512]{1,0:T(8,128)S(1)}, u32[]{:S(2)}, u32[]{:S(2)}) collective-permute-start(f32[64,512]{1,0:T(8,128)S(1)} %get-tuple-element.122), channel_id=1, source_target_pairs={{0,6},{1,7},{2,4},{3,5},{4,2},{5,3},{6,0},{7,1},{8,14},{9,15},{10,... | collective-permute-start | bytes 393224 | tf_op jit(solution)/shard_map/ppermute | solution.py:378
  184.5 6.8 %collective-permute-start.42 = (f32[64,512]{1,0:T(8,128)S(1)}, f32[64,512]{1,0:T(8,128)S(1)}, u32[]{:S(2)}, u32[]{:S(2)}) collective-permute-start(f32[64,512]{1,0:T(8,128)S(1)} %get-tuple-element.125.refs_0_), channel_id=1, source_target_pairs={{0,8},{8,16},{16,24},{24,0},{1,9},{9,17},{17,25},{25,1},{2,10},{10... | collective-permute-start | bytes 393224 | tf_op jit(solution)/shard_map/ppermute | solution.py:381
  191.2 14.6 %collective-permute-start.48 = (f32[192,512]{1,0:T(8,128)S(1)}, f32[192,512]{1,0:T(8,128)S(1)}, u32[]{:S(2)}, u32[]{:S(2)}) collective-permute-start(f32[192,512]{1,0:T(8,128)S(1)} %constant_dynamic-update-slice_fusion.refs_1_), channel_id=1, source_target_pairs={{0,8},{8,16},{16,24},{24,0},{1,9},{9,17},{17,25},{25,1},{2,10},{10... | collective-permute-start | bytes 1179656 | tf_op jit(solution)/shard_map/ppermute | solution.py:381
  192.3 13.5 %collective-permute-start.43 = (f32[64,512]{1,0:T(8,128)S(1)}, f32[64,512]{1,0:T(8,128)S(1)}, u32[]{:S(2)}, u32[]{:S(2)}) collective-permute-start(f32[64,512]{1,0:T(8,128)S(1)} %collective-permute-done.42.refs_0_), channel_id=1, source_target_pairs={{0,8},{8,16},{16,24},{24,0},{1,9},{9,17},{17,25},{25,1},{2,10},{10... | collective-permute-start | bytes 393224 | tf_op jit(solution)/shard_map/ppermute | solution.py:381
  205.8 5.7 %collective-permute-start.51 = (f32[32,512]{1,0:T(8,128)S(1)}, f32[32,512]{1,0:T(8,128)S(1)}, u32[]{:S(2)}, u32[]{:S(2)}) collective-permute-start(f32[32,512]{1,0:T(8,128)S(1)} %get-tuple-element.121), channel_id=1, source_target_pairs={{0,24},{8,0},{16,8},{24,16},{1,25},{9,1},{17,9},{25,17},{2,26},{10... | collective-permute-start | bytes 196616 | tf_op jit(solution)/shard_map/ppermute | solution.py:381
  206.1 5.5 %collective-permute-start.52 = (f32[32,512]{1,0:T(8,128)S(1)}, f32[32,512]{1,0:T(8,128)S(1)}, u32[]{:S(2)}, u32[]{:S(2)}) collective-permute-start(f32[32,512]{1,0:T(8,128)S(1)} %get-tuple-element.120), channel_id=1, source_target_pairs={{0,16},{8,24},{16,0},{24,8},{1,17},{9,25},{17,1},{25,9},{2,18},{10... | collective-permute-start | bytes 196616 | tf_op jit(solution)/shard_map/ppermute | solution.py:381
  206.9 6.3 %collective-permute-start.53 = (f32[32,512]{1,0:T(8,128)S(1)}, f32[32,512]{1,0:T(8,128)S(1)}, u32[]{:S(2)}, u32[]{:S(2)}) collective-permute-start(f32[32,512]{1,0:T(8,128)S(1)} %get-tuple-element.119), channel_id=1, source_target_pairs={{0,8},{8,16},{16,24},{24,0},{1,9},{9,17},{17,25},{25,1},{2,10},{10... | collective-permute-start | bytes 196616 | tf_op jit(solution)/shard_map/ppermute | solution.py:381
  213.3 4.3 %collective-permute-start.54 = (f32[1,32,512]{2,1,0:T(8,128)S(1)}, f32[1,32,512]{2,1,0:T(8,128)S(1)}, u32[]{:S(2)}, u32[]{:S(2)}) collective-permute-start(f32[1,32,512]{2,1,0:T(8,128)S(1)} %get-tuple-element.134), channel_id=1, source_target_pairs={{0,2},{1,3},{2,0},{3,1},{4,6},{5,7},{6,4},{7,5},{8,10},{9,11},{10,... | collective-permute-start | bytes 196616 | tf_op jit(solution)/shard_map/ppermute | solution.py:378
  214.3 12.1 %collective-permute-start.49 = (f32[192,512]{1,0:T(8,128)S(1)}, f32[192,512]{1,0:T(8,128)S(1)}, u32[]{:S(2)}, u32[]{:S(2)}) collective-permute-start(f32[192,512]{1,0:T(8,128)S(1)} %collective-permute-done.48.refs_1_), channel_id=1, source_target_pairs={{0,8},{8,16},{16,24},{24,0},{1,9},{9,17},{17,25},{25,1},{2,10},{10... | collective-permute-start | bytes 1179656 | tf_op jit(solution)/shard_map/ppermute | solution.py:381
  214.3 12.1 %collective-permute-start.44 = (f32[64,512]{1,0:T(8,128)S(1)}, f32[64,512]{1,0:T(8,128)S(1)}, u32[]{:S(2)}, u32[]{:S(2)}) collective-permute-start(f32[64,512]{1,0:T(8,128)S(1)} %collective-permute-done.43.refs_0_), channel_id=1, source_target_pairs={{0,8},{8,16},{16,24},{24,0},{1,9},{9,17},{17,25},{25,1},{2,10},{10... | collective-permute-start | bytes 393224 | tf_op jit(solution)/shard_map/ppermute | solution.py:381
  214.8 4.3 %collective-permute-start.55 = (f32[1,32,512]{2,1,0:T(8,128)S(1)}, f32[1,32,512]{2,1,0:T(8,128)S(1)}, u32[]{:S(2)}, u32[]{:S(2)}) collective-permute-start(f32[1,32,512]{2,1,0:T(8,128)S(1)} %get-tuple-element.133), channel_id=1, source_target_pairs={{0,4},{1,5},{2,6},{3,7},{4,0},{5,1},{6,2},{7,3},{8,12},{9,13},{10,... | collective-permute-start | bytes 196616 | tf_op jit(solution)/shard_map/ppermute | solution.py:378
  216.1 5.2 %collective-permute-start.56 = (f32[1,32,512]{2,1,0:T(8,128)S(1)}, f32[1,32,512]{2,1,0:T(8,128)S(1)}, u32[]{:S(2)}, u32[]{:S(2)}) collective-permute-start(f32[1,32,512]{2,1,0:T(8,128)S(1)} %get-tuple-element.132), channel_id=1, source_target_pairs={{0,6},{1,7},{2,4},{3,5},{4,2},{5,3},{6,0},{7,1},{8,14},{9,15},{10,... | collective-permute-start | bytes 196616 | tf_op jit(solution)/shard_map/ppermute | solution.py:378
  226.3 9.6 %collective-permute-start.50 = (f32[192,512]{1,0:T(8,128)S(1)}, f32[192,512]{1,0:T(8,128)S(1)}, u32[]{:S(2)}, u32[]{:S(2)}) collective-permute-start(f32[192,512]{1,0:T(8,128)S(1)} %collective-permute-done.49.refs_1_), channel_id=1, source_target_pairs={{0,8},{8,16},{16,24},{24,0},{1,9},{9,17},{17,25},{25,1},{2,10},{10... | collective-permute-start | bytes 1179656 | tf_op jit(solution)/shard_map/ppermute | solution.py:381
  226.4 3.7 %collective-permute-start.57 = (f32[2,32,512]{2,1,0:T(8,128)S(1)}, f32[2,32,512]{2,1,0:T(8,128)S(1)}, u32[]{:S(2)}, u32[]{:S(2)}) collective-permute-start(f32[2,32,512]{2,1,0:T(8,128)S(1)} %constant_dynamic-slice_fusion), channel_id=1, source_target_pairs={{0,1},{1,0},{2,3},{3,2},{4,5},{5,4},{6,7},{7,6},{8,9},{9,8},{10,11... | collective-permute-start | bytes 393224 | tf_op jit(solution)/shard_map/ppermute | solution.py:378
  230.1 1.6 copy-start.18
  (16 other events, 22.0 us)

commit v5 on v4

--- a/solution.py
+++ b/solution.py
@@ -11,6 +11,7 @@
 EX_DEV = 512
 LANES = 128
 WINDOW = 256
+PARTS = 4
 F32 = jnp.float32
 BF16 = jnp.bfloat16
 MIB = 1024 * 1024
@@ -32,25 +33,35 @@
     return lax.dot_general(left, right, (((1,), (1,)), ((), ())), preferred_element_type=F32)
 
 
-def project_kernel(order_ref, act_ref, grad_ref, wi_ref, wo_ref, out_ref):
+def project_kernel(order_ref, *refs):
     del order_ref
-    out_ref[...] = jnp.concatenate(
-        [dot_nt(act_ref[...], wi_ref[...]), dot_nt(grad_ref[...], wo_ref[...])], axis=1
-    )
+    acts, grads = refs[:PARTS], refs[PARTS:2 * PARTS]
+    wi_ref, wo_ref, out_ref = refs[2 * PARTS:]
+    rows = acts[0].shape[0]
+    for part, (act_ref, grad_ref) in enumerate(zip(acts, grads)):
+        out_ref[part * rows:(part + 1) * rows, :] = jnp.concatenate(
+            [dot_nt(act_ref[...], wi_ref[...]), dot_nt(grad_ref[...], wo_ref[...])], axis=1
+        )
 
 
 def project(order, activations, out_grads, w_in, w_out, block):
     steps = order.shape[0]
     feats, hidden = activations.shape[1], out_grads.shape[1]
+    rows = block // PARTS
+
+    def parts(width):
+        return [
+            pl.BlockSpec((rows, width), lambda i, order, part=part: (order[i] * PARTS + part, 0))
+            for part in range(PARTS)
+        ]
+
     return pl.pallas_call(
         project_kernel,
         out_shape=jax.ShapeDtypeStruct((steps * block, LANES), F32),
         grid_spec=pltpu.PrefetchScalarGridSpec(
             num_scalar_prefetch=1,
             grid=(steps,),
-            in_specs=[
-                pl.BlockSpec((block, feats), lambda i, order: (order[i], 0)),
-                pl.BlockSpec((block, hidden), lambda i, order: (order[i], 0)),
+            in_specs=parts(feats) + parts(hidden) + [
                 pl.BlockSpec(w_in.shape, lambda i, order: (0, 0)),
                 pl.BlockSpec(w_out.shape, lambda i, order: (0, 0)),
             ],
@@ -62,7 +73,7 @@
             bytes_accessed=2 * steps * block * (feats + hidden),
             transcendentals=0,
         ),
-    )(order, activations, out_grads, w_in, w_out)
+    )(order, *[activations] * PARTS, *[out_grads] * PARTS, w_in, w_out)
 
 
 def build_kernel(ranks, share, ex_block, n_sources, *refs):
@@ -197,6 +208,29 @@
     )(offs, starts, *sources, ids, pick, b)
 
 
+def join_kernel(planes, *refs):
+    inners, squares, b_ref, out_ref = refs[:planes], refs[planes:2 * planes], refs[-2], refs[-1]
+    for k, inner in enumerate(inners):
+        out_ref[:, k * EX_DEV:(k + 1) * EX_DEV] = inner[...]
+    total = squares[0][...]
+    for square in squares[1:]:
+        total = total + square[...]
+    total = jnp.sum(jnp.sum(total, axis=1, keepdims=True), axis=0, keepdims=True)
+    b = b_ref[...]
+    norm = jnp.sum(b * b, axis=1, keepdims=True)
+    shape = (b.shape[0], LANES)
+    out_ref[:, planes * EX_DEV:] = lanes_of([norm, total], shape)
+
+
+def join(inners, squares, b):
+    planes = len(inners)
+    return pl.pallas_call(
+        functools.partial(join_kernel, planes),
+        out_shape=jax.ShapeDtypeStruct((b.shape[0], planes * EX_DEV + LANES), F32),
+        compiler_params=pltpu.CompilerParams(vmem_limit_bytes=STEP * MIB),
+    )(*inners, *squares, b)
+
+
 def column(values, k):
     return values[:, k:k + 1]
 
@@ -402,18 +436,21 @@
         ],
         axis=0,
     )
+    extras = [extra] + [shift(extra, away) for away in range(1, n_dp)]
+    plane_ids = [one[:id_rows].reshape((1, tokens)) for one in extras]
+    firsts = [one[id_rows, :EX_DEV // group].astype(jnp.int32) for one in extras]
 
     share = tokens // n_t
     blocks = jnp.stack(near_chip).astype(jnp.int32) * 2
     w_in, w_out = proj_in.T, proj_out.T
     give = project(blocks + 1 - core, activations, out_grads, w_in, w_out, share)
-    keep = project(tie(blocks + core, slots), activations, out_grads, w_in, w_out, share)
+    keep = project(blocks + core, activations, out_grads, w_in, w_out, share)
     kept = (keep + swap(give, 1)).reshape((n_c, share, LANES))
     own = kept[0]
     for k in range(1, n_c):
         own = own + swap(kept[k], 2 * k)
 
-    rings = [jnp.concatenate([own, extra], axis=0)]
+    rings = [own]
     for _ in range(n_dp - 1):
         rings.append(shift(rings[-1], 1))
 
@@ -422,34 +459,27 @@
     wanted = jnp.stack(wanted[0::2] + wanted[1::2])
     pick = (wanted[:, None] == jnp.arange(LANES)[None, :]).astype(BF16)
 
+    offs = jnp.stack(
+        [near_chip[k] * 2 + which for which in (core, 1 - core) for k in range(n_c)]
+    ).astype(jnp.int32)
+    offs, pick, b, plane_ids, firsts = lax.optimization_barrier((offs, pick, b, plane_ids, firsts))
+
     highs, lows, inners, squares = [], [], [], []
     for away in range(n_dp):
-        piece = rings[away][:share]
+        piece = rings[away]
         near = [piece] + [swap(piece, 2 * k) for k in range(1, n_c)]
         sources = near + [
             swap(part, 1) for part in (tie(near, squares[-1]) if squares else near)
         ]
-        offs = jnp.stack(
-            [near_chip[k] * 2 + which for which in (core, 1 - core) for k in range(n_c)]
-        ).astype(jnp.int32)
-        ids = rings[away][share:share + id_rows].reshape((1, tokens))
-        first = rings[away][share + id_rows, :EX_DEV // group].astype(jnp.int32)
-        high, low, inner, square = build(offs, first, sources, ids, pick, b, ranks, share)
+        high, low, inner, square = build(
+            offs, firsts[away], sources, plane_ids[away], pick, b, ranks, share
+        )
         highs.append(high)
         lows.append(low)
         inners.append(inner)
         squares.append(square)
 
-    square = jnp.sum(jnp.stack(squares))
-    stats = jnp.concatenate(
-        [
-            jnp.sum(b * b, axis=1, keepdims=True),
-            jnp.broadcast_to(square, (q_chip, 1)),
-            jnp.zeros((q_chip, LANES - 2), F32),
-        ],
-        axis=1,
-    )
-    message = jnp.concatenate(inners + [stats], axis=1)
+    message = join(inners, squares, b)
     r, rest = b, ()
     for step in range(ITERS - 1):
         other = swap(message, 1)
@@ -460,43 +490,42 @@
     other = swap(message, 1)
     x, y = last_step(examples, comps_all, message, other, r, *rest)
 
+    n_half = n_c // 2
     per_slot = comps_all // n_t
-    own_x = x[:, :per_slot]
+
+    def send(values, to):
+        pairs = [
+            (di * n_t + 2 * c + c // n_half, to(di, c, c // n_half))
+            for di in range(n_dp) for c in range(n_c)
+        ]
+        return lax.ppermute(values, ("dp", "tensor"), pairs)
+
     others_x = jnp.concatenate(
         [swap(x[:, k * per_slot:(k + 1) * per_slot], 2 * k) for k in range(1, n_c)], axis=0
     )
+    own_x = x[:, :per_slot]
+    by_plane = jnp.zeros((n_dp, q_chip, EX_DEV), F32)
+    for away in range(n_dp):
+        part = y[:, away * EX_DEV:(away + 1) * EX_DEV]
+        if away:
+            part = send(part, lambda di, c, h: ((di - away) % n_dp) * n_t + 2 * c + h)
+        by_plane = lax.dynamic_update_slice(by_plane, part[None], ((i + away) % n_dp, 0, 0))
+    by_chip = jnp.zeros((n_c, q_chip, EX_DEV), F32)
+    for k in range(n_c):
+        part = lax.dynamic_slice_in_dim(by_plane, near_chip[k], 1, 0)
+        if k:
+            part = send(part, lambda di, c, h: di * n_t + 2 * (c ^ k) + h)
+        by_chip = lax.dynamic_update_slice(by_chip, part, (near_chip[k], 0, 0))
+    scores = lax.dynamic_slice_in_dim(by_chip, core * n_half, n_half, 0)
+
     out = None
     for away in range(n_dp):
         if away:
             own_x = shift(own_x, 1)
-            others_x = tie(others_x, own_x)
-            if away == 2:
-                y = tie(y, others_x)
+            others_x = tie(others_x, (own_x, by_plane if away == 1 else scores))
             others_x = shift(others_x, 1)
         where = jnp.stack([(i - away) % n_dp] + near_chip).astype(jnp.int32)
         out = place(where, own_x, others_x, out, (per_slot, n_dp * n_c * q_chip))
-
-    part_q = q_chip // 2
-    mine = lax.dynamic_slice_in_dim(y, core * part_q, part_q, 0)
-    by_plane = jnp.zeros((n_dp, part_q, EX_DEV), F32)
-    for away in range(n_dp):
-        part = mine[:, away * EX_DEV:(away + 1) * EX_DEV]
-        if away:
-            part = shift(part, -away)
-        by_plane = lax.dynamic_update_slice(by_plane, part[None], ((i + away) % n_dp, 0, 0))
-    by_chip = jnp.zeros((n_c, part_q, EX_DEV), F32)
-    for k in range(n_c):
-        part = lax.dynamic_slice_in_dim(by_plane, near_chip[k], 1, 0)
-        if k:
-            part = swap(part, 2 * k)
-        by_chip = lax.dynamic_update_slice(by_chip, part, (near_chip[k], 0, 0))
-    n_half = n_c // 2
-    give = lax.dynamic_slice_in_dim(by_chip, (1 - core) * n_half, n_half, 0)
-    keep = lax.dynamic_slice_in_dim(by_chip, core * n_half, n_half, 0)
-    came = swap(give, 1)
-    scores = jnp.zeros((n_half, 2, part_q, EX_DEV), F32)
-    scores = lax.dynamic_update_slice(scores, keep[:, None], (0, core, 0, 0))
-    scores = lax.dynamic_update_slice(scores, came[:, None], (0, 1 - core, 0, 0))
     return (out, scores.reshape((n_half * q_chip, EX_DEV)))
 
 

time: 238 us -> 237 us (level)
  local copies, waits for them, and re-layouts: 25.4 us -> 3.54 us
  waiting for transfers between devices: 69.3 us -> 89.4 us
  starting transfers between devices: 43.3 us -> 49.3 us
  between operations: 3.87 us -> 1.17 us
    unnamed x46 -> x8, local copies, waits for them, and re-layouts: 22 us -> 1.86 us
    ppermute x0 -> x6, waiting for transfers between devices: none -> 13.6 us  [send(): return lax.ppermute(values, ('dp', 'tensor'), pairs)]
    ppermute x0 -> x6, starting transfers between devices: none -> 12.8 us  [send(): return lax.ppermute(values, ('dp', 'tensor'), pairs)]
    ppermute x12, waiting for transfers between devices: 29.5 us -> 38.5 us  [shift(): lax.ppermute(values, 'dp', [(a, (a + by) % n_dp) for a in range(n_dp)])]
    ppermute x46 -> x42, starting transfers between devices: 34.2 us -> 29.3 us  [swap(): return lax.ppermute(values, 'tensor', [(a, a ^ mask) for a in range(n_t)])]
    reduce_sum x5 -> x0, other arithmetic: 2.75 us -> none  [the longest x4 2.59 us: per_device(): square = jnp.sum(jnp.stack(squares))]
    ppermute x46 -> x42, waiting for transfers between devices: 39.8 us -> 37.4 us  [swap(): return lax.ppermute(values, 'tensor', [(a, a ^ mask) for a in range(n_t)])]
  transfers between devices with their start and end apart: 58 -> 60, of which waited for: 22 -> 24; matrix products, arithmetic and copies ran while one was open for 2% -> 2% of each run, Pallas kernels for 17% -> 21%
where the time goes in v5:
time: 237 us; the launch traced here: 236 us
  waiting for transfers between devices  89.4 us (38%)
  Pallas kernels  88 us (37%)
  starting transfers between devices  49.3 us (21%)
  other arithmetic  4.45 us (2%)
  local copies, waits for them, and re-layouts  3.54 us (1%)
    ppermute x12, waiting for transfers between devices, shift(): lax.ppermute(values, 'dp', [(a, (a + by) % n_dp) for a in range(n_dp)])  38.5 us
    pallas_call x4, Pallas kernels, build(): pl.pallas_call(functools.partial(build_kernel, ranks, share, ex_block, le...  37.7 us
    ppermute x42, waiting for transfers between devices, swap(): return lax.ppermute(values, 'tensor', [(a, a ^ mask) for a in range(n_t)])  37.4 us
    ppermute x42, starting transfers between devices, swap(): return lax.ppermute(values, 'tensor', [(a, a ^ mask) for a in range(n_t)])  29.3 us
    pallas_call x3, Pallas kernels, one_step(): pl.pallas_call(functools.partial(step_kernel, first, planes, examples, co...  27.9 us
    pallas_call x2, Pallas kernels, project(): pl.pallas_call(project_kernel, out_shape=jax.ShapeDtypeStruct((steps * bl...  15.5 us
    ppermute x6, waiting for transfers between devices, send(): return lax.ppermute(values, ('dp', 'tensor'), pairs)  13.6 us
    ppermute x6, starting transfers between devices, send(): return lax.ppermute(values, ('dp', 'tensor'), pairs)  12.8 us
  transfers between devices with their start and end apart: 60, of which 24 were waited for; matrix products, arithmetic and copies ran while one was open for 2% of the time, Pallas kernels for 21%

profile of v5, /device:TPU:0, one launch (start us, length us, event | category | flops | bytes accessed | tf_op | source)
XLA Modules:
  0.0 236.0 jit_solution(3456383609602191774)
XLA Ops:
  0.6 0.7 convert_element_type.33.refs_10_
  1.4 1.0 convert_reduce_fusion
  2.4 3.1 %collective-permute-start.3 = (f32[40,128]{1,0:T(8,128)S(1)}, f32[40,128]{1,0:T(8,128)S(1)}, u32[]{:S(2)}, u32[]{:S(2)}) collective-permute-start(f32[40,128]{1,0:T(8,128)S(1)} %select_maximum_fusion), channel_id=1, source_target_pairs={{0,8},{8,16},{16,24},{24,0},{1,9},{9,17},{17,25},{25,1},{2,10},{10... | collective-permute-start | bytes 61448 | tf_op jit(solution)/shard_map/ppermute | solution.py:415
  5.5 2.6 %collective-permute-start.4 = (f32[40,128]{1,0:T(8,128)S(1)}, f32[40,128]{1,0:T(8,128)S(1)}, u32[]{:S(2)}, u32[]{:S(2)}) collective-permute-start(f32[40,128]{1,0:T(8,128)S(1)} %select_maximum_fusion), channel_id=1, source_target_pairs={{0,16},{8,24},{16,0},{24,8},{1,17},{9,25},{17,1},{25,9},{2,18},{10... | collective-permute-start | bytes 61448 | tf_op jit(solution)/shard_map/ppermute | solution.py:415
  8.7 7.7 %shard_map.78 = f32[2048,128]{1,0:T(8,128)} custom-call(s32[4]{0:T(128)} %get-tuple-element.132.order_ref, bf16[4096,512]{1,0:T(8,128)(2,1)} %refs_3_.3, bf16[4096,512]{1,0:T(8,128)(2,1)} %refs_3_.3, bf16[4096,512]{1,0:T(8,128)(2,1)} %refs_3_.3, bf16[4096,512]{1,0:T(8,128)(2,1)} %refs_3_.3, bf16[4096,1792]{1,0:T(8,128)(2,1)} %refs_7_.3, ...), custom_call_target="tpu_custom_call" | custom-call | flops 9663676416 | bytes 9437184 | tf_op jit(solution)/shard_map/pallas_call | solution.py:58
  16.9 7.7 %shard_map.77 = f32[2048,128]{1,0:T(8,128)} custom-call(s32[4]{0:T(128)} %broadcast_add_fusion.order_ref, bf16[4096,512]{1,0:T(8,128)(2,1)} %refs_3_.3, bf16[4096,512]{1,0:T(8,128)(2,1)} %refs_3_.3, bf16[4096,512]{1,0:T(8,128)(2,1)} %refs_3_.3, bf16[4096,512]{1,0:T(8,128)(2,1)} %refs_3_.3, bf16[4096,1792]{1,0:T(8,128)(2,1)} %refs_7_.3, ...), custom_call_target="tpu_custom_call" | custom-call | flops 9663676416 | bytes 9437184 | tf_op jit(solution)/shard_map/pallas_call | solution.py:58
  24.7 1.4 add.390
  26.2 1.5 collective-permute-start.7
  27.7 1.5 collective-permute-start.8
  30.1 5.3 %collective-permute-done.7 = f32[512,128]{1,0:T(8,128)S(1)} collective-permute-done((f32[512,128]{1,0:T(8,128)S(1)}, f32[512,128]{1,0:T(8,128)S(1)}, u32[]{:S(2)}, u32[]{:S(2)}) %collective-permute-start.7) | collective-permute-done | bytes 262176 | tf_op jit(solution)/shard_map/ppermute | solution.py:412
  35.4 1.4 collective-permute-start.5
  36.7 5.0 %collective-permute-done.8 = f32[512,128]{1,0:T(8,128)S(1)} collective-permute-done((f32[512,128]{1,0:T(8,128)S(1)}, f32[512,128]{1,0:T(8,128)S(1)}, u32[]{:S(2)}, u32[]{:S(2)}) %collective-permute-start.8) | collective-permute-done | bytes 262176 | tf_op jit(solution)/shard_map/ppermute | solution.py:412
  41.8 2.1 collective-permute-start.10
  43.9 1.5 collective-permute-start.11
  45.5 2.0 collective-permute-start.1
  47.4 0.7 collective-permute-done
  48.2 1.4 collective-permute-start.2
  49.6 12.3 %collective-permute-done.1 = f32[64,512]{1,0:T(8,128)S(1)} collective-permute-done((f32[64,512]{1,0:T(8,128)S(1)}, f32[64,512]{1,0:T(8,128)S(1)}, u32[]{:S(2)}, u32[]{:S(2)}) %collective-permute-start.1) | collective-permute-done | bytes 131104 | tf_op jit(solution)/shard_map/ppermute | solution.py:412
  63.1 9.3 %collective-permute-done.17.refs_2_ = f32[512,128]{1,0:T(8,128)S(1)} collective-permute-done((f32[512,128]{1,0:T(8,128)S(1)}, f32[512,128]{1,0:T(8,128)S(1)}, u32[]{:S(2)}, u32[]{:S(2)}) %collective-permute-start.17) | collective-permute-done | bytes 262176 | tf_op jit(solution)/shard_map/ppermute | solution.py:415
  73.1 1.5 collective-permute-start.19
  74.6 1.4 collective-permute-start.20
  76.0 9.4 %shard_map.79 = (bf16[512,2048]{1,0:T(8,128)(2,1)S(1)}, bf16[512,2048]{1,0:T(8,128)(2,1)S(1)}, f32[64,512]{1,0:T(8,128)S(1)}, f32[8,128]{1,0:T(8,128)S(1)}) custom-call(s32[8]{0:T(128)S(1)} %stack.195.refs_0_, s32[64]{0:T(128)S(1)} %get-tuple-element.68.refs_1_, f32[512,128]{1,0:T(8,128)S(1)} %fusion.1.refs_2_, ...), custom_call_target="tpu_custom_call" | custom-call | flops 12884901888 | bytes 6291456 | tf_op jit(solution)/shard_map/pallas_call | solution.py:176
  85.4 1.7 collective-permute-done.20.refs_5_
  88.2 0.6 collective-permute-start.26
  88.8 1.7 collective-permute-start.27
  90.5 1.2 collective-permute-start.28
  91.7 9.4 %shard_map.80 = (bf16[512,2048]{1,0:T(8,128)(2,1)S(1)}, bf16[512,2048]{1,0:T(8,128)(2,1)S(1)}, f32[64,512]{1,0:T(8,128)S(1)}, f32[8,128]{1,0:T(8,128)S(1)}) custom-call(s32[8]{0:T(128)S(1)} %stack.195.refs_0_, s32[64]{0:T(128)S(1)} %fusion.5.refs_1_, f32[512,128]{1,0:T(8,128)S(1)} %collective-permute-done.17.refs_2_, ...), custom_call_target="tpu_custom_call" | custom-call | flops 12884901888 | bytes 6291456 | tf_op jit(solution)/shard_map/pallas_call | solution.py:176
  101.2 1.5 collective-permute-done.27.refs_4_
  103.7 1.1 collective-permute-start.34
  104.8 1.2 collective-permute-start.35
  106.0 1.2 collective-permute-start.36
  107.2 9.4 %shard_map.81 = (bf16[512,2048]{1,0:T(8,128)(2,1)S(1)}, bf16[512,2048]{1,0:T(8,128)(2,1)S(1)}, f32[64,512]{1,0:T(8,128)S(1)}, f32[8,128]{1,0:T(8,128)S(1)}) custom-call(s32[8]{0:T(128)S(1)} %stack.195.refs_0_, s32[64]{0:T(128)S(1)} %fusion.4.refs_1_, f32[512,128]{1,0:T(8,128)S(1)} %collective-permute-done.25.refs_2_, ...), custom_call_target="tpu_custom_call" | custom-call | flops 12884901888 | bytes 6291456 | tf_op jit(solution)/shard_map/pallas_call | solution.py:176
  117.1 1.2 collective-permute-done.36.refs_5_
  121.0 9.4 %shard_map.82 = (bf16[512,2048]{1,0:T(8,128)(2,1)S(1)}, bf16[512,2048]{1,0:T(8,128)(2,1)S(1)}, f32[64,512]{1,0:T(8,128)S(1)}, f32[8,128]{1,0:T(8,128)S(1)}) custom-call(s32[8]{0:T(128)S(1)} %stack.195.refs_0_, s32[64]{0:T(128)S(1)} %fusion.3.refs_1_, f32[512,128]{1,0:T(8,128)S(1)} %collective-permute-done.33.refs_2_, ...), custom_call_target="tpu_custom_call" | custom-call | flops 12884901888 | bytes 6291456 | tf_op jit(solution)/shard_map/pallas_call | solution.py:176
  130.8 1.8 collective-permute-done.41.refs_1_
  132.6 9.2 %shard_map.84 = (f32[64,2176]{1,0:T(8,128)S(1)}, f32[64,2048]{1,0:T(8,128)S(1)}, f32[64,2048]{1,0:T(8,128)S(1)}, f32[64,2048]{1,0:T(8,128)S(1)}, f32[64,2048]{1,...) custom-call(f32[64,2176]{1,0:T(8,128)S(1)} %shard_map.83.refs_0_, ...), custom_call_target="tpu_custom_call" | custom-call | flops 3221225472 | bytes 16777216 | tf_op jit(solution)/shard_map/pallas_call | solution.py:330
  142.1 1.8 collective-permute-done.42.refs_1_
  143.9 9.3 %shard_map.85 = (f32[64,2176]{1,0:T(8,128)S(1)}, f32[64,2048]{1,0:T(8,128)S(1)}, f32[64,2048]{1,0:T(8,128)S(1)}, f32[64,2048]{1,0:T(8,128)S(1)}, f32[64,2048]{1,...) custom-call(f32[64,2176]{1,0:T(8,128)S(1)} %get-tuple-element.106.refs_0_, ...), custom_call_target="tpu_custom_call" | custom-call | flops 3221225472 | bytes 16777216 | tf_op jit(solution)/shard_map/pallas_call | solution.py:330
  153.3 1.8 collective-permute-done.43.refs_1_
  155.2 9.5 %shard_map.86 = (f32[64,2176]{1,0:T(8,128)S(1)}, f32[64,2048]{1,0:T(8,128)S(1)}, f32[64,2048]{1,0:T(8,128)S(1)}, f32[64,2048]{1,0:T(8,128)S(1)}, f32[64,2048]{1,...) custom-call(f32[64,2176]{1,0:T(8,128)S(1)} %get-tuple-element.113.refs_0_, ...), custom_call_target="tpu_custom_call" | custom-call | flops 3221225472 | bytes 16777216 | tf_op jit(solution)/shard_map/pallas_call | solution.py:330
  164.7 0.8 copy-done
  165.6 1.8 collective-permute-done.44.other_ref
  167.4 1.0 copy-done.1
  169.0 1.0 collective-permute-start.48
  170.0 1.4 collective-permute-start.49
  171.4 1.2 collective-permute-start.50
  172.6 4.4 %collective-permute-start.51 = (f32[64,512]{1,0:T(8,128)S(1)}, f32[64,512]{1,0:T(8,128)S(1)}, u32[]{:S(2)}, u32[]{:S(2)}) collective-permute-start(f32[64,512]{1,0:T(8,128)S(1)} %get-tuple-element.143), channel_id=1, source_target_pairs={{0,24},{2,26},{5,29},{7,31},{8,0},{10,2},{13,5},{15,7},{16,8},{18,... | collective-permute-start | bytes 393224 | tf_op jit(solution)/shard_map/ppermute | solution.py:501
  177.0 1.9 collective-permute-start.52
  179.0 1.8 collective-permute-done.51
  180.8 1.9 collective-permute-start.53
  182.8 9.4 %collective-permute-done.52 = f32[64,512]{1,0:T(8,128)S(1)} collective-permute-done((f32[64,512]{1,0:T(8,128)S(1)}, f32[64,512]{1,0:T(8,128)S(1)}, u32[]{:S(2)}, u32[]{:S(2)}) %collective-permute-start.52) | collective-permute-done | bytes 131104 | tf_op jit(solution)/shard_map/ppermute | solution.py:501
  192.3 1.9 collective-permute-start.55
  194.2 1.3 collective-permute-start.56
  195.6 3.3 %collective-permute-done.45.refs_0_ = f32[64,512]{1,0:T(8,128)S(1)} collective-permute-done((f32[64,512]{1,0:T(8,128)S(1)}, f32[64,512]{1,0:T(8,128)S(1)}, u32[]{:S(2)}, u32[]{:S(2)}) %collective-permute-start.45) | collective-permute-done | bytes 131104 | tf_op jit(solution)/shard_map/ppermute | solution.py:415
  198.9 1.3 collective-permute-start.57
  200.3 2.4 %collective-permute-done.57 = f32[1,64,512]{2,1,0:T(8,128)S(1)} collective-permute-done((f32[1,64,512]{2,1,0:T(8,128)S(1)}, f32[1,64,512]{2,1,0:T(8,128)S(1)}, u32[]{:S(2)}, u32[]{:S(2)}) %collective-permute-start.57) | collective-permute-done | bytes 131104 | tf_op jit(solution)/shard_map/ppermute | solution.py:501
  202.7 0.7 constant_dynamic-slice_fusion
  203.4 9.4 %collective-permute-done.46.refs_0_ = f32[64,512]{1,0:T(8,128)S(1)} collective-permute-done((f32[64,512]{1,0:T(8,128)S(1)}, f32[64,512]{1,0:T(8,128)S(1)}, u32[]{:S(2)}, u32[]{:S(2)}) %collective-permute-start.46) | collective-permute-done | bytes 131104 | tf_op jit(solution)/shard_map/ppermute | solution.py:415
  212.9 11.9 %collective-permute-done.47.refs_0_ = f32[64,512]{1,0:T(8,128)S(1)} collective-permute-done((f32[64,512]{1,0:T(8,128)S(1)}, f32[64,512]{1,0:T(8,128)S(1)}, u32[]{:S(2)}, u32[]{:S(2)}) %collective-permute-start.47) | collective-permute-done | bytes 131104 | tf_op jit(solution)/shard_map/ppermute | solution.py:415
  225.2 1.6 shard_map.88.refs_2_
  226.7 1.6 shard_map.89.refs_2_
  228.3 1.6 shard_map.90.refs_2_
  229.9 4.5 %collective-permute-done.59.refs_1_ = f32[192,512]{1,0:T(8,128)S(1)} collective-permute-done((f32[192,512]{1,0:T(8,128)S(1)}, f32[192,512]{1,0:T(8,128)S(1)}, u32[]{:S(2)}, u32[]{:S(2)}) %collective-permute-start.59) | collective-permute-done | bytes 393248 | tf_op jit(solution)/shard_map/ppermute | solution.py:415
  234.4 1.6 shard_map.91
  (118 shorter events, 11.1 us)
Async XLA Ops:
  2.4 41.5 %collective-permute-start.3 = (f32[40,128]{1,0:T(8,128)S(1)}, f32[40,128]{1,0:T(8,128)S(1)}, u32[]{:S(2)}, u32[]{:S(2)}) collective-permute-start(f32[40,128]{1,0:T(8,128)S(1)} %select_maximum_fusion), channel_id=1, source_target_pairs={{0,8},{8,16},{16,24},{24,0},{1,9},{9,17},{17,25},{25,1},{2,10},{10... | collective-permute-start | bytes 61448 | tf_op jit(solution)/shard_map/ppermute | solution.py:415
  5.5 40.0 %collective-permute-start.4 = (f32[40,128]{1,0:T(8,128)S(1)}, f32[40,128]{1,0:T(8,128)S(1)}, u32[]{:S(2)}, u32[]{:S(2)}) collective-permute-start(f32[40,128]{1,0:T(8,128)S(1)} %select_maximum_fusion), channel_id=1, source_target_pairs={{0,16},{8,24},{16,0},{24,8},{1,17},{9,25},{17,1},{25,9},{2,18},{10... | collective-permute-start | bytes 61448 | tf_op jit(solution)/shard_map/ppermute | solution.py:415
  16.4 8.3 %collective-permute-start.6 = (f32[2048,128]{1,0:T(8,128)}, f32[2048,128]{1,0:T(8,128)S(1)}, u32[]{:S(2)}, u32[]{:S(2)}) collective-permute-start(f32[2048,128]{1,0:T(8,128)} %shard_map.78), channel_id=1, source_target_pairs={{0,1},{1,0},{2,3},{3,2},{4,5},{5,4},{6,7},{7,6},{8,9},{9,8},{10,11... | collective-permute-start | bytes 3145736 | tf_op jit(solution)/shard_map/ppermute | solution.py:412
  24.7 5.1 %copy-start.2 = (f32[256,512]{1,0:T(8,128)S(1)}, f32[256,512]{1,0:T(8,128)}, u32[]{:S(2)}) copy-start(f32[256,512]{1,0:T(8,128)} %param.11) | copy-start | bytes 1572868
  26.2 9.2 %collective-permute-start.7 = (f32[512,128]{1,0:T(8,128)S(1)}, f32[512,128]{1,0:T(8,128)S(1)}, u32[]{:S(2)}, u32[]{:S(2)}) collective-permute-start(f32[512,128]{1,0:T(8,128)S(1)} %get-tuple-element.134), channel_id=1, source_target_pairs={{0,2},{1,3},{2,0},{3,1},{4,6},{5,7},{6,4},{7,5},{8,10},{9,11},{10,... | collective-permute-start | bytes 786440 | tf_op jit(solution)/shard_map/ppermute | solution.py:412
  27.7 14.0 %collective-permute-start.8 = (f32[512,128]{1,0:T(8,128)S(1)}, f32[512,128]{1,0:T(8,128)S(1)}, u32[]{:S(2)}, u32[]{:S(2)}) collective-permute-start(f32[512,128]{1,0:T(8,128)S(1)} %get-tuple-element.136), channel_id=1, source_target_pairs={{0,4},{1,5},{2,6},{3,7},{4,0},{5,1},{6,2},{7,3},{8,12},{9,13},{10,... | collective-permute-start | bytes 786440 | tf_op jit(solution)/shard_map/ppermute | solution.py:412
  29.3 12.5 %collective-permute-start.9 = (f32[512,128]{1,0:T(8,128)S(1)}, f32[512,128]{1,0:T(8,128)S(1)}, u32[]{:S(2)}, u32[]{:S(2)}) collective-permute-start(f32[512,128]{1,0:T(8,128)S(1)} %get-tuple-element.135), channel_id=1, source_target_pairs={{0,6},{1,7},{2,4},{3,5},{4,2},{5,3},{6,0},{7,1},{8,14},{9,15},{10,... | collective-permute-start | bytes 786440 | tf_op jit(solution)/shard_map/ppermute | solution.py:412
  35.4 10.1 %collective-permute-start.5 = (f32[40,128]{1,0:T(8,128)S(1)}, f32[40,128]{1,0:T(8,128)S(1)}, u32[]{:S(2)}, u32[]{:S(2)}) collective-permute-start(f32[40,128]{1,0:T(8,128)S(1)} %select_maximum_fusion), channel_id=1, source_target_pairs={{0,24},{8,0},{16,8},{24,16},{1,25},{9,1},{17,9},{25,17},{2,26},{10... | collective-permute-start | bytes 61448 | tf_op jit(solution)/shard_map/ppermute | solution.py:415
  41.8 6.4 %collective-permute-start = (f32[64,512]{1,0:T(8,128)S(1)}, f32[64,512]{1,0:T(8,128)S(1)}, u32[]{:S(2)}, u32[]{:S(2)}) collective-permute-start(f32[64,512]{1,0:T(8,128)S(1)} %get-tuple-element.149), channel_id=1, source_target_pairs={{0,2},{1,3},{2,0},{3,1},{4,6},{5,7},{6,4},{7,5},{8,10},{9,11},{10,... | collective-permute-start | bytes 393224 | tf_op jit(solution)/shard_map/ppermute | solution.py:412
  41.8 20.4 %collective-permute-start.10 = (f32[512,128]{1,0:T(8,128)S(1)}, f32[512,128]{1,0:T(8,128)S(1)}, u32[]{:S(2)}, u32[]{:S(2)}) collective-permute-start(f32[512,128]{1,0:T(8,128)S(1)} %fusion.1.refs_2_), channel_id=1, source_target_pairs={{0,2},{1,3},{2,0},{3,1},{4,6},{5,7},{6,4},{7,5},{8,10},{9,11},{10,... | collective-permute-start | bytes 786440 | tf_op jit(solution)/shard_map/ppermute | solution.py:412
  43.9 18.6 %collective-permute-start.11 = (f32[512,128]{1,0:T(8,128)S(1)}, f32[512,128]{1,0:T(8,128)S(1)}, u32[]{:S(2)}, u32[]{:S(2)}) collective-permute-start(f32[512,128]{1,0:T(8,128)S(1)} %fusion.1.refs_2_), channel_id=1, source_target_pairs={{0,4},{1,5},{2,6},{3,7},{4,0},{5,1},{6,2},{7,3},{8,12},{9,13},{10,... | collective-permute-start | bytes 786440 | tf_op jit(solution)/shard_map/ppermute | solution.py:412
  45.4 17.3 %collective-permute-start.12 = (f32[512,128]{1,0:T(8,128)S(1)}, f32[512,128]{1,0:T(8,128)S(1)}, u32[]{:S(2)}, u32[]{:S(2)}) collective-permute-start(f32[512,128]{1,0:T(8,128)S(1)} %fusion.1.refs_2_), channel_id=1, source_target_pairs={{0,6},{1,7},{2,4},{3,5},{4,2},{5,3},{6,0},{7,1},{8,14},{9,15},{10,... | collective-permute-start | bytes 786440 | tf_op jit(solution)/shard_map/ppermute | solution.py:412
  45.5 16.5 %collective-permute-start.1 = (f32[64,512]{1,0:T(8,128)S(1)}, f32[64,512]{1,0:T(8,128)S(1)}, u32[]{:S(2)}, u32[]{:S(2)}) collective-permute-start(f32[64,512]{1,0:T(8,128)S(1)} %get-tuple-element.151), channel_id=1, source_target_pairs={{0,4},{1,5},{2,6},{3,7},{4,0},{5,1},{6,2},{7,3},{8,12},{9,13},{10,... | collective-permute-start | bytes 393224 | tf_op jit(solution)/shard_map/ppermute | solution.py:412
  48.2 13.8 %collective-permute-start.2 = (f32[64,512]{1,0:T(8,128)S(1)}, f32[64,512]{1,0:T(8,128)S(1)}, u32[]{:S(2)}, u32[]{:S(2)}) collective-permute-start(f32[64,512]{1,0:T(8,128)S(1)} %get-tuple-element.150), channel_id=1, source_target_pairs={{0,6},{1,7},{2,4},{3,5},{4,2},{5,3},{6,0},{7,1},{8,14},{9,15},{10,... | collective-permute-start | bytes 393224 | tf_op jit(solution)/shard_map/ppermute | solution.py:412
  62.0 11.1 %collective-permute-start.13 = (f32[512,128]{1,0:T(8,128)S(1)}, f32[512,128]{1,0:T(8,128)S(1)}, u32[]{:S(2)}, u32[]{:S(2)}) collective-permute-start(f32[512,128]{1,0:T(8,128)S(1)} %fusion.1.refs_2_), channel_id=1, source_target_pairs={{0,1},{1,0},{2,3},{3,2},{4,5},{5,4},{6,7},{7,6},{8,9},{9,8},{10,11... | collective-permute-start | bytes 786440 | tf_op jit(solution)/shard_map/ppermute | solution.py:412
  62.0 10.5 %collective-permute-start.17 = (f32[512,128]{1,0:T(8,128)S(1)}, f32[512,128]{1,0:T(8,128)S(1)}, u32[]{:S(2)}, u32[]{:S(2)}) collective-permute-start(f32[512,128]{1,0:T(8,128)S(1)} %fusion.1.refs_2_), channel_id=1, source_target_pairs={{0,8},{8,16},{16,24},{24,0},{1,9},{9,17},{17,25},{25,1},{2,10},{10... | collective-permute-start | bytes 786440 | tf_op jit(solution)/shard_map/ppermute | solution.py:415
  62.2 12.4 %collective-permute-start.14 = (f32[512,128]{1,0:T(8,128)S(1)}, f32[512,128]{1,0:T(8,128)S(1)}, u32[]{:S(2)}, u32[]{:S(2)}) collective-permute-start(f32[512,128]{1,0:T(8,128)S(1)} %collective-permute-done.10.refs_3_), channel_id=1, source_target_pairs={{0,1},{1,0},{2,3},{3,2},{4,5},{5,4},{6,7},{7,6},{8,9},{9,8},{10,11... | collective-permute-start | bytes 786440 | tf_op jit(solution)/shard_map/ppermute | solution.py:412
  62.5 13.4 %collective-permute-start.15 = (f32[512,128]{1,0:T(8,128)S(1)}, f32[512,128]{1,0:T(8,128)S(1)}, u32[]{:S(2)}, u32[]{:S(2)}) collective-permute-start(f32[512,128]{1,0:T(8,128)S(1)} %collective-permute-done.11.refs_4_), channel_id=1, source_target_pairs={{0,1},{1,0},{2,3},{3,2},{4,5},{5,4},{6,7},{7,6},{8,9},{9,8},{10,11... | collective-permute-start | bytes 786440 | tf_op jit(solution)/shard_map/ppermute | solution.py:412
  62.7 13.3 %collective-permute-start.16 = (f32[512,128]{1,0:T(8,128)S(1)}, f32[512,128]{1,0:T(8,128)S(1)}, u32[]{:S(2)}, u32[]{:S(2)}) collective-permute-start(f32[512,128]{1,0:T(8,128)S(1)} %collective-permute-done.12.refs_5_), channel_id=1, source_target_pairs={{0,1},{1,0},{2,3},{3,2},{4,5},{5,4},{6,7},{7,6},{8,9},{9,8},{10,11... | collective-permute-start | bytes 786440 | tf_op jit(solution)/shard_map/ppermute | solution.py:412
  72.5 12.9 %collective-permute-start.18 = (f32[512,128]{1,0:T(8,128)S(1)}, f32[512,128]{1,0:T(8,128)S(1)}, u32[]{:S(2)}, u32[]{:S(2)}) collective-permute-start(f32[512,128]{1,0:T(8,128)S(1)} %collective-permute-done.17.refs_2_), channel_id=1, source_target_pairs={{0,2},{1,3},{2,0},{3,1},{4,6},{5,7},{6,4},{7,5},{8,10},{9,11},{10,... | collective-permute-start | bytes 786440 | tf_op jit(solution)/shard_map/ppermute | solution.py:412
  73.1 12.4 %collective-permute-start.19 = (f32[512,128]{1,0:T(8,128)S(1)}, f32[512,128]{1,0:T(8,128)S(1)}, u32[]{:S(2)}, u32[]{:S(2)}) collective-permute-start(f32[512,128]{1,0:T(8,128)S(1)} %collective-permute-done.17.refs_2_), channel_id=1, source_target_pairs={{0,4},{1,5},{2,6},{3,7},{4,0},{5,1},{6,2},{7,3},{8,12},{9,13},{10,... | collective-permute-start | bytes 786440 | tf_op jit(solution)/shard_map/ppermute | solution.py:412
  74.6 12.6 %collective-permute-start.20 = (f32[512,128]{1,0:T(8,128)S(1)}, f32[512,128]{1,0:T(8,128)S(1)}, u32[]{:S(2)}, u32[]{:S(2)}) collective-permute-start(f32[512,128]{1,0:T(8,128)S(1)} %collective-permute-done.17.refs_2_), channel_id=1, source_target_pairs={{0,6},{1,7},{2,4},{3,5},{4,2},{5,3},{6,0},{7,1},{8,14},{9,15},{10,... | collective-permute-start | bytes 786440 | tf_op jit(solution)/shard_map/ppermute | solution.py:412
  76.0 12.2 %collective-permute-start.25 = (f32[512,128]{1,0:T(8,128)S(1)}, f32[512,128]{1,0:T(8,128)S(1)}, u32[]{:S(2)}, u32[]{:S(2)}) collective-permute-start(f32[512,128]{1,0:T(8,128)S(1)} %collective-permute-done.17.refs_2_), channel_id=1, source_target_pairs={{0,8},{8,16},{16,24},{24,0},{1,9},{9,17},{17,25},{25,1},{2,10},{10... | collective-permute-start | bytes 786440 | tf_op jit(solution)/shard_map/ppermute | solution.py:415
  87.2 1.6 collective-permute-start.21
  87.2 3.3 %collective-permute-start.22 = (f32[512,128]{1,0:T(8,128)S(1)}, f32[512,128]{1,0:T(8,128)S(1)}, u32[]{:S(2)}, u32[]{:S(2)}) collective-permute-start(f32[512,128]{1,0:T(8,128)S(1)} %collective-permute-done.18.refs_3_), channel_id=1, source_target_pairs={{0,1},{1,0},{2,3},{3,2},{4,5},{5,4},{6,7},{7,6},{8,9},{9,8},{10,11... | collective-permute-start | bytes 786440 | tf_op jit(solution)/shard_map/ppermute | solution.py:412
  87.7 4.0 %collective-permute-start.23 = (f32[512,128]{1,0:T(8,128)S(1)}, f32[512,128]{1,0:T(8,128)S(1)}, u32[]{:S(2)}, u32[]{:S(2)}) collective-permute-start(f32[512,128]{1,0:T(8,128)S(1)} %collective-permute-done.19.refs_4_), channel_id=1, source_target_pairs={{0,1},{1,0},{2,3},{3,2},{4,5},{5,4},{6,7},{7,6},{8,9},{9,8},{10,11... | collective-permute-start | bytes 786440 | tf_op jit(solution)/shard_map/ppermute | solution.py:412
  87.7 4.0 %collective-permute-start.24 = (f32[512,128]{1,0:T(8,128)S(1)}, f32[512,128]{1,0:T(8,128)S(1)}, u32[]{:S(2)}, u32[]{:S(2)}) collective-permute-start(f32[512,128]{1,0:T(8,128)S(1)} %collective-permute-done.20.refs_5_), channel_id=1, source_target_pairs={{0,1},{1,0},{2,3},{3,2},{4,5},{5,4},{6,7},{7,6},{8,9},{9,8},{10,11... | collective-permute-start | bytes 786440 | tf_op jit(solution)/shard_map/ppermute | solution.py:412
  88.2 13.0 %collective-permute-start.26 = (f32[512,128]{1,0:T(8,128)S(1)}, f32[512,128]{1,0:T(8,128)S(1)}, u32[]{:S(2)}, u32[]{:S(2)}) collective-permute-start(f32[512,128]{1,0:T(8,128)S(1)} %collective-permute-done.25.refs_2_), channel_id=1, source_target_pairs={{0,2},{1,3},{2,0},{3,1},{4,6},{5,7},{6,4},{7,5},{8,10},{9,11},{10,... | collective-permute-start | bytes 786440 | tf_op jit(solution)/shard_map/ppermute | solution.py:412
  88.8 13.9 %collective-permute-start.27 = (f32[512,128]{1,0:T(8,128)S(1)}, f32[512,128]{1,0:T(8,128)S(1)}, u32[]{:S(2)}, u32[]{:S(2)}) collective-permute-start(f32[512,128]{1,0:T(8,128)S(1)} %collective-permute-done.25.refs_2_), channel_id=1, source_target_pairs={{0,4},{1,5},{2,6},{3,7},{4,0},{5,1},{6,2},{7,3},{8,12},{9,13},{10,... | collective-permute-start | bytes 786440 | tf_op jit(solution)/shard_map/ppermute | solution.py:412
  90.5 12.2 %collective-permute-start.28 = (f32[512,128]{1,0:T(8,128)S(1)}, f32[512,128]{1,0:T(8,128)S(1)}, u32[]{:S(2)}, u32[]{:S(2)}) collective-permute-start(f32[512,128]{1,0:T(8,128)S(1)} %collective-permute-done.25.refs_2_), channel_id=1, source_target_pairs={{0,6},{1,7},{2,4},{3,5},{4,2},{5,3},{6,0},{7,1},{8,14},{9,15},{10,... | collective-permute-start | bytes 786440 | tf_op jit(solution)/shard_map/ppermute | solution.py:412
  91.7 12.0 %collective-permute-start.33 = (f32[512,128]{1,0:T(8,128)S(1)}, f32[512,128]{1,0:T(8,128)S(1)}, u32[]{:S(2)}, u32[]{:S(2)}) collective-permute-start(f32[512,128]{1,0:T(8,128)S(1)} %collective-permute-done.25.refs_2_), channel_id=1, source_target_pairs={{0,8},{8,16},{16,24},{24,0},{1,9},{9,17},{17,25},{25,1},{2,10},{10... | collective-permute-start | bytes 786440 | tf_op jit(solution)/shard_map/ppermute | solution.py:415
  102.7 2.1 collective-permute-start.29
  102.7 3.3 %collective-permute-start.30 = (f32[512,128]{1,0:T(8,128)S(1)}, f32[512,128]{1,0:T(8,128)S(1)}, u32[]{:S(2)}, u32[]{:S(2)}) collective-permute-start(f32[512,128]{1,0:T(8,128)S(1)} %collective-permute-done.26.refs_3_), channel_id=1, source_target_pairs={{0,1},{1,0},{2,3},{3,2},{4,5},{5,4},{6,7},{7,6},{8,9},{9,8},{10,11... | collective-permute-start | bytes 786440 | tf_op jit(solution)/shard_map/ppermute | solution.py:412
  103.2 4.0 %collective-permute-start.31 = (f32[512,128]{1,0:T(8,128)S(1)}, f32[512,128]{1,0:T(8,128)S(1)}, u32[]{:S(2)}, u32[]{:S(2)}) collective-permute-start(f32[512,128]{1,0:T(8,128)S(1)} %collective-permute-done.27.refs_4_), channel_id=1, source_target_pairs={{0,1},{1,0},{2,3},{3,2},{4,5},{5,4},{6,7},{7,6},{8,9},{9,8},{10,11... | collective-permute-start | bytes 786440 | tf_op jit(solution)/shard_map/ppermute | solution.py:412
  103.2 4.0 %collective-permute-start.32 = (f32[512,128]{1,0:T(8,128)S(1)}, f32[512,128]{1,0:T(8,128)S(1)}, u32[]{:S(2)}, u32[]{:S(2)}) collective-permute-start(f32[512,128]{1,0:T(8,128)S(1)} %collective-permute-done.28.refs_5_), channel_id=1, source_target_pairs={{0,1},{1,0},{2,3},{3,2},{4,5},{5,4},{6,7},{7,6},{8,9},{9,8},{10,11... | collective-permute-start | bytes 786440 | tf_op jit(solution)/shard_map/ppermute | solution.py:412
  103.7 12.9 %collective-permute-start.34 = (f32[512,128]{1,0:T(8,128)S(1)}, f32[512,128]{1,0:T(8,128)S(1)}, u32[]{:S(2)}, u32[]{:S(2)}) collective-permute-start(f32[512,128]{1,0:T(8,128)S(1)} %collective-permute-done.33.refs_2_), channel_id=1, source_target_pairs={{0,2},{1,3},{2,0},{3,1},{4,6},{5,7},{6,4},{7,5},{8,10},{9,11},{10,... | collective-permute-start | bytes 786440 | tf_op jit(solution)/shard_map/ppermute | solution.py:412
  104.8 12.3 %collective-permute-start.35 = (f32[512,128]{1,0:T(8,128)S(1)}, f32[512,128]{1,0:T(8,128)S(1)}, u32[]{:S(2)}, u32[]{:S(2)}) collective-permute-start(f32[512,128]{1,0:T(8,128)S(1)} %collective-permute-done.33.refs_2_), channel_id=1, source_target_pairs={{0,4},{1,5},{2,6},{3,7},{4,0},{5,1},{6,2},{7,3},{8,12},{9,13},{10,... | collective-permute-start | bytes 786440 | tf_op jit(solution)/shard_map/ppermute | solution.py:412
  106.0 12.3 %collective-permute-start.36 = (f32[512,128]{1,0:T(8,128)S(1)}, f32[512,128]{1,0:T(8,128)S(1)}, u32[]{:S(2)}, u32[]{:S(2)}) collective-permute-start(f32[512,128]{1,0:T(8,128)S(1)} %collective-permute-done.33.refs_2_), channel_id=1, source_target_pairs={{0,6},{1,7},{2,4},{3,5},{4,2},{5,3},{6,0},{7,1},{8,14},{9,15},{10,... | collective-permute-start | bytes 786440 | tf_op jit(solution)/shard_map/ppermute | solution.py:412
  118.4 1.5 collective-permute-start.37
  118.4 1.9 collective-permute-start.38
  118.9 1.8 collective-permute-start.39
  118.9 2.1 collective-permute-start.40
  130.6 2.0 collective-permute-start.41
  141.9 2.0 collective-permute-start.42
  153.1 2.0 collective-permute-start.43
  164.7 0.8 copy-start
  165.4 2.0 collective-permute-start.44
  167.4 1.0 copy-start.1
  169.0 25.2 %collective-permute-start.48 = (f32[64,512]{1,0:T(8,128)S(1)}, f32[64,512]{1,0:T(8,128)S(1)}, u32[]{:S(2)}, u32[]{:S(2)}) collective-permute-start(f32[64,512]{1,0:T(8,128)S(1)} %get-tuple-element.146), channel_id=1, source_target_pairs={{0,2},{1,3},{2,0},{3,1},{4,6},{5,7},{6,4},{7,5},{8,10},{9,11},{10,... | collective-permute-start | bytes 393224 | tf_op jit(solution)/shard_map/ppermute | solution.py:412
  170.0 25.6 %collective-permute-start.49 = (f32[64,512]{1,0:T(8,128)S(1)}, f32[64,512]{1,0:T(8,128)S(1)}, u32[]{:S(2)}, u32[]{:S(2)}) collective-permute-start(f32[64,512]{1,0:T(8,128)S(1)} %get-tuple-element.145), channel_id=1, source_target_pairs={{0,4},{1,5},{2,6},{3,7},{4,0},{5,1},{6,2},{7,3},{8,12},{9,13},{10,... | collective-permute-start | bytes 393224 | tf_op jit(solution)/shard_map/ppermute | solution.py:412
  171.4 24.2 %collective-permute-start.50 = (f32[64,512]{1,0:T(8,128)S(1)}, f32[64,512]{1,0:T(8,128)S(1)}, u32[]{:S(2)}, u32[]{:S(2)}) collective-permute-start(f32[64,512]{1,0:T(8,128)S(1)} %get-tuple-element.144), channel_id=1, source_target_pairs={{0,6},{1,7},{2,4},{3,5},{4,2},{5,3},{6,0},{7,1},{8,14},{9,15},{10,... | collective-permute-start | bytes 393224 | tf_op jit(solution)/shard_map/ppermute | solution.py:412
  172.6 8.3 %collective-permute-start.51 = (f32[64,512]{1,0:T(8,128)S(1)}, f32[64,512]{1,0:T(8,128)S(1)}, u32[]{:S(2)}, u32[]{:S(2)}) collective-permute-start(f32[64,512]{1,0:T(8,128)S(1)} %get-tuple-element.143), channel_id=1, source_target_pairs={{0,24},{2,26},{5,29},{7,31},{8,0},{10,2},{13,5},{15,7},{16,8},{18,... | collective-permute-start | bytes 393224 | tf_op jit(solution)/shard_map/ppermute | solution.py:501
  177.0 15.1 %collective-permute-start.52 = (f32[64,512]{1,0:T(8,128)S(1)}, f32[64,512]{1,0:T(8,128)S(1)}, u32[]{:S(2)}, u32[]{:S(2)}) collective-permute-start(f32[64,512]{1,0:T(8,128)S(1)} %get-tuple-element.142), channel_id=1, source_target_pairs={{0,16},{2,18},{5,21},{7,23},{8,24},{10,26},{13,29},{15,31},{16,0},... | collective-permute-start | bytes 393224 | tf_op jit(solution)/shard_map/ppermute | solution.py:501
  180.8 11.3 %collective-permute-start.53 = (f32[64,512]{1,0:T(8,128)S(1)}, f32[64,512]{1,0:T(8,128)S(1)}, u32[]{:S(2)}, u32[]{:S(2)}) collective-permute-start(f32[64,512]{1,0:T(8,128)S(1)} %get-tuple-element.141), channel_id=1, source_target_pairs={{0,8},{2,10},{5,13},{7,15},{8,16},{10,18},{13,21},{15,23},{16,24},... | collective-permute-start | bytes 393224 | tf_op jit(solution)/shard_map/ppermute | solution.py:501
  192.1 6.8 %collective-permute-start.45 = (f32[64,512]{1,0:T(8,128)S(1)}, f32[64,512]{1,0:T(8,128)S(1)}, u32[]{:S(2)}, u32[]{:S(2)}) collective-permute-start(f32[64,512]{1,0:T(8,128)S(1)} %get-tuple-element.147.refs_0_), channel_id=1, source_target_pairs={{0,8},{8,16},{16,24},{24,0},{1,9},{9,17},{17,25},{25,1},{2,10},{10... | collective-permute-start | bytes 393224 | tf_op jit(solution)/shard_map/ppermute | solution.py:415
  192.3 8.0 %collective-permute-start.55 = (f32[1,64,512]{2,1,0:T(8,128)S(1)}, f32[1,64,512]{2,1,0:T(8,128)S(1)}, u32[]{:S(2)}, u32[]{:S(2)}) collective-permute-start(f32[1,64,512]{2,1,0:T(8,128)S(1)} %get-tuple-element.139), channel_id=1, source_target_pairs={{0,2},{2,0},{5,7},{7,5},{8,10},{10,8},{13,15},{15,13},{16,18},{18,... | collective-permute-start | bytes 393224 | tf_op jit(solution)/shard_map/ppermute | solution.py:501
  194.2 6.1 %collective-permute-start.56 = (f32[1,64,512]{2,1,0:T(8,128)S(1)}, f32[1,64,512]{2,1,0:T(8,128)S(1)}, u32[]{:S(2)}, u32[]{:S(2)}) collective-permute-start(f32[1,64,512]{2,1,0:T(8,128)S(1)} %get-tuple-element.138), channel_id=1, source_target_pairs={{0,4},{2,6},{5,1},{7,3},{8,12},{10,14},{13,9},{15,11},{16,20},{18,... | collective-permute-start | bytes 393224 | tf_op jit(solution)/shard_map/ppermute | solution.py:501
  198.9 14.0 %collective-permute-start.54 = (f32[192,512]{1,0:T(8,128)S(1)}, f32[192,512]{1,0:T(8,128)S(1)}, u32[]{:S(2)}, u32[]{:S(2)}) collective-permute-start(f32[192,512]{1,0:T(8,128)S(1)} %constant_dynamic-update-slice_fusion.refs_1_), channel_id=1, source_target_pairs={{0,8},{8,16},{16,24},{24,0},{1,9},{9,17},{17,25},{25,1},{2,10},{10... | collective-permute-start | bytes 1179656 | tf_op jit(solution)/shard_map/ppermute | solution.py:415
  198.9 3.8 %collective-permute-start.57 = (f32[1,64,512]{2,1,0:T(8,128)S(1)}, f32[1,64,512]{2,1,0:T(8,128)S(1)}, u32[]{:S(2)}, u32[]{:S(2)}) collective-permute-start(f32[1,64,512]{2,1,0:T(8,128)S(1)} %get-tuple-element.137), channel_id=1, source_target_pairs={{0,6},{2,4},{5,3},{7,1},{8,14},{10,12},{13,11},{15,9},{16,22},{18,... | collective-permute-start | bytes 393224 | tf_op jit(solution)/shard_map/ppermute | solution.py:501
  200.2 12.7 %collective-permute-start.46 = (f32[64,512]{1,0:T(8,128)S(1)}, f32[64,512]{1,0:T(8,128)S(1)}, u32[]{:S(2)}, u32[]{:S(2)}) collective-permute-start(f32[64,512]{1,0:T(8,128)S(1)} %collective-permute-done.45.refs_0_), channel_id=1, source_target_pairs={{0,8},{8,16},{16,24},{24,0},{1,9},{9,17},{17,25},{25,1},{2,10},{10... | collective-permute-start | bytes 393224 | tf_op jit(solution)/shard_map/ppermute | solution.py:415
  212.9 11.9 %collective-permute-start.58 = (f32[192,512]{1,0:T(8,128)S(1)}, f32[192,512]{1,0:T(8,128)S(1)}, u32[]{:S(2)}, u32[]{:S(2)}) collective-permute-start(f32[192,512]{1,0:T(8,128)S(1)} %collective-permute-done.54.refs_1_), channel_id=1, source_target_pairs={{0,8},{8,16},{16,24},{24,0},{1,9},{9,17},{17,25},{25,1},{2,10},{10... | collective-permute-start | bytes 1179656 | tf_op jit(solution)/shard_map/ppermute | solution.py:415
  212.9 11.9 %collective-permute-start.47 = (f32[64,512]{1,0:T(8,128)S(1)}, f32[64,512]{1,0:T(8,128)S(1)}, u32[]{:S(2)}, u32[]{:S(2)}) collective-permute-start(f32[64,512]{1,0:T(8,128)S(1)} %collective-permute-done.46.refs_0_), channel_id=1, source_target_pairs={{0,8},{8,16},{16,24},{24,0},{1,9},{9,17},{17,25},{25,1},{2,10},{10... | collective-permute-start | bytes 393224 | tf_op jit(solution)/shard_map/ppermute | solution.py:415
  224.8 9.6 %collective-permute-start.59 = (f32[192,512]{1,0:T(8,128)S(1)}, f32[192,512]{1,0:T(8,128)S(1)}, u32[]{:S(2)}, u32[]{:S(2)}) collective-permute-start(f32[192,512]{1,0:T(8,128)S(1)} %collective-permute-done.58.refs_1_), channel_id=1, source_target_pairs={{0,8},{8,16},{16,24},{24,0},{1,9},{9,17},{17,25},{25,1},{2,10},{10... | collective-permute-start | bytes 1179656 | tf_op jit(solution)/shard_map/ppermute | solution.py:415

commit v6 on v5

--- a/solution.py
+++ b/solution.py
@@ -79,9 +79,9 @@
 def build_kernel(ranks, share, ex_block, n_sources, *refs):
     offs_ref, start_ref = refs[:2]
     sources = refs[2:2 + n_sources]
-    ids_ref, pick_ref, b_ref = refs[2 + n_sources:5 + n_sources]
-    high_ref, low_ref, inner_ref, sq_ref = refs[5 + n_sources:9 + n_sources]
-    out_t, in_twice, ids_wide, rows, sketch = refs[9 + n_sources:]
+    ids_ref, pick_ref = refs[2 + n_sources:4 + n_sources]
+    high_ref, low_ref, sq_ref = refs[4 + n_sources:7 + n_sources]
+    out_t, in_twice, ids_wide, rows, sketch = refs[7 + n_sources:]
     step = pl.program_id(0)
     half_ranks = pick_ref.shape[0]
     pairs = half_ranks // 2
@@ -160,16 +160,11 @@
     for k in range(1, values.shape[1] // LANES):
         total = total + sq[:, k * LANES:(k + 1) * LANES]
     sq_ref[...] += total
-    b_both = jnp.concatenate(split2(b_ref[...]), axis=0)
-    count = b_ref.shape[0]
-    both = (dot_nt(high, b_both) + dot_nt(low, b_both)).T
-    inner_ref[...] = both[:count] + both[count:]
-
-
-def build(offs, starts, sources, ids, pick, b, ranks, share):
+
+
+def build(offs, starts, sources, ids, pick, ranks, share, comps):
     tokens = ids.shape[1]
     half_ranks = pick.shape[0]
-    queries, comps = b.shape
     ex_block = 256
     group = 8
     whole = lambda i, *_: (0, 0)
@@ -178,17 +173,15 @@
         out_shape=(
             jax.ShapeDtypeStruct((EX_DEV, comps), BF16),
             jax.ShapeDtypeStruct((EX_DEV, comps), BF16),
-            jax.ShapeDtypeStruct((queries, EX_DEV), F32),
             jax.ShapeDtypeStruct((8, LANES), F32),
         ),
         grid_spec=pltpu.PrefetchScalarGridSpec(
             num_scalar_prefetch=2,
             grid=(EX_DEV // ex_block,),
-            in_specs=[pl.BlockSpec(a.shape, whole) for a in (*sources, ids, pick, b)],
+            in_specs=[pl.BlockSpec(a.shape, whole) for a in (*sources, ids, pick)],
             out_specs=[
                 pl.BlockSpec((ex_block, comps), lambda i, *_: (i, 0)),
                 pl.BlockSpec((ex_block, comps), lambda i, *_: (i, 0)),
-                pl.BlockSpec((queries, ex_block), lambda i, *_: (0, i)),
                 pl.BlockSpec((8, LANES), whole),
             ],
             scratch_shapes=[
@@ -205,30 +198,45 @@
             bytes_accessed=4 * EX_DEV * comps + 4 * tokens * LANES,
             transcendentals=0,
         ),
-    )(offs, starts, *sources, ids, pick, b)
+    )(offs, starts, *sources, ids, pick)
 
 
 def join_kernel(planes, *refs):
-    inners, squares, b_ref, out_ref = refs[:planes], refs[planes:2 * planes], refs[-2], refs[-1]
-    for k, inner in enumerate(inners):
-        out_ref[:, k * EX_DEV:(k + 1) * EX_DEV] = inner[...]
+    highs, lows, squares = refs[:planes], refs[planes:2 * planes], refs[2 * planes:3 * planes]
+    slots, out_ref, b_ref = refs[3 * planes:-2], refs[-2], refs[-1]
+    width = slots[0].shape[1]
+    for k, slot in enumerate(slots):
+        b_ref[:, k * width:(k + 1) * width] = slot[...]
+    b = b_ref[...]
+    count = b.shape[0]
+    b_both = jnp.concatenate(split2(b), axis=0)
+    for k in range(planes):
+        both = (dot_nt(highs[k][...], b_both) + dot_nt(lows[k][...], b_both)).T
+        out_ref[:, k * EX_DEV:(k + 1) * EX_DEV] = both[:count] + both[count:]
     total = squares[0][...]
     for square in squares[1:]:
         total = total + square[...]
     total = jnp.sum(jnp.sum(total, axis=1, keepdims=True), axis=0, keepdims=True)
-    b = b_ref[...]
     norm = jnp.sum(b * b, axis=1, keepdims=True)
-    shape = (b.shape[0], LANES)
-    out_ref[:, planes * EX_DEV:] = lanes_of([norm, total], shape)
-
-
-def join(inners, squares, b):
-    planes = len(inners)
+    out_ref[:, planes * EX_DEV:] = lanes_of([norm, total], (count, LANES))
+
+
+def join(highs, lows, squares, slots):
+    planes = len(highs)
+    count, comps = slots[0].shape[0], highs[0].shape[1]
     return pl.pallas_call(
         functools.partial(join_kernel, planes),
-        out_shape=jax.ShapeDtypeStruct((b.shape[0], planes * EX_DEV + LANES), F32),
+        out_shape=(
+            jax.ShapeDtypeStruct((count, planes * EX_DEV + LANES), F32),
+            jax.ShapeDtypeStruct((count, comps), F32),
+        ),
         compiler_params=pltpu.CompilerParams(vmem_limit_bytes=STEP * MIB),
-    )(*inners, *squares, b)
+        cost_estimate=pl.CostEstimate(
+            flops=6 * planes * EX_DEV * count * comps,
+            bytes_accessed=4 * planes * EX_DEV * comps,
+            transcendentals=0,
+        ),
+    )(*highs, *lows, *squares, *slots)
 
 
 def column(values, k):
@@ -363,37 +371,31 @@
     )(*arrays)
 
 
-def place_kernel(where_ref, *refs):
-    parts, out_ref, held = refs[:-2], refs[-2], refs[-1]
-    parts = parts[:2]
-    rows = parts[0].shape[0]
-    slot = 0
-    for part in parts:
-        for k in range(part.shape[0] // rows):
-            at = pl.multiple_of(where_ref[1 + slot] * rows, rows)
-            held[pl.ds(at, rows), :] = part[k * rows:(k + 1) * rows, :]
-            slot += 1
+def place_kernel(slots, where_ref, part_ref, *refs):
+    out_ref, held = refs[-2:]
+    rows = part_ref.shape[0] // slots
+    for k in range(slots):
+        at = pl.multiple_of(where_ref[1 + k] * rows, rows)
+        held[pl.ds(at, rows), :] = part_ref[k * rows:(k + 1) * rows, :]
     out_ref[...] = held[...].T
 
 
-def place(where, own, others, out, shape):
-    rows = own.shape[0] + others.shape[0]
-    whole = lambda i, where: (0, 0)
-    operands = [own, others] + ([] if out is None else [out])
-    in_specs = [pl.BlockSpec(own.shape, whole), pl.BlockSpec(others.shape, whole)]
+def place(where, part, out, shape):
+    operands, in_specs = [part], [pl.BlockSpec(part.shape, lambda i, where: (0, 0))]
     if out is not None:
+        operands.append(out)
         in_specs.append(pl.BlockSpec(memory_space=pl.ANY))
     return pl.pallas_call(
-        place_kernel,
+        functools.partial(place_kernel, where.shape[0] - 1),
         out_shape=jax.ShapeDtypeStruct(shape, F32),
         grid_spec=pltpu.PrefetchScalarGridSpec(
             num_scalar_prefetch=1,
             grid=(1,),
             in_specs=in_specs,
-            out_specs=pl.BlockSpec((shape[0], rows), lambda i, where: (0, where[0])),
-            scratch_shapes=[pltpu.VMEM((rows, own.shape[1]), F32)],
-        ),
-        input_output_aliases={} if out is None else {3: 0},
+            out_specs=pl.BlockSpec((shape[0], part.shape[0]), lambda i, where: (0, where[0])),
+            scratch_shapes=[pltpu.VMEM(part.shape, F32)],
+        ),
+        input_output_aliases={} if out is None else {2: 0},
         compiler_params=pltpu.CompilerParams(vmem_limit_bytes=24 * MIB),
     )(where, *operands)
 
@@ -421,8 +423,6 @@
 
     q_chip = queries.shape[0] // n_c
     slots = [lax.dynamic_slice_in_dim(queries, near_chip[k] * q_chip, q_chip, 0) for k in range(n_c)]
-    slots = [slots[0]] + [swap(slots[k], 2 * k) for k in range(1, n_c)]
-    b = jnp.concatenate(slots, axis=1)
 
     group = 8
     bounds = group * jnp.arange(EX_DEV // group, dtype=jnp.int32)
@@ -436,15 +436,16 @@
         ],
         axis=0,
     )
-    extras = [extra] + [shift(extra, away) for away in range(1, n_dp)]
-    plane_ids = [one[:id_rows].reshape((1, tokens)) for one in extras]
-    firsts = [one[id_rows, :EX_DEV // group].astype(jnp.int32) for one in extras]
 
     share = tokens // n_t
     blocks = jnp.stack(near_chip).astype(jnp.int32) * 2
     w_in, w_out = proj_in.T, proj_out.T
     give = project(blocks + 1 - core, activations, out_grads, w_in, w_out, share)
     keep = project(blocks + core, activations, out_grads, w_in, w_out, share)
+    extra = tie(extra, give)
+    extras = [extra] + [shift(extra, away) for away in range(1, n_dp)]
+    plane_ids = [one[:id_rows].reshape((1, tokens)) for one in extras]
+    firsts = [one[id_rows, :EX_DEV // group].astype(jnp.int32) for one in extras]
     kept = (keep + swap(give, 1)).reshape((n_c, share, LANES))
     own = kept[0]
     for k in range(1, n_c):
@@ -462,24 +463,26 @@
     offs = jnp.stack(
         [near_chip[k] * 2 + which for which in (core, 1 - core) for k in range(n_c)]
     ).astype(jnp.int32)
-    offs, pick, b, plane_ids, firsts = lax.optimization_barrier((offs, pick, b, plane_ids, firsts))
-
-    highs, lows, inners, squares = [], [], [], []
+    offs, pick, plane_ids, firsts, slots = lax.optimization_barrier(
+        (offs, pick, plane_ids, firsts, slots)
+    )
+
+    highs, lows, squares = [], [], []
     for away in range(n_dp):
         piece = rings[away]
         near = [piece] + [swap(piece, 2 * k) for k in range(1, n_c)]
         sources = near + [
             swap(part, 1) for part in (tie(near, squares[-1]) if squares else near)
         ]
-        high, low, inner, square = build(
-            offs, firsts[away], sources, plane_ids[away], pick, b, ranks, share
+        high, low, square = build(
+            offs, firsts[away], sources, plane_ids[away], pick, ranks, share, comps_all // 2
         )
         highs.append(high)
         lows.append(low)
-        inners.append(inner)
         squares.append(square)
 
-    message = join(inners, squares, b)
+    slots = [slots[0]] + [swap(slots[k], 2 * k) for k in range(1, n_c)]
+    message, b = join(highs, lows, squares, slots)
     r, rest = b, ()
     for step in range(ITERS - 1):
         other = swap(message, 1)
@@ -500,10 +503,9 @@
         ]
         return lax.ppermute(values, ("dp", "tensor"), pairs)
 
-    others_x = jnp.concatenate(
-        [swap(x[:, k * per_slot:(k + 1) * per_slot], 2 * k) for k in range(1, n_c)], axis=0
-    )
-    own_x = x[:, :per_slot]
+    ring = [x[:, k * per_slot:(k + 1) * per_slot] for k in range(n_c)]
+    ring = jnp.concatenate([ring[0]] + [swap(ring[k], 2 * k) for k in range(1, n_c)], axis=0)
+    y = tie(y, ring)
     by_plane = jnp.zeros((n_dp, q_chip, EX_DEV), F32)
     for away in range(n_dp):
         part = y[:, away * EX_DEV:(away + 1) * EX_DEV]
@@ -518,15 +520,14 @@
         by_chip = lax.dynamic_update_slice(by_chip, part, (near_chip[k], 0, 0))
     scores = lax.dynamic_slice_in_dim(by_chip, core * n_half, n_half, 0)
 
-    out = None
+    outs = [None]
     for away in range(n_dp):
         if away:
-            own_x = shift(own_x, 1)
-            others_x = tie(others_x, (own_x, by_plane if away == 1 else scores))
-            others_x = shift(others_x, 1)
+            before = [[], [by_plane, outs[-2]], [scores, outs[-2]]][min(away - 1, 2)]
+            ring = shift(tie(ring, before) if before else ring, 1)
         where = jnp.stack([(i - away) % n_dp] + near_chip).astype(jnp.int32)
-        out = place(where, own_x, others_x, out, (per_slot, n_dp * n_c * q_chip))
-    return (out, scores.reshape((n_half * q_chip, EX_DEV)))
+        outs.append(place(where, ring, outs[-1], (per_slot, n_dp * n_c * q_chip)))
+    return (outs[-1], scores.reshape((n_half * q_chip, EX_DEV)))
 
 
 def solution(mesh):

time: 237 us -> 223 us (0.941)
  waiting for transfers between devices: 89.4 us -> 75.5 us
  starting transfers between devices: 49.3 us -> 52.2 us
    ppermute x12 -> x9, waiting for transfers between devices: 38.5 us -> 23.1 us  [shift(): lax.ppermute(values, 'dp', [(a, (a + by) % n_dp) for a in range(n_dp)])]
    ppermute x6, starting transfers between devices: 12.8 us -> 17.3 us  [send(): return lax.ppermute(values, ('dp', 'tensor'), pairs)]
    pallas_call x5, Pallas kernels: 6.44 us -> 10.9 us  [the longest x4 6.3 us: place(): pl.pallas_call(functools.partial(place_kernel, where.shape[0] - 1), out_s...]
    pallas_call x4, Pallas kernels: 37.7 us -> 34.2 us  [build(): pl.pallas_call(functools.partial(build_kernel, ranks, share, ex_block, le...]
    ppermute x6, waiting for transfers between devices: 13.6 us -> 16.7 us  [send(): return lax.ppermute(values, ('dp', 'tensor'), pairs)]
    ppermute x12 -> x9, starting transfers between devices: 7.32 us -> 5.54 us  [shift(): lax.ppermute(values, 'dp', [(a, (a + by) % n_dp) for a in range(n_dp)])]
  transfers between devices with their start and end apart: 60 -> 57, of which waited for: 24 -> 21; matrix products, arithmetic and copies ran while one was open for 2% -> 2% of each run, Pallas kernels for 21% -> 21%
where the time goes in v6:
time: 223 us
  Pallas kernels  89.1 us (40%)
  waiting for transfers between devices  75.5 us (34%)
  starting transfers between devices  52.2 us (23%)
  other arithmetic  2.92 us (1%)
    ppermute x42, waiting for transfers between devices, swap(): return lax.ppermute(values, 'tensor', [(a, a ^ mask) for a in range(n_t)])  35.8 us
    pallas_call x4, Pallas kernels, build(): pl.pallas_call(functools.partial(build_kernel, ranks, share, ex_block, le...  34.2 us
    ppermute x42, starting transfers between devices, swap(): return lax.ppermute(values, 'tensor', [(a, a ^ mask) for a in range(n_t)])  29.3 us
    pallas_call x3, Pallas kernels, one_step(): pl.pallas_call(functools.partial(step_kernel, first, planes, examples, co...  27.9 us
    ppermute x9, waiting for transfers between devices, shift(): lax.ppermute(values, 'dp', [(a, (a + by) % n_dp) for a in range(n_dp)])  23.1 us
    ppermute x6, starting transfers between devices, send(): return lax.ppermute(values, ('dp', 'tensor'), pairs)  17.3 us
    ppermute x6, waiting for transfers between devices, send(): return lax.ppermute(values, ('dp', 'tensor'), pairs)  16.7 us
    pallas_call x2, Pallas kernels, project(): pl.pallas_call(project_kernel, out_shape=jax.ShapeDtypeStruct((steps * bl...  15.6 us
  transfers between devices with their start and end apart: 57, of which 21 were waited for; matrix products, arithmetic and copies ran while one was open for 2% of the time, Pallas kernels for 21%

profile of v6, /device:TPU:0, one launch (start us, length us, event | category | flops | bytes accessed | tf_op | source)
XLA Modules:
  0.0 222.5 jit_solution(9299726781965428146)
XLA Ops:
  1.8 7.9 %shard_map.77 = f32[2048,128]{1,0:T(8,128)} custom-call(s32[4]{0:T(128)} %add_subtract_fusion.order_ref, bf16[4096,512]{1,0:T(8,128)(2,1)} %refs_3_.3, bf16[4096,512]{1,0:T(8,128)(2,1)} %refs_3_.3, bf16[4096,512]{1,0:T(8,128)(2,1)} %refs_3_.3, bf16[4096,512]{1,0:T(8,128)(2,1)} %refs_3_.3, bf16[4096,1792]{1,0:T(8,128)(2,1)} %refs_7_.3, ...), custom_call_target="tpu_custom_call" | custom-call | flops 9663676416 | bytes 9437184 | tf_op jit(solution)/shard_map/pallas_call | solution.py:58
  10.4 2.7 %collective-permute-start = (f32[40,128]{1,0:T(8,128)S(1)}, f32[40,128]{1,0:T(8,128)S(1)}, u32[]{:S(2)}, u32[]{:S(2)}) collective-permute-start(f32[40,128]{1,0:T(8,128)S(1)} %select_maximum_fusion), channel_id=1, source_target_pairs={{0,8},{8,16},{16,24},{24,0},{1,9},{9,17},{17,25},{25,1},{2,10},{10... | collective-permute-start | bytes 61448 | tf_op jit(solution)/shard_map/ppermute | solution.py:417
  13.0 2.1 collective-permute-start.2
  15.1 7.7 %shard_map.78 = f32[2048,128]{1,0:T(8,128)} custom-call(s32[4]{0:T(128)} %get-tuple-element.136.order_ref, bf16[4096,512]{1,0:T(8,128)(2,1)} %refs_3_.3, bf16[4096,512]{1,0:T(8,128)(2,1)} %refs_3_.3, bf16[4096,512]{1,0:T(8,128)(2,1)} %refs_3_.3, bf16[4096,512]{1,0:T(8,128)(2,1)} %refs_3_.3, bf16[4096,1792]{1,0:T(8,128)(2,1)} %refs_7_.3, ...), custom_call_target="tpu_custom_call" | custom-call | flops 9663676416 | bytes 9437184 | tf_op jit(solution)/shard_map/pallas_call | solution.py:58
  22.9 1.3 add.387
  24.3 1.7 collective-permute-start.4
  26.0 1.5 collective-permute-start.5
  28.0 5.5 %collective-permute-done.4 = f32[512,128]{1,0:T(8,128)S(1)} collective-permute-done((f32[512,128]{1,0:T(8,128)S(1)}, f32[512,128]{1,0:T(8,128)S(1)}, u32[]{:S(2)}, u32[]{:S(2)}) %collective-permute-start.4) | collective-permute-done | bytes 262176 | tf_op jit(solution)/shard_map/ppermute | solution.py:414
  33.5 6.1 %collective-permute-done.5 = f32[512,128]{1,0:T(8,128)S(1)} collective-permute-done((f32[512,128]{1,0:T(8,128)S(1)}, f32[512,128]{1,0:T(8,128)S(1)}, u32[]{:S(2)}, u32[]{:S(2)}) %collective-permute-start.5) | collective-permute-done | bytes 262176 | tf_op jit(solution)/shard_map/ppermute | solution.py:414
  39.6 1.3 collective-permute-start.7
  40.9 0.8 collective-permute-start.8
  41.8 1.4 collective-permute-start.9
  43.4 0.7 collective-permute-start.1
  44.1 4.0 %collective-permute-done.1 = f32[40,128]{1,0:T(8,128)S(1)} collective-permute-done((f32[40,128]{1,0:T(8,128)S(1)}, f32[40,128]{1,0:T(8,128)S(1)}, u32[]{:S(2)}, u32[]{:S(2)}) %collective-permute-start.1) | collective-permute-done | bytes 20512 | tf_op jit(solution)/shard_map/ppermute | solution.py:417
  48.1 0.8 collective-permute-done.7.refs_3_
  49.0 4.7 %collective-permute-done.8.refs_4_ = f32[512,128]{1,0:T(8,128)S(1)} collective-permute-done((f32[512,128]{1,0:T(8,128)S(1)}, f32[512,128]{1,0:T(8,128)S(1)}, u32[]{:S(2)}, u32[]{:S(2)}) %collective-permute-start.8) | collective-permute-done | bytes 262176 | tf_op jit(solution)/shard_map/ppermute | solution.py:414
  54.2 2.1 collective-permute-done.14.refs_2_
  56.3 1.2 collective-permute-start.15
  57.5 0.8 collective-permute-start.16
  58.3 1.4 collective-permute-start.17
  59.8 8.5 %shard_map.79 = (bf16[512,2048]{1,0:T(8,128)(2,1)S(1)}, bf16[512,2048]{1,0:T(8,128)(2,1)S(1)}, f32[8,128]{1,0:T(8,128)S(1)}) custom-call(s32[8]{0:T(128)S(1)} %stack.195.refs_0_, s32[64]{0:T(128)S(1)} %convert_bitcast_fusion.refs_1_, f32[512,128]{1,0:T(8,128)S(1)} %fusion.1.refs_2_, f32[512,128]{1,0:T(8,128)S(1)} %collective-permute-done.7.refs_3_, ...), custom_call_target="tpu_custom_call" | custom-call | flops 12884901888 | bytes 6291456 | tf_op jit(solution)/shard_map/pallas_call | solution.py:171
  69.5 1.4 collective-permute-start.23
  71.6 1.4 collective-permute-start.25
  73.0 8.6 %shard_map.80 = (bf16[512,2048]{1,0:T(8,128)(2,1)S(1)}, bf16[512,2048]{1,0:T(8,128)(2,1)S(1)}, f32[8,128]{1,0:T(8,128)S(1)}) custom-call(s32[8]{0:T(128)S(1)} %stack.195.refs_0_, s32[64]{0:T(128)S(1)} %fusion.5.refs_1_, f32[512,128]{1,0:T(8,128)S(1)} %collective-permute-done.14.refs_2_, f32[512,128]{1,0:T(8,128)S(1)} %collective-permute-done.15.refs_3_, ...), custom_call_target="tpu_custom_call" | custom-call | flops 12884901888 | bytes 6291456 | tf_op jit(solution)/shard_map/pallas_call | solution.py:171
  81.6 2.9 %collective-permute-done.24.refs_4_ = f32[512,128]{1,0:T(8,128)S(1)} collective-permute-done((f32[512,128]{1,0:T(8,128)S(1)}, f32[512,128]{1,0:T(8,128)S(1)}, u32[]{:S(2)}, u32[]{:S(2)}) %collective-permute-start.24) | collective-permute-done | bytes 262176 | tf_op jit(solution)/shard_map/ppermute | solution.py:414
  85.5 0.9 collective-permute-start.31
  86.4 1.2 collective-permute-start.32
  87.7 1.3 collective-permute-start.33
  89.0 8.5 %shard_map.81 = (bf16[512,2048]{1,0:T(8,128)(2,1)S(1)}, bf16[512,2048]{1,0:T(8,128)(2,1)S(1)}, f32[8,128]{1,0:T(8,128)S(1)}) custom-call(s32[8]{0:T(128)S(1)} %stack.195.refs_0_, s32[64]{0:T(128)S(1)} %fusion.4.refs_1_, f32[512,128]{1,0:T(8,128)S(1)} %collective-permute-done.22.refs_2_, f32[512,128]{1,0:T(8,128)S(1)} %collective-permute-done.23.refs_3_, ...), custom_call_target="tpu_custom_call" | custom-call | flops 12884901888 | bytes 6291456 | tf_op jit(solution)/shard_map/pallas_call | solution.py:171
  97.6 2.4 %collective-permute-done.32.refs_4_ = f32[512,128]{1,0:T(8,128)S(1)} collective-permute-done((f32[512,128]{1,0:T(8,128)S(1)}, f32[512,128]{1,0:T(8,128)S(1)}, u32[]{:S(2)}, u32[]{:S(2)}) %collective-permute-start.32) | collective-permute-done | bytes 262176 | tf_op jit(solution)/shard_map/ppermute | solution.py:414
  101.0 1.1 collective-permute-start.38
  102.1 1.0 collective-permute-start.39
  103.2 1.3 collective-permute-start.40
  104.5 8.5 %shard_map.82 = (bf16[512,2048]{1,0:T(8,128)(2,1)S(1)}, bf16[512,2048]{1,0:T(8,128)(2,1)S(1)}, f32[8,128]{1,0:T(8,128)S(1)}) custom-call(s32[8]{0:T(128)S(1)} %stack.195.refs_0_, s32[64]{0:T(128)S(1)} %fusion.3.refs_1_, f32[512,128]{1,0:T(8,128)S(1)} %collective-permute-done.30.refs_2_, f32[512,128]{1,0:T(8,128)S(1)} %collective-permute-done.31.refs_3_, ...), custom_call_target="tpu_custom_call" | custom-call | flops 12884901888 | bytes 6291456 | tf_op jit(solution)/shard_map/pallas_call | solution.py:171
  113.1 4.6 %shard_map.83 = (f32[64,2176]{1,0:T(8,128)S(1)}, f32[64,2048]{1,0:T(8,128)S(1)}) custom-call(bf16[512,2048]{1,0:T(8,128)(2,1)S(1)} %get-tuple-element.74.refs_0_.refs_3_.refs_8_, bf16[512,2048]{1,0:T(8,128)(2,1)S(1)} %get-tuple-element.82.refs_1_.refs_4_.refs_9_, bf16[512,2048]{1,0:T(8,128)(2,1)S(1)} %get-tuple-element.90.refs_2_.refs_5_.refs_10_, ...), custom_call_target="tpu_custom_call" | custom-call | flops 1610612736 | bytes 16777216 | tf_op jit(solution)/shard_map/pallas_call | solution.py:227
  117.8 1.9 collective-permute-done.41.refs_1_
  119.7 9.2 %shard_map.84 = (f32[64,2176]{1,0:T(8,128)S(1)}, f32[64,2048]{1,0:T(8,128)S(1)}, f32[64,2048]{1,0:T(8,128)S(1)}, f32[64,2048]{1,0:T(8,128)S(1)}, f32[64,2048]{1,...) custom-call(f32[64,2176]{1,0:T(8,128)S(1)} %get-tuple-element.108.refs_0_, ...), custom_call_target="tpu_custom_call" | custom-call | flops 3221225472 | bytes 16777216 | tf_op jit(solution)/shard_map/pallas_call | solution.py:338
  129.1 1.8 collective-permute-done.42.refs_1_
  131.0 9.5 %shard_map.85 = (f32[64,2176]{1,0:T(8,128)S(1)}, f32[64,2048]{1,0:T(8,128)S(1)}, f32[64,2048]{1,0:T(8,128)S(1)}, f32[64,2048]{1,0:T(8,128)S(1)}, f32[64,2048]{1,...) custom-call(f32[64,2176]{1,0:T(8,128)S(1)} %get-tuple-element.110.refs_0_, ...), custom_call_target="tpu_custom_call" | custom-call | flops 3221225472 | bytes 16777216 | tf_op jit(solution)/shard_map/pallas_call | solution.py:338
  140.7 1.8 collective-permute-done.43.refs_1_
  142.5 9.3 %shard_map.86 = (f32[64,2176]{1,0:T(8,128)S(1)}, f32[64,2048]{1,0:T(8,128)S(1)}, f32[64,2048]{1,0:T(8,128)S(1)}, f32[64,2048]{1,0:T(8,128)S(1)}, f32[64,2048]{1,...) custom-call(f32[64,2176]{1,0:T(8,128)S(1)} %get-tuple-element.117.refs_0_, ...), custom_call_target="tpu_custom_call" | custom-call | flops 3221225472 | bytes 16777216 | tf_op jit(solution)/shard_map/pallas_call | solution.py:338
  152.0 1.8 collective-permute-done.44.other_ref
  154.3 1.2 collective-permute-start.45
  155.5 1.0 collective-permute-start.46
  156.5 1.3 collective-permute-start.47
  157.9 2.8 %collective-permute-done.45 = f32[64,512]{1,0:T(8,128)S(1)} collective-permute-done((f32[64,512]{1,0:T(8,128)S(1)}, f32[64,512]{1,0:T(8,128)S(1)}, u32[]{:S(2)}, u32[]{:S(2)}) %collective-permute-start.45) | collective-permute-done | bytes 131104 | tf_op jit(solution)/shard_map/ppermute | solution.py:414
  160.7 2.9 %collective-permute-done.46 = f32[64,512]{1,0:T(8,128)S(1)} collective-permute-done((f32[64,512]{1,0:T(8,128)S(1)}, f32[64,512]{1,0:T(8,128)S(1)}, u32[]{:S(2)}, u32[]{:S(2)}) %collective-permute-start.46) | collective-permute-done | bytes 131104 | tf_op jit(solution)/shard_map/ppermute | solution.py:414
  163.7 5.7 %collective-permute-start.49 = (f32[64,512]{1,0:T(8,128)S(1)}, f32[64,512]{1,0:T(8,128)S(1)}, u32[]{:S(2)}, u32[]{:S(2)}) collective-permute-start(f32[64,512]{1,0:T(8,128)S(1)} %get-tuple-element.147), channel_id=1, source_target_pairs={{0,24},{2,26},{5,29},{7,31},{8,0},{10,2},{13,5},{15,7},{16,8},{18,... | collective-permute-start | bytes 393224 | tf_op jit(solution)/shard_map/ppermute | solution.py:504
  169.4 2.3 %collective-permute-start.50 = (f32[64,512]{1,0:T(8,128)S(1)}, f32[64,512]{1,0:T(8,128)S(1)}, u32[]{:S(2)}, u32[]{:S(2)}) collective-permute-start(f32[64,512]{1,0:T(8,128)S(1)} %get-tuple-element.146), channel_id=1, source_target_pairs={{0,16},{2,18},{5,21},{7,23},{8,24},{10,26},{13,29},{15,31},{16,0},... | collective-permute-start | bytes 393224 | tf_op jit(solution)/shard_map/ppermute | solution.py:504
  171.7 3.9 %collective-permute-start.51 = (f32[64,512]{1,0:T(8,128)S(1)}, f32[64,512]{1,0:T(8,128)S(1)}, u32[]{:S(2)}, u32[]{:S(2)}) collective-permute-start(f32[64,512]{1,0:T(8,128)S(1)} %get-tuple-element.145), channel_id=1, source_target_pairs={{0,8},{2,10},{5,13},{7,15},{8,16},{10,18},{13,21},{15,23},{16,24},... | collective-permute-start | bytes 393224 | tf_op jit(solution)/shard_map/ppermute | solution.py:504
  175.7 4.4 %collective-permute-done.49 = f32[64,512]{1,0:T(8,128)S(1)} collective-permute-done((f32[64,512]{1,0:T(8,128)S(1)}, f32[64,512]{1,0:T(8,128)S(1)}, u32[]{:S(2)}, u32[]{:S(2)}) %collective-permute-start.49) | collective-permute-done | bytes 131104 | tf_op jit(solution)/shard_map/ppermute | solution.py:504
  180.1 9.9 %collective-permute-done.50 = f32[64,512]{1,0:T(8,128)S(1)} collective-permute-done((f32[64,512]{1,0:T(8,128)S(1)}, f32[64,512]{1,0:T(8,128)S(1)}, u32[]{:S(2)}, u32[]{:S(2)}) %collective-permute-start.50) | collective-permute-done | bytes 131104 | tf_op jit(solution)/shard_map/ppermute | solution.py:504
  190.1 2.8 %collective-permute-start.53 = (f32[1,64,512]{2,1,0:T(8,128)S(1)}, f32[1,64,512]{2,1,0:T(8,128)S(1)}, u32[]{:S(2)}, u32[]{:S(2)}) collective-permute-start(f32[1,64,512]{2,1,0:T(8,128)S(1)} %get-tuple-element.143), channel_id=1, source_target_pairs={{0,2},{2,0},{5,7},{7,5},{8,10},{10,8},{13,15},{15,13},{16,18},{18,... | collective-permute-start | bytes 393224 | tf_op jit(solution)/shard_map/ppermute | solution.py:504
  193.1 1.6 shard_map.88.refs_0_
  194.6 1.3 collective-permute-start.54
  196.1 1.3 collective-permute-start.55
  197.4 1.1 collective-permute-done.54
  198.5 1.4 collective-permute-done.55
  199.9 0.7 constant_dynamic-slice_fusion
  200.6 1.6 shard_map.89.refs_0_
  202.2 7.8 %collective-permute-done.52.part_ref = f32[256,512]{1,0:T(8,128)S(1)} collective-permute-done((f32[256,512]{1,0:T(8,128)S(1)}, f32[256,512]{1,0:T(8,128)S(1)}, u32[]{:S(2)}, u32[]{:S(2)}) %collective-permute-start.52) | collective-permute-done | bytes 524320 | tf_op jit(solution)/shard_map/ppermute | solution.py:417
  210.1 1.6 shard_map.90.refs_0_
  211.7 9.2 %collective-permute-done.56.part_ref = f32[256,512]{1,0:T(8,128)S(1)} collective-permute-done((f32[256,512]{1,0:T(8,128)S(1)}, f32[256,512]{1,0:T(8,128)S(1)}, u32[]{:S(2)}, u32[]{:S(2)}) %collective-permute-start.56) | collective-permute-done | bytes 524320 | tf_op jit(solution)/shard_map/ppermute | solution.py:417
  220.9 1.6 shard_map.91
  (109 shorter events, 9.0 us)
Async XLA Ops:
  1.8 8.3 %copy-start.1 = (s32[1,4096]{1,0:T(1,128)S(1)}, s32[1,4096]{1,0:T(1,128)}, u32[]{:S(2)}) copy-start(s32[1,4096]{1,0:T(1,128)} %param.10) | copy-start | bytes 49156
  9.6 13.2 %collective-permute-start.3 = (f32[2048,128]{1,0:T(8,128)}, f32[2048,128]{1,0:T(8,128)S(1)}, u32[]{:S(2)}, u32[]{:S(2)}) collective-permute-start(f32[2048,128]{1,0:T(8,128)} %shard_map.77), channel_id=1, source_target_pairs={{0,1},{1,0},{2,3},{3,2},{4,5},{5,4},{6,7},{7,6},{8,9},{9,8},{10,11... | collective-permute-start | bytes 3145736 | tf_op jit(solution)/shard_map/ppermute | solution.py:414
  10.4 33.7 %collective-permute-start = (f32[40,128]{1,0:T(8,128)S(1)}, f32[40,128]{1,0:T(8,128)S(1)}, u32[]{:S(2)}, u32[]{:S(2)}) collective-permute-start(f32[40,128]{1,0:T(8,128)S(1)} %select_maximum_fusion), channel_id=1, source_target_pairs={{0,8},{8,16},{16,24},{24,0},{1,9},{9,17},{17,25},{25,1},{2,10},{10... | collective-permute-start | bytes 61448 | tf_op jit(solution)/shard_map/ppermute | solution.py:417
  13.0 30.3 %collective-permute-start.2 = (f32[40,128]{1,0:T(8,128)S(1)}, f32[40,128]{1,0:T(8,128)S(1)}, u32[]{:S(2)}, u32[]{:S(2)}) collective-permute-start(f32[40,128]{1,0:T(8,128)S(1)} %select_maximum_fusion), channel_id=1, source_target_pairs={{0,24},{8,0},{16,8},{24,16},{1,25},{9,1},{17,9},{25,17},{2,26},{10... | collective-permute-start | bytes 61448 | tf_op jit(solution)/shard_map/ppermute | solution.py:417
  24.2 19.0 %copy-start = (f32[256,512]{1,0:T(8,128)S(1)}, f32[256,512]{1,0:T(8,128)}, u32[]{:S(2)}) copy-start(f32[256,512]{1,0:T(8,128)} %param.11) | copy-start | bytes 1572868
  24.3 9.2 %collective-permute-start.4 = (f32[512,128]{1,0:T(8,128)S(1)}, f32[512,128]{1,0:T(8,128)S(1)}, u32[]{:S(2)}, u32[]{:S(2)}) collective-permute-start(f32[512,128]{1,0:T(8,128)S(1)} %get-tuple-element.138), channel_id=1, source_target_pairs={{0,2},{1,3},{2,0},{3,1},{4,6},{5,7},{6,4},{7,5},{8,10},{9,11},{10,... | collective-permute-start | bytes 786440 | tf_op jit(solution)/shard_map/ppermute | solution.py:414
  26.0 13.6 %collective-permute-start.5 = (f32[512,128]{1,0:T(8,128)S(1)}, f32[512,128]{1,0:T(8,128)S(1)}, u32[]{:S(2)}, u32[]{:S(2)}) collective-permute-start(f32[512,128]{1,0:T(8,128)S(1)} %get-tuple-element.140), channel_id=1, source_target_pairs={{0,4},{1,5},{2,6},{3,7},{4,0},{5,1},{6,2},{7,3},{8,12},{9,13},{10,... | collective-permute-start | bytes 786440 | tf_op jit(solution)/shard_map/ppermute | solution.py:414
  27.5 12.1 %collective-permute-start.6 = (f32[512,128]{1,0:T(8,128)S(1)}, f32[512,128]{1,0:T(8,128)S(1)}, u32[]{:S(2)}, u32[]{:S(2)}) collective-permute-start(f32[512,128]{1,0:T(8,128)S(1)} %get-tuple-element.139), channel_id=1, source_target_pairs={{0,6},{1,7},{2,4},{3,5},{4,2},{5,3},{6,0},{7,1},{8,14},{9,15},{10,... | collective-permute-start | bytes 786440 | tf_op jit(solution)/shard_map/ppermute | solution.py:414
  39.6 9.3 %collective-permute-start.7 = (f32[512,128]{1,0:T(8,128)S(1)}, f32[512,128]{1,0:T(8,128)S(1)}, u32[]{:S(2)}, u32[]{:S(2)}) collective-permute-start(f32[512,128]{1,0:T(8,128)S(1)} %fusion.1.refs_2_), channel_id=1, source_target_pairs={{0,2},{1,3},{2,0},{3,1},{4,6},{5,7},{6,4},{7,5},{8,10},{9,11},{10,... | collective-permute-start | bytes 786440 | tf_op jit(solution)/shard_map/ppermute | solution.py:414
  40.9 12.7 %collective-permute-start.8 = (f32[512,128]{1,0:T(8,128)S(1)}, f32[512,128]{1,0:T(8,128)S(1)}, u32[]{:S(2)}, u32[]{:S(2)}) collective-permute-start(f32[512,128]{1,0:T(8,128)S(1)} %fusion.1.refs_2_), channel_id=1, source_target_pairs={{0,4},{1,5},{2,6},{3,7},{4,0},{5,1},{6,2},{7,3},{8,12},{9,13},{10,... | collective-permute-start | bytes 786440 | tf_op jit(solution)/shard_map/ppermute | solution.py:414
  41.8 11.9 %collective-permute-start.9 = (f32[512,128]{1,0:T(8,128)S(1)}, f32[512,128]{1,0:T(8,128)S(1)}, u32[]{:S(2)}, u32[]{:S(2)}) collective-permute-start(f32[512,128]{1,0:T(8,128)S(1)} %fusion.1.refs_2_), channel_id=1, source_target_pairs={{0,6},{1,7},{2,4},{3,5},{4,2},{5,3},{6,0},{7,1},{8,14},{9,15},{10,... | collective-permute-start | bytes 786440 | tf_op jit(solution)/shard_map/ppermute | solution.py:414
  43.4 4.7 %collective-permute-start.1 = (f32[40,128]{1,0:T(8,128)S(1)}, f32[40,128]{1,0:T(8,128)S(1)}, u32[]{:S(2)}, u32[]{:S(2)}) collective-permute-start(f32[40,128]{1,0:T(8,128)S(1)} %select_maximum_fusion), channel_id=1, source_target_pairs={{0,16},{8,24},{16,0},{24,8},{1,17},{9,25},{17,1},{25,9},{2,18},{10... | collective-permute-start | bytes 61448 | tf_op jit(solution)/shard_map/ppermute | solution.py:417
  44.1 13.4 %collective-permute-start.10 = (f32[512,128]{1,0:T(8,128)S(1)}, f32[512,128]{1,0:T(8,128)S(1)}, u32[]{:S(2)}, u32[]{:S(2)}) collective-permute-start(f32[512,128]{1,0:T(8,128)S(1)} %fusion.1.refs_2_), channel_id=1, source_target_pairs={{0,1},{1,0},{2,3},{3,2},{4,5},{5,4},{6,7},{7,6},{8,9},{9,8},{10,11... | collective-permute-start | bytes 786440 | tf_op jit(solution)/shard_map/ppermute | solution.py:414
  48.1 8.2 %collective-permute-start.14 = (f32[512,128]{1,0:T(8,128)S(1)}, f32[512,128]{1,0:T(8,128)S(1)}, u32[]{:S(2)}, u32[]{:S(2)}) collective-permute-start(f32[512,128]{1,0:T(8,128)S(1)} %fusion.1.refs_2_), channel_id=1, source_target_pairs={{0,8},{8,16},{16,24},{24,0},{1,9},{9,17},{17,25},{25,1},{2,10},{10... | collective-permute-start | bytes 786440 | tf_op jit(solution)/shard_map/ppermute | solution.py:417
  49.0 9.4 %collective-permute-start.11 = (f32[512,128]{1,0:T(8,128)S(1)}, f32[512,128]{1,0:T(8,128)S(1)}, u32[]{:S(2)}, u32[]{:S(2)}) collective-permute-start(f32[512,128]{1,0:T(8,128)S(1)} %collective-permute-done.7.refs_3_), channel_id=1, source_target_pairs={{0,1},{1,0},{2,3},{3,2},{4,5},{5,4},{6,7},{7,6},{8,9},{9,8},{10,11... | collective-permute-start | bytes 786440 | tf_op jit(solution)/shard_map/ppermute | solution.py:414
  53.7 6.1 %collective-permute-start.12 = (f32[512,128]{1,0:T(8,128)S(1)}, f32[512,128]{1,0:T(8,128)S(1)}, u32[]{:S(2)}, u32[]{:S(2)}) collective-permute-start(f32[512,128]{1,0:T(8,128)S(1)} %collective-permute-done.8.refs_4_), channel_id=1, source_target_pairs={{0,1},{1,0},{2,3},{3,2},{4,5},{5,4},{6,7},{7,6},{8,9},{9,8},{10,11... | collective-permute-start | bytes 786440 | tf_op jit(solution)/shard_map/ppermute | solution.py:414
  53.7 6.1 %collective-permute-start.13 = (f32[512,128]{1,0:T(8,128)S(1)}, f32[512,128]{1,0:T(8,128)S(1)}, u32[]{:S(2)}, u32[]{:S(2)}) collective-permute-start(f32[512,128]{1,0:T(8,128)S(1)} %collective-permute-done.9.refs_5_), channel_id=1, source_target_pairs={{0,1},{1,0},{2,3},{3,2},{4,5},{5,4},{6,7},{7,6},{8,9},{9,8},{10,11... | collective-permute-start | bytes 786440 | tf_op jit(solution)/shard_map/ppermute | solution.py:414
  56.3 12.1 %collective-permute-start.15 = (f32[512,128]{1,0:T(8,128)S(1)}, f32[512,128]{1,0:T(8,128)S(1)}, u32[]{:S(2)}, u32[]{:S(2)}) collective-permute-start(f32[512,128]{1,0:T(8,128)S(1)} %collective-permute-done.14.refs_2_), channel_id=1, source_target_pairs={{0,2},{1,3},{2,0},{3,1},{4,6},{5,7},{6,4},{7,5},{8,10},{9,11},{10,... | collective-permute-start | bytes 786440 | tf_op jit(solution)/shard_map/ppermute | solution.py:414
  57.5 10.9 %collective-permute-start.16 = (f32[512,128]{1,0:T(8,128)S(1)}, f32[512,128]{1,0:T(8,128)S(1)}, u32[]{:S(2)}, u32[]{:S(2)}) collective-permute-start(f32[512,128]{1,0:T(8,128)S(1)} %collective-permute-done.14.refs_2_), channel_id=1, source_target_pairs={{0,4},{1,5},{2,6},{3,7},{4,0},{5,1},{6,2},{7,3},{8,12},{9,13},{10,... | collective-permute-start | bytes 786440 | tf_op jit(solution)/shard_map/ppermute | solution.py:414
  58.3 10.1 %collective-permute-start.17 = (f32[512,128]{1,0:T(8,128)S(1)}, f32[512,128]{1,0:T(8,128)S(1)}, u32[]{:S(2)}, u32[]{:S(2)}) collective-permute-start(f32[512,128]{1,0:T(8,128)S(1)} %collective-permute-done.14.refs_2_), channel_id=1, source_target_pairs={{0,6},{1,7},{2,4},{3,5},{4,2},{5,3},{6,0},{7,1},{8,14},{9,15},{10,... | collective-permute-start | bytes 786440 | tf_op jit(solution)/shard_map/ppermute | solution.py:414
  59.8 9.7 %collective-permute-start.22 = (f32[512,128]{1,0:T(8,128)S(1)}, f32[512,128]{1,0:T(8,128)S(1)}, u32[]{:S(2)}, u32[]{:S(2)}) collective-permute-start(f32[512,128]{1,0:T(8,128)S(1)} %collective-permute-done.14.refs_2_), channel_id=1, source_target_pairs={{0,8},{8,16},{16,24},{24,0},{1,9},{9,17},{17,25},{25,1},{2,10},{10... | collective-permute-start | bytes 786440 | tf_op jit(solution)/shard_map/ppermute | solution.py:417
  68.5 2.5 %collective-permute-start.18 = (f32[512,128]{1,0:T(8,128)S(1)}, f32[512,128]{1,0:T(8,128)S(1)}, u32[]{:S(2)}, u32[]{:S(2)}) collective-permute-start(f32[512,128]{1,0:T(8,128)S(1)} %collective-permute-done.14.refs_2_), channel_id=1, source_target_pairs={{0,1},{1,0},{2,3},{3,2},{4,5},{5,4},{6,7},{7,6},{8,9},{9,8},{10,11... | collective-permute-start | bytes 786440 | tf_op jit(solution)/shard_map/ppermute | solution.py:414
  68.5 3.2 %collective-permute-start.19 = (f32[512,128]{1,0:T(8,128)S(1)}, f32[512,128]{1,0:T(8,128)S(1)}, u32[]{:S(2)}, u32[]{:S(2)}) collective-permute-start(f32[512,128]{1,0:T(8,128)S(1)} %collective-permute-done.15.refs_3_), channel_id=1, source_target_pairs={{0,1},{1,0},{2,3},{3,2},{4,5},{5,4},{6,7},{7,6},{8,9},{9,8},{10,11... | collective-permute-start | bytes 786440 | tf_op jit(solution)/shard_map/ppermute | solution.py:414
  69.0 4.0 %collective-permute-start.20 = (f32[512,128]{1,0:T(8,128)S(1)}, f32[512,128]{1,0:T(8,128)S(1)}, u32[]{:S(2)}, u32[]{:S(2)}) collective-permute-start(f32[512,128]{1,0:T(8,128)S(1)} %collective-permute-done.16.refs_4_), channel_id=1, source_target_pairs={{0,1},{1,0},{2,3},{3,2},{4,5},{5,4},{6,7},{7,6},{8,9},{9,8},{10,11... | collective-permute-start | bytes 786440 | tf_op jit(solution)/shard_map/ppermute | solution.py:414
  69.0 4.0 %collective-permute-start.21 = (f32[512,128]{1,0:T(8,128)S(1)}, f32[512,128]{1,0:T(8,128)S(1)}, u32[]{:S(2)}, u32[]{:S(2)}) collective-permute-start(f32[512,128]{1,0:T(8,128)S(1)} %collective-permute-done.17.refs_5_), channel_id=1, source_target_pairs={{0,1},{1,0},{2,3},{3,2},{4,5},{5,4},{6,7},{7,6},{8,9},{9,8},{10,11... | collective-permute-start | bytes 786440 | tf_op jit(solution)/shard_map/ppermute | solution.py:414
  69.5 12.1 %collective-permute-start.23 = (f32[512,128]{1,0:T(8,128)S(1)}, f32[512,128]{1,0:T(8,128)S(1)}, u32[]{:S(2)}, u32[]{:S(2)}) collective-permute-start(f32[512,128]{1,0:T(8,128)S(1)} %collective-permute-done.22.refs_2_), channel_id=1, source_target_pairs={{0,2},{1,3},{2,0},{3,1},{4,6},{5,7},{6,4},{7,5},{8,10},{9,11},{10,... | collective-permute-start | bytes 786440 | tf_op jit(solution)/shard_map/ppermute | solution.py:414
  70.9 13.6 %collective-permute-start.24 = (f32[512,128]{1,0:T(8,128)S(1)}, f32[512,128]{1,0:T(8,128)S(1)}, u32[]{:S(2)}, u32[]{:S(2)}) collective-permute-start(f32[512,128]{1,0:T(8,128)S(1)} %collective-permute-done.22.refs_2_), channel_id=1, source_target_pairs={{0,4},{1,5},{2,6},{3,7},{4,0},{5,1},{6,2},{7,3},{8,12},{9,13},{10,... | collective-permute-start | bytes 786440 | tf_op jit(solution)/shard_map/ppermute | solution.py:414
  71.6 12.9 %collective-permute-start.25 = (f32[512,128]{1,0:T(8,128)S(1)}, f32[512,128]{1,0:T(8,128)S(1)}, u32[]{:S(2)}, u32[]{:S(2)}) collective-permute-start(f32[512,128]{1,0:T(8,128)S(1)} %collective-permute-done.22.refs_2_), channel_id=1, source_target_pairs={{0,6},{1,7},{2,4},{3,5},{4,2},{5,3},{6,0},{7,1},{8,14},{9,15},{10,... | collective-permute-start | bytes 786440 | tf_op jit(solution)/shard_map/ppermute | solution.py:414
  73.0 12.5 %collective-permute-start.30 = (f32[512,128]{1,0:T(8,128)S(1)}, f32[512,128]{1,0:T(8,128)S(1)}, u32[]{:S(2)}, u32[]{:S(2)}) collective-permute-start(f32[512,128]{1,0:T(8,128)S(1)} %collective-permute-done.22.refs_2_), channel_id=1, source_target_pairs={{0,8},{8,16},{16,24},{24,0},{1,9},{9,17},{17,25},{25,1},{2,10},{10... | collective-permute-start | bytes 786440 | tf_op jit(solution)/shard_map/ppermute | solution.py:417
  84.5 1.9 collective-permute-start.26
  84.5 3.2 %collective-permute-start.27 = (f32[512,128]{1,0:T(8,128)S(1)}, f32[512,128]{1,0:T(8,128)S(1)}, u32[]{:S(2)}, u32[]{:S(2)}) collective-permute-start(f32[512,128]{1,0:T(8,128)S(1)} %collective-permute-done.23.refs_3_), channel_id=1, source_target_pairs={{0,1},{1,0},{2,3},{3,2},{4,5},{5,4},{6,7},{7,6},{8,9},{9,8},{10,11... | collective-permute-start | bytes 786440 | tf_op jit(solution)/shard_map/ppermute | solution.py:414
  85.0 4.0 %collective-permute-start.28 = (f32[512,128]{1,0:T(8,128)S(1)}, f32[512,128]{1,0:T(8,128)S(1)}, u32[]{:S(2)}, u32[]{:S(2)}) collective-permute-start(f32[512,128]{1,0:T(8,128)S(1)} %collective-permute-done.24.refs_4_), channel_id=1, source_target_pairs={{0,1},{1,0},{2,3},{3,2},{4,5},{5,4},{6,7},{7,6},{8,9},{9,8},{10,11... | collective-permute-start | bytes 786440 | tf_op jit(solution)/shard_map/ppermute | solution.py:414
  85.0 4.0 %collective-permute-start.29 = (f32[512,128]{1,0:T(8,128)S(1)}, f32[512,128]{1,0:T(8,128)S(1)}, u32[]{:S(2)}, u32[]{:S(2)}) collective-permute-start(f32[512,128]{1,0:T(8,128)S(1)} %collective-permute-done.25.refs_5_), channel_id=1, source_target_pairs={{0,1},{1,0},{2,3},{3,2},{4,5},{5,4},{6,7},{7,6},{8,9},{9,8},{10,11... | collective-permute-start | bytes 786440 | tf_op jit(solution)/shard_map/ppermute | solution.py:414
  85.5 12.0 %collective-permute-start.31 = (f32[512,128]{1,0:T(8,128)S(1)}, f32[512,128]{1,0:T(8,128)S(1)}, u32[]{:S(2)}, u32[]{:S(2)}) collective-permute-start(f32[512,128]{1,0:T(8,128)S(1)} %collective-permute-done.30.refs_2_), channel_id=1, source_target_pairs={{0,2},{1,3},{2,0},{3,1},{4,6},{5,7},{6,4},{7,5},{8,10},{9,11},{10,... | collective-permute-start | bytes 786440 | tf_op jit(solution)/shard_map/ppermute | solution.py:414
  86.4 13.6 %collective-permute-start.32 = (f32[512,128]{1,0:T(8,128)S(1)}, f32[512,128]{1,0:T(8,128)S(1)}, u32[]{:S(2)}, u32[]{:S(2)}) collective-permute-start(f32[512,128]{1,0:T(8,128)S(1)} %collective-permute-done.30.refs_2_), channel_id=1, source_target_pairs={{0,4},{1,5},{2,6},{3,7},{4,0},{5,1},{6,2},{7,3},{8,12},{9,13},{10,... | collective-permute-start | bytes 786440 | tf_op jit(solution)/shard_map/ppermute | solution.py:414
  87.7 12.3 %collective-permute-start.33 = (f32[512,128]{1,0:T(8,128)S(1)}, f32[512,128]{1,0:T(8,128)S(1)}, u32[]{:S(2)}, u32[]{:S(2)}) collective-permute-start(f32[512,128]{1,0:T(8,128)S(1)} %collective-permute-done.30.refs_2_), channel_id=1, source_target_pairs={{0,6},{1,7},{2,4},{3,5},{4,2},{5,3},{6,0},{7,1},{8,14},{9,15},{10,... | collective-permute-start | bytes 786440 | tf_op jit(solution)/shard_map/ppermute | solution.py:414
  100.0 2.1 collective-permute-start.34
  100.0 3.2 %collective-permute-start.35 = (f32[512,128]{1,0:T(8,128)S(1)}, f32[512,128]{1,0:T(8,128)S(1)}, u32[]{:S(2)}, u32[]{:S(2)}) collective-permute-start(f32[512,128]{1,0:T(8,128)S(1)} %collective-permute-done.31.refs_3_), channel_id=1, source_target_pairs={{0,1},{1,0},{2,3},{3,2},{4,5},{5,4},{6,7},{7,6},{8,9},{9,8},{10,11... | collective-permute-start | bytes 786440 | tf_op jit(solution)/shard_map/ppermute | solution.py:414
  100.5 4.0 %collective-permute-start.36 = (f32[512,128]{1,0:T(8,128)S(1)}, f32[512,128]{1,0:T(8,128)S(1)}, u32[]{:S(2)}, u32[]{:S(2)}) collective-permute-start(f32[512,128]{1,0:T(8,128)S(1)} %collective-permute-done.32.refs_4_), channel_id=1, source_target_pairs={{0,1},{1,0},{2,3},{3,2},{4,5},{5,4},{6,7},{7,6},{8,9},{9,8},{10,11... | collective-permute-start | bytes 786440 | tf_op jit(solution)/shard_map/ppermute | solution.py:414
  100.5 4.0 %collective-permute-start.37 = (f32[512,128]{1,0:T(8,128)S(1)}, f32[512,128]{1,0:T(8,128)S(1)}, u32[]{:S(2)}, u32[]{:S(2)}) collective-permute-start(f32[512,128]{1,0:T(8,128)S(1)} %collective-permute-done.33.refs_5_), channel_id=1, source_target_pairs={{0,1},{1,0},{2,3},{3,2},{4,5},{5,4},{6,7},{7,6},{8,9},{9,8},{10,11... | collective-permute-start | bytes 786440 | tf_op jit(solution)/shard_map/ppermute | solution.py:414
  101.0 12.1 %collective-permute-start.38 = (f32[64,512]{1,0:T(8,128)S(1)}, f32[64,512]{1,0:T(8,128)S(1)}, u32[]{:S(2)}, u32[]{:S(2)}) collective-permute-start(f32[64,512]{1,0:T(8,128)S(1)} %get-tuple-element.105), channel_id=1, source_target_pairs={{0,2},{1,3},{2,0},{3,1},{4,6},{5,7},{6,4},{7,5},{8,10},{9,11},{10,... | collective-permute-start | bytes 393224 | tf_op jit(solution)/shard_map/ppermute | solution.py:414
  102.1 11.0 %collective-permute-start.39 = (f32[64,512]{1,0:T(8,128)S(1)}, f32[64,512]{1,0:T(8,128)S(1)}, u32[]{:S(2)}, u32[]{:S(2)}) collective-permute-start(f32[64,512]{1,0:T(8,128)S(1)} %get-tuple-element.106), channel_id=1, source_target_pairs={{0,4},{1,5},{2,6},{3,7},{4,0},{5,1},{6,2},{7,3},{8,12},{9,13},{10,... | collective-permute-start | bytes 393224 | tf_op jit(solution)/shard_map/ppermute | solution.py:414
  103.2 9.9 %collective-permute-start.40 = (f32[64,512]{1,0:T(8,128)S(1)}, f32[64,512]{1,0:T(8,128)S(1)}, u32[]{:S(2)}, u32[]{:S(2)}) collective-permute-start(f32[64,512]{1,0:T(8,128)S(1)} %get-tuple-element.107), channel_id=1, source_target_pairs={{0,6},{1,7},{2,4},{3,5},{4,2},{5,3},{6,0},{7,1},{8,14},{9,15},{10,... | collective-permute-start | bytes 393224 | tf_op jit(solution)/shard_map/ppermute | solution.py:414
  117.7 2.0 collective-permute-start.41
  128.9 2.0 collective-permute-start.42
  140.5 2.0 collective-permute-start.43
  151.8 2.0 collective-permute-start.44
  154.3 6.4 %collective-permute-start.45 = (f32[64,512]{1,0:T(8,128)S(1)}, f32[64,512]{1,0:T(8,128)S(1)}, u32[]{:S(2)}, u32[]{:S(2)}) collective-permute-start(f32[64,512]{1,0:T(8,128)S(1)} %get-tuple-element.151), channel_id=1, source_target_pairs={{0,2},{1,3},{2,0},{3,1},{4,6},{5,7},{6,4},{7,5},{8,10},{9,11},{10,... | collective-permute-start | bytes 393224 | tf_op jit(solution)/shard_map/ppermute | solution.py:414
  155.5 8.1 %collective-permute-start.46 = (f32[64,512]{1,0:T(8,128)S(1)}, f32[64,512]{1,0:T(8,128)S(1)}, u32[]{:S(2)}, u32[]{:S(2)}) collective-permute-start(f32[64,512]{1,0:T(8,128)S(1)} %get-tuple-element.150), channel_id=1, source_target_pairs={{0,4},{1,5},{2,6},{3,7},{4,0},{5,1},{6,2},{7,3},{8,12},{9,13},{10,... | collective-permute-start | bytes 393224 | tf_op jit(solution)/shard_map/ppermute | solution.py:414
  156.5 7.0 %collective-permute-start.47 = (f32[64,512]{1,0:T(8,128)S(1)}, f32[64,512]{1,0:T(8,128)S(1)}, u32[]{:S(2)}, u32[]{:S(2)}) collective-permute-start(f32[64,512]{1,0:T(8,128)S(1)} %get-tuple-element.149), channel_id=1, source_target_pairs={{0,6},{1,7},{2,4},{3,5},{4,2},{5,3},{6,0},{7,1},{8,14},{9,15},{10,... | collective-permute-start | bytes 393224 | tf_op jit(solution)/shard_map/ppermute | solution.py:414
  163.6 31.0 %collective-permute-start.48 = (f32[256,512]{1,0:T(8,128)S(1)}, f32[256,512]{1,0:T(8,128)S(1)}, u32[]{:S(2)}, u32[]{:S(2)}) collective-permute-start(f32[256,512]{1,0:T(8,128)S(1)} %pad_maximum_fusion.part_ref), channel_id=1, source_target_pairs={{0,8},{8,16},{16,24},{24,0},{1,9},{9,17},{17,25},{25,1},{2,10},{10... | collective-permute-start | bytes 1572872 | tf_op jit(solution)/shard_map/ppermute | solution.py:417
  163.7 16.4 %collective-permute-start.49 = (f32[64,512]{1,0:T(8,128)S(1)}, f32[64,512]{1,0:T(8,128)S(1)}, u32[]{:S(2)}, u32[]{:S(2)}) collective-permute-start(f32[64,512]{1,0:T(8,128)S(1)} %get-tuple-element.147), channel_id=1, source_target_pairs={{0,24},{2,26},{5,29},{7,31},{8,0},{10,2},{13,5},{15,7},{16,8},{18,... | collective-permute-start | bytes 393224 | tf_op jit(solution)/shard_map/ppermute | solution.py:504
  169.4 20.5 %collective-permute-start.50 = (f32[64,512]{1,0:T(8,128)S(1)}, f32[64,512]{1,0:T(8,128)S(1)}, u32[]{:S(2)}, u32[]{:S(2)}) collective-permute-start(f32[64,512]{1,0:T(8,128)S(1)} %get-tuple-element.146), channel_id=1, source_target_pairs={{0,16},{2,18},{5,21},{7,23},{8,24},{10,26},{13,29},{15,31},{16,0},... | collective-permute-start | bytes 393224 | tf_op jit(solution)/shard_map/ppermute | solution.py:504
  171.7 18.3 %collective-permute-start.51 = (f32[64,512]{1,0:T(8,128)S(1)}, f32[64,512]{1,0:T(8,128)S(1)}, u32[]{:S(2)}, u32[]{:S(2)}) collective-permute-start(f32[64,512]{1,0:T(8,128)S(1)} %get-tuple-element.145), channel_id=1, source_target_pairs={{0,8},{2,10},{5,13},{7,15},{8,16},{10,18},{13,21},{15,23},{16,24},... | collective-permute-start | bytes 393224 | tf_op jit(solution)/shard_map/ppermute | solution.py:504
  190.1 7.2 %collective-permute-start.53 = (f32[1,64,512]{2,1,0:T(8,128)S(1)}, f32[1,64,512]{2,1,0:T(8,128)S(1)}, u32[]{:S(2)}, u32[]{:S(2)}) collective-permute-start(f32[1,64,512]{2,1,0:T(8,128)S(1)} %get-tuple-element.143), channel_id=1, source_target_pairs={{0,2},{2,0},{5,7},{7,5},{8,10},{10,8},{13,15},{15,13},{16,18},{18,... | collective-permute-start | bytes 393224 | tf_op jit(solution)/shard_map/ppermute | solution.py:504
  194.6 15.3 %collective-permute-start.52 = (f32[256,512]{1,0:T(8,128)S(1)}, f32[256,512]{1,0:T(8,128)S(1)}, u32[]{:S(2)}, u32[]{:S(2)}) collective-permute-start(f32[256,512]{1,0:T(8,128)S(1)} %collective-permute-done.48.part_ref), channel_id=1, source_target_pairs={{0,8},{8,16},{16,24},{24,0},{1,9},{9,17},{17,25},{25,1},{2,10},{10... | collective-permute-start | bytes 1572872 | tf_op jit(solution)/shard_map/ppermute | solution.py:417
  194.6 3.8 %collective-permute-start.54 = (f32[1,64,512]{2,1,0:T(8,128)S(1)}, f32[1,64,512]{2,1,0:T(8,128)S(1)}, u32[]{:S(2)}, u32[]{:S(2)}) collective-permute-start(f32[1,64,512]{2,1,0:T(8,128)S(1)} %get-tuple-element.142), channel_id=1, source_target_pairs={{0,4},{2,6},{5,1},{7,3},{8,12},{10,14},{13,9},{15,11},{16,20},{18,... | collective-permute-start | bytes 393224 | tf_op jit(solution)/shard_map/ppermute | solution.py:504
  196.1 3.8 %collective-permute-start.55 = (f32[1,64,512]{2,1,0:T(8,128)S(1)}, f32[1,64,512]{2,1,0:T(8,128)S(1)}, u32[]{:S(2)}, u32[]{:S(2)}) collective-permute-start(f32[1,64,512]{2,1,0:T(8,128)S(1)} %get-tuple-element.141), channel_id=1, source_target_pairs={{0,6},{2,4},{5,3},{7,1},{8,14},{10,12},{13,11},{15,9},{16,22},{18,... | collective-permute-start | bytes 393224 | tf_op jit(solution)/shard_map/ppermute | solution.py:504
  210.0 11.0 %collective-permute-start.56 = (f32[256,512]{1,0:T(8,128)S(1)}, f32[256,512]{1,0:T(8,128)S(1)}, u32[]{:S(2)}, u32[]{:S(2)}) collective-permute-start(f32[256,512]{1,0:T(8,128)S(1)} %collective-permute-done.52.part_ref), channel_id=1, source_target_pairs={{0,8},{8,16},{16,24},{24,0},{1,9},{9,17},{17,25},{25,1},{2,10},{10... | collective-permute-start | bytes 1572872 | tf_op jit(solution)/shard_map/ppermute | solution.py:417

commit v7 on v6

--- a/solution.py
+++ b/solution.py
@@ -11,7 +11,7 @@
 EX_DEV = 512
 LANES = 128
 WINDOW = 256
-PARTS = 4
+PARTS = 2
 F32 = jnp.float32
 BF16 = jnp.bfloat16
 MIB = 1024 * 1024
@@ -33,47 +33,45 @@
     return lax.dot_general(left, right, (((1,), (1,)), ((), ())), preferred_element_type=F32)
 
 
-def project_kernel(order_ref, *refs):
+def project_kernel(order_ref, act_ref, grad_ref, wi_ref, wo_ref, *outs):
     del order_ref
-    acts, grads = refs[:PARTS], refs[PARTS:2 * PARTS]
-    wi_ref, wo_ref, out_ref = refs[2 * PARTS:]
-    rows = acts[0].shape[0]
-    for part, (act_ref, grad_ref) in enumerate(zip(acts, grads)):
-        out_ref[part * rows:(part + 1) * rows, :] = jnp.concatenate(
-            [dot_nt(act_ref[...], wi_ref[...]), dot_nt(grad_ref[...], wo_ref[...])], axis=1
-        )
+    values = jnp.concatenate(
+        [dot_nt(act_ref[...], wi_ref[...]), dot_nt(grad_ref[...], wo_ref[...])], axis=1
+    )
+    for which, out_ref in enumerate(outs):
+        @pl.when(pl.program_id(0) // PARTS == which)
+        def _():
+            out_ref[...] = values
 
 
 def project(order, activations, out_grads, w_in, w_out, block):
-    steps = order.shape[0]
     feats, hidden = activations.shape[1], out_grads.shape[1]
     rows = block // PARTS
-
-    def parts(width):
-        return [
-            pl.BlockSpec((rows, width), lambda i, order, part=part: (order[i] * PARTS + part, 0))
-            for part in range(PARTS)
-        ]
-
+    at = lambda i, order: (order[i // PARTS] * PARTS + i % PARTS, 0)
     return pl.pallas_call(
         project_kernel,
-        out_shape=jax.ShapeDtypeStruct((steps * block, LANES), F32),
+        out_shape=(jax.ShapeDtypeStruct((block, LANES), F32),) * 2,
         grid_spec=pltpu.PrefetchScalarGridSpec(
             num_scalar_prefetch=1,
-            grid=(steps,),
-            in_specs=parts(feats) + parts(hidden) + [
+            grid=(2 * PARTS,),
+            in_specs=[
+                pl.BlockSpec((rows, feats), at),
+                pl.BlockSpec((rows, hidden), at),
                 pl.BlockSpec(w_in.shape, lambda i, order: (0, 0)),
                 pl.BlockSpec(w_out.shape, lambda i, order: (0, 0)),
             ],
-            out_specs=pl.BlockSpec((block, LANES), lambda i, order: (i, 0)),
+            out_specs=[
+                pl.BlockSpec((rows, LANES), lambda i, order: (jnp.minimum(i, PARTS - 1), 0)),
+                pl.BlockSpec((rows, LANES), lambda i, order: (jnp.maximum(i - PARTS, 0), 0)),
+            ],
         ),
         compiler_params=pltpu.CompilerParams(vmem_limit_bytes=61 * MIB),
         cost_estimate=pl.CostEstimate(
-            flops=2 * steps * block * (feats + hidden) * 4 * WINDOW,
-            bytes_accessed=2 * steps * block * (feats + hidden),
+            flops=4 * block * (feats + hidden) * 4 * WINDOW,
+            bytes_accessed=4 * block * (feats + hidden),
             transcendentals=0,
         ),
-    )(order, *[activations] * PARTS, *[out_grads] * PARTS, w_in, w_out)
+    )(order, activations, out_grads, w_in, w_out)
 
 
 def build_kernel(ranks, share, ex_block, n_sources, *refs):
@@ -371,33 +369,59 @@
     )(*arrays)
 
 
-def place_kernel(slots, where_ref, part_ref, *refs):
-    out_ref, held = refs[-2:]
-    rows = part_ref.shape[0] // slots
-    for k in range(slots):
-        at = pl.multiple_of(where_ref[1 + k] * rows, rows)
-        held[pl.ds(at, rows), :] = part_ref[k * rows:(k + 1) * rows, :]
-    out_ref[...] = held[...].T
-
-
-def place(where, part, out, shape):
-    operands, in_specs = [part], [pl.BlockSpec(part.shape, lambda i, where: (0, 0))]
-    if out is not None:
-        operands.append(out)
-        in_specs.append(pl.BlockSpec(memory_space=pl.ANY))
-    return pl.pallas_call(
-        functools.partial(place_kernel, where.shape[0] - 1),
-        out_shape=jax.ShapeDtypeStruct(shape, F32),
+def arrange_kernel(count, origin_ref, *refs):
+    parts, outs, held = refs[:count], refs[count:-1], refs[-1]
+    rows = parts[0].shape[0]
+    for k, part in enumerate(parts):
+        held[k * rows:(k + 1) * rows, :] = part[...]
+    for k, out in enumerate(outs):
+        out[...] = held[pl.ds(pl.multiple_of(origin_ref[k] * rows, rows), rows), :]
+
+
+def arrange(origin, parts):
+    rows, columns = parts[0].shape
+    whole = pl.BlockSpec((rows, columns), lambda i, origin: (0, 0))
+    return pl.pallas_call(
+        functools.partial(arrange_kernel, len(parts)),
+        out_shape=(jax.ShapeDtypeStruct((rows, columns), F32),) * origin.shape[0],
         grid_spec=pltpu.PrefetchScalarGridSpec(
             num_scalar_prefetch=1,
             grid=(1,),
-            in_specs=in_specs,
-            out_specs=pl.BlockSpec((shape[0], part.shape[0]), lambda i, where: (0, where[0])),
-            scratch_shapes=[pltpu.VMEM(part.shape, F32)],
-        ),
-        input_output_aliases={} if out is None else {2: 0},
+            in_specs=[whole] * len(parts),
+            out_specs=[whole] * origin.shape[0],
+            scratch_shapes=[pltpu.VMEM((len(parts) * rows, columns), F32)],
+        ),
+        compiler_params=pltpu.CompilerParams(vmem_limit_bytes=8 * MIB),
+    )(origin, *parts)
+
+
+def place_kernel(slots, planes, where_ref, *refs):
+    rings, out_ref, held = refs[:planes], refs[planes], refs[planes + 1]
+    rows = rings[0].shape[0] // slots
+    step = pl.program_id(0)
+    for away, ring in enumerate(rings):
+        to = pl.multiple_of(where_ref[slots + away] * rows, rows)
+        k = where_ref[step]
+        held[pl.ds(to, rows), :] = ring[pl.ds(pl.multiple_of(k * rows, rows), rows), :]
+    out_ref[...] = held[...].T
+
+
+def place(where, rings, slots):
+    planes = len(rings)
+    rows, comps = rings[0].shape[0] // slots * planes, rings[0].shape[1]
+    whole = pl.BlockSpec(rings[0].shape, lambda i, where: (0, 0))
+    return pl.pallas_call(
+        functools.partial(place_kernel, slots, planes),
+        out_shape=jax.ShapeDtypeStruct((comps, slots * rows), F32),
+        grid_spec=pltpu.PrefetchScalarGridSpec(
+            num_scalar_prefetch=1,
+            grid=(slots,),
+            in_specs=[whole] * planes,
+            out_specs=pl.BlockSpec((comps, rows), lambda i, where: (0, i)),
+            scratch_shapes=[pltpu.VMEM((rows, comps), F32)],
+        ),
         compiler_params=pltpu.CompilerParams(vmem_limit_bytes=24 * MIB),
-    )(where, *operands)
+    )(where, *rings)
 
 
 def per_device(n_dp, n_t, activations, out_grads, proj_in, proj_out, example_ids, queries):
@@ -421,8 +445,11 @@
 
     near_chip = [chip ^ k for k in range(n_c)]
 
-    q_chip = queries.shape[0] // n_c
-    slots = [lax.dynamic_slice_in_dim(queries, near_chip[k] * q_chip, q_chip, 0) for k in range(n_c)]
+    q_chip = queries.shape[0] // n_dp
+    parts = [
+        lax.dynamic_slice_in_dim(queries, (i + away) % n_dp * q_chip, q_chip, 0) for away in range(n_dp)
+    ]
+    origin = jnp.stack([(i - near_chip[k]) % n_dp for k in range(n_c)]).astype(jnp.int32)
 
     group = 8
     bounds = group * jnp.arange(EX_DEV // group, dtype=jnp.int32)
@@ -438,18 +465,26 @@
     )
 
     share = tokens // n_t
-    blocks = jnp.stack(near_chip).astype(jnp.int32) * 2
     w_in, w_out = proj_in.T, proj_out.T
-    give = project(blocks + 1 - core, activations, out_grads, w_in, w_out, share)
-    keep = project(blocks + core, activations, out_grads, w_in, w_out, share)
-    extra = tie(extra, give)
+    own, came = None, []
+    for k in reversed(range(n_c)):
+        order = jnp.stack([near_chip[k] * 2 + 1 - core, near_chip[k] * 2 + core]).astype(jnp.int32)
+        if k < n_c - 1:
+            order = tie(order, [give] if k else [came[:-2], part])
+        give, keep = project(order, activations, out_grads, w_in, w_out, share)
+        part = keep + swap(give, 1)
+        if k == n_c - 1:
+            first_give = give
+        if k:
+            came.append(swap(part, 2 * k))
+        else:
+            own = part
+    for part in came:
+        own = own + part
+    extra = tie(extra, first_give)
     extras = [extra] + [shift(extra, away) for away in range(1, n_dp)]
     plane_ids = [one[:id_rows].reshape((1, tokens)) for one in extras]
     firsts = [one[id_rows, :EX_DEV // group].astype(jnp.int32) for one in extras]
-    kept = (keep + swap(give, 1)).reshape((n_c, share, LANES))
-    own = kept[0]
-    for k in range(1, n_c):
-        own = own + swap(kept[k], 2 * k)
 
     rings = [own]
     for _ in range(n_dp - 1):
@@ -463,8 +498,8 @@
     offs = jnp.stack(
         [near_chip[k] * 2 + which for which in (core, 1 - core) for k in range(n_c)]
     ).astype(jnp.int32)
-    offs, pick, plane_ids, firsts, slots = lax.optimization_barrier(
-        (offs, pick, plane_ids, firsts, slots)
+    offs, pick, plane_ids, firsts, parts, origin = lax.optimization_barrier(
+        (offs, pick, plane_ids, firsts, parts, origin)
     )
 
     highs, lows, squares = [], [], []
@@ -481,6 +516,7 @@
         lows.append(low)
         squares.append(square)
 
+    slots = arrange(origin, [parts[0]] + [shift(parts[away], away) for away in range(1, n_dp)])
     slots = [slots[0]] + [swap(slots[k], 2 * k) for k in range(1, n_c)]
     message, b = join(highs, lows, squares, slots)
     r, rest = b, ()
@@ -493,41 +529,34 @@
     other = swap(message, 1)
     x, y = last_step(examples, comps_all, message, other, r, *rest)
 
-    n_half = n_c // 2
+    n_half = n_dp // 2
     per_slot = comps_all // n_t
 
-    def send(values, to):
+    def send(values, by):
         pairs = [
-            (di * n_t + 2 * c + c // n_half, to(di, c, c // n_half))
-            for di in range(n_dp) for c in range(n_c)
+            (a * n_t + 2 * c + a // n_half, (a + by) % n_dp * n_t + 2 * c + a // n_half)
+            for a in range(n_dp) for c in range(n_c)
         ]
         return lax.ppermute(values, ("dp", "tensor"), pairs)
 
-    ring = [x[:, k * per_slot:(k + 1) * per_slot] for k in range(n_c)]
-    ring = jnp.concatenate([ring[0]] + [swap(ring[k], 2 * k) for k in range(1, n_c)], axis=0)
-    y = tie(y, ring)
     by_plane = jnp.zeros((n_dp, q_chip, EX_DEV), F32)
     for away in range(n_dp):
         part = y[:, away * EX_DEV:(away + 1) * EX_DEV]
         if away:
-            part = send(part, lambda di, c, h: ((di - away) % n_dp) * n_t + 2 * c + h)
+            part = send(part, -away)
         by_plane = lax.dynamic_update_slice(by_plane, part[None], ((i + away) % n_dp, 0, 0))
-    by_chip = jnp.zeros((n_c, q_chip, EX_DEV), F32)
-    for k in range(n_c):
-        part = lax.dynamic_slice_in_dim(by_plane, near_chip[k], 1, 0)
-        if k:
-            part = send(part, lambda di, c, h: di * n_t + 2 * (c ^ k) + h)
-        by_chip = lax.dynamic_update_slice(by_chip, part, (near_chip[k], 0, 0))
-    scores = lax.dynamic_slice_in_dim(by_chip, core * n_half, n_half, 0)
-
-    outs = [None]
-    for away in range(n_dp):
-        if away:
-            before = [[], [by_plane, outs[-2]], [scores, outs[-2]]][min(away - 1, 2)]
-            ring = shift(tie(ring, before) if before else ring, 1)
-        where = jnp.stack([(i - away) % n_dp] + near_chip).astype(jnp.int32)
-        outs.append(place(where, ring, outs[-1], (per_slot, n_dp * n_c * q_chip)))
-    return (outs[-1], scores.reshape((n_half * q_chip, EX_DEV)))
+    scores = lax.dynamic_slice_in_dim(by_plane, core * n_half, n_half, 0)
+
+    ring = [x[:, k * per_slot:(k + 1) * per_slot] for k in range(n_c)]
+    ring = jnp.concatenate([ring[0]] + [swap(ring[k], 2 * k) for k in range(1, n_c)], axis=0)
+    rings = [ring]
+    for away in range(1, n_dp):
+        rings.append(shift(tie(rings[-1], scores) if away == 2 else rings[-1], 1))
+    where = jnp.stack(
+        [chip ^ c for c in range(n_c)] + [(i - away) % n_dp for away in range(n_dp)]
+    ).astype(jnp.int32)
+    out = place(where, rings, n_c)
+    return (out, scores.reshape((n_half * q_chip, EX_DEV)))
 
 
 def solution(mesh):

time: 223 us -> 233 us (1.045)
  Pallas kernels: 89.1 us -> 93.9 us
  other arithmetic: 2.92 us -> 5.94 us
    ppermute x9 -> x12, waiting for transfers between devices: 23.1 us -> 42.9 us  [shift(): lax.ppermute(values, 'dp', [(a, (a + by) % n_dp) for a in range(n_dp)])]
    ppermute x6 -> x3, waiting for transfers between devices: 16.7 us -> 3.99 us  [send(): return lax.ppermute(values, ('dp', 'tensor'), pairs)]
    ppermute x9 -> x12, starting transfers between devices: 5.54 us -> 14 us  [shift(): lax.ppermute(values, 'dp', [(a, (a + by) % n_dp) for a in range(n_dp)])]
    ppermute x6 -> x3, starting transfers between devices: 17.3 us -> 9.01 us  [send(): return lax.ppermute(values, ('dp', 'tensor'), pairs)]
    ppermute x42 -> x45, waiting for transfers between devices: 35.8 us -> 28 us  [swap(): return lax.ppermute(values, 'tensor', [(a, a ^ mask) for a in range(n_t)])]
    pallas_call x6, Pallas kernels: 21.9 us -> 26.9 us  [the longest x4 23.4 us: project(): pl.pallas_call(project_kernel, out_shape=(jax.ShapeDtypeStruct((block, LA...]
    ppermute x42 -> x45, starting transfers between devices: 29.3 us -> 30 us  [swap(): return lax.ppermute(values, 'tensor', [(a, a ^ mask) for a in range(n_t)])]
  transfers between devices with their start and end apart: 57 -> 60, of which waited for: 21 -> 22; matrix products, arithmetic and copies ran while one was open for 2% -> 2% of each run, Pallas kernels for 21% -> 23%
where the time goes in v7:
time: 233 us; the launch traced here: 232 us
  Pallas kernels  93.9 us (40%)
  waiting for transfers between devices  74.9 us (32%)
  starting transfers between devices  53 us (23%)
  other arithmetic  5.94 us (3%)
  local copies, waits for them, and re-layouts  3.08 us (1%)
    ppermute x12, waiting for transfers between devices, shift(): lax.ppermute(values, 'dp', [(a, (a + by) % n_dp) for a in range(n_dp)])  42.9 us
    pallas_call x4, Pallas kernels, build(): pl.pallas_call(functools.partial(build_kernel, ranks, share, ex_block, le...  34.2 us
    ppermute x45, starting transfers between devices, swap(): return lax.ppermute(values, 'tensor', [(a, a ^ mask) for a in range(n_t)])  30 us
    ppermute x45, waiting for transfers between devices, swap(): return lax.ppermute(values, 'tensor', [(a, a ^ mask) for a in range(n_t)])  28 us
    pallas_call x3, Pallas kernels, one_step(): pl.pallas_call(functools.partial(step_kernel, first, planes, examples, co...  27.7 us
    pallas_call x4, Pallas kernels, project(): pl.pallas_call(project_kernel, out_shape=(jax.ShapeDtypeStruct((block, LA...  23.4 us
    ppermute x12, starting transfers between devices, shift(): lax.ppermute(values, 'dp', [(a, (a + by) % n_dp) for a in range(n_dp)])  14 us
    ppermute x3, starting transfers between devices, send(): return lax.ppermute(values, ('dp', 'tensor'), pairs)  9.01 us
  transfers between devices with their start and end apart: 60, of which 22 were waited for; matrix products, arithmetic and copies ran while one was open for 2% of the time, Pallas kernels for 23%

profile of v7, /device:TPU:0, one launch (start us, length us, event | category | flops | bytes accessed | tf_op | source)
XLA Modules:
  0.0 232.0 jit_solution(5029610707317254602)
XLA Ops:
  1.4 1.0 convert_reduce_fusion
  3.1 5.8 %shard_map.77 = (f32[512,128]{1,0:T(8,128)}, f32[512,128]{1,0:T(8,128)}) custom-call(s32[2]{0:T(128)} %get-tuple-element.175.order_ref, bf16[4096,512]{1,0:T(8,128)(2,1)} %act_ref.7, bf16[4096,1792]{1,0:T(8,128)(2,1)} %grad_ref.7, bf16[64,512]{1,0:T(8,128)(2,1)} %bitcast.91, bf16[64,1792]{1,0:T(8,128)(2,1)} %bitcast.87), custom_call_target="tpu_custom_call" | custom-call | flops 4831838208 | bytes 4718592 | tf_op jit(solution)/shard_map/pallas_call | solution.py:51
  8.9 3.0 %collective-permute-start = (f32[40,128]{1,0:T(8,128)S(1)}, f32[40,128]{1,0:T(8,128)S(1)}, u32[]{:S(2)}, u32[]{:S(2)}) collective-permute-start(f32[40,128]{1,0:T(8,128)S(1)} %select_maximum_fusion), channel_id=1, source_target_pairs={{0,8},{8,16},{16,24},{24,0},{1,9},{9,17},{17,25},{25,1},{2,10},{10... | collective-permute-start | bytes 61448 | tf_op jit(solution)/shard_map/ppermute | solution.py:441
  11.9 2.6 %collective-permute-start.1 = (f32[40,128]{1,0:T(8,128)S(1)}, f32[40,128]{1,0:T(8,128)S(1)}, u32[]{:S(2)}, u32[]{:S(2)}) collective-permute-start(f32[40,128]{1,0:T(8,128)S(1)} %select_maximum_fusion), channel_id=1, source_target_pairs={{0,16},{8,24},{16,0},{24,8},{1,17},{9,25},{17,1},{25,9},{2,18},{10... | collective-permute-start | bytes 61448 | tf_op jit(solution)/shard_map/ppermute | solution.py:441
  15.1 5.8 %shard_map.78 = (f32[512,128]{1,0:T(8,128)}, f32[512,128]{1,0:T(8,128)}) custom-call(s32[2]{0:T(128)} %pad_add_fusion.4.order_ref, bf16[4096,512]{1,0:T(8,128)(2,1)} %act_ref.7, bf16[4096,1792]{1,0:T(8,128)(2,1)} %grad_ref.7, bf16[64,512]{1,0:T(8,128)(2,1)} %bitcast.92, bf16[64,1792]{1,0:T(8,128)(2,1)} %bitcast.88), custom_call_target="tpu_custom_call" | custom-call | flops 4831838208 | bytes 4718592 | tf_op jit(solution)/shard_map/pallas_call | solution.py:51
  21.5 5.9 %shard_map.79 = (f32[512,128]{1,0:T(8,128)}, f32[512,128]{1,0:T(8,128)}) custom-call(s32[2]{0:T(128)} %get-tuple-element.90.order_ref, bf16[4096,512]{1,0:T(8,128)(2,1)} %act_ref.7, bf16[4096,1792]{1,0:T(8,128)(2,1)} %grad_ref.7, bf16[64,512]{1,0:T(8,128)(2,1)} %bitcast.93, bf16[64,1792]{1,0:T(8,128)(2,1)} %bitcast.89), custom_call_target="tpu_custom_call" | custom-call | flops 4831838208 | bytes 4718592 | tf_op jit(solution)/shard_map/pallas_call | solution.py:51
  27.5 2.5 %collective-permute-start.4 = (f32[512,128]{1,0:T(8,128)S(1)}, f32[512,128]{1,0:T(8,128)S(1)}, u32[]{:S(2)}, u32[]{:S(2)}) collective-permute-start(f32[512,128]{1,0:T(8,128)S(1)} %add.421), channel_id=1, source_target_pairs={{0,6},{1,7},{2,4},{3,5},{4,2},{5,3},{6,0},{7,1},{8,14},{9,15},{10,... | collective-permute-start | bytes 786440 | tf_op jit(solution)/shard_map/ppermute | solution.py:438
  30.7 1.0 add.424
  32.3 1.0 collective-permute-start.8
  33.3 4.2 %collective-permute-done.4 = f32[512,128]{1,0:T(8,128)S(1)} collective-permute-done((f32[512,128]{1,0:T(8,128)S(1)}, f32[512,128]{1,0:T(8,128)S(1)}, u32[]{:S(2)}, u32[]{:S(2)}) %collective-permute-start.4) | collective-permute-done | bytes 262176 | tf_op jit(solution)/shard_map/ppermute | solution.py:438
  37.6 5.8 %shard_map.80 = (f32[512,128]{1,0:T(8,128)}, f32[512,128]{1,0:T(8,128)}) custom-call(s32[2]{0:T(128)} %pad_add_fusion.2.order_ref, bf16[4096,512]{1,0:T(8,128)(2,1)} %act_ref.7, bf16[4096,1792]{1,0:T(8,128)(2,1)} %grad_ref.7, bf16[64,512]{1,0:T(8,128)(2,1)} %bitcast.94, bf16[64,1792]{1,0:T(8,128)(2,1)} %bitcast.90), custom_call_target="tpu_custom_call" | custom-call | flops 4831838208 | bytes 4718592 | tf_op jit(solution)/shard_map/pallas_call | solution.py:51
  43.8 1.4 collective-permute-done.6
  45.1 1.0 add_add_fusion.refs_2_
  46.2 1.6 collective-permute-start.10
  47.7 1.5 collective-permute-start.11
  49.9 1.4 collective-permute-start.2
  51.3 2.4 %collective-permute-done.2 = f32[40,128]{1,0:T(8,128)S(1)} collective-permute-done((f32[40,128]{1,0:T(8,128)S(1)}, f32[40,128]{1,0:T(8,128)S(1)}, u32[]{:S(2)}, u32[]{:S(2)}) %collective-permute-start.2) | collective-permute-done | bytes 20512 | tf_op jit(solution)/shard_map/ppermute | solution.py:441
  53.8 1.6 collective-permute-done.10.refs_3_
  55.4 6.0 %collective-permute-done.11.refs_4_ = f32[512,128]{1,0:T(8,128)S(1)} collective-permute-done((f32[512,128]{1,0:T(8,128)S(1)}, f32[512,128]{1,0:T(8,128)S(1)}, u32[]{:S(2)}, u32[]{:S(2)}) %collective-permute-start.11) | collective-permute-done | bytes 262176 | tf_op jit(solution)/shard_map/ppermute | solution.py:438
  62.2 1.5 collective-permute-start.18
  63.7 1.5 collective-permute-start.19
  65.8 8.5 %shard_map.81 = (bf16[512,2048]{1,0:T(8,128)(2,1)S(1)}, bf16[512,2048]{1,0:T(8,128)(2,1)S(1)}, f32[8,128]{1,0:T(8,128)S(1)}) custom-call(s32[8]{0:T(128)S(1)} %stack.213.refs_0_, s32[64]{0:T(128)S(1)} %convert_bitcast_fusion.refs_1_, f32[512,128]{1,0:T(8,128)S(1)} %add_add_fusion.refs_2_, f32[512,128]{1,0:T(8,128)S(1)} %collective-permute-done.10.refs_3_, ...), custom_call_target="tpu_custom_call" | custom-call | flops 12884901888 | bytes 6291456 | tf_op jit(solution)/shard_map/pallas_call | solution.py:169
  74.3 0.9 collective-permute-done.19.refs_4_
  75.2 1.6 collective-permute-done.20.refs_5_
  77.9 0.8 collective-permute-start.26
  78.7 1.5 collective-permute-start.27
  80.2 1.2 collective-permute-start.28
  81.6 8.5 %shard_map.82 = (bf16[512,2048]{1,0:T(8,128)(2,1)S(1)}, bf16[512,2048]{1,0:T(8,128)(2,1)S(1)}, f32[8,128]{1,0:T(8,128)S(1)}) custom-call(s32[8]{0:T(128)S(1)} %stack.213.refs_0_, s32[64]{0:T(128)S(1)} %fusion.3.refs_1_, f32[512,128]{1,0:T(8,128)S(1)} %collective-permute-done.17.refs_2_, f32[512,128]{1,0:T(8,128)S(1)} %collective-permute-done.18.refs_3_, ...), custom_call_target="tpu_custom_call" | custom-call | flops 12884901888 | bytes 6291456 | tf_op jit(solution)/shard_map/pallas_call | solution.py:169
  90.1 2.2 collective-permute-done.27.refs_4_
  93.9 2.0 collective-permute-start.42
  95.9 1.2 collective-permute-start.34
  97.1 1.1 collective-permute-start.35
  98.3 1.1 collective-permute-start.36
  99.4 8.5 %shard_map.83 = (bf16[512,2048]{1,0:T(8,128)(2,1)S(1)}, bf16[512,2048]{1,0:T(8,128)(2,1)S(1)}, f32[8,128]{1,0:T(8,128)S(1)}) custom-call(s32[8]{0:T(128)S(1)} %stack.213.refs_0_, s32[64]{0:T(128)S(1)} %fusion.2.refs_1_, f32[512,128]{1,0:T(8,128)S(1)} %collective-permute-done.25.refs_2_, f32[512,128]{1,0:T(8,128)S(1)} %collective-permute-done.26.refs_3_, ...), custom_call_target="tpu_custom_call" | custom-call | flops 12884901888 | bytes 6291456 | tf_op jit(solution)/shard_map/pallas_call | solution.py:169
  107.9 0.9 collective-permute-done.35.refs_4_
  108.8 1.3 collective-permute-done.36.refs_5_
  111.1 1.6 collective-permute-start.43
  112.7 3.9 %collective-permute-done.43.refs_3_ = f32[64,512]{1,0:T(8,128)S(1)} collective-permute-done((f32[64,512]{1,0:T(8,128)S(1)}, f32[64,512]{1,0:T(8,128)S(1)}, u32[]{:S(2)}, u32[]{:S(2)}) %collective-permute-start.43) | collective-permute-done | bytes 131104 | tf_op jit(solution)/shard_map/ppermute | solution.py:441
  117.3 1.0 collective-permute-start.44
  118.2 1.4 collective-permute-start.45
  119.6 1.2 collective-permute-start.46
  120.8 8.7 %shard_map.84 = (bf16[512,2048]{1,0:T(8,128)(2,1)S(1)}, bf16[512,2048]{1,0:T(8,128)(2,1)S(1)}, f32[8,128]{1,0:T(8,128)S(1)}) custom-call(s32[8]{0:T(128)S(1)} %stack.213.refs_0_, s32[64]{0:T(128)S(1)} %fusion.1.refs_1_, f32[512,128]{1,0:T(8,128)S(1)} %collective-permute-done.33.refs_2_, f32[512,128]{1,0:T(8,128)S(1)} %collective-permute-done.34.refs_3_, ...), custom_call_target="tpu_custom_call" | custom-call | flops 12884901888 | bytes 6291456 | tf_op jit(solution)/shard_map/pallas_call | solution.py:169
  129.6 4.6 %shard_map.86 = (f32[64,2176]{1,0:T(8,128)S(1)}, f32[64,2048]{1,0:T(8,128)S(1)}) custom-call(bf16[512,2048]{1,0:T(8,128)(2,1)S(1)} %get-tuple-element.99.refs_0_.refs_3_.refs_8_, bf16[512,2048]{1,0:T(8,128)(2,1)S(1)} %get-tuple-element.107.refs_1_.refs_4_.refs_9_, bf16[512,2048]{1,0:T(8,128)(2,1)S(1)} %get-tuple-element.115.refs_2_.refs_5_.refs_10_, ...), custom_call_target="tpu_custom_call" | custom-call | flops 1610612736 | bytes 16777216 | tf_op jit(solution)/shard_map/pallas_call | solution.py:225
  134.2 1.9 collective-permute-done.47.refs_1_
  136.2 9.2 %shard_map.87 = (f32[64,2176]{1,0:T(8,128)S(1)}, f32[64,2048]{1,0:T(8,128)S(1)}, f32[64,2048]{1,0:T(8,128)S(1)}, f32[64,2048]{1,0:T(8,128)S(1)}, f32[64,2048]{1,...) custom-call(f32[64,2176]{1,0:T(8,128)S(1)} %get-tuple-element.138.refs_0_, ...), custom_call_target="tpu_custom_call" | custom-call | flops 3221225472 | bytes 16777216 | tf_op jit(solution)/shard_map/pallas_call | solution.py:336
  145.6 1.8 collective-permute-done.48.refs_1_
  147.4 9.2 %shard_map.88 = (f32[64,2176]{1,0:T(8,128)S(1)}, f32[64,2048]{1,0:T(8,128)S(1)}, f32[64,2048]{1,0:T(8,128)S(1)}, f32[64,2048]{1,0:T(8,128)S(1)}, f32[64,2048]{1,...) custom-call(f32[64,2176]{1,0:T(8,128)S(1)} %get-tuple-element.140.refs_0_, ...), custom_call_target="tpu_custom_call" | custom-call | flops 3221225472 | bytes 16777216 | tf_op jit(solution)/shard_map/pallas_call | solution.py:336
  156.9 1.8 collective-permute-done.49.refs_1_
  158.7 9.2 %shard_map.89 = (f32[64,2176]{1,0:T(8,128)S(1)}, f32[64,2048]{1,0:T(8,128)S(1)}, f32[64,2048]{1,0:T(8,128)S(1)}, f32[64,2048]{1,0:T(8,128)S(1)}, f32[64,2048]{1,...) custom-call(f32[64,2176]{1,0:T(8,128)S(1)} %get-tuple-element.147.refs_0_, ...), custom_call_target="tpu_custom_call" | custom-call | flops 3221225472 | bytes 16777216 | tf_op jit(solution)/shard_map/pallas_call | solution.py:336
  167.9 0.8 copy-done
  168.9 1.8 collective-permute-done.50.other_ref
  170.7 1.0 copy-done.1
  172.3 1.8 collective-permute-start.53
  174.7 1.1 collective-permute-start.51
  175.8 5.2 %collective-permute-start.55 = (f32[64,512]{1,0:T(8,128)S(1)}, f32[64,512]{1,0:T(8,128)S(1)}, u32[]{:S(2)}, u32[]{:S(2)}) collective-permute-start(f32[64,512]{1,0:T(8,128)S(1)} %get-tuple-element.166), channel_id=1, source_target_pairs={{0,24},{2,26},{4,28},{6,30},{8,0},{10,2},{12,4},{14,6},{17,9},{19,... | collective-permute-start | bytes 393224 | tf_op jit(solution)/shard_map/ppermute | solution.py:540
  181.1 1.3 collective-permute-start.56
  182.5 2.5 %collective-permute-start.57 = (f32[64,512]{1,0:T(8,128)S(1)}, f32[64,512]{1,0:T(8,128)S(1)}, u32[]{:S(2)}, u32[]{:S(2)}) collective-permute-start(f32[64,512]{1,0:T(8,128)S(1)} %get-tuple-element.164), channel_id=1, source_target_pairs={{0,8},{2,10},{4,12},{6,14},{8,16},{10,18},{12,20},{14,22},{17,25},... | collective-permute-start | bytes 393224 | tf_op jit(solution)/shard_map/ppermute | solution.py:540
  185.1 1.2 collective-permute-done.56
  186.3 2.8 %collective-permute-done.57 = f32[64,512]{1,0:T(8,128)S(1)} collective-permute-done((f32[64,512]{1,0:T(8,128)S(1)}, f32[64,512]{1,0:T(8,128)S(1)}, u32[]{:S(2)}, u32[]{:S(2)}) %collective-permute-start.57) | collective-permute-done | bytes 131104 | tf_op jit(solution)/shard_map/ppermute | solution.py:540
  189.9 7.8 %collective-permute-done.54.refs_1_ = f32[256,512]{1,0:T(8,128)S(1)} collective-permute-done((f32[256,512]{1,0:T(8,128)S(1)}, f32[256,512]{1,0:T(8,128)S(1)}, u32[]{:S(2)}, u32[]{:S(2)}) %collective-permute-start.54) | collective-permute-done | bytes 524320 | tf_op jit(solution)/shard_map/ppermute | solution.py:441
  197.7 2.8 %collective-permute-start.58 = (f32[256,512]{1,0:T(8,128)S(1)}, f32[256,512]{1,0:T(8,128)S(1)}, u32[]{:S(2)}, u32[]{:S(2)}) collective-permute-start(f32[256,512]{1,0:T(8,128)S(1)} %collective-permute-done.54.refs_1_), channel_id=1, source_target_pairs={{0,8},{8,16},{16,24},{24,0},{1,9},{9,17},{17,25},{25,1},{2,10},{10... | collective-permute-start | bytes 1572872 | tf_op jit(solution)/shard_map/ppermute | solution.py:441
  200.5 13.3 %collective-permute-done.58.refs_2_ = f32[256,512]{1,0:T(8,128)S(1)} collective-permute-done((f32[256,512]{1,0:T(8,128)S(1)}, f32[256,512]{1,0:T(8,128)S(1)}, u32[]{:S(2)}, u32[]{:S(2)}) %collective-permute-start.58) | collective-permute-done | bytes 524320 | tf_op jit(solution)/shard_map/ppermute | solution.py:441
  213.9 15.2 %collective-permute-done.59.refs_3_ = f32[256,512]{1,0:T(8,128)S(1)} collective-permute-done((f32[256,512]{1,0:T(8,128)S(1)}, f32[256,512]{1,0:T(8,128)S(1)}, u32[]{:S(2)}, u32[]{:S(2)}) %collective-permute-start.59) | collective-permute-done | bytes 524320 | tf_op jit(solution)/shard_map/ppermute | solution.py:441
  229.1 2.9 %shard_map.91 = f32[512,1024]{1,0:T(8,128)} custom-call(s32[8]{0:T(128)S(1)} %stack.204.where_ref, f32[256,512]{1,0:T(8,128)S(1)} %pad_maximum_fusion.refs_0_, f32[256,512]{1,0:T(8,128)S(1)} %collective-permute-done.54.refs_1_, f32[256,512]{1,0:T(8,128)S(1)} %collective-permute-done.58.refs_2_, f32[256,512]{1,0:T(8,128)S(1)} %collective-permute-done.59.refs_3_), custom_call_target="tpu_custom_call" | custom-call | tf_op jit(solution)/shard_map/pallas_call | solution.py:413
  (116 shorter events, 13.4 us)
Async XLA Ops:
  8.9 41.0 %collective-permute-start = (f32[40,128]{1,0:T(8,128)S(1)}, f32[40,128]{1,0:T(8,128)S(1)}, u32[]{:S(2)}, u32[]{:S(2)}) collective-permute-start(f32[40,128]{1,0:T(8,128)S(1)} %select_maximum_fusion), channel_id=1, source_target_pairs={{0,8},{8,16},{16,24},{24,0},{1,9},{9,17},{17,25},{25,1},{2,10},{10... | collective-permute-start | bytes 61448 | tf_op jit(solution)/shard_map/ppermute | solution.py:441
  11.9 39.4 %collective-permute-start.1 = (f32[40,128]{1,0:T(8,128)S(1)}, f32[40,128]{1,0:T(8,128)S(1)}, u32[]{:S(2)}, u32[]{:S(2)}) collective-permute-start(f32[40,128]{1,0:T(8,128)S(1)} %select_maximum_fusion), channel_id=1, source_target_pairs={{0,16},{8,24},{16,0},{24,8},{1,17},{9,25},{17,1},{25,9},{2,18},{10... | collective-permute-start | bytes 61448 | tf_op jit(solution)/shard_map/ppermute | solution.py:441
  14.5 12.9 %collective-permute-start.3 = (f32[512,128]{1,0:T(8,128)}, f32[512,128]{1,0:T(8,128)S(1)}, u32[]{:S(2)}, u32[]{:S(2)}) collective-permute-start(f32[512,128]{1,0:T(8,128)} %get-tuple-element.83), channel_id=1, source_target_pairs={{0,1},{1,0},{2,3},{3,2},{4,5},{5,4},{6,7},{7,6},{8,9},{9,8},{10,11... | collective-permute-start | bytes 786440 | tf_op jit(solution)/shard_map/ppermute | solution.py:438
  21.0 11.3 %collective-permute-start.7 = (f32[512,128]{1,0:T(8,128)}, f32[512,128]{1,0:T(8,128)S(1)}, u32[]{:S(2)}, u32[]{:S(2)}) collective-permute-start(f32[512,128]{1,0:T(8,128)} %get-tuple-element.89), channel_id=1, source_target_pairs={{0,1},{1,0},{2,3},{3,2},{4,5},{5,4},{6,7},{7,6},{8,9},{9,8},{10,11... | collective-permute-start | bytes 786440 | tf_op jit(solution)/shard_map/ppermute | solution.py:438
  21.5 6.0 %copy-start.4 = (f32[512,128]{1,0:T(8,128)S(1)}, f32[512,128]{1,0:T(8,128)}, u32[]{:S(2)}) copy-start(f32[512,128]{1,0:T(8,128)} %get-tuple-element.87) | copy-start | bytes 786436
  21.5 10.8 %copy-start.3 = (f32[512,128]{1,0:T(8,128)S(1)}, f32[512,128]{1,0:T(8,128)}, u32[]{:S(2)}) copy-start(f32[512,128]{1,0:T(8,128)} %get-tuple-element.96) | copy-start | bytes 786436
  27.4 3.2 %collective-permute-start.5 = (f32[512,128]{1,0:T(8,128)}, f32[512,128]{1,0:T(8,128)S(1)}, u32[]{:S(2)}, u32[]{:S(2)}) collective-permute-start(f32[512,128]{1,0:T(8,128)} %get-tuple-element.92), channel_id=1, source_target_pairs={{0,1},{1,0},{2,3},{3,2},{4,5},{5,4},{6,7},{7,6},{8,9},{9,8},{10,11... | collective-permute-start | bytes 786440 | tf_op jit(solution)/shard_map/ppermute | solution.py:438
  27.5 10.1 %collective-permute-start.4 = (f32[512,128]{1,0:T(8,128)S(1)}, f32[512,128]{1,0:T(8,128)S(1)}, u32[]{:S(2)}, u32[]{:S(2)}) collective-permute-start(f32[512,128]{1,0:T(8,128)S(1)} %add.421), channel_id=1, source_target_pairs={{0,6},{1,7},{2,4},{3,5},{4,2},{5,3},{6,0},{7,1},{8,14},{9,15},{10,... | collective-permute-start | bytes 786440 | tf_op jit(solution)/shard_map/ppermute | solution.py:438
  31.6 12.1 %collective-permute-start.9 = (f32[512,128]{1,0:T(8,128)S(1)}, f32[512,128]{1,0:T(8,128)S(1)}, u32[]{:S(2)}, u32[]{:S(2)}) collective-permute-start(f32[512,128]{1,0:T(8,128)S(1)} %add.424), channel_id=1, source_target_pairs={{0,2},{1,3},{2,0},{3,1},{4,6},{5,7},{6,4},{7,5},{8,10},{9,11},{10,... | collective-permute-start | bytes 786440 | tf_op jit(solution)/shard_map/ppermute | solution.py:438
  32.3 11.1 %copy-start.2 = (f32[256,512]{1,0:T(8,128)S(1)}, f32[256,512]{1,0:T(8,128)}, u32[]{:S(2)}) copy-start(f32[256,512]{1,0:T(8,128)} %param.11) | copy-start | bytes 1572868
  32.3 11.4 %collective-permute-start.8 = (f32[512,128]{1,0:T(8,128)S(1)}, f32[512,128]{1,0:T(8,128)S(1)}, u32[]{:S(2)}, u32[]{:S(2)}) collective-permute-start(f32[512,128]{1,0:T(8,128)S(1)} %add.427), channel_id=1, source_target_pairs={{0,4},{1,5},{2,6},{3,7},{4,0},{5,1},{6,2},{7,3},{8,12},{9,13},{10,... | collective-permute-start | bytes 786440 | tf_op jit(solution)/shard_map/ppermute | solution.py:438
  43.4 1.7 collective-permute-start.6
  46.2 9.2 %collective-permute-start.10 = (f32[512,128]{1,0:T(8,128)S(1)}, f32[512,128]{1,0:T(8,128)S(1)}, u32[]{:S(2)}, u32[]{:S(2)}) collective-permute-start(f32[512,128]{1,0:T(8,128)S(1)} %add_add_fusion.refs_2_), channel_id=1, source_target_pairs={{0,2},{1,3},{2,0},{3,1},{4,6},{5,7},{6,4},{7,5},{8,10},{9,11},{10,... | collective-permute-start | bytes 786440 | tf_op jit(solution)/shard_map/ppermute | solution.py:438
  47.7 13.7 %collective-permute-start.11 = (f32[512,128]{1,0:T(8,128)S(1)}, f32[512,128]{1,0:T(8,128)S(1)}, u32[]{:S(2)}, u32[]{:S(2)}) collective-permute-start(f32[512,128]{1,0:T(8,128)S(1)} %add_add_fusion.refs_2_), channel_id=1, source_target_pairs={{0,4},{1,5},{2,6},{3,7},{4,0},{5,1},{6,2},{7,3},{8,12},{9,13},{10,... | collective-permute-start | bytes 786440 | tf_op jit(solution)/shard_map/ppermute | solution.py:438
  49.3 12.2 %collective-permute-start.12 = (f32[512,128]{1,0:T(8,128)S(1)}, f32[512,128]{1,0:T(8,128)S(1)}, u32[]{:S(2)}, u32[]{:S(2)}) collective-permute-start(f32[512,128]{1,0:T(8,128)S(1)} %add_add_fusion.refs_2_), channel_id=1, source_target_pairs={{0,6},{1,7},{2,4},{3,5},{4,2},{5,3},{6,0},{7,1},{8,14},{9,15},{10,... | collective-permute-start | bytes 786440 | tf_op jit(solution)/shard_map/ppermute | solution.py:438
  49.9 3.8 %collective-permute-start.2 = (f32[40,128]{1,0:T(8,128)S(1)}, f32[40,128]{1,0:T(8,128)S(1)}, u32[]{:S(2)}, u32[]{:S(2)}) collective-permute-start(f32[40,128]{1,0:T(8,128)S(1)} %select_maximum_fusion), channel_id=1, source_target_pairs={{0,24},{8,0},{16,8},{24,16},{1,25},{9,1},{17,9},{25,17},{2,26},{10... | collective-permute-start | bytes 61448 | tf_op jit(solution)/shard_map/ppermute | solution.py:441
  51.3 12.4 %collective-permute-start.13 = (f32[512,128]{1,0:T(8,128)S(1)}, f32[512,128]{1,0:T(8,128)S(1)}, u32[]{:S(2)}, u32[]{:S(2)}) collective-permute-start(f32[512,128]{1,0:T(8,128)S(1)} %add_add_fusion.refs_2_), channel_id=1, source_target_pairs={{0,1},{1,0},{2,3},{3,2},{4,5},{5,4},{6,7},{7,6},{8,9},{9,8},{10,11... | collective-permute-start | bytes 786440 | tf_op jit(solution)/shard_map/ppermute | solution.py:438
  53.7 8.5 %collective-permute-start.17 = (f32[512,128]{1,0:T(8,128)S(1)}, f32[512,128]{1,0:T(8,128)S(1)}, u32[]{:S(2)}, u32[]{:S(2)}) collective-permute-start(f32[512,128]{1,0:T(8,128)S(1)} %add_add_fusion.refs_2_), channel_id=1, source_target_pairs={{0,8},{8,16},{16,24},{24,0},{1,9},{9,17},{17,25},{25,1},{2,10},{10... | collective-permute-start | bytes 786440 | tf_op jit(solution)/shard_map/ppermute | solution.py:441
  55.4 9.8 %collective-permute-start.14 = (f32[512,128]{1,0:T(8,128)S(1)}, f32[512,128]{1,0:T(8,128)S(1)}, u32[]{:S(2)}, u32[]{:S(2)}) collective-permute-start(f32[512,128]{1,0:T(8,128)S(1)} %collective-permute-done.10.refs_3_), channel_id=1, source_target_pairs={{0,1},{1,0},{2,3},{3,2},{4,5},{5,4},{6,7},{7,6},{8,9},{9,8},{10,11... | collective-permute-start | bytes 786440 | tf_op jit(solution)/shard_map/ppermute | solution.py:438
  61.4 4.3 %collective-permute-start.15 = (f32[512,128]{1,0:T(8,128)S(1)}, f32[512,128]{1,0:T(8,128)S(1)}, u32[]{:S(2)}, u32[]{:S(2)}) collective-permute-start(f32[512,128]{1,0:T(8,128)S(1)} %collective-permute-done.11.refs_4_), channel_id=1, source_target_pairs={{0,1},{1,0},{2,3},{3,2},{4,5},{5,4},{6,7},{7,6},{8,9},{9,8},{10,11... | collective-permute-start | bytes 786440 | tf_op jit(solution)/shard_map/ppermute | solution.py:438
  61.4 4.3 %collective-permute-start.16 = (f32[512,128]{1,0:T(8,128)S(1)}, f32[512,128]{1,0:T(8,128)S(1)}, u32[]{:S(2)}, u32[]{:S(2)}) collective-permute-start(f32[512,128]{1,0:T(8,128)S(1)} %collective-permute-done.12.refs_5_), channel_id=1, source_target_pairs={{0,1},{1,0},{2,3},{3,2},{4,5},{5,4},{6,7},{7,6},{8,9},{9,8},{10,11... | collective-permute-start | bytes 786440 | tf_op jit(solution)/shard_map/ppermute | solution.py:438
  62.2 12.1 %collective-permute-start.18 = (f32[512,128]{1,0:T(8,128)S(1)}, f32[512,128]{1,0:T(8,128)S(1)}, u32[]{:S(2)}, u32[]{:S(2)}) collective-permute-start(f32[512,128]{1,0:T(8,128)S(1)} %collective-permute-done.17.refs_2_), channel_id=1, source_target_pairs={{0,2},{1,3},{2,0},{3,1},{4,6},{5,7},{6,4},{7,5},{8,10},{9,11},{10,... | collective-permute-start | bytes 786440 | tf_op jit(solution)/shard_map/ppermute | solution.py:438
  63.7 11.5 %collective-permute-start.19 = (f32[512,128]{1,0:T(8,128)S(1)}, f32[512,128]{1,0:T(8,128)S(1)}, u32[]{:S(2)}, u32[]{:S(2)}) collective-permute-start(f32[512,128]{1,0:T(8,128)S(1)} %collective-permute-done.17.refs_2_), channel_id=1, source_target_pairs={{0,4},{1,5},{2,6},{3,7},{4,0},{5,1},{6,2},{7,3},{8,12},{9,13},{10,... | collective-permute-start | bytes 786440 | tf_op jit(solution)/shard_map/ppermute | solution.py:438
  65.2 11.6 %collective-permute-start.20 = (f32[512,128]{1,0:T(8,128)S(1)}, f32[512,128]{1,0:T(8,128)S(1)}, u32[]{:S(2)}, u32[]{:S(2)}) collective-permute-start(f32[512,128]{1,0:T(8,128)S(1)} %collective-permute-done.17.refs_2_), channel_id=1, source_target_pairs={{0,6},{1,7},{2,4},{3,5},{4,2},{5,3},{6,0},{7,1},{8,14},{9,15},{10,... | collective-permute-start | bytes 786440 | tf_op jit(solution)/shard_map/ppermute | solution.py:438
  65.7 12.2 %collective-permute-start.25 = (f32[512,128]{1,0:T(8,128)S(1)}, f32[512,128]{1,0:T(8,128)S(1)}, u32[]{:S(2)}, u32[]{:S(2)}) collective-permute-start(f32[512,128]{1,0:T(8,128)S(1)} %collective-permute-done.17.refs_2_), channel_id=1, source_target_pairs={{0,8},{8,16},{16,24},{24,0},{1,9},{9,17},{17,25},{25,1},{2,10},{10... | collective-permute-start | bytes 786440 | tf_op jit(solution)/shard_map/ppermute | solution.py:441
  76.9 1.8 collective-permute-start.21
  76.9 3.3 %collective-permute-start.22 = (f32[512,128]{1,0:T(8,128)S(1)}, f32[512,128]{1,0:T(8,128)S(1)}, u32[]{:S(2)}, u32[]{:S(2)}) collective-permute-start(f32[512,128]{1,0:T(8,128)S(1)} %collective-permute-done.18.refs_3_), channel_id=1, source_target_pairs={{0,1},{1,0},{2,3},{3,2},{4,5},{5,4},{6,7},{7,6},{8,9},{9,8},{10,11... | collective-permute-start | bytes 786440 | tf_op jit(solution)/shard_map/ppermute | solution.py:438
  77.4 4.0 %collective-permute-start.23 = (f32[512,128]{1,0:T(8,128)S(1)}, f32[512,128]{1,0:T(8,128)S(1)}, u32[]{:S(2)}, u32[]{:S(2)}) collective-permute-start(f32[512,128]{1,0:T(8,128)S(1)} %collective-permute-done.19.refs_4_), channel_id=1, source_target_pairs={{0,1},{1,0},{2,3},{3,2},{4,5},{5,4},{6,7},{7,6},{8,9},{9,8},{10,11... | collective-permute-start | bytes 786440 | tf_op jit(solution)/shard_map/ppermute | solution.py:438
  77.4 4.2 %collective-permute-start.24 = (f32[512,128]{1,0:T(8,128)S(1)}, f32[512,128]{1,0:T(8,128)S(1)}, u32[]{:S(2)}, u32[]{:S(2)}) collective-permute-start(f32[512,128]{1,0:T(8,128)S(1)} %collective-permute-done.20.refs_5_), channel_id=1, source_target_pairs={{0,1},{1,0},{2,3},{3,2},{4,5},{5,4},{6,7},{7,6},{8,9},{9,8},{10,11... | collective-permute-start | bytes 786440 | tf_op jit(solution)/shard_map/ppermute | solution.py:438
  77.9 12.3 %collective-permute-start.26 = (f32[512,128]{1,0:T(8,128)S(1)}, f32[512,128]{1,0:T(8,128)S(1)}, u32[]{:S(2)}, u32[]{:S(2)}) collective-permute-start(f32[512,128]{1,0:T(8,128)S(1)} %collective-permute-done.25.refs_2_), channel_id=1, source_target_pairs={{0,2},{1,3},{2,0},{3,1},{4,6},{5,7},{6,4},{7,5},{8,10},{9,11},{10,... | collective-permute-start | bytes 786440 | tf_op jit(solution)/shard_map/ppermute | solution.py:438
  78.7 13.7 %collective-permute-start.27 = (f32[512,128]{1,0:T(8,128)S(1)}, f32[512,128]{1,0:T(8,128)S(1)}, u32[]{:S(2)}, u32[]{:S(2)}) collective-permute-start(f32[512,128]{1,0:T(8,128)S(1)} %collective-permute-done.25.refs_2_), channel_id=1, source_target_pairs={{0,4},{1,5},{2,6},{3,7},{4,0},{5,1},{6,2},{7,3},{8,12},{9,13},{10,... | collective-permute-start | bytes 786440 | tf_op jit(solution)/shard_map/ppermute | solution.py:438
  80.2 12.2 %collective-permute-start.28 = (f32[512,128]{1,0:T(8,128)S(1)}, f32[512,128]{1,0:T(8,128)S(1)}, u32[]{:S(2)}, u32[]{:S(2)}) collective-permute-start(f32[512,128]{1,0:T(8,128)S(1)} %collective-permute-done.25.refs_2_), channel_id=1, source_target_pairs={{0,6},{1,7},{2,4},{3,5},{4,2},{5,3},{6,0},{7,1},{8,14},{9,15},{10,... | collective-permute-start | bytes 786440 | tf_op jit(solution)/shard_map/ppermute | solution.py:438
  81.4 12.0 %collective-permute-start.33 = (f32[512,128]{1,0:T(8,128)S(1)}, f32[512,128]{1,0:T(8,128)S(1)}, u32[]{:S(2)}, u32[]{:S(2)}) collective-permute-start(f32[512,128]{1,0:T(8,128)S(1)} %collective-permute-done.25.refs_2_), channel_id=1, source_target_pairs={{0,8},{8,16},{16,24},{24,0},{1,9},{9,17},{17,25},{25,1},{2,10},{10... | collective-permute-start | bytes 786440 | tf_op jit(solution)/shard_map/ppermute | solution.py:441
  92.4 1.5 collective-permute-start.29
  92.4 3.5 %collective-permute-start.30 = (f32[512,128]{1,0:T(8,128)S(1)}, f32[512,128]{1,0:T(8,128)S(1)}, u32[]{:S(2)}, u32[]{:S(2)}) collective-permute-start(f32[512,128]{1,0:T(8,128)S(1)} %collective-permute-done.26.refs_3_), channel_id=1, source_target_pairs={{0,1},{1,0},{2,3},{3,2},{4,5},{5,4},{6,7},{7,6},{8,9},{9,8},{10,11... | collective-permute-start | bytes 786440 | tf_op jit(solution)/shard_map/ppermute | solution.py:438
  92.9 4.3 %collective-permute-start.31 = (f32[512,128]{1,0:T(8,128)S(1)}, f32[512,128]{1,0:T(8,128)S(1)}, u32[]{:S(2)}, u32[]{:S(2)}) collective-permute-start(f32[512,128]{1,0:T(8,128)S(1)} %collective-permute-done.27.refs_4_), channel_id=1, source_target_pairs={{0,1},{1,0},{2,3},{3,2},{4,5},{5,4},{6,7},{7,6},{8,9},{9,8},{10,11... | collective-permute-start | bytes 786440 | tf_op jit(solution)/shard_map/ppermute | solution.py:438
  92.9 5.4 %collective-permute-start.32 = (f32[512,128]{1,0:T(8,128)S(1)}, f32[512,128]{1,0:T(8,128)S(1)}, u32[]{:S(2)}, u32[]{:S(2)}) collective-permute-start(f32[512,128]{1,0:T(8,128)S(1)} %collective-permute-done.28.refs_5_), channel_id=1, source_target_pairs={{0,1},{1,0},{2,3},{3,2},{4,5},{5,4},{6,7},{7,6},{8,9},{9,8},{10,11... | collective-permute-start | bytes 786440 | tf_op jit(solution)/shard_map/ppermute | solution.py:438
  93.4 17.3 %collective-permute-start.41 = (f32[64,512]{1,0:T(8,128)S(1)}, f32[64,512]{1,0:T(8,128)S(1)}, u32[]{:S(2)}, u32[]{:S(2)}) collective-permute-start(f32[64,512]{1,0:T(8,128)S(1)} %get-tuple-element.131), channel_id=1, source_target_pairs={{0,8},{8,16},{16,24},{24,0},{1,9},{9,17},{17,25},{25,1},{2,10},{10... | collective-permute-start | bytes 393224 | tf_op jit(solution)/shard_map/ppermute | solution.py:441
  93.9 17.3 %collective-permute-start.42 = (f32[64,512]{1,0:T(8,128)S(1)}, f32[64,512]{1,0:T(8,128)S(1)}, u32[]{:S(2)}, u32[]{:S(2)}) collective-permute-start(f32[64,512]{1,0:T(8,128)S(1)} %get-tuple-element.132), channel_id=1, source_target_pairs={{0,16},{8,24},{16,0},{24,8},{1,17},{9,25},{17,1},{25,9},{2,18},{10... | collective-permute-start | bytes 393224 | tf_op jit(solution)/shard_map/ppermute | solution.py:441
  95.9 12.0 %collective-permute-start.34 = (f32[512,128]{1,0:T(8,128)S(1)}, f32[512,128]{1,0:T(8,128)S(1)}, u32[]{:S(2)}, u32[]{:S(2)}) collective-permute-start(f32[512,128]{1,0:T(8,128)S(1)} %collective-permute-done.33.refs_2_), channel_id=1, source_target_pairs={{0,2},{1,3},{2,0},{3,1},{4,6},{5,7},{6,4},{7,5},{8,10},{9,11},{10,... | collective-permute-start | bytes 786440 | tf_op jit(solution)/shard_map/ppermute | solution.py:438
  97.1 11.7 %collective-permute-start.35 = (f32[512,128]{1,0:T(8,128)S(1)}, f32[512,128]{1,0:T(8,128)S(1)}, u32[]{:S(2)}, u32[]{:S(2)}) collective-permute-start(f32[512,128]{1,0:T(8,128)S(1)} %collective-permute-done.33.refs_2_), channel_id=1, source_target_pairs={{0,4},{1,5},{2,6},{3,7},{4,0},{5,1},{6,2},{7,3},{8,12},{9,13},{10,... | collective-permute-start | bytes 786440 | tf_op jit(solution)/shard_map/ppermute | solution.py:438
  98.3 11.9 %collective-permute-start.36 = (f32[512,128]{1,0:T(8,128)S(1)}, f32[512,128]{1,0:T(8,128)S(1)}, u32[]{:S(2)}, u32[]{:S(2)}) collective-permute-start(f32[512,128]{1,0:T(8,128)S(1)} %collective-permute-done.33.refs_2_), channel_id=1, source_target_pairs={{0,6},{1,7},{2,4},{3,5},{4,2},{5,3},{6,0},{7,1},{8,14},{9,15},{10,... | collective-permute-start | bytes 786440 | tf_op jit(solution)/shard_map/ppermute | solution.py:438
  110.1 8.1 %collective-permute-start.37 = (f32[512,128]{1,0:T(8,128)S(1)}, f32[512,128]{1,0:T(8,128)S(1)}, u32[]{:S(2)}, u32[]{:S(2)}) collective-permute-start(f32[512,128]{1,0:T(8,128)S(1)} %collective-permute-done.33.refs_2_), channel_id=1, source_target_pairs={{0,1},{1,0},{2,3},{3,2},{4,5},{5,4},{6,7},{7,6},{8,9},{9,8},{10,11... | collective-permute-start | bytes 786440 | tf_op jit(solution)/shard_map/ppermute | solution.py:438
  110.1 9.5 %collective-permute-start.38 = (f32[512,128]{1,0:T(8,128)S(1)}, f32[512,128]{1,0:T(8,128)S(1)}, u32[]{:S(2)}, u32[]{:S(2)}) collective-permute-start(f32[512,128]{1,0:T(8,128)S(1)} %collective-permute-done.34.refs_3_), channel_id=1, source_target_pairs={{0,1},{1,0},{2,3},{3,2},{4,5},{5,4},{6,7},{7,6},{8,9},{9,8},{10,11... | collective-permute-start | bytes 786440 | tf_op jit(solution)/shard_map/ppermute | solution.py:438
  110.6 10.2 %collective-permute-start.39 = (f32[512,128]{1,0:T(8,128)S(1)}, f32[512,128]{1,0:T(8,128)S(1)}, u32[]{:S(2)}, u32[]{:S(2)}) collective-permute-start(f32[512,128]{1,0:T(8,128)S(1)} %collective-permute-done.35.refs_4_), channel_id=1, source_target_pairs={{0,1},{1,0},{2,3},{3,2},{4,5},{5,4},{6,7},{7,6},{8,9},{9,8},{10,11... | collective-permute-start | bytes 786440 | tf_op jit(solution)/shard_map/ppermute | solution.py:438
  110.6 10.2 %collective-permute-start.40 = (f32[512,128]{1,0:T(8,128)S(1)}, f32[512,128]{1,0:T(8,128)S(1)}, u32[]{:S(2)}, u32[]{:S(2)}) collective-permute-start(f32[512,128]{1,0:T(8,128)S(1)} %collective-permute-done.36.refs_5_), channel_id=1, source_target_pairs={{0,1},{1,0},{2,3},{3,2},{4,5},{5,4},{6,7},{7,6},{8,9},{9,8},{10,11... | collective-permute-start | bytes 786440 | tf_op jit(solution)/shard_map/ppermute | solution.py:438
  111.1 5.5 %collective-permute-start.43 = (f32[64,512]{1,0:T(8,128)S(1)}, f32[64,512]{1,0:T(8,128)S(1)}, u32[]{:S(2)}, u32[]{:S(2)}) collective-permute-start(f32[64,512]{1,0:T(8,128)S(1)} %get-tuple-element.133), channel_id=1, source_target_pairs={{0,24},{8,0},{16,8},{24,16},{1,25},{9,1},{17,9},{25,17},{2,26},{10... | collective-permute-start | bytes 393224 | tf_op jit(solution)/shard_map/ppermute | solution.py:441
  117.3 12.3 %collective-permute-start.44 = (f32[64,512]{1,0:T(8,128)S(1)}, f32[64,512]{1,0:T(8,128)S(1)}, u32[]{:S(2)}, u32[]{:S(2)}) collective-permute-start(f32[64,512]{1,0:T(8,128)S(1)} %get-tuple-element.135), channel_id=1, source_target_pairs={{0,2},{1,3},{2,0},{3,1},{4,6},{5,7},{6,4},{7,5},{8,10},{9,11},{10,... | collective-permute-start | bytes 393224 | tf_op jit(solution)/shard_map/ppermute | solution.py:438
  118.2 11.3 %collective-permute-start.45 = (f32[64,512]{1,0:T(8,128)S(1)}, f32[64,512]{1,0:T(8,128)S(1)}, u32[]{:S(2)}, u32[]{:S(2)}) collective-permute-start(f32[64,512]{1,0:T(8,128)S(1)} %get-tuple-element.136), channel_id=1, source_target_pairs={{0,4},{1,5},{2,6},{3,7},{4,0},{5,1},{6,2},{7,3},{8,12},{9,13},{10,... | collective-permute-start | bytes 393224 | tf_op jit(solution)/shard_map/ppermute | solution.py:438
  119.6 9.9 %collective-permute-start.46 = (f32[64,512]{1,0:T(8,128)S(1)}, f32[64,512]{1,0:T(8,128)S(1)}, u32[]{:S(2)}, u32[]{:S(2)}) collective-permute-start(f32[64,512]{1,0:T(8,128)S(1)} %get-tuple-element.137), channel_id=1, source_target_pairs={{0,6},{1,7},{2,4},{3,5},{4,2},{5,3},{6,0},{7,1},{8,14},{9,15},{10,... | collective-permute-start | bytes 393224 | tf_op jit(solution)/shard_map/ppermute | solution.py:438
  134.2 2.0 collective-permute-start.47
  145.4 2.0 collective-permute-start.48
  156.7 2.0 collective-permute-start.49
  168.7 2.0 collective-permute-start.50
  170.7 1.0 copy-start.1
  172.3 10.2 %collective-permute-start.53 = (f32[64,512]{1,0:T(8,128)S(1)}, f32[64,512]{1,0:T(8,128)S(1)}, u32[]{:S(2)}, u32[]{:S(2)}) collective-permute-start(f32[64,512]{1,0:T(8,128)S(1)} %get-tuple-element.168), channel_id=1, source_target_pairs={{0,6},{1,7},{2,4},{3,5},{4,2},{5,3},{6,0},{7,1},{8,14},{9,15},{10,... | collective-permute-start | bytes 393224 | tf_op jit(solution)/shard_map/ppermute | solution.py:438
  174.1 10.9 %collective-permute-start.52 = (f32[64,512]{1,0:T(8,128)S(1)}, f32[64,512]{1,0:T(8,128)S(1)}, u32[]{:S(2)}, u32[]{:S(2)}) collective-permute-start(f32[64,512]{1,0:T(8,128)S(1)} %get-tuple-element.169), channel_id=1, source_target_pairs={{0,4},{1,5},{2,6},{3,7},{4,0},{5,1},{6,2},{7,3},{8,12},{9,13},{10,... | collective-permute-start | bytes 393224 | tf_op jit(solution)/shard_map/ppermute | solution.py:438
  174.7 10.3 %collective-permute-start.51 = (f32[64,512]{1,0:T(8,128)S(1)}, f32[64,512]{1,0:T(8,128)S(1)}, u32[]{:S(2)}, u32[]{:S(2)}) collective-permute-start(f32[64,512]{1,0:T(8,128)S(1)} %get-tuple-element.170), channel_id=1, source_target_pairs={{0,2},{1,3},{2,0},{3,1},{4,6},{5,7},{6,4},{7,5},{8,10},{9,11},{10,... | collective-permute-start | bytes 393224 | tf_op jit(solution)/shard_map/ppermute | solution.py:438
  175.8 9.3 %collective-permute-start.55 = (f32[64,512]{1,0:T(8,128)S(1)}, f32[64,512]{1,0:T(8,128)S(1)}, u32[]{:S(2)}, u32[]{:S(2)}) collective-permute-start(f32[64,512]{1,0:T(8,128)S(1)} %get-tuple-element.166), channel_id=1, source_target_pairs={{0,24},{2,26},{4,28},{6,30},{8,0},{10,2},{12,4},{14,6},{17,9},{19,... | collective-permute-start | bytes 393224 | tf_op jit(solution)/shard_map/ppermute | solution.py:540
  181.1 5.2 %collective-permute-start.56 = (f32[64,512]{1,0:T(8,128)S(1)}, f32[64,512]{1,0:T(8,128)S(1)}, u32[]{:S(2)}, u32[]{:S(2)}) collective-permute-start(f32[64,512]{1,0:T(8,128)S(1)} %get-tuple-element.165), channel_id=1, source_target_pairs={{0,16},{2,18},{4,20},{6,22},{8,24},{10,26},{12,28},{14,30},{17,1},... | collective-permute-start | bytes 393224 | tf_op jit(solution)/shard_map/ppermute | solution.py:540
  182.5 6.7 %collective-permute-start.57 = (f32[64,512]{1,0:T(8,128)S(1)}, f32[64,512]{1,0:T(8,128)S(1)}, u32[]{:S(2)}, u32[]{:S(2)}) collective-permute-start(f32[64,512]{1,0:T(8,128)S(1)} %get-tuple-element.164), channel_id=1, source_target_pairs={{0,8},{2,10},{4,12},{6,14},{8,16},{10,18},{12,20},{14,22},{17,25},... | collective-permute-start | bytes 393224 | tf_op jit(solution)/shard_map/ppermute | solution.py:540
  185.0 12.6 %collective-permute-start.54 = (f32[256,512]{1,0:T(8,128)S(1)}, f32[256,512]{1,0:T(8,128)S(1)}, u32[]{:S(2)}, u32[]{:S(2)}) collective-permute-start(f32[256,512]{1,0:T(8,128)S(1)} %pad_maximum_fusion.refs_0_), channel_id=1, source_target_pairs={{0,8},{8,16},{16,24},{24,0},{1,9},{9,17},{17,25},{25,1},{2,10},{10... | collective-permute-start | bytes 1572872 | tf_op jit(solution)/shard_map/ppermute | solution.py:441
  197.7 16.1 %collective-permute-start.58 = (f32[256,512]{1,0:T(8,128)S(1)}, f32[256,512]{1,0:T(8,128)S(1)}, u32[]{:S(2)}, u32[]{:S(2)}) collective-permute-start(f32[256,512]{1,0:T(8,128)S(1)} %collective-permute-done.54.refs_1_), channel_id=1, source_target_pairs={{0,8},{8,16},{16,24},{24,0},{1,9},{9,17},{17,25},{25,1},{2,10},{10... | collective-permute-start | bytes 1572872 | tf_op jit(solution)/shard_map/ppermute | solution.py:441
  213.8 15.3 %collective-permute-start.59 = (f32[256,512]{1,0:T(8,128)S(1)}, f32[256,512]{1,0:T(8,128)S(1)}, u32[]{:S(2)}, u32[]{:S(2)}) collective-permute-start(f32[256,512]{1,0:T(8,128)S(1)} %collective-permute-done.58.refs_2_), channel_id=1, source_target_pairs={{0,8},{8,16},{16,24},{24,0},{1,9},{9,17},{17,25},{25,1},{2,10},{10... | collective-permute-start | bytes 1572872 | tf_op jit(solution)/shard_map/ppermute | solution.py:441
  (1 other events, 0.8 us)

commit v8 on v6

--- a/solution.py
+++ b/solution.py
@@ -371,33 +371,63 @@
     )(*arrays)
 
 
-def place_kernel(slots, where_ref, part_ref, *refs):
-    out_ref, held = refs[-2:]
-    rows = part_ref.shape[0] // slots
-    for k in range(slots):
-        at = pl.multiple_of(where_ref[1 + k] * rows, rows)
-        held[pl.ds(at, rows), :] = part_ref[k * rows:(k + 1) * rows, :]
-    out_ref[...] = held[...].T
-
-
-def place(where, part, out, shape):
-    operands, in_specs = [part], [pl.BlockSpec(part.shape, lambda i, where: (0, 0))]
-    if out is not None:
-        operands.append(out)
-        in_specs.append(pl.BlockSpec(memory_space=pl.ANY))
-    return pl.pallas_call(
-        functools.partial(place_kernel, where.shape[0] - 1),
-        out_shape=jax.ShapeDtypeStruct(shape, F32),
+def arrange_kernel(count, origin_ref, *refs):
+    parts, outs, held = refs[:count], refs[count:-1], refs[-1]
+    rows = parts[0].shape[0]
+    for k, part in enumerate(parts):
+        held[k * rows:(k + 1) * rows, :] = part[...]
+    for k, out in enumerate(outs):
+        out[...] = held[pl.ds(pl.multiple_of(origin_ref[k] * rows, rows), rows), :]
+
+
+def arrange(origin, parts):
+    rows, columns = parts[0].shape
+    whole = pl.BlockSpec((rows, columns), lambda i, origin: (0, 0))
+    return pl.pallas_call(
+        functools.partial(arrange_kernel, len(parts)),
+        out_shape=(jax.ShapeDtypeStruct((rows, columns), F32),) * origin.shape[0],
         grid_spec=pltpu.PrefetchScalarGridSpec(
             num_scalar_prefetch=1,
             grid=(1,),
-            in_specs=in_specs,
-            out_specs=pl.BlockSpec((shape[0], part.shape[0]), lambda i, where: (0, where[0])),
-            scratch_shapes=[pltpu.VMEM(part.shape, F32)],
-        ),
-        input_output_aliases={} if out is None else {2: 0},
+            in_specs=[whole] * len(parts),
+            out_specs=[whole] * origin.shape[0],
+            scratch_shapes=[pltpu.VMEM((len(parts) * rows, columns), F32)],
+        ),
+        compiler_params=pltpu.CompilerParams(vmem_limit_bytes=8 * MIB),
+    )(origin, *parts)
+
+
+def place_kernel(slots, count, where_ref, *refs):
+    arrays, out_ref, held = refs[:count], refs[count], refs[count + 1]
+    rows = arrays[0].shape[0] // slots
+    k = where_ref[pl.program_id(0)]
+    for number, array in enumerate(arrays):
+        to = where_ref[slots + number]
+
+        @pl.when(to >= 0)
+        def _():
+            held[pl.ds(pl.multiple_of(to * rows, rows), rows), :] = array[
+                pl.ds(pl.multiple_of(k * rows, rows), rows), :
+            ]
+
+    out_ref[...] = held[...].T
+
+
+def place(where, arrays, slots, planes):
+    rows, comps = arrays[0].shape[0] // slots * planes, arrays[0].shape[1]
+    whole = pl.BlockSpec(arrays[0].shape, lambda i, where: (0, 0))
+    return pl.pallas_call(
+        functools.partial(place_kernel, slots, len(arrays)),
+        out_shape=jax.ShapeDtypeStruct((comps, slots * rows), F32),
+        grid_spec=pltpu.PrefetchScalarGridSpec(
+            num_scalar_prefetch=1,
+            grid=(slots,),
+            in_specs=[whole] * len(arrays),
+            out_specs=pl.BlockSpec((comps, rows), lambda i, where: (0, i)),
+            scratch_shapes=[pltpu.VMEM((rows, comps), F32)],
+        ),
         compiler_params=pltpu.CompilerParams(vmem_limit_bytes=24 * MIB),
-    )(where, *operands)
+    )(where, *arrays)
 
 
 def per_device(n_dp, n_t, activations, out_grads, proj_in, proj_out, example_ids, queries):
@@ -421,8 +451,11 @@
 
     near_chip = [chip ^ k for k in range(n_c)]
 
-    q_chip = queries.shape[0] // n_c
-    slots = [lax.dynamic_slice_in_dim(queries, near_chip[k] * q_chip, q_chip, 0) for k in range(n_c)]
+    q_chip = queries.shape[0] // n_dp
+    parts = [
+        lax.dynamic_slice_in_dim(queries, (i + away) % n_dp * q_chip, q_chip, 0) for away in range(n_dp)
+    ]
+    origin = jnp.stack([(i - near_chip[k]) % n_dp for k in range(n_c)]).astype(jnp.int32)
 
     group = 8
     bounds = group * jnp.arange(EX_DEV // group, dtype=jnp.int32)
@@ -463,12 +496,15 @@
     offs = jnp.stack(
         [near_chip[k] * 2 + which for which in (core, 1 - core) for k in range(n_c)]
     ).astype(jnp.int32)
-    offs, pick, plane_ids, firsts, slots = lax.optimization_barrier(
-        (offs, pick, plane_ids, firsts, slots)
+    offs, pick, plane_ids, firsts, parts, origin = lax.optimization_barrier(
+        (offs, pick, plane_ids, firsts, parts, origin)
     )
 
     highs, lows, squares = [], [], []
     for away in range(n_dp):
+        if away == n_dp // 2:
+            slots = arrange(origin, [parts[0]] + [shift(parts[k], k) for k in range(1, n_dp)])
+            pick = tie(pick, slots)
         piece = rings[away]
         near = [piece] + [swap(piece, 2 * k) for k in range(1, n_c)]
         sources = near + [
@@ -493,41 +529,38 @@
     other = swap(message, 1)
     x, y = last_step(examples, comps_all, message, other, r, *rest)
 
-    n_half = n_c // 2
+    n_half = n_dp // 2
     per_slot = comps_all // n_t
 
-    def send(values, to):
+    def send(values, by):
         pairs = [
-            (di * n_t + 2 * c + c // n_half, to(di, c, c // n_half))
-            for di in range(n_dp) for c in range(n_c)
+            (a * n_t + 2 * c + a // n_half, (a + by) % n_dp * n_t + 2 * c + a // n_half)
+            for a in range(n_dp) for c in range(n_c)
         ]
         return lax.ppermute(values, ("dp", "tensor"), pairs)
 
-    ring = [x[:, k * per_slot:(k + 1) * per_slot] for k in range(n_c)]
-    ring = jnp.concatenate([ring[0]] + [swap(ring[k], 2 * k) for k in range(1, n_c)], axis=0)
-    y = tie(y, ring)
     by_plane = jnp.zeros((n_dp, q_chip, EX_DEV), F32)
     for away in range(n_dp):
         part = y[:, away * EX_DEV:(away + 1) * EX_DEV]
         if away:
-            part = send(part, lambda di, c, h: ((di - away) % n_dp) * n_t + 2 * c + h)
+            part = send(part, -away)
         by_plane = lax.dynamic_update_slice(by_plane, part[None], ((i + away) % n_dp, 0, 0))
-    by_chip = jnp.zeros((n_c, q_chip, EX_DEV), F32)
-    for k in range(n_c):
-        part = lax.dynamic_slice_in_dim(by_plane, near_chip[k], 1, 0)
-        if k:
-            part = send(part, lambda di, c, h: di * n_t + 2 * (c ^ k) + h)
-        by_chip = lax.dynamic_update_slice(by_chip, part, (near_chip[k], 0, 0))
-    scores = lax.dynamic_slice_in_dim(by_chip, core * n_half, n_half, 0)
-
-    outs = [None]
-    for away in range(n_dp):
-        if away:
-            before = [[], [by_plane, outs[-2]], [scores, outs[-2]]][min(away - 1, 2)]
-            ring = shift(tie(ring, before) if before else ring, 1)
-        where = jnp.stack([(i - away) % n_dp] + near_chip).astype(jnp.int32)
-        outs.append(place(where, ring, outs[-1], (per_slot, n_dp * n_c * q_chip)))
-    return (outs[-1], scores.reshape((n_half * q_chip, EX_DEV)))
+    scores = lax.dynamic_slice_in_dim(by_plane, core * n_half, n_half, 0)
+
+    ring = [x[:, k * per_slot:(k + 1) * per_slot] for k in range(n_c)]
+    ring = jnp.concatenate([ring[0]] + [swap(ring[k], 2 * k) for k in range(1, n_c)], axis=0)
+    arrays, places = [ring], [i]
+    ups = downs = ring
+    for away in range(1, n_dp):
+        if away == 2:
+            ups, downs = tie((ups, downs), scores)
+        ups = lax.ppermute(ups, "dp", [(a, a + 1) for a in range(away - 1, n_dp - 1)])
+        downs = lax.ppermute(downs, "dp", [(a, a - 1) for a in range(1, n_dp - away + 1)])
+        arrays += [ups, downs]
+        places += [jnp.maximum(i - away, -1), jnp.where(i + away < n_dp, i + away, -1)]
+    where = jnp.stack([chip ^ c for c in range(n_c)] + places).astype(jnp.int32)
+    out = place(where, arrays, n_c, n_dp)
+    return (out, scores.reshape((n_half * q_chip, EX_DEV)))
 
 
 def solution(mesh):

time: 223 us -> 233 us (1.045)
  waiting for transfers between devices: 75.5 us -> 81.1 us
  starting transfers between devices: 52.2 us -> 54.7 us
    ppermute x0 -> x6, waiting for transfers between devices: none -> 40.5 us  [the longest x3 32.3 us: per_device(): lax.ppermute(downs, 'dp', [(a, a - 1) for a in range(1, n_dp - away + 1)])]
    ppermute x6 -> x3, waiting for transfers between devices: 16.7 us -> 0.46 us  [send(): return lax.ppermute(values, ('dp', 'tensor'), pairs)]
    ppermute x9, waiting for transfers between devices: 23.1 us -> 9 us  [shift(): lax.ppermute(values, 'dp', [(a, (a + by) % n_dp) for a in range(n_dp)])]
    ppermute x6 -> x3, starting transfers between devices: 17.3 us -> 7.1 us  [send(): return lax.ppermute(values, ('dp', 'tensor'), pairs)]
    ppermute x0 -> x6, starting transfers between devices: none -> 7.19 us  [the longest x3 3.86 us: per_device(): lax.ppermute(downs, 'dp', [(a, a - 1) for a in range(1, n_dp - away + 1)])]
    ppermute x9, starting transfers between devices: 5.54 us -> 11.8 us  [shift(): lax.ppermute(values, 'dp', [(a, (a + by) % n_dp) for a in range(n_dp)])]
    ppermute x42, waiting for transfers between devices: 35.8 us -> 31.1 us  [swap(): return lax.ppermute(values, 'tensor', [(a, a ^ mask) for a in range(n_t)])]
    pallas_call x4 -> x2, Pallas kernels: 6.3 us -> 4.63 us  [the longest x1 4.02 us: place(): pl.pallas_call(functools.partial(place_kernel, slots, len(arrays)), out_s...]
  transfers between devices with their start and end apart: 57 -> 60, of which waited for: 21 -> 22; matrix products, arithmetic and copies ran while one was open for 2% -> 2% of each run, Pallas kernels for 21% -> 18%
where the time goes in v8:
time: 233 us
  Pallas kernels  87.3 us (37%)
  waiting for transfers between devices  81.1 us (35%)
  starting transfers between devices  54.7 us (23%)
  other arithmetic  4.53 us (2%)
  local copies, waits for them, and re-layouts  3.84 us (2%)
    pallas_call x4, Pallas kernels, build(): pl.pallas_call(functools.partial(build_kernel, ranks, share, ex_block, le...  34.2 us
    ppermute x3, waiting for transfers between devices, per_device(): lax.ppermute(downs, 'dp', [(a, a - 1) for a in range(1, n_dp - away + 1)])  32.3 us
    ppermute x42, waiting for transfers between devices, swap(): return lax.ppermute(values, 'tensor', [(a, a ^ mask) for a in range(n_t)])  31.1 us
    ppermute x42, starting transfers between devices, swap(): return lax.ppermute(values, 'tensor', [(a, a ^ mask) for a in range(n_t)])  28.7 us
    pallas_call x3, Pallas kernels, one_step(): pl.pallas_call(functools.partial(step_kernel, first, planes, examples, co...  27.9 us
    pallas_call x2, Pallas kernels, project(): pl.pallas_call(project_kernel, out_shape=jax.ShapeDtypeStruct((steps * bl...  15.5 us
    ppermute x9, starting transfers between devices, shift(): lax.ppermute(values, 'dp', [(a, (a + by) % n_dp) for a in range(n_dp)])  11.8 us
    ppermute x9, waiting for transfers between devices, shift(): lax.ppermute(values, 'dp', [(a, (a + by) % n_dp) for a in range(n_dp)])  9 us
  transfers between devices with their start and end apart: 60, of which 22 were waited for; matrix products, arithmetic and copies ran while one was open for 2% of the time, Pallas kernels for 18%

profile of v8, /device:TPU:0, one launch (start us, length us, event | category | flops | bytes accessed | tf_op | source)
XLA Modules:
  0.0 232.7 jit_solution(12432266476800788336)
XLA Ops:
  0.7 0.7 convert_element_type.36
  1.4 1.0 convert_reduce_fusion
  3.5 7.8 %shard_map.77 = f32[2048,128]{1,0:T(8,128)} custom-call(s32[4]{0:T(128)} %add_subtract_fusion.order_ref, bf16[4096,512]{1,0:T(8,128)(2,1)} %refs_3_.3, bf16[4096,512]{1,0:T(8,128)(2,1)} %refs_3_.3, bf16[4096,512]{1,0:T(8,128)(2,1)} %refs_3_.3, bf16[4096,512]{1,0:T(8,128)(2,1)} %refs_3_.3, bf16[4096,1792]{1,0:T(8,128)(2,1)} %refs_7_.3, ...), custom_call_target="tpu_custom_call" | custom-call | flops 9663676416 | bytes 9437184 | tf_op jit(solution)/shard_map/pallas_call | solution.py:58
  11.3 3.0 %collective-permute-start = (f32[40,128]{1,0:T(8,128)S(1)}, f32[40,128]{1,0:T(8,128)S(1)}, u32[]{:S(2)}, u32[]{:S(2)}) collective-permute-start(f32[40,128]{1,0:T(8,128)S(1)} %select_maximum_fusion), channel_id=1, source_target_pairs={{0,8},{8,16},{16,24},{24,0},{1,9},{9,17},{17,25},{25,1},{2,10},{10... | collective-permute-start | bytes 61448 | tf_op jit(solution)/shard_map/ppermute | solution.py:447
  14.3 2.6 %collective-permute-start.1 = (f32[40,128]{1,0:T(8,128)S(1)}, f32[40,128]{1,0:T(8,128)S(1)}, u32[]{:S(2)}, u32[]{:S(2)}) collective-permute-start(f32[40,128]{1,0:T(8,128)S(1)} %select_maximum_fusion), channel_id=1, source_target_pairs={{0,16},{8,24},{16,0},{24,8},{1,17},{9,25},{17,1},{25,9},{2,18},{10... | collective-permute-start | bytes 61448 | tf_op jit(solution)/shard_map/ppermute | solution.py:447
  16.9 7.7 %shard_map.78 = f32[2048,128]{1,0:T(8,128)} custom-call(s32[4]{0:T(128)} %get-tuple-element.146.order_ref, bf16[4096,512]{1,0:T(8,128)(2,1)} %refs_3_.3, bf16[4096,512]{1,0:T(8,128)(2,1)} %refs_3_.3, bf16[4096,512]{1,0:T(8,128)(2,1)} %refs_3_.3, bf16[4096,512]{1,0:T(8,128)(2,1)} %refs_3_.3, bf16[4096,1792]{1,0:T(8,128)(2,1)} %refs_7_.3, ...), custom_call_target="tpu_custom_call" | custom-call | flops 9663676416 | bytes 9437184 | tf_op jit(solution)/shard_map/pallas_call | solution.py:58
  24.6 1.4 add.396
  26.1 2.5 %collective-permute-start.6 = (f32[512,128]{1,0:T(8,128)S(1)}, f32[512,128]{1,0:T(8,128)S(1)}, u32[]{:S(2)}, u32[]{:S(2)}) collective-permute-start(f32[512,128]{1,0:T(8,128)S(1)} %get-tuple-element.149), channel_id=1, source_target_pairs={{0,6},{1,7},{2,4},{3,5},{4,2},{5,3},{6,0},{7,1},{8,14},{9,15},{10,... | collective-permute-start | bytes 786440 | tf_op jit(solution)/shard_map/ppermute | solution.py:444
  29.7 0.7 constant_dynamic-slice_fusion.1
  30.6 5.6 %collective-permute-done.6 = f32[512,128]{1,0:T(8,128)S(1)} collective-permute-done((f32[512,128]{1,0:T(8,128)S(1)}, f32[512,128]{1,0:T(8,128)S(1)}, u32[]{:S(2)}, u32[]{:S(2)}) %collective-permute-start.6) | collective-permute-done | bytes 262176 | tf_op jit(solution)/shard_map/ppermute | solution.py:444
  36.2 5.2 %collective-permute-done.5 = f32[512,128]{1,0:T(8,128)S(1)} collective-permute-done((f32[512,128]{1,0:T(8,128)S(1)}, f32[512,128]{1,0:T(8,128)S(1)}, u32[]{:S(2)}, u32[]{:S(2)}) %collective-permute-start.5) | collective-permute-done | bytes 262176 | tf_op jit(solution)/shard_map/ppermute | solution.py:444
  41.6 1.5 collective-permute-start.7
  43.1 0.7 collective-permute-start.8
  43.9 1.3 collective-permute-start.9
  45.3 1.4 collective-permute-start.2
  46.7 2.4 %collective-permute-done.2 = f32[40,128]{1,0:T(8,128)S(1)} collective-permute-done((f32[40,128]{1,0:T(8,128)S(1)}, f32[40,128]{1,0:T(8,128)S(1)}, u32[]{:S(2)}, u32[]{:S(2)}) %collective-permute-start.2) | collective-permute-done | bytes 20512 | tf_op jit(solution)/shard_map/ppermute | solution.py:447
  49.4 1.5 collective-permute-done.7.refs_3_
  50.8 5.8 %collective-permute-done.8.refs_4_ = f32[512,128]{1,0:T(8,128)S(1)} collective-permute-done((f32[512,128]{1,0:T(8,128)S(1)}, f32[512,128]{1,0:T(8,128)S(1)}, u32[]{:S(2)}, u32[]{:S(2)}) %collective-permute-start.8) | collective-permute-done | bytes 262176 | tf_op jit(solution)/shard_map/ppermute | solution.py:444
  57.4 1.5 collective-permute-start.15
  59.5 1.4 collective-permute-start.17
  61.0 8.5 %shard_map.79 = (bf16[512,2048]{1,0:T(8,128)(2,1)S(1)}, bf16[512,2048]{1,0:T(8,128)(2,1)S(1)}, f32[8,128]{1,0:T(8,128)S(1)}) custom-call(s32[8]{0:T(128)S(1)} %stack.204.refs_0_, s32[64]{0:T(128)S(1)} %convert_bitcast_fusion.refs_1_, f32[512,128]{1,0:T(8,128)S(1)} %fusion.1.refs_2_, f32[512,128]{1,0:T(8,128)S(1)} %collective-permute-done.7.refs_3_, ...), custom_call_target="tpu_custom_call" | custom-call | flops 12884901888 | bytes 6291456 | tf_op jit(solution)/shard_map/pallas_call | solution.py:171
  69.6 1.8 collective-permute-done.16.refs_4_
  72.4 1.5 collective-permute-start.23
  74.1 2.3 collective-permute-start.31
  76.5 1.4 collective-permute-start.32
  78.4 2.3 collective-permute-done.23.refs_3_
  80.6 1.3 collective-permute-start.25
  82.0 8.5 %shard_map.80 = (bf16[512,2048]{1,0:T(8,128)(2,1)S(1)}, bf16[512,2048]{1,0:T(8,128)(2,1)S(1)}, f32[8,128]{1,0:T(8,128)S(1)}) custom-call(s32[8]{0:T(128)S(1)} %stack.204.refs_0_, s32[64]{0:T(128)S(1)} %fusion.5.refs_1_, f32[512,128]{1,0:T(8,128)S(1)} %collective-permute-done.14.refs_2_, f32[512,128]{1,0:T(8,128)S(1)} %collective-permute-done.15.refs_3_, ...), custom_call_target="tpu_custom_call" | custom-call | flops 12884901888 | bytes 6291456 | tf_op jit(solution)/shard_map/pallas_call | solution.py:171
  93.1 6.4 %collective-permute-done.33.refs_2_ = f32[512,128]{1,0:T(8,128)S(1)} collective-permute-done((f32[512,128]{1,0:T(8,128)S(1)}, f32[512,128]{1,0:T(8,128)S(1)}, u32[]{:S(2)}, u32[]{:S(2)}) %collective-permute-start.33) | collective-permute-done | bytes 262176 | tf_op jit(solution)/shard_map/ppermute | solution.py:447
  99.4 1.7 collective-permute-start.34
  101.6 1.3 collective-permute-start.36
  102.9 8.7 %shard_map.82 = (bf16[512,2048]{1,0:T(8,128)(2,1)S(1)}, bf16[512,2048]{1,0:T(8,128)(2,1)S(1)}, f32[8,128]{1,0:T(8,128)S(1)}) custom-call(s32[8]{0:T(128)S(1)} %stack.204.refs_0_, s32[64]{0:T(128)S(1)} %fusion.4.refs_1_, f32[512,128]{1,0:T(8,128)S(1)} %collective-permute-done.22.refs_2_, f32[512,128]{1,0:T(8,128)S(1)} %collective-permute-done.23.refs_3_, ...), custom_call_target="tpu_custom_call" | custom-call | flops 12884901888 | bytes 6291456 | tf_op jit(solution)/shard_map/pallas_call | solution.py:171
  111.6 0.9 collective-permute-done.35.refs_4_
  113.6 0.8 collective-permute-start.41
  114.4 1.2 collective-permute-start.42
  115.6 1.5 collective-permute-start.43
  117.1 8.5 %shard_map.83 = (bf16[512,2048]{1,0:T(8,128)(2,1)S(1)}, bf16[512,2048]{1,0:T(8,128)(2,1)S(1)}, f32[8,128]{1,0:T(8,128)S(1)}) custom-call(s32[8]{0:T(128)S(1)} %stack.204.refs_0_, s32[64]{0:T(128)S(1)} %fusion.3.refs_1_, f32[512,128]{1,0:T(8,128)S(1)} %collective-permute-done.33.refs_2_, f32[512,128]{1,0:T(8,128)S(1)} %collective-permute-done.34.refs_3_, ...), custom_call_target="tpu_custom_call" | custom-call | flops 12884901888 | bytes 6291456 | tf_op jit(solution)/shard_map/pallas_call | solution.py:171
  125.7 4.6 %shard_map.84 = (f32[64,2176]{1,0:T(8,128)S(1)}, f32[64,2048]{1,0:T(8,128)S(1)}) custom-call(bf16[512,2048]{1,0:T(8,128)(2,1)S(1)} %get-tuple-element.79.refs_0_.refs_3_.refs_8_, bf16[512,2048]{1,0:T(8,128)(2,1)S(1)} %get-tuple-element.87.refs_1_.refs_4_.refs_9_, bf16[512,2048]{1,0:T(8,128)(2,1)S(1)} %get-tuple-element.105.refs_2_.refs_5_.refs_10_, ...), custom_call_target="tpu_custom_call" | custom-call | flops 1610612736 | bytes 16777216 | tf_op jit(solution)/shard_map/pallas_call | solution.py:227
  130.4 1.9 collective-permute-done.44.refs_1_
  132.3 9.2 %shard_map.85 = (f32[64,2176]{1,0:T(8,128)S(1)}, f32[64,2048]{1,0:T(8,128)S(1)}, f32[64,2048]{1,0:T(8,128)S(1)}, f32[64,2048]{1,0:T(8,128)S(1)}, f32[64,2048]{1,...) custom-call(f32[64,2176]{1,0:T(8,128)S(1)} %get-tuple-element.119.refs_0_, ...), custom_call_target="tpu_custom_call" | custom-call | flops 3221225472 | bytes 16777216 | tf_op jit(solution)/shard_map/pallas_call | solution.py:338
  141.7 1.8 collective-permute-done.45.refs_1_
  143.6 9.2 %shard_map.86 = (f32[64,2176]{1,0:T(8,128)S(1)}, f32[64,2048]{1,0:T(8,128)S(1)}, f32[64,2048]{1,0:T(8,128)S(1)}, f32[64,2048]{1,0:T(8,128)S(1)}, f32[64,2048]{1,...) custom-call(f32[64,2176]{1,0:T(8,128)S(1)} %get-tuple-element.121.refs_0_, ...), custom_call_target="tpu_custom_call" | custom-call | flops 3221225472 | bytes 16777216 | tf_op jit(solution)/shard_map/pallas_call | solution.py:338
  153.0 1.8 collective-permute-done.46.refs_1_
  154.8 9.5 %shard_map.87 = (f32[64,2176]{1,0:T(8,128)S(1)}, f32[64,2048]{1,0:T(8,128)S(1)}, f32[64,2048]{1,0:T(8,128)S(1)}, f32[64,2048]{1,0:T(8,128)S(1)}, f32[64,2048]{1,...) custom-call(f32[64,2176]{1,0:T(8,128)S(1)} %get-tuple-element.128.refs_0_, ...), custom_call_target="tpu_custom_call" | custom-call | flops 3221225472 | bytes 16777216 | tf_op jit(solution)/shard_map/pallas_call | solution.py:338
  164.3 0.8 copy-done
  165.2 1.8 collective-permute-done.47.other_ref
  167.0 1.0 copy-done.1
  168.6 1.5 collective-permute-start.50
  170.1 0.8 collective-permute-start.49
  170.9 1.2 collective-permute-start.48
  172.2 2.3 collective-permute-start.53
  174.5 1.3 collective-permute-start.54
  176.0 3.5 %collective-permute-start.55 = (f32[64,512]{1,0:T(8,128)S(1)}, f32[64,512]{1,0:T(8,128)S(1)}, u32[]{:S(2)}, u32[]{:S(2)}) collective-permute-start(f32[64,512]{1,0:T(8,128)S(1)} %get-tuple-element.151), channel_id=1, source_target_pairs={{0,8},{2,10},{4,12},{6,14},{8,16},{10,18},{12,20},{14,22},{17,25},... | collective-permute-start | bytes 393224 | tf_op jit(solution)/shard_map/ppermute | solution.py:540
  179.5 1.9 collective-permute-start.51
  181.5 1.3 collective-permute-start.52
  183.3 0.7 constant_dynamic-slice_fusion
  184.0 8.3 %collective-permute-done.51.refs_1_ = f32[256,512]{1,0:T(8,128)S(1)} collective-permute-done((f32[256,512]{1,0:T(8,128)S(1)}, f32[256,512]{1,0:T(8,128)S(1)}, u32[]{:S(2)}, u32[]{:S(2)}) %collective-permute-start.51) | collective-permute-done | bytes 524320 | tf_op jit(solution)/shard_map/ppermute | solution.py:557
  192.3 2.7 %collective-permute-done.52.refs_2_ = f32[256,512]{1,0:T(8,128)S(1)} collective-permute-done((f32[256,512]{1,0:T(8,128)S(1)}, f32[256,512]{1,0:T(8,128)S(1)}, u32[]{:S(2)}, u32[]{:S(2)}) %collective-permute-start.52) | collective-permute-done | bytes 524320 | tf_op jit(solution)/shard_map/ppermute | solution.py:558
  195.7 1.3 collective-permute-start.57
  197.0 0.7 collective-permute-start.58
  197.7 15.8 %collective-permute-done.57.refs_4_ = f32[256,512]{1,0:T(8,128)S(1)} collective-permute-done((f32[256,512]{1,0:T(8,128)S(1)}, f32[256,512]{1,0:T(8,128)S(1)}, u32[]{:S(2)}, u32[]{:S(2)}) %collective-permute-start.57) | collective-permute-done | bytes 524320 | tf_op jit(solution)/shard_map/ppermute | solution.py:558
  213.6 1.3 collective-permute-start.59
  215.0 13.7 %collective-permute-done.59.refs_6_ = f32[256,512]{1,0:T(8,128)} collective-permute-done((f32[256,512]{1,0:T(8,128)S(1)}, f32[256,512]{1,0:T(8,128)}, u32[]{:S(2)}, u32[]{:S(2)}) %collective-permute-start.59) | collective-permute-done | bytes 524320 | tf_op jit(solution)/shard_map/ppermute | solution.py:558
  228.7 4.0 %shard_map.89 = f32[512,1024]{1,0:T(8,128)} custom-call(s32[11]{0:T(128)S(1)} %stack.195.where_ref, f32[256,512]{1,0:T(8,128)S(1)} %pad_maximum_fusion.refs_0_, f32[256,512]{1,0:T(8,128)S(1)} %collective-permute-done.51.refs_1_, f32[256,512]{1,0:T(8,128)S(1)} %collective-permute-done.52.refs_2_, f32[256,512]{1,0:T(8,128)S(1)} %collective-permute-done.56.refs_3_, ...), custom_call_target="tpu_custom_call" | custom-call | tf_op jit(solution)/shard_map/pallas_call | solution.py:419
  (112 shorter events, 12.9 us)
Async XLA Ops:
  11.3 34.0 %collective-permute-start = (f32[40,128]{1,0:T(8,128)S(1)}, f32[40,128]{1,0:T(8,128)S(1)}, u32[]{:S(2)}, u32[]{:S(2)}) collective-permute-start(f32[40,128]{1,0:T(8,128)S(1)} %select_maximum_fusion), channel_id=1, source_target_pairs={{0,8},{8,16},{16,24},{24,0},{1,9},{9,17},{17,25},{25,1},{2,10},{10... | collective-permute-start | bytes 61448 | tf_op jit(solution)/shard_map/ppermute | solution.py:447
  14.3 32.4 %collective-permute-start.1 = (f32[40,128]{1,0:T(8,128)S(1)}, f32[40,128]{1,0:T(8,128)S(1)}, u32[]{:S(2)}, u32[]{:S(2)}) collective-permute-start(f32[40,128]{1,0:T(8,128)S(1)} %select_maximum_fusion), channel_id=1, source_target_pairs={{0,16},{8,24},{16,0},{24,8},{1,17},{9,25},{17,1},{25,9},{2,18},{10... | collective-permute-start | bytes 61448 | tf_op jit(solution)/shard_map/ppermute | solution.py:447
  16.9 7.7 %collective-permute-start.3 = (f32[2048,128]{1,0:T(8,128)}, f32[2048,128]{1,0:T(8,128)S(1)}, u32[]{:S(2)}, u32[]{:S(2)}) collective-permute-start(f32[2048,128]{1,0:T(8,128)} %shard_map.77), channel_id=1, source_target_pairs={{0,1},{1,0},{2,3},{3,2},{4,5},{5,4},{6,7},{7,6},{8,9},{9,8},{10,11... | collective-permute-start | bytes 3145736 | tf_op jit(solution)/shard_map/ppermute | solution.py:444
  24.6 5.1 %copy-start.2 = (f32[256,512]{1,0:T(8,128)S(1)}, f32[256,512]{1,0:T(8,128)}, u32[]{:S(2)}) copy-start(f32[256,512]{1,0:T(8,128)} %param.11) | copy-start | bytes 1572868
  26.1 10.1 %collective-permute-start.6 = (f32[512,128]{1,0:T(8,128)S(1)}, f32[512,128]{1,0:T(8,128)S(1)}, u32[]{:S(2)}, u32[]{:S(2)}) collective-permute-start(f32[512,128]{1,0:T(8,128)S(1)} %get-tuple-element.149), channel_id=1, source_target_pairs={{0,6},{1,7},{2,4},{3,5},{4,2},{5,3},{6,0},{7,1},{8,14},{9,15},{10,... | collective-permute-start | bytes 786440 | tf_op jit(solution)/shard_map/ppermute | solution.py:444
  28.6 12.8 %collective-permute-start.5 = (f32[512,128]{1,0:T(8,128)S(1)}, f32[512,128]{1,0:T(8,128)S(1)}, u32[]{:S(2)}, u32[]{:S(2)}) collective-permute-start(f32[512,128]{1,0:T(8,128)S(1)} %get-tuple-element.150), channel_id=1, source_target_pairs={{0,4},{1,5},{2,6},{3,7},{4,0},{5,1},{6,2},{7,3},{8,12},{9,13},{10,... | collective-permute-start | bytes 786440 | tf_op jit(solution)/shard_map/ppermute | solution.py:444
  29.2 12.4 %collective-permute-start.4 = (f32[512,128]{1,0:T(8,128)S(1)}, f32[512,128]{1,0:T(8,128)S(1)}, u32[]{:S(2)}, u32[]{:S(2)}) collective-permute-start(f32[512,128]{1,0:T(8,128)S(1)} %get-tuple-element.148), channel_id=1, source_target_pairs={{0,2},{1,3},{2,0},{3,1},{4,6},{5,7},{6,4},{7,5},{8,10},{9,11},{10,... | collective-permute-start | bytes 786440 | tf_op jit(solution)/shard_map/ppermute | solution.py:444
  41.6 9.2 %collective-permute-start.7 = (f32[512,128]{1,0:T(8,128)S(1)}, f32[512,128]{1,0:T(8,128)S(1)}, u32[]{:S(2)}, u32[]{:S(2)}) collective-permute-start(f32[512,128]{1,0:T(8,128)S(1)} %fusion.1.refs_2_), channel_id=1, source_target_pairs={{0,2},{1,3},{2,0},{3,1},{4,6},{5,7},{6,4},{7,5},{8,10},{9,11},{10,... | collective-permute-start | bytes 786440 | tf_op jit(solution)/shard_map/ppermute | solution.py:444
  43.1 13.5 %collective-permute-start.8 = (f32[512,128]{1,0:T(8,128)S(1)}, f32[512,128]{1,0:T(8,128)S(1)}, u32[]{:S(2)}, u32[]{:S(2)}) collective-permute-start(f32[512,128]{1,0:T(8,128)S(1)} %fusion.1.refs_2_), channel_id=1, source_target_pairs={{0,4},{1,5},{2,6},{3,7},{4,0},{5,1},{6,2},{7,3},{8,12},{9,13},{10,... | collective-permute-start | bytes 786440 | tf_op jit(solution)/shard_map/ppermute | solution.py:444
  43.9 12.8 %collective-permute-start.9 = (f32[512,128]{1,0:T(8,128)S(1)}, f32[512,128]{1,0:T(8,128)S(1)}, u32[]{:S(2)}, u32[]{:S(2)}) collective-permute-start(f32[512,128]{1,0:T(8,128)S(1)} %fusion.1.refs_2_), channel_id=1, source_target_pairs={{0,6},{1,7},{2,4},{3,5},{4,2},{5,3},{6,0},{7,1},{8,14},{9,15},{10,... | collective-permute-start | bytes 786440 | tf_op jit(solution)/shard_map/ppermute | solution.py:444
  45.3 3.8 %collective-permute-start.2 = (f32[40,128]{1,0:T(8,128)S(1)}, f32[40,128]{1,0:T(8,128)S(1)}, u32[]{:S(2)}, u32[]{:S(2)}) collective-permute-start(f32[40,128]{1,0:T(8,128)S(1)} %select_maximum_fusion), channel_id=1, source_target_pairs={{0,24},{8,0},{16,8},{24,16},{1,25},{9,1},{17,9},{25,17},{2,26},{10... | collective-permute-start | bytes 61448 | tf_op jit(solution)/shard_map/ppermute | solution.py:447
  46.7 12.2 %collective-permute-start.10 = (f32[512,128]{1,0:T(8,128)S(1)}, f32[512,128]{1,0:T(8,128)S(1)}, u32[]{:S(2)}, u32[]{:S(2)}) collective-permute-start(f32[512,128]{1,0:T(8,128)S(1)} %fusion.1.refs_2_), channel_id=1, source_target_pairs={{0,1},{1,0},{2,3},{3,2},{4,5},{5,4},{6,7},{7,6},{8,9},{9,8},{10,11... | collective-permute-start | bytes 786440 | tf_op jit(solution)/shard_map/ppermute | solution.py:444
  49.2 8.3 %collective-permute-start.14 = (f32[512,128]{1,0:T(8,128)S(1)}, f32[512,128]{1,0:T(8,128)S(1)}, u32[]{:S(2)}, u32[]{:S(2)}) collective-permute-start(f32[512,128]{1,0:T(8,128)S(1)} %fusion.1.refs_2_), channel_id=1, source_target_pairs={{0,8},{8,16},{16,24},{24,0},{1,9},{9,17},{17,25},{25,1},{2,10},{10... | collective-permute-start | bytes 786440 | tf_op jit(solution)/shard_map/ppermute | solution.py:447
  50.8 8.7 %collective-permute-start.11 = (f32[512,128]{1,0:T(8,128)S(1)}, f32[512,128]{1,0:T(8,128)S(1)}, u32[]{:S(2)}, u32[]{:S(2)}) collective-permute-start(f32[512,128]{1,0:T(8,128)S(1)} %collective-permute-done.7.refs_3_), channel_id=1, source_target_pairs={{0,1},{1,0},{2,3},{3,2},{4,5},{5,4},{6,7},{7,6},{8,9},{9,8},{10,11... | collective-permute-start | bytes 786440 | tf_op jit(solution)/shard_map/ppermute | solution.py:444
  56.6 4.3 %collective-permute-start.12 = (f32[512,128]{1,0:T(8,128)S(1)}, f32[512,128]{1,0:T(8,128)S(1)}, u32[]{:S(2)}, u32[]{:S(2)}) collective-permute-start(f32[512,128]{1,0:T(8,128)S(1)} %collective-permute-done.8.refs_4_), channel_id=1, source_target_pairs={{0,1},{1,0},{2,3},{3,2},{4,5},{5,4},{6,7},{7,6},{8,9},{9,8},{10,11... | collective-permute-start | bytes 786440 | tf_op jit(solution)/shard_map/ppermute | solution.py:444
  56.7 4.4 %collective-permute-start.13 = (f32[512,128]{1,0:T(8,128)S(1)}, f32[512,128]{1,0:T(8,128)S(1)}, u32[]{:S(2)}, u32[]{:S(2)}) collective-permute-start(f32[512,128]{1,0:T(8,128)S(1)} %collective-permute-done.9.refs_5_), channel_id=1, source_target_pairs={{0,1},{1,0},{2,3},{3,2},{4,5},{5,4},{6,7},{7,6},{8,9},{9,8},{10,11... | collective-permute-start | bytes 786440 | tf_op jit(solution)/shard_map/ppermute | solution.py:444
  57.2 16.7 %copy-start.4 = (f32[64,512]{1,0:T(8,128)S(1)}, f32[64,512]{1,0:T(8,128)}, u32[]{:S(2)}) copy-start(f32[64,512]{1,0:T(8,128)} %get-tuple-element.97) | copy-start | bytes 393220
  57.2 16.9 %copy-start.3 = (f32[64,512]{1,0:T(8,128)S(1)}, f32[64,512]{1,0:T(8,128)}, u32[]{:S(2)}) copy-start(f32[64,512]{1,0:T(8,128)} %get-tuple-element.98) | copy-start | bytes 393220
  57.4 12.1 %collective-permute-start.15 = (f32[512,128]{1,0:T(8,128)S(1)}, f32[512,128]{1,0:T(8,128)S(1)}, u32[]{:S(2)}, u32[]{:S(2)}) collective-permute-start(f32[512,128]{1,0:T(8,128)S(1)} %collective-permute-done.14.refs_2_), channel_id=1, source_target_pairs={{0,2},{1,3},{2,0},{3,1},{4,6},{5,7},{6,4},{7,5},{8,10},{9,11},{10,... | collective-permute-start | bytes 786440 | tf_op jit(solution)/shard_map/ppermute | solution.py:444
  58.9 12.5 %collective-permute-start.16 = (f32[512,128]{1,0:T(8,128)S(1)}, f32[512,128]{1,0:T(8,128)S(1)}, u32[]{:S(2)}, u32[]{:S(2)}) collective-permute-start(f32[512,128]{1,0:T(8,128)S(1)} %collective-permute-done.14.refs_2_), channel_id=1, source_target_pairs={{0,4},{1,5},{2,6},{3,7},{4,0},{5,1},{6,2},{7,3},{8,12},{9,13},{10,... | collective-permute-start | bytes 786440 | tf_op jit(solution)/shard_map/ppermute | solution.py:444
  59.5 11.9 %collective-permute-start.17 = (f32[512,128]{1,0:T(8,128)S(1)}, f32[512,128]{1,0:T(8,128)S(1)}, u32[]{:S(2)}, u32[]{:S(2)}) collective-permute-start(f32[512,128]{1,0:T(8,128)S(1)} %collective-permute-done.14.refs_2_), channel_id=1, source_target_pairs={{0,6},{1,7},{2,4},{3,5},{4,2},{5,3},{6,0},{7,1},{8,14},{9,15},{10,... | collective-permute-start | bytes 786440 | tf_op jit(solution)/shard_map/ppermute | solution.py:444
  60.9 11.5 %collective-permute-start.22 = (f32[512,128]{1,0:T(8,128)S(1)}, f32[512,128]{1,0:T(8,128)S(1)}, u32[]{:S(2)}, u32[]{:S(2)}) collective-permute-start(f32[512,128]{1,0:T(8,128)S(1)} %collective-permute-done.14.refs_2_), channel_id=1, source_target_pairs={{0,8},{8,16},{16,24},{24,0},{1,9},{9,17},{17,25},{25,1},{2,10},{10... | collective-permute-start | bytes 786440 | tf_op jit(solution)/shard_map/ppermute | solution.py:447
  71.4 2.5 %collective-permute-start.18 = (f32[512,128]{1,0:T(8,128)S(1)}, f32[512,128]{1,0:T(8,128)S(1)}, u32[]{:S(2)}, u32[]{:S(2)}) collective-permute-start(f32[512,128]{1,0:T(8,128)S(1)} %collective-permute-done.14.refs_2_), channel_id=1, source_target_pairs={{0,1},{1,0},{2,3},{3,2},{4,5},{5,4},{6,7},{7,6},{8,9},{9,8},{10,11... | collective-permute-start | bytes 786440 | tf_op jit(solution)/shard_map/ppermute | solution.py:444
  71.4 2.7 %collective-permute-start.19 = (f32[512,128]{1,0:T(8,128)S(1)}, f32[512,128]{1,0:T(8,128)S(1)}, u32[]{:S(2)}, u32[]{:S(2)}) collective-permute-start(f32[512,128]{1,0:T(8,128)S(1)} %collective-permute-done.15.refs_3_), channel_id=1, source_target_pairs={{0,1},{1,0},{2,3},{3,2},{4,5},{5,4},{6,7},{7,6},{8,9},{9,8},{10,11... | collective-permute-start | bytes 786440 | tf_op jit(solution)/shard_map/ppermute | solution.py:444
  71.9 4.6 %collective-permute-start.20 = (f32[512,128]{1,0:T(8,128)S(1)}, f32[512,128]{1,0:T(8,128)S(1)}, u32[]{:S(2)}, u32[]{:S(2)}) collective-permute-start(f32[512,128]{1,0:T(8,128)S(1)} %collective-permute-done.16.refs_4_), channel_id=1, source_target_pairs={{0,1},{1,0},{2,3},{3,2},{4,5},{5,4},{6,7},{7,6},{8,9},{9,8},{10,11... | collective-permute-start | bytes 786440 | tf_op jit(solution)/shard_map/ppermute | solution.py:444
  71.9 5.9 %collective-permute-start.21 = (f32[512,128]{1,0:T(8,128)S(1)}, f32[512,128]{1,0:T(8,128)S(1)}, u32[]{:S(2)}, u32[]{:S(2)}) collective-permute-start(f32[512,128]{1,0:T(8,128)S(1)} %collective-permute-done.17.refs_5_), channel_id=1, source_target_pairs={{0,1},{1,0},{2,3},{3,2},{4,5},{5,4},{6,7},{7,6},{8,9},{9,8},{10,11... | collective-permute-start | bytes 786440 | tf_op jit(solution)/shard_map/ppermute | solution.py:444
  72.4 8.2 %collective-permute-start.23 = (f32[512,128]{1,0:T(8,128)S(1)}, f32[512,128]{1,0:T(8,128)S(1)}, u32[]{:S(2)}, u32[]{:S(2)}) collective-permute-start(f32[512,128]{1,0:T(8,128)S(1)} %collective-permute-done.22.refs_2_), channel_id=1, source_target_pairs={{0,2},{1,3},{2,0},{3,1},{4,6},{5,7},{6,4},{7,5},{8,10},{9,11},{10,... | collective-permute-start | bytes 786440 | tf_op jit(solution)/shard_map/ppermute | solution.py:444
  73.9 17.5 %collective-permute-start.30 = (f32[64,512]{1,0:T(8,128)S(1)}, f32[64,512]{1,0:T(8,128)S(1)}, u32[]{:S(2)}, u32[]{:S(2)}) collective-permute-start(f32[64,512]{1,0:T(8,128)S(1)} %copy-done.4), channel_id=1, source_target_pairs={{0,8},{8,16},{16,24},{24,0},{1,9},{9,17},{17,25},{25,1},{2,10},{10... | collective-permute-start | bytes 393224 | tf_op jit(solution)/shard_map/ppermute | solution.py:447
  74.1 17.8 %collective-permute-start.31 = (f32[64,512]{1,0:T(8,128)S(1)}, f32[64,512]{1,0:T(8,128)S(1)}, u32[]{:S(2)}, u32[]{:S(2)}) collective-permute-start(f32[64,512]{1,0:T(8,128)S(1)} %copy-done.3), channel_id=1, source_target_pairs={{0,16},{8,24},{16,0},{24,8},{1,17},{9,25},{17,1},{25,9},{2,18},{10... | collective-permute-start | bytes 393224 | tf_op jit(solution)/shard_map/ppermute | solution.py:447
  76.5 15.5 %collective-permute-start.32 = (f32[64,512]{1,0:T(8,128)S(1)}, f32[64,512]{1,0:T(8,128)S(1)}, u32[]{:S(2)}, u32[]{:S(2)}) collective-permute-start(f32[64,512]{1,0:T(8,128)S(1)} %get-tuple-element.99), channel_id=1, source_target_pairs={{0,24},{8,0},{16,8},{24,16},{1,25},{9,1},{17,9},{25,17},{2,26},{10... | collective-permute-start | bytes 393224 | tf_op jit(solution)/shard_map/ppermute | solution.py:447
  77.8 13.0 %collective-permute-start.24 = (f32[512,128]{1,0:T(8,128)S(1)}, f32[512,128]{1,0:T(8,128)S(1)}, u32[]{:S(2)}, u32[]{:S(2)}) collective-permute-start(f32[512,128]{1,0:T(8,128)S(1)} %collective-permute-done.22.refs_2_), channel_id=1, source_target_pairs={{0,4},{1,5},{2,6},{3,7},{4,0},{5,1},{6,2},{7,3},{8,12},{9,13},{10,... | collective-permute-start | bytes 786440 | tf_op jit(solution)/shard_map/ppermute | solution.py:444
  80.6 10.8 %collective-permute-start.25 = (f32[512,128]{1,0:T(8,128)S(1)}, f32[512,128]{1,0:T(8,128)S(1)}, u32[]{:S(2)}, u32[]{:S(2)}) collective-permute-start(f32[512,128]{1,0:T(8,128)S(1)} %collective-permute-done.22.refs_2_), channel_id=1, source_target_pairs={{0,6},{1,7},{2,4},{3,5},{4,2},{5,3},{6,0},{7,1},{8,14},{9,15},{10,... | collective-permute-start | bytes 786440 | tf_op jit(solution)/shard_map/ppermute | solution.py:444
  90.8 8.6 %collective-permute-start.33 = (f32[512,128]{1,0:T(8,128)S(1)}, f32[512,128]{1,0:T(8,128)S(1)}, u32[]{:S(2)}, u32[]{:S(2)}) collective-permute-start(f32[512,128]{1,0:T(8,128)S(1)} %collective-permute-done.22.refs_2_), channel_id=1, source_target_pairs={{0,8},{8,16},{16,24},{24,0},{1,9},{9,17},{17,25},{25,1},{2,10},{10... | collective-permute-start | bytes 786440 | tf_op jit(solution)/shard_map/ppermute | solution.py:447
  91.4 9.7 %collective-permute-start.26 = (f32[512,128]{1,0:T(8,128)S(1)}, f32[512,128]{1,0:T(8,128)S(1)}, u32[]{:S(2)}, u32[]{:S(2)}) collective-permute-start(f32[512,128]{1,0:T(8,128)S(1)} %collective-permute-done.22.refs_2_), channel_id=1, source_target_pairs={{0,1},{1,0},{2,3},{3,2},{4,5},{5,4},{6,7},{7,6},{8,9},{9,8},{10,11... | collective-permute-start | bytes 786440 | tf_op jit(solution)/shard_map/ppermute | solution.py:444
  91.4 10.2 %collective-permute-start.27 = (f32[512,128]{1,0:T(8,128)S(1)}, f32[512,128]{1,0:T(8,128)S(1)}, u32[]{:S(2)}, u32[]{:S(2)}) collective-permute-start(f32[512,128]{1,0:T(8,128)S(1)} %collective-permute-done.23.refs_3_), channel_id=1, source_target_pairs={{0,1},{1,0},{2,3},{3,2},{4,5},{5,4},{6,7},{7,6},{8,9},{9,8},{10,11... | collective-permute-start | bytes 786440 | tf_op jit(solution)/shard_map/ppermute | solution.py:444
  91.9 11.0 %collective-permute-start.28 = (f32[512,128]{1,0:T(8,128)S(1)}, f32[512,128]{1,0:T(8,128)S(1)}, u32[]{:S(2)}, u32[]{:S(2)}) collective-permute-start(f32[512,128]{1,0:T(8,128)S(1)} %collective-permute-done.24.refs_4_), channel_id=1, source_target_pairs={{0,1},{1,0},{2,3},{3,2},{4,5},{5,4},{6,7},{7,6},{8,9},{9,8},{10,11... | collective-permute-start | bytes 786440 | tf_op jit(solution)/shard_map/ppermute | solution.py:444
  92.0 10.9 %collective-permute-start.29 = (f32[512,128]{1,0:T(8,128)S(1)}, f32[512,128]{1,0:T(8,128)S(1)}, u32[]{:S(2)}, u32[]{:S(2)}) collective-permute-start(f32[512,128]{1,0:T(8,128)S(1)} %collective-permute-done.25.refs_5_), channel_id=1, source_target_pairs={{0,1},{1,0},{2,3},{3,2},{4,5},{5,4},{6,7},{7,6},{8,9},{9,8},{10,11... | collective-permute-start | bytes 786440 | tf_op jit(solution)/shard_map/ppermute | solution.py:444
  99.4 12.2 %collective-permute-start.34 = (f32[512,128]{1,0:T(8,128)S(1)}, f32[512,128]{1,0:T(8,128)S(1)}, u32[]{:S(2)}, u32[]{:S(2)}) collective-permute-start(f32[512,128]{1,0:T(8,128)S(1)} %collective-permute-done.33.refs_2_), channel_id=1, source_target_pairs={{0,2},{1,3},{2,0},{3,1},{4,6},{5,7},{6,4},{7,5},{8,10},{9,11},{10,... | collective-permute-start | bytes 786440 | tf_op jit(solution)/shard_map/ppermute | solution.py:444
  101.1 11.5 %collective-permute-start.35 = (f32[512,128]{1,0:T(8,128)S(1)}, f32[512,128]{1,0:T(8,128)S(1)}, u32[]{:S(2)}, u32[]{:S(2)}) collective-permute-start(f32[512,128]{1,0:T(8,128)S(1)} %collective-permute-done.33.refs_2_), channel_id=1, source_target_pairs={{0,4},{1,5},{2,6},{3,7},{4,0},{5,1},{6,2},{7,3},{8,12},{9,13},{10,... | collective-permute-start | bytes 786440 | tf_op jit(solution)/shard_map/ppermute | solution.py:444
  101.6 11.0 %collective-permute-start.36 = (f32[512,128]{1,0:T(8,128)S(1)}, f32[512,128]{1,0:T(8,128)S(1)}, u32[]{:S(2)}, u32[]{:S(2)}) collective-permute-start(f32[512,128]{1,0:T(8,128)S(1)} %collective-permute-done.33.refs_2_), channel_id=1, source_target_pairs={{0,6},{1,7},{2,4},{3,5},{4,2},{5,3},{6,0},{7,1},{8,14},{9,15},{10,... | collective-permute-start | bytes 786440 | tf_op jit(solution)/shard_map/ppermute | solution.py:444
  112.6 1.8 collective-permute-start.37
  112.6 3.0 %collective-permute-start.38 = (f32[512,128]{1,0:T(8,128)S(1)}, f32[512,128]{1,0:T(8,128)S(1)}, u32[]{:S(2)}, u32[]{:S(2)}) collective-permute-start(f32[512,128]{1,0:T(8,128)S(1)} %collective-permute-done.34.refs_3_), channel_id=1, source_target_pairs={{0,1},{1,0},{2,3},{3,2},{4,5},{5,4},{6,7},{7,6},{8,9},{9,8},{10,11... | collective-permute-start | bytes 786440 | tf_op jit(solution)/shard_map/ppermute | solution.py:444
  113.1 4.0 %collective-permute-start.39 = (f32[512,128]{1,0:T(8,128)S(1)}, f32[512,128]{1,0:T(8,128)S(1)}, u32[]{:S(2)}, u32[]{:S(2)}) collective-permute-start(f32[512,128]{1,0:T(8,128)S(1)} %collective-permute-done.35.refs_4_), channel_id=1, source_target_pairs={{0,1},{1,0},{2,3},{3,2},{4,5},{5,4},{6,7},{7,6},{8,9},{9,8},{10,11... | collective-permute-start | bytes 786440 | tf_op jit(solution)/shard_map/ppermute | solution.py:444
  113.1 4.0 %collective-permute-start.40 = (f32[512,128]{1,0:T(8,128)S(1)}, f32[512,128]{1,0:T(8,128)S(1)}, u32[]{:S(2)}, u32[]{:S(2)}) collective-permute-start(f32[512,128]{1,0:T(8,128)S(1)} %collective-permute-done.36.refs_5_), channel_id=1, source_target_pairs={{0,1},{1,0},{2,3},{3,2},{4,5},{5,4},{6,7},{7,6},{8,9},{9,8},{10,11... | collective-permute-start | bytes 786440 | tf_op jit(solution)/shard_map/ppermute | solution.py:444
  113.6 12.0 %collective-permute-start.41 = (f32[64,512]{1,0:T(8,128)S(1)}, f32[64,512]{1,0:T(8,128)S(1)}, u32[]{:S(2)}, u32[]{:S(2)}) collective-permute-start(f32[64,512]{1,0:T(8,128)S(1)} %get-tuple-element.101), channel_id=1, source_target_pairs={{0,2},{1,3},{2,0},{3,1},{4,6},{5,7},{6,4},{7,5},{8,10},{9,11},{10,... | collective-permute-start | bytes 393224 | tf_op jit(solution)/shard_map/ppermute | solution.py:444
  114.4 11.2 %collective-permute-start.42 = (f32[64,512]{1,0:T(8,128)S(1)}, f32[64,512]{1,0:T(8,128)S(1)}, u32[]{:S(2)}, u32[]{:S(2)}) collective-permute-start(f32[64,512]{1,0:T(8,128)S(1)} %get-tuple-element.102), channel_id=1, source_target_pairs={{0,4},{1,5},{2,6},{3,7},{4,0},{5,1},{6,2},{7,3},{8,12},{9,13},{10,... | collective-permute-start | bytes 393224 | tf_op jit(solution)/shard_map/ppermute | solution.py:444
  115.6 10.0 %collective-permute-start.43 = (f32[64,512]{1,0:T(8,128)S(1)}, f32[64,512]{1,0:T(8,128)S(1)}, u32[]{:S(2)}, u32[]{:S(2)}) collective-permute-start(f32[64,512]{1,0:T(8,128)S(1)} %get-tuple-element.103), channel_id=1, source_target_pairs={{0,6},{1,7},{2,4},{3,5},{4,2},{5,3},{6,0},{7,1},{8,14},{9,15},{10,... | collective-permute-start | bytes 393224 | tf_op jit(solution)/shard_map/ppermute | solution.py:444
  130.3 2.0 collective-permute-start.44
  141.5 2.0 collective-permute-start.45
  152.8 2.0 collective-permute-start.46
  165.1 2.0 collective-permute-start.47
  167.0 1.0 copy-start.1
  168.6 7.3 %collective-permute-start.50 = (f32[64,512]{1,0:T(8,128)S(1)}, f32[64,512]{1,0:T(8,128)S(1)}, u32[]{:S(2)}, u32[]{:S(2)}) collective-permute-start(f32[64,512]{1,0:T(8,128)S(1)} %get-tuple-element.155), channel_id=1, source_target_pairs={{0,6},{1,7},{2,4},{3,5},{4,2},{5,3},{6,0},{7,1},{8,14},{9,15},{10,... | collective-permute-start | bytes 393224 | tf_op jit(solution)/shard_map/ppermute | solution.py:444
  170.1 9.4 %collective-permute-start.49 = (f32[64,512]{1,0:T(8,128)S(1)}, f32[64,512]{1,0:T(8,128)S(1)}, u32[]{:S(2)}, u32[]{:S(2)}) collective-permute-start(f32[64,512]{1,0:T(8,128)S(1)} %get-tuple-element.156), channel_id=1, source_target_pairs={{0,4},{1,5},{2,6},{3,7},{4,0},{5,1},{6,2},{7,3},{8,12},{9,13},{10,... | collective-permute-start | bytes 393224 | tf_op jit(solution)/shard_map/ppermute | solution.py:444
  170.9 8.5 %collective-permute-start.48 = (f32[64,512]{1,0:T(8,128)S(1)}, f32[64,512]{1,0:T(8,128)S(1)}, u32[]{:S(2)}, u32[]{:S(2)}) collective-permute-start(f32[64,512]{1,0:T(8,128)S(1)} %get-tuple-element.157), channel_id=1, source_target_pairs={{0,2},{1,3},{2,0},{3,1},{4,6},{5,7},{6,4},{7,5},{8,10},{9,11},{10,... | collective-permute-start | bytes 393224 | tf_op jit(solution)/shard_map/ppermute | solution.py:444
  172.2 10.6 %collective-permute-start.53 = (f32[64,512]{1,0:T(8,128)S(1)}, f32[64,512]{1,0:T(8,128)S(1)}, u32[]{:S(2)}, u32[]{:S(2)}) collective-permute-start(f32[64,512]{1,0:T(8,128)S(1)} %get-tuple-element.153), channel_id=1, source_target_pairs={{0,24},{2,26},{4,28},{6,30},{8,0},{10,2},{12,4},{14,6},{17,9},{19,... | collective-permute-start | bytes 393224 | tf_op jit(solution)/shard_map/ppermute | solution.py:540
  174.5 8.3 %collective-permute-start.54 = (f32[64,512]{1,0:T(8,128)S(1)}, f32[64,512]{1,0:T(8,128)S(1)}, u32[]{:S(2)}, u32[]{:S(2)}) collective-permute-start(f32[64,512]{1,0:T(8,128)S(1)} %get-tuple-element.152), channel_id=1, source_target_pairs={{0,16},{2,18},{4,20},{6,22},{8,24},{10,26},{12,28},{14,30},{17,1},... | collective-permute-start | bytes 393224 | tf_op jit(solution)/shard_map/ppermute | solution.py:540
  176.0 7.3 %collective-permute-start.55 = (f32[64,512]{1,0:T(8,128)S(1)}, f32[64,512]{1,0:T(8,128)S(1)}, u32[]{:S(2)}, u32[]{:S(2)}) collective-permute-start(f32[64,512]{1,0:T(8,128)S(1)} %get-tuple-element.151), channel_id=1, source_target_pairs={{0,8},{2,10},{4,12},{6,14},{8,16},{10,18},{12,20},{14,22},{17,25},... | collective-permute-start | bytes 393224 | tf_op jit(solution)/shard_map/ppermute | solution.py:540
  179.5 12.8 %collective-permute-start.51 = (f32[256,512]{1,0:T(8,128)S(1)}, f32[256,512]{1,0:T(8,128)S(1)}, u32[]{:S(2)}, u32[]{:S(2)}) collective-permute-start(f32[256,512]{1,0:T(8,128)S(1)} %pad_maximum_fusion.refs_0_), channel_id=1, source_target_pairs={{0,8},{8,16},{16,24},{1,9},{9,17},{17,25},{2,10},{10,18},{18,26},{... | collective-permute-start | bytes 1572872 | tf_op jit(solution)/shard_map/ppermute | solution.py:557
  181.5 13.6 %collective-permute-start.52 = (f32[256,512]{1,0:T(8,128)S(1)}, f32[256,512]{1,0:T(8,128)S(1)}, u32[]{:S(2)}, u32[]{:S(2)}) collective-permute-start(f32[256,512]{1,0:T(8,128)S(1)} %pad_maximum_fusion.refs_0_), channel_id=1, source_target_pairs={{8,0},{16,8},{24,16},{9,1},{17,9},{25,17},{10,2},{18,10},{26,18},{... | collective-permute-start | bytes 1572872 | tf_op jit(solution)/shard_map/ppermute | solution.py:558
  195.0 2.0 collective-permute-start.56
  195.7 17.9 %collective-permute-start.57 = (f32[256,512]{1,0:T(8,128)S(1)}, f32[256,512]{1,0:T(8,128)S(1)}, u32[]{:S(2)}, u32[]{:S(2)}) collective-permute-start(f32[256,512]{1,0:T(8,128)S(1)} %collective-permute-done.52.refs_2_), channel_id=1, source_target_pairs={{8,0},{16,8},{9,1},{17,9},{10,2},{18,10},{11,3},{19,11},{12,4},{20... | collective-permute-start | bytes 1572872 | tf_op jit(solution)/shard_map/ppermute | solution.py:558
  197.0 18.0 %collective-permute-start.58 = (f32[256,512]{1,0:T(8,128)S(1)}, f32[256,512]{1,0:T(8,128)S(1)}, u32[]{:S(2)}, u32[]{:S(2)}) collective-permute-start(f32[256,512]{1,0:T(8,128)S(1)} %collective-permute-done.56.refs_3_), channel_id=1, source_target_pairs={{16,24},{17,25},{18,26},{19,27},{20,28},{21,29},{22,30},{23,31}} | collective-permute-start | bytes 1572872 | tf_op jit(solution)/shard_map/ppermute | solution.py:557
  213.6 15.1 %collective-permute-start.59 = (f32[256,512]{1,0:T(8,128)S(1)}, f32[256,512]{1,0:T(8,128)}, u32[]{:S(2)}, u32[]{:S(2)}) collective-permute-start(f32[256,512]{1,0:T(8,128)S(1)} %collective-permute-done.57.refs_4_), channel_id=1, source_target_pairs={{8,0},{9,1},{10,2},{11,3},{12,4},{13,5},{14,6},{15,7}} | collective-permute-start | bytes 1572872 | tf_op jit(solution)/shard_map/ppermute | solution.py:558
  (1 other events, 0.8 us)

commit v9 on v8

--- a/solution.py
+++ b/solution.py
@@ -403,13 +403,9 @@
     k = where_ref[pl.program_id(0)]
     for number, array in enumerate(arrays):
         to = where_ref[slots + number]
-
-        @pl.when(to >= 0)
-        def _():
-            held[pl.ds(pl.multiple_of(to * rows, rows), rows), :] = array[
-                pl.ds(pl.multiple_of(k * rows, rows), rows), :
-            ]
-
+        held[pl.ds(pl.multiple_of(to * rows, rows), rows), :] = array[
+            pl.ds(pl.multiple_of(k * rows, rows), rows), :
+        ]
     out_ref[...] = held[...].T
 
 
@@ -475,14 +471,17 @@
     w_in, w_out = proj_in.T, proj_out.T
     give = project(blocks + 1 - core, activations, out_grads, w_in, w_out, share)
     keep = project(blocks + core, activations, out_grads, w_in, w_out, share)
-    extra = tie(extra, give)
+    kept = (keep + swap(give, 1)).reshape((n_c, share, LANES))
+    kept, extra, parts = lax.optimization_barrier((kept, extra, parts))
     extras = [extra] + [shift(extra, away) for away in range(1, n_dp)]
     plane_ids = [one[:id_rows].reshape((1, tokens)) for one in extras]
     firsts = [one[id_rows, :EX_DEV // group].astype(jnp.int32) for one in extras]
-    kept = (keep + swap(give, 1)).reshape((n_c, share, LANES))
     own = kept[0]
     for k in range(1, n_c):
         own = own + swap(kept[k], 2 * k)
+
+    parts = [parts[0]] + [shift(parts[k], k) for k in range(1, n_dp)]
+    own, parts, plane_ids, firsts = lax.optimization_barrier((own, parts, plane_ids, firsts))
 
     rings = [own]
     for _ in range(n_dp - 1):
@@ -496,15 +495,12 @@
     offs = jnp.stack(
         [near_chip[k] * 2 + which for which in (core, 1 - core) for k in range(n_c)]
     ).astype(jnp.int32)
-    offs, pick, plane_ids, firsts, parts, origin = lax.optimization_barrier(
-        (offs, pick, plane_ids, firsts, parts, origin)
+    offs, pick, plane_ids, firsts, slots = lax.optimization_barrier(
+        (offs, pick, plane_ids, firsts, arrange(origin, parts))
     )
 
     highs, lows, squares = [], [], []
     for away in range(n_dp):
-        if away == n_dp // 2:
-            slots = arrange(origin, [parts[0]] + [shift(parts[k], k) for k in range(1, n_dp)])
-            pick = tie(pick, slots)
         piece = rings[away]
         near = [piece] + [swap(piece, 2 * k) for k in range(1, n_c)]
         sources = near + [
@@ -550,14 +546,10 @@
     ring = [x[:, k * per_slot:(k + 1) * per_slot] for k in range(n_c)]
     ring = jnp.concatenate([ring[0]] + [swap(ring[k], 2 * k) for k in range(1, n_c)], axis=0)
     arrays, places = [ring], [i]
-    ups = downs = ring
     for away in range(1, n_dp):
-        if away == 2:
-            ups, downs = tie((ups, downs), scores)
-        ups = lax.ppermute(ups, "dp", [(a, a + 1) for a in range(away - 1, n_dp - 1)])
-        downs = lax.ppermute(downs, "dp", [(a, a - 1) for a in range(1, n_dp - away + 1)])
-        arrays += [ups, downs]
-        places += [jnp.maximum(i - away, -1), jnp.where(i + away < n_dp, i + away, -1)]
+        ring = shift(tie(ring, scores) if away == 2 else ring, 1)
+        arrays.append(ring)
+        places.append((i - away) % n_dp)
     where = jnp.stack([chip ^ c for c in range(n_c)] + places).astype(jnp.int32)
     out = place(where, arrays, n_c, n_dp)
     return (out, scores.reshape((n_half * q_chip, EX_DEV)))

time: 233 us -> 217 us (0.931)
  waiting for transfers between devices: 81.1 us -> 69.1 us
    ppermute x6 -> x0, waiting for transfers between devices: 40.5 us -> none  [the longest x3 32.3 us: per_device(): lax.ppermute(downs, 'dp', [(a, a - 1) for a in range(1, n_dp - away + 1)])]
    ppermute x9 -> x12, waiting for transfers between devices: 9 us -> 38.1 us  [shift(): lax.ppermute(values, 'dp', [(a, (a + by) % n_dp) for a in range(n_dp)])]
    ppermute x6 -> x0, starting transfers between devices: 7.19 us -> none  [the longest x3 3.86 us: per_device(): lax.ppermute(downs, 'dp', [(a, a - 1) for a in range(1, n_dp - away + 1)])]
    ppermute x9 -> x12, starting transfers between devices: 11.8 us -> 17 us  [shift(): lax.ppermute(values, 'dp', [(a, (a + by) % n_dp) for a in range(n_dp)])]
    ppermute x42, waiting for transfers between devices: 31.1 us -> 27.5 us  [swap(): return lax.ppermute(values, 'tensor', [(a, a ^ mask) for a in range(n_t)])]
    ppermute x3, waiting for transfers between devices: 0.46 us -> 3.58 us  [send(): return lax.ppermute(values, ('dp', 'tensor'), pairs)]
  transfers between devices with their start and end apart: 60 -> 57, of which waited for: 22 -> 18; matrix products, arithmetic and copies ran while one was open for 2% -> 1% of each run, Pallas kernels for 18% -> 20%
where the time goes in v9:
time: 217 us
  Pallas kernels  86.1 us (40%)
  waiting for transfers between devices  69.1 us (32%)
  starting transfers between devices  54.3 us (25%)
  local copies, waits for them, and re-layouts  3.12 us (1%)
  other arithmetic  3 us (1%)
    ppermute x12, waiting for transfers between devices, shift(): lax.ppermute(values, 'dp', [(a, (a + by) % n_dp) for a in range(n_dp)])  38.1 us
    pallas_call x4, Pallas kernels, build(): pl.pallas_call(functools.partial(build_kernel, ranks, share, ex_block, le...  34.1 us
    ppermute x42, starting transfers between devices, swap(): return lax.ppermute(values, 'tensor', [(a, a ^ mask) for a in range(n_t)])  29.3 us
    pallas_call x3, Pallas kernels, one_step(): pl.pallas_call(functools.partial(step_kernel, first, planes, examples, co...  27.9 us
    ppermute x42, waiting for transfers between devices, swap(): return lax.ppermute(values, 'tensor', [(a, a ^ mask) for a in range(n_t)])  27.5 us
    ppermute x12, starting transfers between devices, shift(): lax.ppermute(values, 'dp', [(a, (a + by) % n_dp) for a in range(n_dp)])  17 us
    pallas_call x2, Pallas kernels, project(): pl.pallas_call(project_kernel, out_shape=jax.ShapeDtypeStruct((steps * bl...  15.6 us
    ppermute x3, starting transfers between devices, send(): return lax.ppermute(values, ('dp', 'tensor'), pairs)  7.96 us
  transfers between devices with their start and end apart: 57, of which 18 were waited for; matrix products, arithmetic and copies ran while one was open for 1% of the time, Pallas kernels for 20%

profile of v9, /device:TPU:0, one launch (start us, length us, event | category | flops | bytes accessed | tf_op | source)
XLA Modules:
  0.0 216.8 jit_solution(15236211558534535101)
XLA Ops:
  0.7 0.6 add_subtract_fusion
  1.3 7.9 %shard_map.78 = f32[2048,128]{1,0:T(8,128)} custom-call(s32[4]{0:T(128)} %get-tuple-element.176.order_ref, bf16[4096,512]{1,0:T(8,128)(2,1)} %refs_3_.3, bf16[4096,512]{1,0:T(8,128)(2,1)} %refs_3_.3, bf16[4096,512]{1,0:T(8,128)(2,1)} %refs_3_.3, bf16[4096,512]{1,0:T(8,128)(2,1)} %refs_3_.3, bf16[4096,1792]{1,0:T(8,128)(2,1)} %refs_7_.3, ...), custom_call_target="tpu_custom_call" | custom-call | flops 9663676416 | bytes 9437184 | tf_op jit(solution)/shard_map/pallas_call | solution.py:58
  10.6 7.7 %shard_map.77 = f32[2048,128]{1,0:T(8,128)} custom-call(s32[4]{0:T(128)} %broadcast_add_fusion.order_ref, bf16[4096,512]{1,0:T(8,128)(2,1)} %refs_3_.3, bf16[4096,512]{1,0:T(8,128)(2,1)} %refs_3_.3, bf16[4096,512]{1,0:T(8,128)(2,1)} %refs_3_.3, bf16[4096,512]{1,0:T(8,128)(2,1)} %refs_3_.3, bf16[4096,1792]{1,0:T(8,128)(2,1)} %refs_7_.3, ...), custom_call_target="tpu_custom_call" | custom-call | flops 9663676416 | bytes 9437184 | tf_op jit(solution)/shard_map/pallas_call | solution.py:58
  18.4 1.4 add.390
  19.8 2.6 %collective-permute-start.7 = (f32[40,128]{1,0:T(8,128)S(1)}, f32[40,128]{1,0:T(8,128)S(1)}, u32[]{:S(2)}, u32[]{:S(2)}) collective-permute-start(f32[40,128]{1,0:T(8,128)S(1)} %select_maximum_fusion), channel_id=1, source_target_pairs={{0,8},{8,16},{16,24},{24,0},{1,9},{9,17},{17,25},{25,1},{2,10},{10... | collective-permute-start | bytes 61448 | tf_op jit(solution)/shard_map/ppermute | solution.py:443
  22.4 2.6 %collective-permute-start.8 = (f32[40,128]{1,0:T(8,128)S(1)}, f32[40,128]{1,0:T(8,128)S(1)}, u32[]{:S(2)}, u32[]{:S(2)}) collective-permute-start(f32[40,128]{1,0:T(8,128)S(1)} %select_maximum_fusion), channel_id=1, source_target_pairs={{0,16},{8,24},{16,0},{24,8},{1,17},{9,25},{17,1},{25,9},{2,18},{10... | collective-permute-start | bytes 61448 | tf_op jit(solution)/shard_map/ppermute | solution.py:443
  25.0 1.3 collective-permute-start.9
  26.4 2.5 %collective-permute-start.3 = (f32[512,128]{1,0:T(8,128)S(1)}, f32[512,128]{1,0:T(8,128)S(1)}, u32[]{:S(2)}, u32[]{:S(2)}) collective-permute-start(f32[512,128]{1,0:T(8,128)S(1)} %get-tuple-element.179), channel_id=1, source_target_pairs={{0,6},{1,7},{2,4},{3,5},{4,2},{5,3},{6,0},{7,1},{8,14},{9,15},{10,... | collective-permute-start | bytes 786440 | tf_op jit(solution)/shard_map/ppermute | solution.py:440
  29.4 0.5 collective-permute-start.1
  30.0 0.7 collective-permute-start.4
  31.1 5.6 %collective-permute-done.3 = f32[512,128]{1,0:T(8,128)S(1)} collective-permute-done((f32[512,128]{1,0:T(8,128)S(1)}, f32[512,128]{1,0:T(8,128)S(1)}, u32[]{:S(2)}, u32[]{:S(2)}) %collective-permute-start.3) | collective-permute-done | bytes 262176 | tf_op jit(solution)/shard_map/ppermute | solution.py:440
  37.1 3.8 %collective-permute-done.2 = f32[512,128]{1,0:T(8,128)S(1)} collective-permute-done((f32[512,128]{1,0:T(8,128)S(1)}, f32[512,128]{1,0:T(8,128)S(1)}, u32[]{:S(2)}, u32[]{:S(2)}) %collective-permute-start.2) | collective-permute-done | bytes 262176 | tf_op jit(solution)/shard_map/ppermute | solution.py:440
  41.0 0.8 collective-permute-done.5.refs_2_
  41.8 0.8 collective-permute-done.6.refs_3_
  42.6 1.5 collective-permute-start.10
  44.1 1.5 collective-permute-start.11
  45.6 0.5 collective-permute-start.12
  46.1 2.0 collective-permute-start.17
  48.1 3.7 %collective-permute-done.10.refs_3_ = f32[512,128]{1,0:T(8,128)S(1)} collective-permute-done((f32[512,128]{1,0:T(8,128)S(1)}, f32[512,128]{1,0:T(8,128)S(1)}, u32[]{:S(2)}, u32[]{:S(2)}) %collective-permute-start.10) | collective-permute-done | bytes 262176 | tf_op jit(solution)/shard_map/ppermute | solution.py:440
  51.8 4.2 %collective-permute-done.11.refs_4_ = f32[512,128]{1,0:T(8,128)S(1)} collective-permute-done((f32[512,128]{1,0:T(8,128)S(1)}, f32[512,128]{1,0:T(8,128)S(1)}, u32[]{:S(2)}, u32[]{:S(2)}) %collective-permute-start.11) | collective-permute-done | bytes 262176 | tf_op jit(solution)/shard_map/ppermute | solution.py:440
  56.8 0.6 shard_map.79
  57.5 0.5 collective-permute-start.18
  58.0 1.6 collective-permute-start.19
  59.6 1.4 collective-permute-start.20
  61.0 3.2 %collective-permute-start.25 = (f32[512,128]{1,0:T(8,128)S(1)}, f32[512,128]{1,0:T(8,128)S(1)}, u32[]{:S(2)}, u32[]{:S(2)}) collective-permute-start(f32[512,128]{1,0:T(8,128)S(1)} %collective-permute-done.17.refs_2_), channel_id=1, source_target_pairs={{0,8},{8,16},{16,24},{24,0},{1,9},{9,17},{17,25},{25,1},{2,10},{10... | collective-permute-start | bytes 786440 | tf_op jit(solution)/shard_map/ppermute | solution.py:443
  64.2 8.5 %shard_map.80 = (bf16[512,2048]{1,0:T(8,128)(2,1)S(1)}, bf16[512,2048]{1,0:T(8,128)(2,1)S(1)}, f32[8,128]{1,0:T(8,128)S(1)}) custom-call(s32[8]{0:T(128)S(1)} %stack.192.refs_0_, s32[64]{0:T(128)S(1)} %convert_bitcast_fusion.refs_1_, f32[512,128]{1,0:T(8,128)S(1)} %fusion.1.refs_2_, f32[512,128]{1,0:T(8,128)S(1)} %collective-permute-done.10.refs_3_, ...), custom_call_target="tpu_custom_call" | custom-call | flops 12884901888 | bytes 6291456 | tf_op jit(solution)/shard_map/pallas_call | solution.py:171
  73.9 0.7 collective-permute-start.26
  74.6 1.4 collective-permute-start.27
  75.9 1.5 collective-permute-start.28
  77.4 2.6 %collective-permute-start.33 = (f32[512,128]{1,0:T(8,128)S(1)}, f32[512,128]{1,0:T(8,128)S(1)}, u32[]{:S(2)}, u32[]{:S(2)}) collective-permute-start(f32[512,128]{1,0:T(8,128)S(1)} %collective-permute-done.25.refs_2_), channel_id=1, source_target_pairs={{0,8},{8,16},{16,24},{24,0},{1,9},{9,17},{17,25},{25,1},{2,10},{10... | collective-permute-start | bytes 786440 | tf_op jit(solution)/shard_map/ppermute | solution.py:443
  80.0 8.5 %shard_map.81 = (bf16[512,2048]{1,0:T(8,128)(2,1)S(1)}, bf16[512,2048]{1,0:T(8,128)(2,1)S(1)}, f32[8,128]{1,0:T(8,128)S(1)}) custom-call(s32[8]{0:T(128)S(1)} %stack.192.refs_0_, s32[64]{0:T(128)S(1)} %fusion.5.refs_1_, f32[512,128]{1,0:T(8,128)S(1)} %collective-permute-done.17.refs_2_, f32[512,128]{1,0:T(8,128)S(1)} %collective-permute-done.18.refs_3_, ...), custom_call_target="tpu_custom_call" | custom-call | flops 12884901888 | bytes 6291456 | tf_op jit(solution)/shard_map/pallas_call | solution.py:171
  89.7 0.8 collective-permute-start.34
  90.6 1.5 collective-permute-start.35
  92.0 1.2 collective-permute-start.36
  93.2 8.5 %shard_map.82 = (bf16[512,2048]{1,0:T(8,128)(2,1)S(1)}, bf16[512,2048]{1,0:T(8,128)(2,1)S(1)}, f32[8,128]{1,0:T(8,128)S(1)}) custom-call(s32[8]{0:T(128)S(1)} %stack.192.refs_0_, s32[64]{0:T(128)S(1)} %fusion.4.refs_1_, f32[512,128]{1,0:T(8,128)S(1)} %collective-permute-done.25.refs_2_, f32[512,128]{1,0:T(8,128)S(1)} %collective-permute-done.26.refs_3_, ...), custom_call_target="tpu_custom_call" | custom-call | flops 12884901888 | bytes 6291456 | tf_op jit(solution)/shard_map/pallas_call | solution.py:171
  101.7 1.4 collective-permute-done.35.refs_4_
  103.2 1.0 collective-permute-done.36.refs_5_
  105.2 1.1 collective-permute-start.41
  106.3 1.2 collective-permute-start.42
  107.5 1.2 collective-permute-start.43
  108.7 8.5 %shard_map.83 = (bf16[512,2048]{1,0:T(8,128)(2,1)S(1)}, bf16[512,2048]{1,0:T(8,128)(2,1)S(1)}, f32[8,128]{1,0:T(8,128)S(1)}) custom-call(s32[8]{0:T(128)S(1)} %stack.192.refs_0_, s32[64]{0:T(128)S(1)} %fusion.3.refs_1_, f32[512,128]{1,0:T(8,128)S(1)} %collective-permute-done.33.refs_2_, f32[512,128]{1,0:T(8,128)S(1)} %collective-permute-done.34.refs_3_, ...), custom_call_target="tpu_custom_call" | custom-call | flops 12884901888 | bytes 6291456 | tf_op jit(solution)/shard_map/pallas_call | solution.py:171
  117.3 4.6 %shard_map.84 = (f32[64,2176]{1,0:T(8,128)S(1)}, f32[64,2048]{1,0:T(8,128)S(1)}) custom-call(bf16[512,2048]{1,0:T(8,128)(2,1)S(1)} %get-tuple-element.116.refs_0_.refs_3_.refs_8_, bf16[512,2048]{1,0:T(8,128)(2,1)S(1)} %get-tuple-element.124.refs_1_.refs_4_.refs_9_, bf16[512,2048]{1,0:T(8,128)(2,1)S(1)} %get-tuple-element.132.refs_2_.refs_5_.refs_10_, ...), custom_call_target="tpu_custom_call" | custom-call | flops 1610612736 | bytes 16777216 | tf_op jit(solution)/shard_map/pallas_call | solution.py:227
  122.0 1.9 collective-permute-done.44.refs_1_
  123.9 9.2 %shard_map.85 = (f32[64,2176]{1,0:T(8,128)S(1)}, f32[64,2048]{1,0:T(8,128)S(1)}, f32[64,2048]{1,0:T(8,128)S(1)}, f32[64,2048]{1,0:T(8,128)S(1)}, f32[64,2048]{1,...) custom-call(f32[64,2176]{1,0:T(8,128)S(1)} %get-tuple-element.150.refs_0_, ...), custom_call_target="tpu_custom_call" | custom-call | flops 3221225472 | bytes 16777216 | tf_op jit(solution)/shard_map/pallas_call | solution.py:338
  133.3 1.8 collective-permute-done.45.refs_1_
  135.1 9.5 %shard_map.86 = (f32[64,2176]{1,0:T(8,128)S(1)}, f32[64,2048]{1,0:T(8,128)S(1)}, f32[64,2048]{1,0:T(8,128)S(1)}, f32[64,2048]{1,0:T(8,128)S(1)}, f32[64,2048]{1,...) custom-call(f32[64,2176]{1,0:T(8,128)S(1)} %get-tuple-element.152.refs_0_, ...), custom_call_target="tpu_custom_call" | custom-call | flops 3221225472 | bytes 16777216 | tf_op jit(solution)/shard_map/pallas_call | solution.py:338
  144.8 1.8 collective-permute-done.46.refs_1_
  146.6 9.2 %shard_map.87 = (f32[64,2176]{1,0:T(8,128)S(1)}, f32[64,2048]{1,0:T(8,128)S(1)}, f32[64,2048]{1,0:T(8,128)S(1)}, f32[64,2048]{1,0:T(8,128)S(1)}, f32[64,2048]{1,...) custom-call(f32[64,2176]{1,0:T(8,128)S(1)} %get-tuple-element.159.refs_0_, ...), custom_call_target="tpu_custom_call" | custom-call | flops 3221225472 | bytes 16777216 | tf_op jit(solution)/shard_map/pallas_call | solution.py:338
  155.9 0.8 copy-done
  156.8 1.8 collective-permute-done.47.other_ref
  158.6 1.0 copy-done.1
  160.2 1.8 collective-permute-start.50
  162.0 0.8 collective-permute-start.49
  162.8 0.9 collective-permute-start.48
  163.8 3.4 %collective-permute-start.52 = (f32[64,512]{1,0:T(8,128)S(1)}, f32[64,512]{1,0:T(8,128)S(1)}, u32[]{:S(2)}, u32[]{:S(2)}) collective-permute-start(f32[64,512]{1,0:T(8,128)S(1)} %get-tuple-element.183), channel_id=1, source_target_pairs={{0,24},{2,26},{4,28},{6,30},{8,0},{10,2},{12,4},{14,6},{17,9},{19,... | collective-permute-start | bytes 393224 | tf_op jit(solution)/shard_map/ppermute | solution.py:536
  167.2 1.3 collective-permute-start.53
  168.6 3.3 %collective-permute-start.54 = (f32[64,512]{1,0:T(8,128)S(1)}, f32[64,512]{1,0:T(8,128)S(1)}, u32[]{:S(2)}, u32[]{:S(2)}) collective-permute-start(f32[64,512]{1,0:T(8,128)S(1)} %get-tuple-element.181), channel_id=1, source_target_pairs={{0,8},{2,10},{4,12},{6,14},{8,16},{10,18},{12,20},{14,22},{17,25},... | collective-permute-start | bytes 393224 | tf_op jit(solution)/shard_map/ppermute | solution.py:536
  172.1 3.6 %collective-permute-done.54 = f32[64,512]{1,0:T(8,128)S(1)} collective-permute-done((f32[64,512]{1,0:T(8,128)S(1)}, f32[64,512]{1,0:T(8,128)S(1)}, u32[]{:S(2)}, u32[]{:S(2)}) %collective-permute-start.54) | collective-permute-done | bytes 131104 | tf_op jit(solution)/shard_map/ppermute | solution.py:536
  175.7 0.7 constant_dynamic-slice_fusion
  176.4 9.9 %collective-permute-done.51.refs_1_ = f32[256,512]{1,0:T(8,128)S(1)} collective-permute-done((f32[256,512]{1,0:T(8,128)S(1)}, f32[256,512]{1,0:T(8,128)S(1)}, u32[]{:S(2)}, u32[]{:S(2)}) %collective-permute-start.51) | collective-permute-done | bytes 524320 | tf_op jit(solution)/shard_map/ppermute | solution.py:443
  186.3 1.0 collective-permute-start.55
  187.3 13.2 %collective-permute-done.55.refs_2_ = f32[256,512]{1,0:T(8,128)S(1)} collective-permute-done((f32[256,512]{1,0:T(8,128)S(1)}, f32[256,512]{1,0:T(8,128)S(1)}, u32[]{:S(2)}, u32[]{:S(2)}) %collective-permute-start.55) | collective-permute-done | bytes 524320 | tf_op jit(solution)/shard_map/ppermute | solution.py:443
  200.6 13.4 %collective-permute-done.56.refs_3_ = f32[256,512]{1,0:T(8,128)S(1)} collective-permute-done((f32[256,512]{1,0:T(8,128)S(1)}, f32[256,512]{1,0:T(8,128)S(1)}, u32[]{:S(2)}, u32[]{:S(2)}) %collective-permute-start.56) | collective-permute-done | bytes 524320 | tf_op jit(solution)/shard_map/ppermute | solution.py:443
  214.0 2.9 %shard_map.89 = f32[512,1024]{1,0:T(8,128)} custom-call(s32[8]{0:T(128)S(1)} %stack.183.where_ref, f32[256,512]{1,0:T(8,128)S(1)} %pad_maximum_fusion.refs_0_, f32[256,512]{1,0:T(8,128)S(1)} %collective-permute-done.51.refs_1_, f32[256,512]{1,0:T(8,128)S(1)} %collective-permute-done.55.refs_2_, f32[256,512]{1,0:T(8,128)S(1)} %collective-permute-done.56.refs_3_), custom_call_target="tpu_custom_call" | custom-call | tf_op jit(solution)/shard_map/pallas_call | solution.py:415
  (103 shorter events, 8.6 us)
Async XLA Ops:
  1.3 8.8 %copy-start.3 = (s32[1,4096]{1,0:T(1,128)S(1)}, s32[1,4096]{1,0:T(1,128)}, u32[]{:S(2)}) copy-start(s32[1,4096]{1,0:T(1,128)} %param.10) | copy-start | bytes 49156
  1.3 9.2 %copy-start.2 = (f32[256,512]{1,0:T(8,128)S(1)}, f32[256,512]{1,0:T(8,128)}, u32[]{:S(2)}) copy-start(f32[256,512]{1,0:T(8,128)} %param.11) | copy-start | bytes 1572868
  9.2 9.2 %collective-permute-start = (f32[2048,128]{1,0:T(8,128)}, f32[2048,128]{1,0:T(8,128)S(1)}, u32[]{:S(2)}, u32[]{:S(2)}) collective-permute-start(f32[2048,128]{1,0:T(8,128)} %shard_map.78), channel_id=1, source_target_pairs={{0,1},{1,0},{2,3},{3,2},{4,5},{5,4},{6,7},{7,6},{8,9},{9,8},{10,11... | collective-permute-start | bytes 3145736 | tf_op jit(solution)/shard_map/ppermute | solution.py:440
  19.8 9.7 %collective-permute-start.7 = (f32[40,128]{1,0:T(8,128)S(1)}, f32[40,128]{1,0:T(8,128)S(1)}, u32[]{:S(2)}, u32[]{:S(2)}) collective-permute-start(f32[40,128]{1,0:T(8,128)S(1)} %select_maximum_fusion), channel_id=1, source_target_pairs={{0,8},{8,16},{16,24},{24,0},{1,9},{9,17},{17,25},{25,1},{2,10},{10... | collective-permute-start | bytes 61448 | tf_op jit(solution)/shard_map/ppermute | solution.py:443
  22.4 7.6 %collective-permute-start.8 = (f32[40,128]{1,0:T(8,128)S(1)}, f32[40,128]{1,0:T(8,128)S(1)}, u32[]{:S(2)}, u32[]{:S(2)}) collective-permute-start(f32[40,128]{1,0:T(8,128)S(1)} %select_maximum_fusion), channel_id=1, source_target_pairs={{0,16},{8,24},{16,0},{24,8},{1,17},{9,25},{17,1},{25,9},{2,18},{10... | collective-permute-start | bytes 61448 | tf_op jit(solution)/shard_map/ppermute | solution.py:443
  25.0 5.7 %collective-permute-start.9 = (f32[40,128]{1,0:T(8,128)S(1)}, f32[40,128]{1,0:T(8,128)S(1)}, u32[]{:S(2)}, u32[]{:S(2)}) collective-permute-start(f32[40,128]{1,0:T(8,128)S(1)} %select_maximum_fusion), channel_id=1, source_target_pairs={{0,24},{8,0},{16,8},{24,16},{1,25},{9,1},{17,9},{25,17},{2,26},{10... | collective-permute-start | bytes 61448 | tf_op jit(solution)/shard_map/ppermute | solution.py:443
  26.4 10.2 %collective-permute-start.3 = (f32[512,128]{1,0:T(8,128)S(1)}, f32[512,128]{1,0:T(8,128)S(1)}, u32[]{:S(2)}, u32[]{:S(2)}) collective-permute-start(f32[512,128]{1,0:T(8,128)S(1)} %get-tuple-element.179), channel_id=1, source_target_pairs={{0,6},{1,7},{2,4},{3,5},{4,2},{5,3},{6,0},{7,1},{8,14},{9,15},{10,... | collective-permute-start | bytes 786440 | tf_op jit(solution)/shard_map/ppermute | solution.py:440
  28.9 11.9 %collective-permute-start.2 = (f32[512,128]{1,0:T(8,128)S(1)}, f32[512,128]{1,0:T(8,128)S(1)}, u32[]{:S(2)}, u32[]{:S(2)}) collective-permute-start(f32[512,128]{1,0:T(8,128)S(1)} %get-tuple-element.180), channel_id=1, source_target_pairs={{0,4},{1,5},{2,6},{3,7},{4,0},{5,1},{6,2},{7,3},{8,12},{9,13},{10,... | collective-permute-start | bytes 786440 | tf_op jit(solution)/shard_map/ppermute | solution.py:440
  29.4 11.5 %collective-permute-start.1 = (f32[512,128]{1,0:T(8,128)S(1)}, f32[512,128]{1,0:T(8,128)S(1)}, u32[]{:S(2)}, u32[]{:S(2)}) collective-permute-start(f32[512,128]{1,0:T(8,128)S(1)} %get-tuple-element.178), channel_id=1, source_target_pairs={{0,2},{1,3},{2,0},{3,1},{4,6},{5,7},{6,4},{7,5},{8,10},{9,11},{10,... | collective-permute-start | bytes 786440 | tf_op jit(solution)/shard_map/ppermute | solution.py:440
  30.0 11.0 %collective-permute-start.4 = (f32[64,512]{1,0:T(8,128)S(1)}, f32[64,512]{1,0:T(8,128)S(1)}, u32[]{:S(2)}, u32[]{:S(2)}) collective-permute-start(f32[64,512]{1,0:T(8,128)S(1)} %get-tuple-element.91), channel_id=1, source_target_pairs={{0,8},{8,16},{16,24},{24,0},{1,9},{9,17},{17,25},{25,1},{2,10},{10... | collective-permute-start | bytes 393224 | tf_op jit(solution)/shard_map/ppermute | solution.py:443
  30.7 11.1 %collective-permute-start.5 = (f32[64,512]{1,0:T(8,128)S(1)}, f32[64,512]{1,0:T(8,128)S(1)}, u32[]{:S(2)}, u32[]{:S(2)}) collective-permute-start(f32[64,512]{1,0:T(8,128)S(1)} %get-tuple-element.92), channel_id=1, source_target_pairs={{0,16},{8,24},{16,0},{24,8},{1,17},{9,25},{17,1},{25,9},{2,18},{10... | collective-permute-start | bytes 393224 | tf_op jit(solution)/shard_map/ppermute | solution.py:443
  36.6 6.0 %collective-permute-start.6 = (f32[64,512]{1,0:T(8,128)S(1)}, f32[64,512]{1,0:T(8,128)S(1)}, u32[]{:S(2)}, u32[]{:S(2)}) collective-permute-start(f32[64,512]{1,0:T(8,128)S(1)} %get-tuple-element.93), channel_id=1, source_target_pairs={{0,24},{8,0},{16,8},{24,16},{1,25},{9,1},{17,9},{25,17},{2,26},{10... | collective-permute-start | bytes 393224 | tf_op jit(solution)/shard_map/ppermute | solution.py:443
  42.6 9.2 %collective-permute-start.10 = (f32[512,128]{1,0:T(8,128)S(1)}, f32[512,128]{1,0:T(8,128)S(1)}, u32[]{:S(2)}, u32[]{:S(2)}) collective-permute-start(f32[512,128]{1,0:T(8,128)S(1)} %fusion.1.refs_2_), channel_id=1, source_target_pairs={{0,2},{1,3},{2,0},{3,1},{4,6},{5,7},{6,4},{7,5},{8,10},{9,11},{10,... | collective-permute-start | bytes 786440 | tf_op jit(solution)/shard_map/ppermute | solution.py:440
  44.1 12.0 %collective-permute-start.11 = (f32[512,128]{1,0:T(8,128)S(1)}, f32[512,128]{1,0:T(8,128)S(1)}, u32[]{:S(2)}, u32[]{:S(2)}) collective-permute-start(f32[512,128]{1,0:T(8,128)S(1)} %fusion.1.refs_2_), channel_id=1, source_target_pairs={{0,4},{1,5},{2,6},{3,7},{4,0},{5,1},{6,2},{7,3},{8,12},{9,13},{10,... | collective-permute-start | bytes 786440 | tf_op jit(solution)/shard_map/ppermute | solution.py:440
  45.6 10.5 %collective-permute-start.12 = (f32[512,128]{1,0:T(8,128)S(1)}, f32[512,128]{1,0:T(8,128)S(1)}, u32[]{:S(2)}, u32[]{:S(2)}) collective-permute-start(f32[512,128]{1,0:T(8,128)S(1)} %fusion.1.refs_2_), channel_id=1, source_target_pairs={{0,6},{1,7},{2,4},{3,5},{4,2},{5,3},{6,0},{7,1},{8,14},{9,15},{10,... | collective-permute-start | bytes 786440 | tf_op jit(solution)/shard_map/ppermute | solution.py:440
  46.1 11.4 %collective-permute-start.17 = (f32[512,128]{1,0:T(8,128)S(1)}, f32[512,128]{1,0:T(8,128)S(1)}, u32[]{:S(2)}, u32[]{:S(2)}) collective-permute-start(f32[512,128]{1,0:T(8,128)S(1)} %fusion.1.refs_2_), channel_id=1, source_target_pairs={{0,8},{8,16},{16,24},{24,0},{1,9},{9,17},{17,25},{25,1},{2,10},{10... | collective-permute-start | bytes 786440 | tf_op jit(solution)/shard_map/ppermute | solution.py:443
  48.1 9.9 %collective-permute-start.13 = (f32[512,128]{1,0:T(8,128)S(1)}, f32[512,128]{1,0:T(8,128)S(1)}, u32[]{:S(2)}, u32[]{:S(2)}) collective-permute-start(f32[512,128]{1,0:T(8,128)S(1)} %fusion.1.refs_2_), channel_id=1, source_target_pairs={{0,1},{1,0},{2,3},{3,2},{4,5},{5,4},{6,7},{7,6},{8,9},{9,8},{10,11... | collective-permute-start | bytes 786440 | tf_op jit(solution)/shard_map/ppermute | solution.py:440
  51.8 7.8 %collective-permute-start.14 = (f32[512,128]{1,0:T(8,128)S(1)}, f32[512,128]{1,0:T(8,128)S(1)}, u32[]{:S(2)}, u32[]{:S(2)}) collective-permute-start(f32[512,128]{1,0:T(8,128)S(1)} %collective-permute-done.10.refs_3_), channel_id=1, source_target_pairs={{0,1},{1,0},{2,3},{3,2},{4,5},{5,4},{6,7},{7,6},{8,9},{9,8},{10,11... | collective-permute-start | bytes 786440 | tf_op jit(solution)/shard_map/ppermute | solution.py:440
  56.1 5.0 %collective-permute-start.15 = (f32[512,128]{1,0:T(8,128)S(1)}, f32[512,128]{1,0:T(8,128)S(1)}, u32[]{:S(2)}, u32[]{:S(2)}) collective-permute-start(f32[512,128]{1,0:T(8,128)S(1)} %collective-permute-done.11.refs_4_), channel_id=1, source_target_pairs={{0,1},{1,0},{2,3},{3,2},{4,5},{5,4},{6,7},{7,6},{8,9},{9,8},{10,11... | collective-permute-start | bytes 786440 | tf_op jit(solution)/shard_map/ppermute | solution.py:440
  56.1 8.1 %collective-permute-start.16 = (f32[512,128]{1,0:T(8,128)S(1)}, f32[512,128]{1,0:T(8,128)S(1)}, u32[]{:S(2)}, u32[]{:S(2)}) collective-permute-start(f32[512,128]{1,0:T(8,128)S(1)} %collective-permute-done.12.refs_5_), channel_id=1, source_target_pairs={{0,1},{1,0},{2,3},{3,2},{4,5},{5,4},{6,7},{7,6},{8,9},{9,8},{10,11... | collective-permute-start | bytes 786440 | tf_op jit(solution)/shard_map/ppermute | solution.py:440
  57.5 15.3 %collective-permute-start.18 = (f32[512,128]{1,0:T(8,128)S(1)}, f32[512,128]{1,0:T(8,128)S(1)}, u32[]{:S(2)}, u32[]{:S(2)}) collective-permute-start(f32[512,128]{1,0:T(8,128)S(1)} %collective-permute-done.17.refs_2_), channel_id=1, source_target_pairs={{0,2},{1,3},{2,0},{3,1},{4,6},{5,7},{6,4},{7,5},{8,10},{9,11},{10,... | collective-permute-start | bytes 786440 | tf_op jit(solution)/shard_map/ppermute | solution.py:440
  58.0 14.8 %collective-permute-start.19 = (f32[512,128]{1,0:T(8,128)S(1)}, f32[512,128]{1,0:T(8,128)S(1)}, u32[]{:S(2)}, u32[]{:S(2)}) collective-permute-start(f32[512,128]{1,0:T(8,128)S(1)} %collective-permute-done.17.refs_2_), channel_id=1, source_target_pairs={{0,4},{1,5},{2,6},{3,7},{4,0},{5,1},{6,2},{7,3},{8,12},{9,13},{10,... | collective-permute-start | bytes 786440 | tf_op jit(solution)/shard_map/ppermute | solution.py:440
  59.6 13.1 %collective-permute-start.20 = (f32[512,128]{1,0:T(8,128)S(1)}, f32[512,128]{1,0:T(8,128)S(1)}, u32[]{:S(2)}, u32[]{:S(2)}) collective-permute-start(f32[512,128]{1,0:T(8,128)S(1)} %collective-permute-done.17.refs_2_), channel_id=1, source_target_pairs={{0,6},{1,7},{2,4},{3,5},{4,2},{5,3},{6,0},{7,1},{8,14},{9,15},{10,... | collective-permute-start | bytes 786440 | tf_op jit(solution)/shard_map/ppermute | solution.py:440
  61.0 12.8 %collective-permute-start.25 = (f32[512,128]{1,0:T(8,128)S(1)}, f32[512,128]{1,0:T(8,128)S(1)}, u32[]{:S(2)}, u32[]{:S(2)}) collective-permute-start(f32[512,128]{1,0:T(8,128)S(1)} %collective-permute-done.17.refs_2_), channel_id=1, source_target_pairs={{0,8},{8,16},{16,24},{24,0},{1,9},{9,17},{17,25},{25,1},{2,10},{10... | collective-permute-start | bytes 786440 | tf_op jit(solution)/shard_map/ppermute | solution.py:443
  72.8 1.8 collective-permute-start.21
  72.9 3.0 %collective-permute-start.22 = (f32[512,128]{1,0:T(8,128)S(1)}, f32[512,128]{1,0:T(8,128)S(1)}, u32[]{:S(2)}, u32[]{:S(2)}) collective-permute-start(f32[512,128]{1,0:T(8,128)S(1)} %collective-permute-done.18.refs_3_), channel_id=1, source_target_pairs={{0,1},{1,0},{2,3},{3,2},{4,5},{5,4},{6,7},{7,6},{8,9},{9,8},{10,11... | collective-permute-start | bytes 786440 | tf_op jit(solution)/shard_map/ppermute | solution.py:440
  73.4 4.0 %collective-permute-start.23 = (f32[512,128]{1,0:T(8,128)S(1)}, f32[512,128]{1,0:T(8,128)S(1)}, u32[]{:S(2)}, u32[]{:S(2)}) collective-permute-start(f32[512,128]{1,0:T(8,128)S(1)} %collective-permute-done.19.refs_4_), channel_id=1, source_target_pairs={{0,1},{1,0},{2,3},{3,2},{4,5},{5,4},{6,7},{7,6},{8,9},{9,8},{10,11... | collective-permute-start | bytes 786440 | tf_op jit(solution)/shard_map/ppermute | solution.py:440
  73.4 6.5 %collective-permute-start.24 = (f32[512,128]{1,0:T(8,128)S(1)}, f32[512,128]{1,0:T(8,128)S(1)}, u32[]{:S(2)}, u32[]{:S(2)}) collective-permute-start(f32[512,128]{1,0:T(8,128)S(1)} %collective-permute-done.20.refs_5_), channel_id=1, source_target_pairs={{0,1},{1,0},{2,3},{3,2},{4,5},{5,4},{6,7},{7,6},{8,9},{9,8},{10,11... | collective-permute-start | bytes 786440 | tf_op jit(solution)/shard_map/ppermute | solution.py:440
  73.9 14.6 %collective-permute-start.26 = (f32[512,128]{1,0:T(8,128)S(1)}, f32[512,128]{1,0:T(8,128)S(1)}, u32[]{:S(2)}, u32[]{:S(2)}) collective-permute-start(f32[512,128]{1,0:T(8,128)S(1)} %collective-permute-done.25.refs_2_), channel_id=1, source_target_pairs={{0,2},{1,3},{2,0},{3,1},{4,6},{5,7},{6,4},{7,5},{8,10},{9,11},{10,... | collective-permute-start | bytes 786440 | tf_op jit(solution)/shard_map/ppermute | solution.py:440
  74.6 14.0 %collective-permute-start.27 = (f32[512,128]{1,0:T(8,128)S(1)}, f32[512,128]{1,0:T(8,128)S(1)}, u32[]{:S(2)}, u32[]{:S(2)}) collective-permute-start(f32[512,128]{1,0:T(8,128)S(1)} %collective-permute-done.25.refs_2_), channel_id=1, source_target_pairs={{0,4},{1,5},{2,6},{3,7},{4,0},{5,1},{6,2},{7,3},{8,12},{9,13},{10,... | collective-permute-start | bytes 786440 | tf_op jit(solution)/shard_map/ppermute | solution.py:440
  75.9 12.8 %collective-permute-start.28 = (f32[512,128]{1,0:T(8,128)S(1)}, f32[512,128]{1,0:T(8,128)S(1)}, u32[]{:S(2)}, u32[]{:S(2)}) collective-permute-start(f32[512,128]{1,0:T(8,128)S(1)} %collective-permute-done.25.refs_2_), channel_id=1, source_target_pairs={{0,6},{1,7},{2,4},{3,5},{4,2},{5,3},{6,0},{7,1},{8,14},{9,15},{10,... | collective-permute-start | bytes 786440 | tf_op jit(solution)/shard_map/ppermute | solution.py:440
  77.4 12.3 %collective-permute-start.33 = (f32[512,128]{1,0:T(8,128)S(1)}, f32[512,128]{1,0:T(8,128)S(1)}, u32[]{:S(2)}, u32[]{:S(2)}) collective-permute-start(f32[512,128]{1,0:T(8,128)S(1)} %collective-permute-done.25.refs_2_), channel_id=1, source_target_pairs={{0,8},{8,16},{16,24},{24,0},{1,9},{9,17},{17,25},{25,1},{2,10},{10... | collective-permute-start | bytes 786440 | tf_op jit(solution)/shard_map/ppermute | solution.py:443
  88.7 1.9 collective-permute-start.29
  88.7 3.3 %collective-permute-start.30 = (f32[512,128]{1,0:T(8,128)S(1)}, f32[512,128]{1,0:T(8,128)S(1)}, u32[]{:S(2)}, u32[]{:S(2)}) collective-permute-start(f32[512,128]{1,0:T(8,128)S(1)} %collective-permute-done.26.refs_3_), channel_id=1, source_target_pairs={{0,1},{1,0},{2,3},{3,2},{4,5},{5,4},{6,7},{7,6},{8,9},{9,8},{10,11... | collective-permute-start | bytes 786440 | tf_op jit(solution)/shard_map/ppermute | solution.py:440
  89.2 4.0 %collective-permute-start.31 = (f32[512,128]{1,0:T(8,128)S(1)}, f32[512,128]{1,0:T(8,128)S(1)}, u32[]{:S(2)}, u32[]{:S(2)}) collective-permute-start(f32[512,128]{1,0:T(8,128)S(1)} %collective-permute-done.27.refs_4_), channel_id=1, source_target_pairs={{0,1},{1,0},{2,3},{3,2},{4,5},{5,4},{6,7},{7,6},{8,9},{9,8},{10,11... | collective-permute-start | bytes 786440 | tf_op jit(solution)/shard_map/ppermute | solution.py:440
  89.2 4.0 %collective-permute-start.32 = (f32[512,128]{1,0:T(8,128)S(1)}, f32[512,128]{1,0:T(8,128)S(1)}, u32[]{:S(2)}, u32[]{:S(2)}) collective-permute-start(f32[512,128]{1,0:T(8,128)S(1)} %collective-permute-done.28.refs_5_), channel_id=1, source_target_pairs={{0,1},{1,0},{2,3},{3,2},{4,5},{5,4},{6,7},{7,6},{8,9},{9,8},{10,11... | collective-permute-start | bytes 786440 | tf_op jit(solution)/shard_map/ppermute | solution.py:440
  89.7 12.0 %collective-permute-start.34 = (f32[512,128]{1,0:T(8,128)S(1)}, f32[512,128]{1,0:T(8,128)S(1)}, u32[]{:S(2)}, u32[]{:S(2)}) collective-permute-start(f32[512,128]{1,0:T(8,128)S(1)} %collective-permute-done.33.refs_2_), channel_id=1, source_target_pairs={{0,2},{1,3},{2,0},{3,1},{4,6},{5,7},{6,4},{7,5},{8,10},{9,11},{10,... | collective-permute-start | bytes 786440 | tf_op jit(solution)/shard_map/ppermute | solution.py:440
  90.6 12.6 %collective-permute-start.35 = (f32[512,128]{1,0:T(8,128)S(1)}, f32[512,128]{1,0:T(8,128)S(1)}, u32[]{:S(2)}, u32[]{:S(2)}) collective-permute-start(f32[512,128]{1,0:T(8,128)S(1)} %collective-permute-done.33.refs_2_), channel_id=1, source_target_pairs={{0,4},{1,5},{2,6},{3,7},{4,0},{5,1},{6,2},{7,3},{8,12},{9,13},{10,... | collective-permute-start | bytes 786440 | tf_op jit(solution)/shard_map/ppermute | solution.py:440
  92.0 12.2 %collective-permute-start.36 = (f32[512,128]{1,0:T(8,128)S(1)}, f32[512,128]{1,0:T(8,128)S(1)}, u32[]{:S(2)}, u32[]{:S(2)}) collective-permute-start(f32[512,128]{1,0:T(8,128)S(1)} %collective-permute-done.33.refs_2_), channel_id=1, source_target_pairs={{0,6},{1,7},{2,4},{3,5},{4,2},{5,3},{6,0},{7,1},{8,14},{9,15},{10,... | collective-permute-start | bytes 786440 | tf_op jit(solution)/shard_map/ppermute | solution.py:440
  104.2 2.2 collective-permute-start.37
  104.2 3.3 %collective-permute-start.38 = (f32[512,128]{1,0:T(8,128)S(1)}, f32[512,128]{1,0:T(8,128)S(1)}, u32[]{:S(2)}, u32[]{:S(2)}) collective-permute-start(f32[512,128]{1,0:T(8,128)S(1)} %collective-permute-done.34.refs_3_), channel_id=1, source_target_pairs={{0,1},{1,0},{2,3},{3,2},{4,5},{5,4},{6,7},{7,6},{8,9},{9,8},{10,11... | collective-permute-start | bytes 786440 | tf_op jit(solution)/shard_map/ppermute | solution.py:440
  104.7 4.0 %collective-permute-start.39 = (f32[512,128]{1,0:T(8,128)S(1)}, f32[512,128]{1,0:T(8,128)S(1)}, u32[]{:S(2)}, u32[]{:S(2)}) collective-permute-start(f32[512,128]{1,0:T(8,128)S(1)} %collective-permute-done.35.refs_4_), channel_id=1, source_target_pairs={{0,1},{1,0},{2,3},{3,2},{4,5},{5,4},{6,7},{7,6},{8,9},{9,8},{10,11... | collective-permute-start | bytes 786440 | tf_op jit(solution)/shard_map/ppermute | solution.py:440
  104.7 4.0 %collective-permute-start.40 = (f32[512,128]{1,0:T(8,128)S(1)}, f32[512,128]{1,0:T(8,128)S(1)}, u32[]{:S(2)}, u32[]{:S(2)}) collective-permute-start(f32[512,128]{1,0:T(8,128)S(1)} %collective-permute-done.36.refs_5_), channel_id=1, source_target_pairs={{0,1},{1,0},{2,3},{3,2},{4,5},{5,4},{6,7},{7,6},{8,9},{9,8},{10,11... | collective-permute-start | bytes 786440 | tf_op jit(solution)/shard_map/ppermute | solution.py:440
  105.2 12.0 %collective-permute-start.41 = (f32[64,512]{1,0:T(8,128)S(1)}, f32[64,512]{1,0:T(8,128)S(1)}, u32[]{:S(2)}, u32[]{:S(2)}) collective-permute-start(f32[64,512]{1,0:T(8,128)S(1)} %get-tuple-element.147), channel_id=1, source_target_pairs={{0,2},{1,3},{2,0},{3,1},{4,6},{5,7},{6,4},{7,5},{8,10},{9,11},{10,... | collective-permute-start | bytes 393224 | tf_op jit(solution)/shard_map/ppermute | solution.py:440
  106.3 10.9 %collective-permute-start.42 = (f32[64,512]{1,0:T(8,128)S(1)}, f32[64,512]{1,0:T(8,128)S(1)}, u32[]{:S(2)}, u32[]{:S(2)}) collective-permute-start(f32[64,512]{1,0:T(8,128)S(1)} %get-tuple-element.148), channel_id=1, source_target_pairs={{0,4},{1,5},{2,6},{3,7},{4,0},{5,1},{6,2},{7,3},{8,12},{9,13},{10,... | collective-permute-start | bytes 393224 | tf_op jit(solution)/shard_map/ppermute | solution.py:440
  107.5 9.7 %collective-permute-start.43 = (f32[64,512]{1,0:T(8,128)S(1)}, f32[64,512]{1,0:T(8,128)S(1)}, u32[]{:S(2)}, u32[]{:S(2)}) collective-permute-start(f32[64,512]{1,0:T(8,128)S(1)} %get-tuple-element.149), channel_id=1, source_target_pairs={{0,6},{1,7},{2,4},{3,5},{4,2},{5,3},{6,0},{7,1},{8,14},{9,15},{10,... | collective-permute-start | bytes 393224 | tf_op jit(solution)/shard_map/ppermute | solution.py:440
  121.9 2.0 collective-permute-start.44
  133.1 2.0 collective-permute-start.45
  144.6 2.0 collective-permute-start.46
  155.9 0.8 copy-start
  156.6 2.0 collective-permute-start.47
  158.6 1.0 copy-start.1
  160.2 8.4 %collective-permute-start.50 = (f32[64,512]{1,0:T(8,128)S(1)}, f32[64,512]{1,0:T(8,128)S(1)}, u32[]{:S(2)}, u32[]{:S(2)}) collective-permute-start(f32[64,512]{1,0:T(8,128)S(1)} %get-tuple-element.185), channel_id=1, source_target_pairs={{0,6},{1,7},{2,4},{3,5},{4,2},{5,3},{6,0},{7,1},{8,14},{9,15},{10,... | collective-permute-start | bytes 393224 | tf_op jit(solution)/shard_map/ppermute | solution.py:440
  162.0 9.8 %collective-permute-start.49 = (f32[64,512]{1,0:T(8,128)S(1)}, f32[64,512]{1,0:T(8,128)S(1)}, u32[]{:S(2)}, u32[]{:S(2)}) collective-permute-start(f32[64,512]{1,0:T(8,128)S(1)} %get-tuple-element.186), channel_id=1, source_target_pairs={{0,4},{1,5},{2,6},{3,7},{4,0},{5,1},{6,2},{7,3},{8,12},{9,13},{10,... | collective-permute-start | bytes 393224 | tf_op jit(solution)/shard_map/ppermute | solution.py:440
  162.8 9.0 %collective-permute-start.48 = (f32[64,512]{1,0:T(8,128)S(1)}, f32[64,512]{1,0:T(8,128)S(1)}, u32[]{:S(2)}, u32[]{:S(2)}) collective-permute-start(f32[64,512]{1,0:T(8,128)S(1)} %get-tuple-element.187), channel_id=1, source_target_pairs={{0,2},{1,3},{2,0},{3,1},{4,6},{5,7},{6,4},{7,5},{8,10},{9,11},{10,... | collective-permute-start | bytes 393224 | tf_op jit(solution)/shard_map/ppermute | solution.py:440
  163.8 8.3 %collective-permute-start.52 = (f32[64,512]{1,0:T(8,128)S(1)}, f32[64,512]{1,0:T(8,128)S(1)}, u32[]{:S(2)}, u32[]{:S(2)}) collective-permute-start(f32[64,512]{1,0:T(8,128)S(1)} %get-tuple-element.183), channel_id=1, source_target_pairs={{0,24},{2,26},{4,28},{6,30},{8,0},{10,2},{12,4},{14,6},{17,9},{19,... | collective-permute-start | bytes 393224 | tf_op jit(solution)/shard_map/ppermute | solution.py:536
  167.2 4.9 %collective-permute-start.53 = (f32[64,512]{1,0:T(8,128)S(1)}, f32[64,512]{1,0:T(8,128)S(1)}, u32[]{:S(2)}, u32[]{:S(2)}) collective-permute-start(f32[64,512]{1,0:T(8,128)S(1)} %get-tuple-element.182), channel_id=1, source_target_pairs={{0,16},{2,18},{4,20},{6,22},{8,24},{10,26},{12,28},{14,30},{17,1},... | collective-permute-start | bytes 393224 | tf_op jit(solution)/shard_map/ppermute | solution.py:536
  168.6 7.1 %collective-permute-start.54 = (f32[64,512]{1,0:T(8,128)S(1)}, f32[64,512]{1,0:T(8,128)S(1)}, u32[]{:S(2)}, u32[]{:S(2)}) collective-permute-start(f32[64,512]{1,0:T(8,128)S(1)} %get-tuple-element.181), channel_id=1, source_target_pairs={{0,8},{2,10},{4,12},{6,14},{8,16},{10,18},{12,20},{14,22},{17,25},... | collective-permute-start | bytes 393224 | tf_op jit(solution)/shard_map/ppermute | solution.py:536
  171.9 14.4 %collective-permute-start.51 = (f32[256,512]{1,0:T(8,128)S(1)}, f32[256,512]{1,0:T(8,128)S(1)}, u32[]{:S(2)}, u32[]{:S(2)}) collective-permute-start(f32[256,512]{1,0:T(8,128)S(1)} %pad_maximum_fusion.refs_0_), channel_id=1, source_target_pairs={{0,8},{8,16},{16,24},{24,0},{1,9},{9,17},{17,25},{25,1},{2,10},{10... | collective-permute-start | bytes 1572872 | tf_op jit(solution)/shard_map/ppermute | solution.py:443
  186.3 14.2 %collective-permute-start.55 = (f32[256,512]{1,0:T(8,128)S(1)}, f32[256,512]{1,0:T(8,128)S(1)}, u32[]{:S(2)}, u32[]{:S(2)}) collective-permute-start(f32[256,512]{1,0:T(8,128)S(1)} %collective-permute-done.51.refs_1_), channel_id=1, source_target_pairs={{0,8},{8,16},{16,24},{24,0},{1,9},{9,17},{17,25},{25,1},{2,10},{10... | collective-permute-start | bytes 1572872 | tf_op jit(solution)/shard_map/ppermute | solution.py:443
  200.5 13.5 %collective-permute-start.56 = (f32[256,512]{1,0:T(8,128)S(1)}, f32[256,512]{1,0:T(8,128)S(1)}, u32[]{:S(2)}, u32[]{:S(2)}) collective-permute-start(f32[256,512]{1,0:T(8,128)S(1)} %collective-permute-done.55.refs_2_), channel_id=1, source_target_pairs={{0,8},{8,16},{16,24},{24,0},{1,9},{9,17},{17,25},{25,1},{2,10},{10... | collective-permute-start | bytes 1572872 | tf_op jit(solution)/shard_map/ppermute | solution.py:443

commit v10 on v9

--- a/solution.py
+++ b/solution.py
@@ -472,16 +472,17 @@
     give = project(blocks + 1 - core, activations, out_grads, w_in, w_out, share)
     keep = project(blocks + core, activations, out_grads, w_in, w_out, share)
     kept = (keep + swap(give, 1)).reshape((n_c, share, LANES))
-    kept, extra, parts = lax.optimization_barrier((kept, extra, parts))
+    own, parts = lax.optimization_barrier((kept[0], parts))
+    came = [swap(kept[k], 2 * k) for k in range(1, n_c)]
+    came[0], extra = lax.optimization_barrier((came[0], extra))
+    for part in came:
+        own = own + part
     extras = [extra] + [shift(extra, away) for away in range(1, n_dp)]
     plane_ids = [one[:id_rows].reshape((1, tokens)) for one in extras]
     firsts = [one[id_rows, :EX_DEV // group].astype(jnp.int32) for one in extras]
-    own = kept[0]
-    for k in range(1, n_c):
-        own = own + swap(kept[k], 2 * k)
 
     parts = [parts[0]] + [shift(parts[k], k) for k in range(1, n_dp)]
-    own, parts, plane_ids, firsts = lax.optimization_barrier((own, parts, plane_ids, firsts))
+    own, parts = lax.optimization_barrier((own, parts))
 
     rings = [own]
     for _ in range(n_dp - 1):

time: 217 us -> 220 us (1.014)
  starting transfers between devices: 54.3 us -> 58.8 us
  waiting for transfers between devices: 69.1 us -> 66.8 us
    ppermute x42, waiting for transfers between devices: 27.5 us -> 18.7 us  [swap(): return lax.ppermute(values, 'tensor', [(a, a ^ mask) for a in range(n_t)])]
    ppermute x12, waiting for transfers between devices: 38.1 us -> 42.8 us  [shift(): lax.ppermute(values, 'dp', [(a, (a + by) % n_dp) for a in range(n_dp)])]
    ppermute x12, starting transfers between devices: 17 us -> 19.5 us  [shift(): lax.ppermute(values, 'dp', [(a, (a + by) % n_dp) for a in range(n_dp)])]
  transfers between devices with their start and end apart: 57 -> 57, of which waited for: 18 -> 22; matrix products, arithmetic and copies ran while one was open for 1% -> 1% of each run, Pallas kernels for 20% -> 19%
where the time goes in v10:
time: 220 us; the launch traced here: 219 us
  Pallas kernels  86.2 us (39%)
  waiting for transfers between devices  66.8 us (30%)
  starting transfers between devices  58.8 us (27%)
  local copies, waits for them, and re-layouts  3.14 us (1%)
  other arithmetic  3.03 us (1%)
    ppermute x12, waiting for transfers between devices, shift(): lax.ppermute(values, 'dp', [(a, (a + by) % n_dp) for a in range(n_dp)])  42.8 us
    pallas_call x4, Pallas kernels, build(): pl.pallas_call(functools.partial(build_kernel, ranks, share, ex_block, le...  34.1 us
    ppermute x42, starting transfers between devices, swap(): return lax.ppermute(values, 'tensor', [(a, a ^ mask) for a in range(n_t)])  29.8 us
    pallas_call x3, Pallas kernels, one_step(): pl.pallas_call(functools.partial(step_kernel, first, planes, examples, co...  27.9 us
    ppermute x12, starting transfers between devices, shift(): lax.ppermute(values, 'dp', [(a, (a + by) % n_dp) for a in range(n_dp)])  19.5 us
    ppermute x42, waiting for transfers between devices, swap(): return lax.ppermute(values, 'tensor', [(a, a ^ mask) for a in range(n_t)])  18.7 us
    pallas_call x2, Pallas kernels, project(): pl.pallas_call(project_kernel, out_shape=jax.ShapeDtypeStruct((steps * bl...  15.6 us
    ppermute x3, starting transfers between devices, send(): return lax.ppermute(values, ('dp', 'tensor'), pairs)  9.49 us
  transfers between devices with their start and end apart: 57, of which 22 were waited for; matrix products, arithmetic and copies ran while one was open for 1% of the time, Pallas kernels for 19%

profile of v10, /device:TPU:0, one launch (start us, length us, event | category | flops | bytes accessed | tf_op | source)
XLA Modules:
  0.0 219.2 jit_solution(45883615317902316)
XLA Ops:
  1.3 7.9 %shard_map.78 = f32[2048,128]{1,0:T(8,128)} custom-call(s32[4]{0:T(128)} %get-tuple-element.162.order_ref, bf16[4096,512]{1,0:T(8,128)(2,1)} %refs_3_.3, bf16[4096,512]{1,0:T(8,128)(2,1)} %refs_3_.3, bf16[4096,512]{1,0:T(8,128)(2,1)} %refs_3_.3, bf16[4096,512]{1,0:T(8,128)(2,1)} %refs_3_.3, bf16[4096,1792]{1,0:T(8,128)(2,1)} %refs_7_.3, ...), custom_call_target="tpu_custom_call" | custom-call | flops 9663676416 | bytes 9437184 | tf_op jit(solution)/shard_map/pallas_call | solution.py:58
  10.6 7.7 %shard_map.77 = f32[2048,128]{1,0:T(8,128)} custom-call(s32[4]{0:T(128)} %broadcast_add_fusion.order_ref, bf16[4096,512]{1,0:T(8,128)(2,1)} %refs_3_.3, bf16[4096,512]{1,0:T(8,128)(2,1)} %refs_3_.3, bf16[4096,512]{1,0:T(8,128)(2,1)} %refs_3_.3, bf16[4096,512]{1,0:T(8,128)(2,1)} %refs_3_.3, bf16[4096,1792]{1,0:T(8,128)(2,1)} %refs_7_.3, ...), custom_call_target="tpu_custom_call" | custom-call | flops 9663676416 | bytes 9437184 | tf_op jit(solution)/shard_map/pallas_call | solution.py:58
  18.4 1.4 add.390
  19.8 2.6 %collective-permute-start.1 = (f32[512,128]{1,0:T(8,128)S(1)}, f32[512,128]{1,0:T(8,128)S(1)}, u32[]{:S(2)}, u32[]{:S(2)}) collective-permute-start(f32[512,128]{1,0:T(8,128)S(1)} %get-tuple-element.167), channel_id=1, source_target_pairs={{0,2},{1,3},{2,0},{3,1},{4,6},{5,7},{6,4},{7,5},{8,10},{9,11},{10,... | collective-permute-start | bytes 786440 | tf_op jit(solution)/shard_map/ppermute | solution.py:440
  22.4 1.5 collective-permute-start.6
  24.2 2.0 collective-permute-start.7
  26.2 2.6 %collective-permute-start.8 = (f32[64,512]{1,0:T(8,128)S(1)}, f32[64,512]{1,0:T(8,128)S(1)}, u32[]{:S(2)}, u32[]{:S(2)}) collective-permute-start(f32[64,512]{1,0:T(8,128)S(1)} %get-tuple-element.87), channel_id=1, source_target_pairs={{0,16},{8,24},{16,0},{24,8},{1,17},{9,25},{17,1},{25,9},{2,18},{10... | collective-permute-start | bytes 393224 | tf_op jit(solution)/shard_map/ppermute | solution.py:443
  28.8 0.7 collective-permute-done.1
  29.5 4.1 %collective-permute-start.9 = (f32[64,512]{1,0:T(8,128)S(1)}, f32[64,512]{1,0:T(8,128)S(1)}, u32[]{:S(2)}, u32[]{:S(2)}) collective-permute-start(f32[64,512]{1,0:T(8,128)S(1)} %get-tuple-element.88), channel_id=1, source_target_pairs={{0,24},{8,0},{16,8},{24,16},{1,25},{9,1},{17,9},{25,17},{2,26},{10... | collective-permute-start | bytes 393224 | tf_op jit(solution)/shard_map/ppermute | solution.py:443
  33.6 2.7 %collective-permute-done.6 = f32[512,128]{1,0:T(8,128)S(1)} collective-permute-done((f32[512,128]{1,0:T(8,128)S(1)}, f32[512,128]{1,0:T(8,128)S(1)}, u32[]{:S(2)}, u32[]{:S(2)}) %collective-permute-start.6) | collective-permute-done | bytes 262176 | tf_op jit(solution)/shard_map/ppermute | solution.py:440
  36.3 1.4 collective-permute-done.5
  37.8 1.6 collective-permute-start.10
  39.4 1.5 collective-permute-start.11
  41.3 2.8 %collective-permute-start.2 = (f32[40,128]{1,0:T(8,128)S(1)}, f32[40,128]{1,0:T(8,128)S(1)}, u32[]{:S(2)}, u32[]{:S(2)}) collective-permute-start(f32[40,128]{1,0:T(8,128)S(1)} %select_maximum_fusion), channel_id=1, source_target_pairs={{0,8},{8,16},{16,24},{24,0},{1,9},{9,17},{17,25},{25,1},{2,10},{10... | collective-permute-start | bytes 61448 | tf_op jit(solution)/shard_map/ppermute | solution.py:443
  44.1 1.6 collective-permute-start.3
  46.3 0.6 collective-permute-done.2
  46.9 2.0 collective-permute-start.4
  48.9 1.8 collective-permute-done.4
  50.7 0.9 collective-permute-start.17
  51.7 0.6 collective-permute-done.11.refs_4_
  52.9 6.6 %collective-permute-done.17.refs_2_ = f32[512,128]{1,0:T(8,128)S(1)} collective-permute-done((f32[512,128]{1,0:T(8,128)S(1)}, f32[512,128]{1,0:T(8,128)S(1)}, u32[]{:S(2)}, u32[]{:S(2)}) %collective-permute-start.17) | collective-permute-done | bytes 262176 | tf_op jit(solution)/shard_map/ppermute | solution.py:443
  59.4 1.5 collective-permute-start.18
  60.9 1.5 collective-permute-start.19
  63.0 8.5 %shard_map.80 = (bf16[512,2048]{1,0:T(8,128)(2,1)S(1)}, bf16[512,2048]{1,0:T(8,128)(2,1)S(1)}, f32[8,128]{1,0:T(8,128)S(1)}) custom-call(s32[8]{0:T(128)S(1)} %stack.192.refs_0_, s32[64]{0:T(128)S(1)} %convert_bitcast_fusion.refs_1_, f32[512,128]{1,0:T(8,128)S(1)} %add_add_fusion.refs_2_, f32[512,128]{1,0:T(8,128)S(1)} %collective-permute-done.10.refs_3_, ...), custom_call_target="tpu_custom_call" | custom-call | flops 12884901888 | bytes 6291456 | tf_op jit(solution)/shard_map/pallas_call | solution.py:171
  73.1 1.2 collective-permute-start.26
  74.4 1.3 collective-permute-start.27
  75.6 1.0 collective-permute-start.28
  76.7 8.5 %shard_map.81 = (bf16[512,2048]{1,0:T(8,128)(2,1)S(1)}, bf16[512,2048]{1,0:T(8,128)(2,1)S(1)}, f32[8,128]{1,0:T(8,128)S(1)}) custom-call(s32[8]{0:T(128)S(1)} %stack.192.refs_0_, s32[64]{0:T(128)S(1)} %fusion.3.refs_1_, f32[512,128]{1,0:T(8,128)S(1)} %collective-permute-done.17.refs_2_, f32[512,128]{1,0:T(8,128)S(1)} %collective-permute-done.18.refs_3_, ...), custom_call_target="tpu_custom_call" | custom-call | flops 12884901888 | bytes 6291456 | tf_op jit(solution)/shard_map/pallas_call | solution.py:171
  85.2 1.6 collective-permute-done.27.refs_4_
  86.8 1.2 collective-permute-done.28.refs_5_
  88.9 1.0 collective-permute-start.34
  90.0 1.3 collective-permute-start.35
  91.3 1.2 collective-permute-start.36
  92.4 8.5 %shard_map.82 = (bf16[512,2048]{1,0:T(8,128)(2,1)S(1)}, bf16[512,2048]{1,0:T(8,128)(2,1)S(1)}, f32[8,128]{1,0:T(8,128)S(1)}) custom-call(s32[8]{0:T(128)S(1)} %stack.192.refs_0_, s32[64]{0:T(128)S(1)} %fusion.2.refs_1_, f32[512,128]{1,0:T(8,128)S(1)} %collective-permute-done.25.refs_2_, f32[512,128]{1,0:T(8,128)S(1)} %collective-permute-done.26.refs_3_, ...), custom_call_target="tpu_custom_call" | custom-call | flops 12884901888 | bytes 6291456 | tf_op jit(solution)/shard_map/pallas_call | solution.py:171
  101.0 1.4 collective-permute-done.35.refs_4_
  102.4 1.2 collective-permute-done.36.refs_5_
  104.6 1.0 collective-permute-start.41
  105.6 1.3 collective-permute-start.42
  106.9 1.2 collective-permute-start.43
  108.1 8.5 %shard_map.83 = (bf16[512,2048]{1,0:T(8,128)(2,1)S(1)}, bf16[512,2048]{1,0:T(8,128)(2,1)S(1)}, f32[8,128]{1,0:T(8,128)S(1)}) custom-call(s32[8]{0:T(128)S(1)} %stack.192.refs_0_, s32[64]{0:T(128)S(1)} %fusion.1.refs_1_, f32[512,128]{1,0:T(8,128)S(1)} %collective-permute-done.33.refs_2_, f32[512,128]{1,0:T(8,128)S(1)} %collective-permute-done.34.refs_3_, ...), custom_call_target="tpu_custom_call" | custom-call | flops 12884901888 | bytes 6291456 | tf_op jit(solution)/shard_map/pallas_call | solution.py:171
  116.7 4.6 %shard_map.84 = (f32[64,2176]{1,0:T(8,128)S(1)}, f32[64,2048]{1,0:T(8,128)S(1)}) custom-call(bf16[512,2048]{1,0:T(8,128)(2,1)S(1)} %get-tuple-element.102.refs_0_.refs_3_.refs_8_, bf16[512,2048]{1,0:T(8,128)(2,1)S(1)} %get-tuple-element.110.refs_1_.refs_4_.refs_9_, bf16[512,2048]{1,0:T(8,128)(2,1)S(1)} %get-tuple-element.118.refs_2_.refs_5_.refs_10_, ...), custom_call_target="tpu_custom_call" | custom-call | flops 1610612736 | bytes 16777216 | tf_op jit(solution)/shard_map/pallas_call | solution.py:227
  121.4 1.9 collective-permute-done.44.refs_1_
  123.3 9.2 %shard_map.85 = (f32[64,2176]{1,0:T(8,128)S(1)}, f32[64,2048]{1,0:T(8,128)S(1)}, f32[64,2048]{1,0:T(8,128)S(1)}, f32[64,2048]{1,0:T(8,128)S(1)}, f32[64,2048]{1,...) custom-call(f32[64,2176]{1,0:T(8,128)S(1)} %get-tuple-element.136.refs_0_, ...), custom_call_target="tpu_custom_call" | custom-call | flops 3221225472 | bytes 16777216 | tf_op jit(solution)/shard_map/pallas_call | solution.py:338
  132.7 1.8 collective-permute-done.45.refs_1_
  134.5 9.5 %shard_map.86 = (f32[64,2176]{1,0:T(8,128)S(1)}, f32[64,2048]{1,0:T(8,128)S(1)}, f32[64,2048]{1,0:T(8,128)S(1)}, f32[64,2048]{1,0:T(8,128)S(1)}, f32[64,2048]{1,...) custom-call(f32[64,2176]{1,0:T(8,128)S(1)} %get-tuple-element.138.refs_0_, ...), custom_call_target="tpu_custom_call" | custom-call | flops 3221225472 | bytes 16777216 | tf_op jit(solution)/shard_map/pallas_call | solution.py:338
  144.2 1.8 collective-permute-done.46.refs_1_
  146.0 9.3 %shard_map.87 = (f32[64,2176]{1,0:T(8,128)S(1)}, f32[64,2048]{1,0:T(8,128)S(1)}, f32[64,2048]{1,0:T(8,128)S(1)}, f32[64,2048]{1,0:T(8,128)S(1)}, f32[64,2048]{1,...) custom-call(f32[64,2176]{1,0:T(8,128)S(1)} %get-tuple-element.145.refs_0_, ...), custom_call_target="tpu_custom_call" | custom-call | flops 3221225472 | bytes 16777216 | tf_op jit(solution)/shard_map/pallas_call | solution.py:338
  155.3 0.8 copy-done
  156.2 1.8 collective-permute-done.47.other_ref
  158.0 1.0 copy-done.1
  159.6 1.8 collective-permute-start.50
  161.4 0.7 collective-permute-start.49
  162.1 1.0 collective-permute-start.48
  163.2 5.7 %collective-permute-start.52 = (f32[64,512]{1,0:T(8,128)S(1)}, f32[64,512]{1,0:T(8,128)S(1)}, u32[]{:S(2)}, u32[]{:S(2)}) collective-permute-start(f32[64,512]{1,0:T(8,128)S(1)} %get-tuple-element.170), channel_id=1, source_target_pairs={{0,24},{2,26},{4,28},{6,30},{8,0},{10,2},{12,4},{14,6},{17,9},{19,... | collective-permute-start | bytes 393224 | tf_op jit(solution)/shard_map/ppermute | solution.py:537
  168.9 1.3 collective-permute-start.53
  170.3 2.5 %collective-permute-start.54 = (f32[64,512]{1,0:T(8,128)S(1)}, f32[64,512]{1,0:T(8,128)S(1)}, u32[]{:S(2)}, u32[]{:S(2)}) collective-permute-start(f32[64,512]{1,0:T(8,128)S(1)} %get-tuple-element.168), channel_id=1, source_target_pairs={{0,8},{2,10},{4,12},{6,14},{8,16},{10,18},{12,20},{14,22},{17,25},... | collective-permute-start | bytes 393224 | tf_op jit(solution)/shard_map/ppermute | solution.py:537
  173.0 2.6 %collective-permute-done.53 = f32[64,512]{1,0:T(8,128)S(1)} collective-permute-done((f32[64,512]{1,0:T(8,128)S(1)}, f32[64,512]{1,0:T(8,128)S(1)}, u32[]{:S(2)}, u32[]{:S(2)}) %collective-permute-start.53) | collective-permute-done | bytes 131104 | tf_op jit(solution)/shard_map/ppermute | solution.py:537
  175.5 2.8 %collective-permute-done.54 = f32[64,512]{1,0:T(8,128)S(1)} collective-permute-done((f32[64,512]{1,0:T(8,128)S(1)}, f32[64,512]{1,0:T(8,128)S(1)}, u32[]{:S(2)}, u32[]{:S(2)}) %collective-permute-start.54) | collective-permute-done | bytes 131104 | tf_op jit(solution)/shard_map/ppermute | solution.py:537
  178.3 0.7 constant_dynamic-slice_fusion
  179.1 5.9 %collective-permute-done.51.refs_1_ = f32[256,512]{1,0:T(8,128)S(1)} collective-permute-done((f32[256,512]{1,0:T(8,128)S(1)}, f32[256,512]{1,0:T(8,128)S(1)}, u32[]{:S(2)}, u32[]{:S(2)}) %collective-permute-start.51) | collective-permute-done | bytes 524320 | tf_op jit(solution)/shard_map/ppermute | solution.py:443
  185.0 3.5 %collective-permute-start.55 = (f32[256,512]{1,0:T(8,128)S(1)}, f32[256,512]{1,0:T(8,128)S(1)}, u32[]{:S(2)}, u32[]{:S(2)}) collective-permute-start(f32[256,512]{1,0:T(8,128)S(1)} %collective-permute-done.51.refs_1_), channel_id=1, source_target_pairs={{0,8},{8,16},{16,24},{24,0},{1,9},{9,17},{17,25},{25,1},{2,10},{10... | collective-permute-start | bytes 1572872 | tf_op jit(solution)/shard_map/ppermute | solution.py:443
  188.5 12.6 %collective-permute-done.55.refs_2_ = f32[256,512]{1,0:T(8,128)S(1)} collective-permute-done((f32[256,512]{1,0:T(8,128)S(1)}, f32[256,512]{1,0:T(8,128)S(1)}, u32[]{:S(2)}, u32[]{:S(2)}) %collective-permute-start.55) | collective-permute-done | bytes 524320 | tf_op jit(solution)/shard_map/ppermute | solution.py:443
  201.2 15.1 %collective-permute-done.56.refs_3_ = f32[256,512]{1,0:T(8,128)S(1)} collective-permute-done((f32[256,512]{1,0:T(8,128)S(1)}, f32[256,512]{1,0:T(8,128)S(1)}, u32[]{:S(2)}, u32[]{:S(2)}) %collective-permute-start.56) | collective-permute-done | bytes 524320 | tf_op jit(solution)/shard_map/ppermute | solution.py:443
  216.3 2.9 %shard_map.89 = f32[512,1024]{1,0:T(8,128)} custom-call(s32[8]{0:T(128)S(1)} %stack.183.where_ref, f32[256,512]{1,0:T(8,128)S(1)} %pad_maximum_fusion.refs_0_, f32[256,512]{1,0:T(8,128)S(1)} %collective-permute-done.51.refs_1_, f32[256,512]{1,0:T(8,128)S(1)} %collective-permute-done.55.refs_2_, f32[256,512]{1,0:T(8,128)S(1)} %collective-permute-done.56.refs_3_), custom_call_target="tpu_custom_call" | custom-call | tf_op jit(solution)/shard_map/pallas_call | solution.py:415
  (103 shorter events, 9.7 us)
Async XLA Ops:
  1.3 8.8 %copy-start.3 = (s32[1,4096]{1,0:T(1,128)S(1)}, s32[1,4096]{1,0:T(1,128)}, u32[]{:S(2)}) copy-start(s32[1,4096]{1,0:T(1,128)} %param.10) | copy-start | bytes 49156
  1.3 9.2 %copy-start.2 = (f32[256,512]{1,0:T(8,128)S(1)}, f32[256,512]{1,0:T(8,128)}, u32[]{:S(2)}) copy-start(f32[256,512]{1,0:T(8,128)} %param.11) | copy-start | bytes 1572868
  9.2 9.2 %collective-permute-start = (f32[2048,128]{1,0:T(8,128)}, f32[2048,128]{1,0:T(8,128)S(1)}, u32[]{:S(2)}, u32[]{:S(2)}) collective-permute-start(f32[2048,128]{1,0:T(8,128)} %shard_map.78), channel_id=1, source_target_pairs={{0,1},{1,0},{2,3},{3,2},{4,5},{5,4},{6,7},{7,6},{8,9},{9,8},{10,11... | collective-permute-start | bytes 3145736 | tf_op jit(solution)/shard_map/ppermute | solution.py:440
  19.8 9.7 %collective-permute-start.1 = (f32[512,128]{1,0:T(8,128)S(1)}, f32[512,128]{1,0:T(8,128)S(1)}, u32[]{:S(2)}, u32[]{:S(2)}) collective-permute-start(f32[512,128]{1,0:T(8,128)S(1)} %get-tuple-element.167), channel_id=1, source_target_pairs={{0,2},{1,3},{2,0},{3,1},{4,6},{5,7},{6,4},{7,5},{8,10},{9,11},{10,... | collective-permute-start | bytes 786440 | tf_op jit(solution)/shard_map/ppermute | solution.py:440
  22.4 13.9 %collective-permute-start.6 = (f32[512,128]{1,0:T(8,128)S(1)}, f32[512,128]{1,0:T(8,128)S(1)}, u32[]{:S(2)}, u32[]{:S(2)}) collective-permute-start(f32[512,128]{1,0:T(8,128)S(1)} %get-tuple-element.165), channel_id=1, source_target_pairs={{0,6},{1,7},{2,4},{3,5},{4,2},{5,3},{6,0},{7,1},{8,14},{9,15},{10,... | collective-permute-start | bytes 786440 | tf_op jit(solution)/shard_map/ppermute | solution.py:440
  23.9 13.8 %collective-permute-start.5 = (f32[512,128]{1,0:T(8,128)S(1)}, f32[512,128]{1,0:T(8,128)S(1)}, u32[]{:S(2)}, u32[]{:S(2)}) collective-permute-start(f32[512,128]{1,0:T(8,128)S(1)} %get-tuple-element.166), channel_id=1, source_target_pairs={{0,4},{1,5},{2,6},{3,7},{4,0},{5,1},{6,2},{7,3},{8,12},{9,13},{10,... | collective-permute-start | bytes 786440 | tf_op jit(solution)/shard_map/ppermute | solution.py:440
  24.2 13.5 %collective-permute-start.7 = (f32[64,512]{1,0:T(8,128)S(1)}, f32[64,512]{1,0:T(8,128)S(1)}, u32[]{:S(2)}, u32[]{:S(2)}) collective-permute-start(f32[64,512]{1,0:T(8,128)S(1)} %get-tuple-element.86), channel_id=1, source_target_pairs={{0,8},{8,16},{16,24},{24,0},{1,9},{9,17},{17,25},{25,1},{2,10},{10... | collective-permute-start | bytes 393224 | tf_op jit(solution)/shard_map/ppermute | solution.py:443
  26.2 11.5 %collective-permute-start.8 = (f32[64,512]{1,0:T(8,128)S(1)}, f32[64,512]{1,0:T(8,128)S(1)}, u32[]{:S(2)}, u32[]{:S(2)}) collective-permute-start(f32[64,512]{1,0:T(8,128)S(1)} %get-tuple-element.87), channel_id=1, source_target_pairs={{0,16},{8,24},{16,0},{24,8},{1,17},{9,25},{17,1},{25,9},{2,18},{10... | collective-permute-start | bytes 393224 | tf_op jit(solution)/shard_map/ppermute | solution.py:443
  29.5 8.3 %collective-permute-start.9 = (f32[64,512]{1,0:T(8,128)S(1)}, f32[64,512]{1,0:T(8,128)S(1)}, u32[]{:S(2)}, u32[]{:S(2)}) collective-permute-start(f32[64,512]{1,0:T(8,128)S(1)} %get-tuple-element.88), channel_id=1, source_target_pairs={{0,24},{8,0},{16,8},{24,16},{1,25},{9,1},{17,9},{25,17},{2,26},{10... | collective-permute-start | bytes 393224 | tf_op jit(solution)/shard_map/ppermute | solution.py:443
  37.8 13.9 %collective-permute-start.10 = (f32[512,128]{1,0:T(8,128)S(1)}, f32[512,128]{1,0:T(8,128)S(1)}, u32[]{:S(2)}, u32[]{:S(2)}) collective-permute-start(f32[512,128]{1,0:T(8,128)S(1)} %add_add_fusion.refs_2_), channel_id=1, source_target_pairs={{0,2},{1,3},{2,0},{3,1},{4,6},{5,7},{6,4},{7,5},{8,10},{9,11},{10,... | collective-permute-start | bytes 786440 | tf_op jit(solution)/shard_map/ppermute | solution.py:440
  39.4 12.9 %collective-permute-start.11 = (f32[512,128]{1,0:T(8,128)S(1)}, f32[512,128]{1,0:T(8,128)S(1)}, u32[]{:S(2)}, u32[]{:S(2)}) collective-permute-start(f32[512,128]{1,0:T(8,128)S(1)} %add_add_fusion.refs_2_), channel_id=1, source_target_pairs={{0,4},{1,5},{2,6},{3,7},{4,0},{5,1},{6,2},{7,3},{8,12},{9,13},{10,... | collective-permute-start | bytes 786440 | tf_op jit(solution)/shard_map/ppermute | solution.py:440
  41.0 11.3 %collective-permute-start.12 = (f32[512,128]{1,0:T(8,128)S(1)}, f32[512,128]{1,0:T(8,128)S(1)}, u32[]{:S(2)}, u32[]{:S(2)}) collective-permute-start(f32[512,128]{1,0:T(8,128)S(1)} %add_add_fusion.refs_2_), channel_id=1, source_target_pairs={{0,6},{1,7},{2,4},{3,5},{4,2},{5,3},{6,0},{7,1},{8,14},{9,15},{10,... | collective-permute-start | bytes 786440 | tf_op jit(solution)/shard_map/ppermute | solution.py:440
  41.3 5.6 %collective-permute-start.2 = (f32[40,128]{1,0:T(8,128)S(1)}, f32[40,128]{1,0:T(8,128)S(1)}, u32[]{:S(2)}, u32[]{:S(2)}) collective-permute-start(f32[40,128]{1,0:T(8,128)S(1)} %select_maximum_fusion), channel_id=1, source_target_pairs={{0,8},{8,16},{16,24},{24,0},{1,9},{9,17},{17,25},{25,1},{2,10},{10... | collective-permute-start | bytes 61448 | tf_op jit(solution)/shard_map/ppermute | solution.py:443
  44.1 4.8 %collective-permute-start.3 = (f32[40,128]{1,0:T(8,128)S(1)}, f32[40,128]{1,0:T(8,128)S(1)}, u32[]{:S(2)}, u32[]{:S(2)}) collective-permute-start(f32[40,128]{1,0:T(8,128)S(1)} %select_maximum_fusion), channel_id=1, source_target_pairs={{0,16},{8,24},{16,0},{24,8},{1,17},{9,25},{17,1},{25,9},{2,18},{10... | collective-permute-start | bytes 61448 | tf_op jit(solution)/shard_map/ppermute | solution.py:443
  46.9 3.8 %collective-permute-start.4 = (f32[40,128]{1,0:T(8,128)S(1)}, f32[40,128]{1,0:T(8,128)S(1)}, u32[]{:S(2)}, u32[]{:S(2)}) collective-permute-start(f32[40,128]{1,0:T(8,128)S(1)} %select_maximum_fusion), channel_id=1, source_target_pairs={{0,24},{8,0},{16,8},{24,16},{1,25},{9,1},{17,9},{25,17},{2,26},{10... | collective-permute-start | bytes 61448 | tf_op jit(solution)/shard_map/ppermute | solution.py:443
  48.9 12.0 %collective-permute-start.13 = (f32[512,128]{1,0:T(8,128)S(1)}, f32[512,128]{1,0:T(8,128)S(1)}, u32[]{:S(2)}, u32[]{:S(2)}) collective-permute-start(f32[512,128]{1,0:T(8,128)S(1)} %add_add_fusion.refs_2_), channel_id=1, source_target_pairs={{0,1},{1,0},{2,3},{3,2},{4,5},{5,4},{6,7},{7,6},{8,9},{9,8},{10,11... | collective-permute-start | bytes 786440 | tf_op jit(solution)/shard_map/ppermute | solution.py:440
  50.7 8.7 %collective-permute-start.17 = (f32[512,128]{1,0:T(8,128)S(1)}, f32[512,128]{1,0:T(8,128)S(1)}, u32[]{:S(2)}, u32[]{:S(2)}) collective-permute-start(f32[512,128]{1,0:T(8,128)S(1)} %add_add_fusion.refs_2_), channel_id=1, source_target_pairs={{0,8},{8,16},{16,24},{24,0},{1,9},{9,17},{17,25},{25,1},{2,10},{10... | collective-permute-start | bytes 786440 | tf_op jit(solution)/shard_map/ppermute | solution.py:443
  51.7 10.8 %collective-permute-start.14 = (f32[512,128]{1,0:T(8,128)S(1)}, f32[512,128]{1,0:T(8,128)S(1)}, u32[]{:S(2)}, u32[]{:S(2)}) collective-permute-start(f32[512,128]{1,0:T(8,128)S(1)} %collective-permute-done.10.refs_3_), channel_id=1, source_target_pairs={{0,1},{1,0},{2,3},{3,2},{4,5},{5,4},{6,7},{7,6},{8,9},{9,8},{10,11... | collective-permute-start | bytes 786440 | tf_op jit(solution)/shard_map/ppermute | solution.py:440
  52.3 10.6 %collective-permute-start.15 = (f32[512,128]{1,0:T(8,128)S(1)}, f32[512,128]{1,0:T(8,128)S(1)}, u32[]{:S(2)}, u32[]{:S(2)}) collective-permute-start(f32[512,128]{1,0:T(8,128)S(1)} %collective-permute-done.11.refs_4_), channel_id=1, source_target_pairs={{0,1},{1,0},{2,3},{3,2},{4,5},{5,4},{6,7},{7,6},{8,9},{9,8},{10,11... | collective-permute-start | bytes 786440 | tf_op jit(solution)/shard_map/ppermute | solution.py:440
  52.3 10.6 %collective-permute-start.16 = (f32[512,128]{1,0:T(8,128)S(1)}, f32[512,128]{1,0:T(8,128)S(1)}, u32[]{:S(2)}, u32[]{:S(2)}) collective-permute-start(f32[512,128]{1,0:T(8,128)S(1)} %collective-permute-done.12.refs_5_), channel_id=1, source_target_pairs={{0,1},{1,0},{2,3},{3,2},{4,5},{5,4},{6,7},{7,6},{8,9},{9,8},{10,11... | collective-permute-start | bytes 786440 | tf_op jit(solution)/shard_map/ppermute | solution.py:440
  59.4 12.0 %collective-permute-start.18 = (f32[512,128]{1,0:T(8,128)S(1)}, f32[512,128]{1,0:T(8,128)S(1)}, u32[]{:S(2)}, u32[]{:S(2)}) collective-permute-start(f32[512,128]{1,0:T(8,128)S(1)} %collective-permute-done.17.refs_2_), channel_id=1, source_target_pairs={{0,2},{1,3},{2,0},{3,1},{4,6},{5,7},{6,4},{7,5},{8,10},{9,11},{10,... | collective-permute-start | bytes 786440 | tf_op jit(solution)/shard_map/ppermute | solution.py:440
  60.9 11.2 %collective-permute-start.19 = (f32[512,128]{1,0:T(8,128)S(1)}, f32[512,128]{1,0:T(8,128)S(1)}, u32[]{:S(2)}, u32[]{:S(2)}) collective-permute-start(f32[512,128]{1,0:T(8,128)S(1)} %collective-permute-done.17.refs_2_), channel_id=1, source_target_pairs={{0,4},{1,5},{2,6},{3,7},{4,0},{5,1},{6,2},{7,3},{8,12},{9,13},{10,... | collective-permute-start | bytes 786440 | tf_op jit(solution)/shard_map/ppermute | solution.py:440
  62.5 9.7 %collective-permute-start.20 = (f32[512,128]{1,0:T(8,128)S(1)}, f32[512,128]{1,0:T(8,128)S(1)}, u32[]{:S(2)}, u32[]{:S(2)}) collective-permute-start(f32[512,128]{1,0:T(8,128)S(1)} %collective-permute-done.17.refs_2_), channel_id=1, source_target_pairs={{0,6},{1,7},{2,4},{3,5},{4,2},{5,3},{6,0},{7,1},{8,14},{9,15},{10,... | collective-permute-start | bytes 786440 | tf_op jit(solution)/shard_map/ppermute | solution.py:440
  62.9 10.2 %collective-permute-start.25 = (f32[512,128]{1,0:T(8,128)S(1)}, f32[512,128]{1,0:T(8,128)S(1)}, u32[]{:S(2)}, u32[]{:S(2)}) collective-permute-start(f32[512,128]{1,0:T(8,128)S(1)} %collective-permute-done.17.refs_2_), channel_id=1, source_target_pairs={{0,8},{8,16},{16,24},{24,0},{1,9},{9,17},{17,25},{25,1},{2,10},{10... | collective-permute-start | bytes 786440 | tf_op jit(solution)/shard_map/ppermute | solution.py:443
  72.1 2.2 %collective-permute-start.21 = (f32[512,128]{1,0:T(8,128)S(1)}, f32[512,128]{1,0:T(8,128)S(1)}, u32[]{:S(2)}, u32[]{:S(2)}) collective-permute-start(f32[512,128]{1,0:T(8,128)S(1)} %collective-permute-done.17.refs_2_), channel_id=1, source_target_pairs={{0,1},{1,0},{2,3},{3,2},{4,5},{5,4},{6,7},{7,6},{8,9},{9,8},{10,11... | collective-permute-start | bytes 786440 | tf_op jit(solution)/shard_map/ppermute | solution.py:440
  72.1 3.5 %collective-permute-start.22 = (f32[512,128]{1,0:T(8,128)S(1)}, f32[512,128]{1,0:T(8,128)S(1)}, u32[]{:S(2)}, u32[]{:S(2)}) collective-permute-start(f32[512,128]{1,0:T(8,128)S(1)} %collective-permute-done.18.refs_3_), channel_id=1, source_target_pairs={{0,1},{1,0},{2,3},{3,2},{4,5},{5,4},{6,7},{7,6},{8,9},{9,8},{10,11... | collective-permute-start | bytes 786440 | tf_op jit(solution)/shard_map/ppermute | solution.py:440
  72.6 4.0 %collective-permute-start.23 = (f32[512,128]{1,0:T(8,128)S(1)}, f32[512,128]{1,0:T(8,128)S(1)}, u32[]{:S(2)}, u32[]{:S(2)}) collective-permute-start(f32[512,128]{1,0:T(8,128)S(1)} %collective-permute-done.19.refs_4_), channel_id=1, source_target_pairs={{0,1},{1,0},{2,3},{3,2},{4,5},{5,4},{6,7},{7,6},{8,9},{9,8},{10,11... | collective-permute-start | bytes 786440 | tf_op jit(solution)/shard_map/ppermute | solution.py:440
  72.6 4.0 %collective-permute-start.24 = (f32[512,128]{1,0:T(8,128)S(1)}, f32[512,128]{1,0:T(8,128)S(1)}, u32[]{:S(2)}, u32[]{:S(2)}) collective-permute-start(f32[512,128]{1,0:T(8,128)S(1)} %collective-permute-done.20.refs_5_), channel_id=1, source_target_pairs={{0,1},{1,0},{2,3},{3,2},{4,5},{5,4},{6,7},{7,6},{8,9},{9,8},{10,11... | collective-permute-start | bytes 786440 | tf_op jit(solution)/shard_map/ppermute | solution.py:440
  73.1 12.0 %collective-permute-start.26 = (f32[512,128]{1,0:T(8,128)S(1)}, f32[512,128]{1,0:T(8,128)S(1)}, u32[]{:S(2)}, u32[]{:S(2)}) collective-permute-start(f32[512,128]{1,0:T(8,128)S(1)} %collective-permute-done.25.refs_2_), channel_id=1, source_target_pairs={{0,2},{1,3},{2,0},{3,1},{4,6},{5,7},{6,4},{7,5},{8,10},{9,11},{10,... | collective-permute-start | bytes 786440 | tf_op jit(solution)/shard_map/ppermute | solution.py:440
  74.4 12.4 %collective-permute-start.27 = (f32[512,128]{1,0:T(8,128)S(1)}, f32[512,128]{1,0:T(8,128)S(1)}, u32[]{:S(2)}, u32[]{:S(2)}) collective-permute-start(f32[512,128]{1,0:T(8,128)S(1)} %collective-permute-done.25.refs_2_), channel_id=1, source_target_pairs={{0,4},{1,5},{2,6},{3,7},{4,0},{5,1},{6,2},{7,3},{8,12},{9,13},{10,... | collective-permute-start | bytes 786440 | tf_op jit(solution)/shard_map/ppermute | solution.py:440
  75.6 12.3 %collective-permute-start.28 = (f32[512,128]{1,0:T(8,128)S(1)}, f32[512,128]{1,0:T(8,128)S(1)}, u32[]{:S(2)}, u32[]{:S(2)}) collective-permute-start(f32[512,128]{1,0:T(8,128)S(1)} %collective-permute-done.25.refs_2_), channel_id=1, source_target_pairs={{0,6},{1,7},{2,4},{3,5},{4,2},{5,3},{6,0},{7,1},{8,14},{9,15},{10,... | collective-permute-start | bytes 786440 | tf_op jit(solution)/shard_map/ppermute | solution.py:440
  76.6 12.3 %collective-permute-start.33 = (f32[512,128]{1,0:T(8,128)S(1)}, f32[512,128]{1,0:T(8,128)S(1)}, u32[]{:S(2)}, u32[]{:S(2)}) collective-permute-start(f32[512,128]{1,0:T(8,128)S(1)} %collective-permute-done.25.refs_2_), channel_id=1, source_target_pairs={{0,8},{8,16},{16,24},{24,0},{1,9},{9,17},{17,25},{25,1},{2,10},{10... | collective-permute-start | bytes 786440 | tf_op jit(solution)/shard_map/ppermute | solution.py:443
  87.9 2.1 collective-permute-start.29
  87.9 3.3 %collective-permute-start.30 = (f32[512,128]{1,0:T(8,128)S(1)}, f32[512,128]{1,0:T(8,128)S(1)}, u32[]{:S(2)}, u32[]{:S(2)}) collective-permute-start(f32[512,128]{1,0:T(8,128)S(1)} %collective-permute-done.26.refs_3_), channel_id=1, source_target_pairs={{0,1},{1,0},{2,3},{3,2},{4,5},{5,4},{6,7},{7,6},{8,9},{9,8},{10,11... | collective-permute-start | bytes 786440 | tf_op jit(solution)/shard_map/ppermute | solution.py:440
  88.4 4.0 %collective-permute-start.31 = (f32[512,128]{1,0:T(8,128)S(1)}, f32[512,128]{1,0:T(8,128)S(1)}, u32[]{:S(2)}, u32[]{:S(2)}) collective-permute-start(f32[512,128]{1,0:T(8,128)S(1)} %collective-permute-done.27.refs_4_), channel_id=1, source_target_pairs={{0,1},{1,0},{2,3},{3,2},{4,5},{5,4},{6,7},{7,6},{8,9},{9,8},{10,11... | collective-permute-start | bytes 786440 | tf_op jit(solution)/shard_map/ppermute | solution.py:440
  88.4 4.0 %collective-permute-start.32 = (f32[512,128]{1,0:T(8,128)S(1)}, f32[512,128]{1,0:T(8,128)S(1)}, u32[]{:S(2)}, u32[]{:S(2)}) collective-permute-start(f32[512,128]{1,0:T(8,128)S(1)} %collective-permute-done.28.refs_5_), channel_id=1, source_target_pairs={{0,1},{1,0},{2,3},{3,2},{4,5},{5,4},{6,7},{7,6},{8,9},{9,8},{10,11... | collective-permute-start | bytes 786440 | tf_op jit(solution)/shard_map/ppermute | solution.py:440
  88.9 12.0 %collective-permute-start.34 = (f32[512,128]{1,0:T(8,128)S(1)}, f32[512,128]{1,0:T(8,128)S(1)}, u32[]{:S(2)}, u32[]{:S(2)}) collective-permute-start(f32[512,128]{1,0:T(8,128)S(1)} %collective-permute-done.33.refs_2_), channel_id=1, source_target_pairs={{0,2},{1,3},{2,0},{3,1},{4,6},{5,7},{6,4},{7,5},{8,10},{9,11},{10,... | collective-permute-start | bytes 786440 | tf_op jit(solution)/shard_map/ppermute | solution.py:440
  90.0 12.4 %collective-permute-start.35 = (f32[512,128]{1,0:T(8,128)S(1)}, f32[512,128]{1,0:T(8,128)S(1)}, u32[]{:S(2)}, u32[]{:S(2)}) collective-permute-start(f32[512,128]{1,0:T(8,128)S(1)} %collective-permute-done.33.refs_2_), channel_id=1, source_target_pairs={{0,4},{1,5},{2,6},{3,7},{4,0},{5,1},{6,2},{7,3},{8,12},{9,13},{10,... | collective-permute-start | bytes 786440 | tf_op jit(solution)/shard_map/ppermute | solution.py:440
  91.3 12.3 %collective-permute-start.36 = (f32[512,128]{1,0:T(8,128)S(1)}, f32[512,128]{1,0:T(8,128)S(1)}, u32[]{:S(2)}, u32[]{:S(2)}) collective-permute-start(f32[512,128]{1,0:T(8,128)S(1)} %collective-permute-done.33.refs_2_), channel_id=1, source_target_pairs={{0,6},{1,7},{2,4},{3,5},{4,2},{5,3},{6,0},{7,1},{8,14},{9,15},{10,... | collective-permute-start | bytes 786440 | tf_op jit(solution)/shard_map/ppermute | solution.py:440
  103.5 2.0 collective-permute-start.37
  103.5 3.3 %collective-permute-start.38 = (f32[512,128]{1,0:T(8,128)S(1)}, f32[512,128]{1,0:T(8,128)S(1)}, u32[]{:S(2)}, u32[]{:S(2)}) collective-permute-start(f32[512,128]{1,0:T(8,128)S(1)} %collective-permute-done.34.refs_3_), channel_id=1, source_target_pairs={{0,1},{1,0},{2,3},{3,2},{4,5},{5,4},{6,7},{7,6},{8,9},{9,8},{10,11... | collective-permute-start | bytes 786440 | tf_op jit(solution)/shard_map/ppermute | solution.py:440
  104.1 4.0 %collective-permute-start.39 = (f32[512,128]{1,0:T(8,128)S(1)}, f32[512,128]{1,0:T(8,128)S(1)}, u32[]{:S(2)}, u32[]{:S(2)}) collective-permute-start(f32[512,128]{1,0:T(8,128)S(1)} %collective-permute-done.35.refs_4_), channel_id=1, source_target_pairs={{0,1},{1,0},{2,3},{3,2},{4,5},{5,4},{6,7},{7,6},{8,9},{9,8},{10,11... | collective-permute-start | bytes 786440 | tf_op jit(solution)/shard_map/ppermute | solution.py:440
  104.1 4.0 %collective-permute-start.40 = (f32[512,128]{1,0:T(8,128)S(1)}, f32[512,128]{1,0:T(8,128)S(1)}, u32[]{:S(2)}, u32[]{:S(2)}) collective-permute-start(f32[512,128]{1,0:T(8,128)S(1)} %collective-permute-done.36.refs_5_), channel_id=1, source_target_pairs={{0,1},{1,0},{2,3},{3,2},{4,5},{5,4},{6,7},{7,6},{8,9},{9,8},{10,11... | collective-permute-start | bytes 786440 | tf_op jit(solution)/shard_map/ppermute | solution.py:440
  104.6 12.1 %collective-permute-start.41 = (f32[64,512]{1,0:T(8,128)S(1)}, f32[64,512]{1,0:T(8,128)S(1)}, u32[]{:S(2)}, u32[]{:S(2)}) collective-permute-start(f32[64,512]{1,0:T(8,128)S(1)} %get-tuple-element.133), channel_id=1, source_target_pairs={{0,2},{1,3},{2,0},{3,1},{4,6},{5,7},{6,4},{7,5},{8,10},{9,11},{10,... | collective-permute-start | bytes 393224 | tf_op jit(solution)/shard_map/ppermute | solution.py:440
  105.6 11.1 %collective-permute-start.42 = (f32[64,512]{1,0:T(8,128)S(1)}, f32[64,512]{1,0:T(8,128)S(1)}, u32[]{:S(2)}, u32[]{:S(2)}) collective-permute-start(f32[64,512]{1,0:T(8,128)S(1)} %get-tuple-element.134), channel_id=1, source_target_pairs={{0,4},{1,5},{2,6},{3,7},{4,0},{5,1},{6,2},{7,3},{8,12},{9,13},{10,... | collective-permute-start | bytes 393224 | tf_op jit(solution)/shard_map/ppermute | solution.py:440
  106.9 9.8 %collective-permute-start.43 = (f32[64,512]{1,0:T(8,128)S(1)}, f32[64,512]{1,0:T(8,128)S(1)}, u32[]{:S(2)}, u32[]{:S(2)}) collective-permute-start(f32[64,512]{1,0:T(8,128)S(1)} %get-tuple-element.135), channel_id=1, source_target_pairs={{0,6},{1,7},{2,4},{3,5},{4,2},{5,3},{6,0},{7,1},{8,14},{9,15},{10,... | collective-permute-start | bytes 393224 | tf_op jit(solution)/shard_map/ppermute | solution.py:440
  121.3 2.0 collective-permute-start.44
  132.5 2.0 collective-permute-start.45
  144.0 2.0 collective-permute-start.46
  155.3 0.8 copy-start
  156.1 2.0 collective-permute-start.47
  158.0 1.0 copy-start.1
  159.6 10.7 %collective-permute-start.50 = (f32[64,512]{1,0:T(8,128)S(1)}, f32[64,512]{1,0:T(8,128)S(1)}, u32[]{:S(2)}, u32[]{:S(2)}) collective-permute-start(f32[64,512]{1,0:T(8,128)S(1)} %get-tuple-element.172), channel_id=1, source_target_pairs={{0,6},{1,7},{2,4},{3,5},{4,2},{5,3},{6,0},{7,1},{8,14},{9,15},{10,... | collective-permute-start | bytes 393224 | tf_op jit(solution)/shard_map/ppermute | solution.py:440
  161.4 11.4 %collective-permute-start.49 = (f32[64,512]{1,0:T(8,128)S(1)}, f32[64,512]{1,0:T(8,128)S(1)}, u32[]{:S(2)}, u32[]{:S(2)}) collective-permute-start(f32[64,512]{1,0:T(8,128)S(1)} %get-tuple-element.173), channel_id=1, source_target_pairs={{0,4},{1,5},{2,6},{3,7},{4,0},{5,1},{6,2},{7,3},{8,12},{9,13},{10,... | collective-permute-start | bytes 393224 | tf_op jit(solution)/shard_map/ppermute | solution.py:440
  162.1 10.7 %collective-permute-start.48 = (f32[64,512]{1,0:T(8,128)S(1)}, f32[64,512]{1,0:T(8,128)S(1)}, u32[]{:S(2)}, u32[]{:S(2)}) collective-permute-start(f32[64,512]{1,0:T(8,128)S(1)} %get-tuple-element.174), channel_id=1, source_target_pairs={{0,2},{1,3},{2,0},{3,1},{4,6},{5,7},{6,4},{7,5},{8,10},{9,11},{10,... | collective-permute-start | bytes 393224 | tf_op jit(solution)/shard_map/ppermute | solution.py:440
  163.2 9.7 %collective-permute-start.52 = (f32[64,512]{1,0:T(8,128)S(1)}, f32[64,512]{1,0:T(8,128)S(1)}, u32[]{:S(2)}, u32[]{:S(2)}) collective-permute-start(f32[64,512]{1,0:T(8,128)S(1)} %get-tuple-element.170), channel_id=1, source_target_pairs={{0,24},{2,26},{4,28},{6,30},{8,0},{10,2},{12,4},{14,6},{17,9},{19,... | collective-permute-start | bytes 393224 | tf_op jit(solution)/shard_map/ppermute | solution.py:537
  168.9 6.6 %collective-permute-start.53 = (f32[64,512]{1,0:T(8,128)S(1)}, f32[64,512]{1,0:T(8,128)S(1)}, u32[]{:S(2)}, u32[]{:S(2)}) collective-permute-start(f32[64,512]{1,0:T(8,128)S(1)} %get-tuple-element.169), channel_id=1, source_target_pairs={{0,16},{2,18},{4,20},{6,22},{8,24},{10,26},{12,28},{14,30},{17,1},... | collective-permute-start | bytes 393224 | tf_op jit(solution)/shard_map/ppermute | solution.py:537
  170.3 8.0 %collective-permute-start.54 = (f32[64,512]{1,0:T(8,128)S(1)}, f32[64,512]{1,0:T(8,128)S(1)}, u32[]{:S(2)}, u32[]{:S(2)}) collective-permute-start(f32[64,512]{1,0:T(8,128)S(1)} %get-tuple-element.168), channel_id=1, source_target_pairs={{0,8},{2,10},{4,12},{6,14},{8,16},{10,18},{12,20},{14,22},{17,25},... | collective-permute-start | bytes 393224 | tf_op jit(solution)/shard_map/ppermute | solution.py:537
  172.9 12.1 %collective-permute-start.51 = (f32[256,512]{1,0:T(8,128)S(1)}, f32[256,512]{1,0:T(8,128)S(1)}, u32[]{:S(2)}, u32[]{:S(2)}) collective-permute-start(f32[256,512]{1,0:T(8,128)S(1)} %pad_maximum_fusion.refs_0_), channel_id=1, source_target_pairs={{0,8},{8,16},{16,24},{24,0},{1,9},{9,17},{17,25},{25,1},{2,10},{10... | collective-permute-start | bytes 1572872 | tf_op jit(solution)/shard_map/ppermute | solution.py:443
  185.0 16.1 %collective-permute-start.55 = (f32[256,512]{1,0:T(8,128)S(1)}, f32[256,512]{1,0:T(8,128)S(1)}, u32[]{:S(2)}, u32[]{:S(2)}) collective-permute-start(f32[256,512]{1,0:T(8,128)S(1)} %collective-permute-done.51.refs_1_), channel_id=1, source_target_pairs={{0,8},{8,16},{16,24},{24,0},{1,9},{9,17},{17,25},{25,1},{2,10},{10... | collective-permute-start | bytes 1572872 | tf_op jit(solution)/shard_map/ppermute | solution.py:443
  201.1 15.2 %collective-permute-start.56 = (f32[256,512]{1,0:T(8,128)S(1)}, f32[256,512]{1,0:T(8,128)S(1)}, u32[]{:S(2)}, u32[]{:S(2)}) collective-permute-start(f32[256,512]{1,0:T(8,128)S(1)} %collective-permute-done.55.refs_2_), channel_id=1, source_target_pairs={{0,8},{8,16},{16,24},{24,0},{1,9},{9,17},{17,25},{25,1},{2,10},{10... | collective-permute-start | bytes 1572872 | tf_op jit(solution)/shard_map/ppermute | solution.py:443

commit v11 on v9

--- a/solution.py
+++ b/solution.py
@@ -188,7 +188,7 @@
                 pltpu.VMEM((half_ranks, tokens), F32),
                 pltpu.VMEM((tokens, LANES), F32),
                 pltpu.VMEM((8, tokens), F32),
-                pltpu.VMEM((4, group * half_ranks // 2, LANES), F32),
+                pltpu.VMEM((8, group * half_ranks // 2, LANES), F32),
                 pltpu.VMEM((ex_block, comps), F32),
             ],
         ),

time: 217 us -> 215 us (level)
  Pallas kernels: 86.1 us -> 78.1 us
  waiting for transfers between devices: 69.1 us -> 73 us
    pallas_call x4, Pallas kernels: 34.1 us -> 26 us  [build(): pl.pallas_call(functools.partial(build_kernel, ranks, share, ex_block, le...]
    ppermute x42, waiting for transfers between devices: 27.5 us -> 31.9 us  [swap(): return lax.ppermute(values, 'tensor', [(a, a ^ mask) for a in range(n_t)])]
  transfers between devices with their start and end apart: 57 -> 57, of which waited for: 18 -> 19; matrix products, arithmetic and copies ran while one was open for 1% -> 1% of each run, Pallas kernels for 20% -> 16%
where the time goes in v11:
time: 215 us; the launch traced here: 214 us
  Pallas kernels  78.1 us (36%)
  waiting for transfers between devices  73 us (34%)
  starting transfers between devices  55.9 us (26%)
  local copies, waits for them, and re-layouts  3.12 us (1%)
  other arithmetic  3 us (1%)
    ppermute x12, waiting for transfers between devices, shift(): lax.ppermute(values, 'dp', [(a, (a + by) % n_dp) for a in range(n_dp)])  37.5 us
    ppermute x42, waiting for transfers between devices, swap(): return lax.ppermute(values, 'tensor', [(a, a ^ mask) for a in range(n_t)])  31.9 us
    ppermute x42, starting transfers between devices, swap(): return lax.ppermute(values, 'tensor', [(a, a ^ mask) for a in range(n_t)])  29.2 us
    pallas_call x3, Pallas kernels, one_step(): pl.pallas_call(functools.partial(step_kernel, first, planes, examples, co...  27.9 us
    pallas_call x4, Pallas kernels, build(): pl.pallas_call(functools.partial(build_kernel, ranks, share, ex_block, le...  26 us
    ppermute x12, starting transfers between devices, shift(): lax.ppermute(values, 'dp', [(a, (a + by) % n_dp) for a in range(n_dp)])  17.8 us
    pallas_call x2, Pallas kernels, project(): pl.pallas_call(project_kernel, out_shape=jax.ShapeDtypeStruct((steps * bl...  15.6 us
    ppermute x3, starting transfers between devices, send(): return lax.ppermute(values, ('dp', 'tensor'), pairs)  8.88 us
  transfers between devices with their start and end apart: 57, of which 19 were waited for; matrix products, arithmetic and copies ran while one was open for 1% of the time, Pallas kernels for 16%

profile of v11, /device:TPU:0, one launch (start us, length us, event | category | flops | bytes accessed | tf_op | source)
XLA Modules:
  0.0 214.3 jit_solution(1670472316556147287)
XLA Ops:
  0.7 0.6 add_subtract_fusion
  1.3 7.9 %shard_map.78 = f32[2048,128]{1,0:T(8,128)} custom-call(s32[4]{0:T(128)} %get-tuple-element.176.order_ref, bf16[4096,512]{1,0:T(8,128)(2,1)} %refs_3_.3, bf16[4096,512]{1,0:T(8,128)(2,1)} %refs_3_.3, bf16[4096,512]{1,0:T(8,128)(2,1)} %refs_3_.3, bf16[4096,512]{1,0:T(8,128)(2,1)} %refs_3_.3, bf16[4096,1792]{1,0:T(8,128)(2,1)} %refs_7_.3, ...), custom_call_target="tpu_custom_call" | custom-call | flops 9663676416 | bytes 9437184 | tf_op jit(solution)/shard_map/pallas_call | solution.py:58
  10.6 7.7 %shard_map.77 = f32[2048,128]{1,0:T(8,128)} custom-call(s32[4]{0:T(128)} %broadcast_add_fusion.order_ref, bf16[4096,512]{1,0:T(8,128)(2,1)} %refs_3_.3, bf16[4096,512]{1,0:T(8,128)(2,1)} %refs_3_.3, bf16[4096,512]{1,0:T(8,128)(2,1)} %refs_3_.3, bf16[4096,512]{1,0:T(8,128)(2,1)} %refs_3_.3, bf16[4096,1792]{1,0:T(8,128)(2,1)} %refs_7_.3, ...), custom_call_target="tpu_custom_call" | custom-call | flops 9663676416 | bytes 9437184 | tf_op jit(solution)/shard_map/pallas_call | solution.py:58
  18.4 1.4 add.390
  19.8 2.6 %collective-permute-start.7 = (f32[40,128]{1,0:T(8,128)S(1)}, f32[40,128]{1,0:T(8,128)S(1)}, u32[]{:S(2)}, u32[]{:S(2)}) collective-permute-start(f32[40,128]{1,0:T(8,128)S(1)} %select_maximum_fusion), channel_id=1, source_target_pairs={{0,8},{8,16},{16,24},{24,0},{1,9},{9,17},{17,25},{25,1},{2,10},{10... | collective-permute-start | bytes 61448 | tf_op jit(solution)/shard_map/ppermute | solution.py:443
  22.4 2.6 %collective-permute-start.8 = (f32[40,128]{1,0:T(8,128)S(1)}, f32[40,128]{1,0:T(8,128)S(1)}, u32[]{:S(2)}, u32[]{:S(2)}) collective-permute-start(f32[40,128]{1,0:T(8,128)S(1)} %select_maximum_fusion), channel_id=1, source_target_pairs={{0,16},{8,24},{16,0},{24,8},{1,17},{9,25},{17,1},{25,9},{2,18},{10... | collective-permute-start | bytes 61448 | tf_op jit(solution)/shard_map/ppermute | solution.py:443
  25.0 1.3 collective-permute-start.9
  26.4 2.5 %collective-permute-start.3 = (f32[512,128]{1,0:T(8,128)S(1)}, f32[512,128]{1,0:T(8,128)S(1)}, u32[]{:S(2)}, u32[]{:S(2)}) collective-permute-start(f32[512,128]{1,0:T(8,128)S(1)} %get-tuple-element.179), channel_id=1, source_target_pairs={{0,6},{1,7},{2,4},{3,5},{4,2},{5,3},{6,0},{7,1},{8,14},{9,15},{10,... | collective-permute-start | bytes 786440 | tf_op jit(solution)/shard_map/ppermute | solution.py:440
  29.4 0.5 collective-permute-start.1
  30.0 0.7 collective-permute-start.4
  31.1 5.6 %collective-permute-done.3 = f32[512,128]{1,0:T(8,128)S(1)} collective-permute-done((f32[512,128]{1,0:T(8,128)S(1)}, f32[512,128]{1,0:T(8,128)S(1)}, u32[]{:S(2)}, u32[]{:S(2)}) %collective-permute-start.3) | collective-permute-done | bytes 262176 | tf_op jit(solution)/shard_map/ppermute | solution.py:440
  37.1 3.8 %collective-permute-done.2 = f32[512,128]{1,0:T(8,128)S(1)} collective-permute-done((f32[512,128]{1,0:T(8,128)S(1)}, f32[512,128]{1,0:T(8,128)S(1)}, u32[]{:S(2)}, u32[]{:S(2)}) %collective-permute-start.2) | collective-permute-done | bytes 262176 | tf_op jit(solution)/shard_map/ppermute | solution.py:440
  41.0 0.8 collective-permute-done.5.refs_2_
  41.8 0.8 collective-permute-done.6.refs_3_
  42.6 1.5 collective-permute-start.10
  44.1 1.5 collective-permute-start.11
  46.1 2.0 collective-permute-start.17
  48.1 3.7 %collective-permute-done.10.refs_3_ = f32[512,128]{1,0:T(8,128)S(1)} collective-permute-done((f32[512,128]{1,0:T(8,128)S(1)}, f32[512,128]{1,0:T(8,128)S(1)}, u32[]{:S(2)}, u32[]{:S(2)}) %collective-permute-start.10) | collective-permute-done | bytes 262176 | tf_op jit(solution)/shard_map/ppermute | solution.py:440
  51.8 4.2 %collective-permute-done.11.refs_4_ = f32[512,128]{1,0:T(8,128)S(1)} collective-permute-done((f32[512,128]{1,0:T(8,128)S(1)}, f32[512,128]{1,0:T(8,128)S(1)}, u32[]{:S(2)}, u32[]{:S(2)}) %collective-permute-start.11) | collective-permute-done | bytes 262176 | tf_op jit(solution)/shard_map/ppermute | solution.py:440
  56.8 0.6 shard_map.79
  58.0 1.6 collective-permute-start.19
  59.6 1.4 collective-permute-start.20
  61.0 3.2 %collective-permute-start.25 = (f32[512,128]{1,0:T(8,128)S(1)}, f32[512,128]{1,0:T(8,128)S(1)}, u32[]{:S(2)}, u32[]{:S(2)}) collective-permute-start(f32[512,128]{1,0:T(8,128)S(1)} %collective-permute-done.17.refs_2_), channel_id=1, source_target_pairs={{0,8},{8,16},{16,24},{24,0},{1,9},{9,17},{17,25},{25,1},{2,10},{10... | collective-permute-start | bytes 786440 | tf_op jit(solution)/shard_map/ppermute | solution.py:443
  64.2 6.5 %shard_map.80 = (bf16[512,2048]{1,0:T(8,128)(2,1)S(1)}, bf16[512,2048]{1,0:T(8,128)(2,1)S(1)}, f32[8,128]{1,0:T(8,128)S(1)}) custom-call(s32[8]{0:T(128)S(1)} %stack.192.refs_0_, s32[64]{0:T(128)S(1)} %convert_bitcast_fusion.refs_1_, f32[512,128]{1,0:T(8,128)S(1)} %fusion.1.refs_2_, f32[512,128]{1,0:T(8,128)S(1)} %collective-permute-done.10.refs_3_, ...), custom_call_target="tpu_custom_call" | custom-call | flops 12884901888 | bytes 6291456 | tf_op jit(solution)/shard_map/pallas_call | solution.py:171
  70.8 1.3 collective-permute-done.20.refs_5_
  73.1 1.1 collective-permute-start.26
  74.2 1.3 collective-permute-start.27
  75.4 1.2 collective-permute-start.28
  76.6 3.4 %collective-permute-start.33 = (f32[512,128]{1,0:T(8,128)S(1)}, f32[512,128]{1,0:T(8,128)S(1)}, u32[]{:S(2)}, u32[]{:S(2)}) collective-permute-start(f32[512,128]{1,0:T(8,128)S(1)} %collective-permute-done.25.refs_2_), channel_id=1, source_target_pairs={{0,8},{8,16},{16,24},{24,0},{1,9},{9,17},{17,25},{25,1},{2,10},{10... | collective-permute-start | bytes 786440 | tf_op jit(solution)/shard_map/ppermute | solution.py:443
  80.0 6.5 %shard_map.81 = (bf16[512,2048]{1,0:T(8,128)(2,1)S(1)}, bf16[512,2048]{1,0:T(8,128)(2,1)S(1)}, f32[8,128]{1,0:T(8,128)S(1)}) custom-call(s32[8]{0:T(128)S(1)} %stack.192.refs_0_, s32[64]{0:T(128)S(1)} %fusion.5.refs_1_, f32[512,128]{1,0:T(8,128)S(1)} %collective-permute-done.17.refs_2_, f32[512,128]{1,0:T(8,128)S(1)} %collective-permute-done.18.refs_3_, ...), custom_call_target="tpu_custom_call" | custom-call | flops 12884901888 | bytes 6291456 | tf_op jit(solution)/shard_map/pallas_call | solution.py:171
  86.5 1.2 collective-permute-done.27.refs_4_
  88.7 1.0 collective-permute-start.34
  89.7 1.2 collective-permute-start.35
  90.9 1.3 collective-permute-start.36
  92.2 6.5 %shard_map.82 = (bf16[512,2048]{1,0:T(8,128)(2,1)S(1)}, bf16[512,2048]{1,0:T(8,128)(2,1)S(1)}, f32[8,128]{1,0:T(8,128)S(1)}) custom-call(s32[8]{0:T(128)S(1)} %stack.192.refs_0_, s32[64]{0:T(128)S(1)} %fusion.4.refs_1_, f32[512,128]{1,0:T(8,128)S(1)} %collective-permute-done.25.refs_2_, f32[512,128]{1,0:T(8,128)S(1)} %collective-permute-done.26.refs_3_, ...), custom_call_target="tpu_custom_call" | custom-call | flops 12884901888 | bytes 6291456 | tf_op jit(solution)/shard_map/pallas_call | solution.py:171
  98.8 3.3 %collective-permute-done.35.refs_4_ = f32[512,128]{1,0:T(8,128)S(1)} collective-permute-done((f32[512,128]{1,0:T(8,128)S(1)}, f32[512,128]{1,0:T(8,128)S(1)}, u32[]{:S(2)}, u32[]{:S(2)}) %collective-permute-start.35) | collective-permute-done | bytes 262176 | tf_op jit(solution)/shard_map/ppermute | solution.py:440
  102.0 1.2 collective-permute-done.36.refs_5_
  104.3 1.1 collective-permute-start.41
  105.4 1.3 collective-permute-start.42
  106.6 1.2 collective-permute-start.43
  107.8 6.5 %shard_map.83 = (bf16[512,2048]{1,0:T(8,128)(2,1)S(1)}, bf16[512,2048]{1,0:T(8,128)(2,1)S(1)}, f32[8,128]{1,0:T(8,128)S(1)}) custom-call(s32[8]{0:T(128)S(1)} %stack.192.refs_0_, s32[64]{0:T(128)S(1)} %fusion.3.refs_1_, f32[512,128]{1,0:T(8,128)S(1)} %collective-permute-done.33.refs_2_, f32[512,128]{1,0:T(8,128)S(1)} %collective-permute-done.34.refs_3_, ...), custom_call_target="tpu_custom_call" | custom-call | flops 12884901888 | bytes 6291456 | tf_op jit(solution)/shard_map/pallas_call | solution.py:171
  114.3 4.6 %shard_map.84 = (f32[64,2176]{1,0:T(8,128)S(1)}, f32[64,2048]{1,0:T(8,128)S(1)}) custom-call(bf16[512,2048]{1,0:T(8,128)(2,1)S(1)} %get-tuple-element.116.refs_0_.refs_3_.refs_8_, bf16[512,2048]{1,0:T(8,128)(2,1)S(1)} %get-tuple-element.124.refs_1_.refs_4_.refs_9_, bf16[512,2048]{1,0:T(8,128)(2,1)S(1)} %get-tuple-element.132.refs_2_.refs_5_.refs_10_, ...), custom_call_target="tpu_custom_call" | custom-call | flops 1610612736 | bytes 16777216 | tf_op jit(solution)/shard_map/pallas_call | solution.py:227
  119.0 1.9 collective-permute-done.44.refs_1_
  121.0 9.2 %shard_map.85 = (f32[64,2176]{1,0:T(8,128)S(1)}, f32[64,2048]{1,0:T(8,128)S(1)}, f32[64,2048]{1,0:T(8,128)S(1)}, f32[64,2048]{1,0:T(8,128)S(1)}, f32[64,2048]{1,...) custom-call(f32[64,2176]{1,0:T(8,128)S(1)} %get-tuple-element.150.refs_0_, ...), custom_call_target="tpu_custom_call" | custom-call | flops 3221225472 | bytes 16777216 | tf_op jit(solution)/shard_map/pallas_call | solution.py:338
  130.4 1.8 collective-permute-done.45.refs_1_
  132.2 9.5 %shard_map.86 = (f32[64,2176]{1,0:T(8,128)S(1)}, f32[64,2048]{1,0:T(8,128)S(1)}, f32[64,2048]{1,0:T(8,128)S(1)}, f32[64,2048]{1,0:T(8,128)S(1)}, f32[64,2048]{1,...) custom-call(f32[64,2176]{1,0:T(8,128)S(1)} %get-tuple-element.152.refs_0_, ...), custom_call_target="tpu_custom_call" | custom-call | flops 3221225472 | bytes 16777216 | tf_op jit(solution)/shard_map/pallas_call | solution.py:338
  141.9 1.8 collective-permute-done.46.refs_1_
  143.7 9.2 %shard_map.87 = (f32[64,2176]{1,0:T(8,128)S(1)}, f32[64,2048]{1,0:T(8,128)S(1)}, f32[64,2048]{1,0:T(8,128)S(1)}, f32[64,2048]{1,0:T(8,128)S(1)}, f32[64,2048]{1,...) custom-call(f32[64,2176]{1,0:T(8,128)S(1)} %get-tuple-element.159.refs_0_, ...), custom_call_target="tpu_custom_call" | custom-call | flops 3221225472 | bytes 16777216 | tf_op jit(solution)/shard_map/pallas_call | solution.py:338
  152.9 0.8 copy-done
  153.8 1.8 collective-permute-done.47.other_ref
  155.7 1.0 copy-done.1
  157.3 1.8 collective-permute-start.50
  159.1 0.8 collective-permute-start.49
  159.8 1.0 collective-permute-start.48
  160.8 3.7 %collective-permute-start.52 = (f32[64,512]{1,0:T(8,128)S(1)}, f32[64,512]{1,0:T(8,128)S(1)}, u32[]{:S(2)}, u32[]{:S(2)}) collective-permute-start(f32[64,512]{1,0:T(8,128)S(1)} %get-tuple-element.183), channel_id=1, source_target_pairs={{0,24},{2,26},{4,28},{6,30},{8,0},{10,2},{12,4},{14,6},{17,9},{19,... | collective-permute-start | bytes 393224 | tf_op jit(solution)/shard_map/ppermute | solution.py:536
  164.5 1.3 collective-permute-start.53
  165.9 3.9 %collective-permute-start.54 = (f32[64,512]{1,0:T(8,128)S(1)}, f32[64,512]{1,0:T(8,128)S(1)}, u32[]{:S(2)}, u32[]{:S(2)}) collective-permute-start(f32[64,512]{1,0:T(8,128)S(1)} %get-tuple-element.181), channel_id=1, source_target_pairs={{0,8},{2,10},{4,12},{6,14},{8,16},{10,18},{12,20},{14,22},{17,25},... | collective-permute-start | bytes 393224 | tf_op jit(solution)/shard_map/ppermute | solution.py:536
  170.1 3.6 %collective-permute-done.54 = f32[64,512]{1,0:T(8,128)S(1)} collective-permute-done((f32[64,512]{1,0:T(8,128)S(1)}, f32[64,512]{1,0:T(8,128)S(1)}, u32[]{:S(2)}, u32[]{:S(2)}) %collective-permute-start.54) | collective-permute-done | bytes 131104 | tf_op jit(solution)/shard_map/ppermute | solution.py:536
  173.7 0.7 constant_dynamic-slice_fusion
  174.4 9.9 %collective-permute-done.51.refs_1_ = f32[256,512]{1,0:T(8,128)S(1)} collective-permute-done((f32[256,512]{1,0:T(8,128)S(1)}, f32[256,512]{1,0:T(8,128)S(1)}, u32[]{:S(2)}, u32[]{:S(2)}) %collective-permute-start.51) | collective-permute-done | bytes 524320 | tf_op jit(solution)/shard_map/ppermute | solution.py:443
  184.3 1.0 collective-permute-start.55
  185.3 12.6 %collective-permute-done.55.refs_2_ = f32[256,512]{1,0:T(8,128)S(1)} collective-permute-done((f32[256,512]{1,0:T(8,128)S(1)}, f32[256,512]{1,0:T(8,128)S(1)}, u32[]{:S(2)}, u32[]{:S(2)}) %collective-permute-start.55) | collective-permute-done | bytes 524320 | tf_op jit(solution)/shard_map/ppermute | solution.py:443
  198.0 13.5 %collective-permute-done.56.refs_3_ = f32[256,512]{1,0:T(8,128)S(1)} collective-permute-done((f32[256,512]{1,0:T(8,128)S(1)}, f32[256,512]{1,0:T(8,128)S(1)}, u32[]{:S(2)}, u32[]{:S(2)}) %collective-permute-start.56) | collective-permute-done | bytes 524320 | tf_op jit(solution)/shard_map/ppermute | solution.py:443
  211.4 2.9 %shard_map.89 = f32[512,1024]{1,0:T(8,128)} custom-call(s32[8]{0:T(128)S(1)} %stack.183.where_ref, f32[256,512]{1,0:T(8,128)S(1)} %pad_maximum_fusion.refs_0_, f32[256,512]{1,0:T(8,128)S(1)} %collective-permute-done.51.refs_1_, f32[256,512]{1,0:T(8,128)S(1)} %collective-permute-done.55.refs_2_, f32[256,512]{1,0:T(8,128)S(1)} %collective-permute-done.56.refs_3_), custom_call_target="tpu_custom_call" | custom-call | tf_op jit(solution)/shard_map/pallas_call | solution.py:415
  (103 shorter events, 9.4 us)
Async XLA Ops:
  1.3 8.8 %copy-start.3 = (s32[1,4096]{1,0:T(1,128)S(1)}, s32[1,4096]{1,0:T(1,128)}, u32[]{:S(2)}) copy-start(s32[1,4096]{1,0:T(1,128)} %param.10) | copy-start | bytes 49156
  1.3 9.2 %copy-start.2 = (f32[256,512]{1,0:T(8,128)S(1)}, f32[256,512]{1,0:T(8,128)}, u32[]{:S(2)}) copy-start(f32[256,512]{1,0:T(8,128)} %param.11) | copy-start | bytes 1572868
  9.2 9.2 %collective-permute-start = (f32[2048,128]{1,0:T(8,128)}, f32[2048,128]{1,0:T(8,128)S(1)}, u32[]{:S(2)}, u32[]{:S(2)}) collective-permute-start(f32[2048,128]{1,0:T(8,128)} %shard_map.78), channel_id=1, source_target_pairs={{0,1},{1,0},{2,3},{3,2},{4,5},{5,4},{6,7},{7,6},{8,9},{9,8},{10,11... | collective-permute-start | bytes 3145736 | tf_op jit(solution)/shard_map/ppermute | solution.py:440
  19.8 9.7 %collective-permute-start.7 = (f32[40,128]{1,0:T(8,128)S(1)}, f32[40,128]{1,0:T(8,128)S(1)}, u32[]{:S(2)}, u32[]{:S(2)}) collective-permute-start(f32[40,128]{1,0:T(8,128)S(1)} %select_maximum_fusion), channel_id=1, source_target_pairs={{0,8},{8,16},{16,24},{24,0},{1,9},{9,17},{17,25},{25,1},{2,10},{10... | collective-permute-start | bytes 61448 | tf_op jit(solution)/shard_map/ppermute | solution.py:443
  22.4 7.6 %collective-permute-start.8 = (f32[40,128]{1,0:T(8,128)S(1)}, f32[40,128]{1,0:T(8,128)S(1)}, u32[]{:S(2)}, u32[]{:S(2)}) collective-permute-start(f32[40,128]{1,0:T(8,128)S(1)} %select_maximum_fusion), channel_id=1, source_target_pairs={{0,16},{8,24},{16,0},{24,8},{1,17},{9,25},{17,1},{25,9},{2,18},{10... | collective-permute-start | bytes 61448 | tf_op jit(solution)/shard_map/ppermute | solution.py:443
  25.0 5.7 %collective-permute-start.9 = (f32[40,128]{1,0:T(8,128)S(1)}, f32[40,128]{1,0:T(8,128)S(1)}, u32[]{:S(2)}, u32[]{:S(2)}) collective-permute-start(f32[40,128]{1,0:T(8,128)S(1)} %select_maximum_fusion), channel_id=1, source_target_pairs={{0,24},{8,0},{16,8},{24,16},{1,25},{9,1},{17,9},{25,17},{2,26},{10... | collective-permute-start | bytes 61448 | tf_op jit(solution)/shard_map/ppermute | solution.py:443
  26.4 10.2 %collective-permute-start.3 = (f32[512,128]{1,0:T(8,128)S(1)}, f32[512,128]{1,0:T(8,128)S(1)}, u32[]{:S(2)}, u32[]{:S(2)}) collective-permute-start(f32[512,128]{1,0:T(8,128)S(1)} %get-tuple-element.179), channel_id=1, source_target_pairs={{0,6},{1,7},{2,4},{3,5},{4,2},{5,3},{6,0},{7,1},{8,14},{9,15},{10,... | collective-permute-start | bytes 786440 | tf_op jit(solution)/shard_map/ppermute | solution.py:440
  28.9 11.9 %collective-permute-start.2 = (f32[512,128]{1,0:T(8,128)S(1)}, f32[512,128]{1,0:T(8,128)S(1)}, u32[]{:S(2)}, u32[]{:S(2)}) collective-permute-start(f32[512,128]{1,0:T(8,128)S(1)} %get-tuple-element.180), channel_id=1, source_target_pairs={{0,4},{1,5},{2,6},{3,7},{4,0},{5,1},{6,2},{7,3},{8,12},{9,13},{10,... | collective-permute-start | bytes 786440 | tf_op jit(solution)/shard_map/ppermute | solution.py:440
  29.4 11.5 %collective-permute-start.1 = (f32[512,128]{1,0:T(8,128)S(1)}, f32[512,128]{1,0:T(8,128)S(1)}, u32[]{:S(2)}, u32[]{:S(2)}) collective-permute-start(f32[512,128]{1,0:T(8,128)S(1)} %get-tuple-element.178), channel_id=1, source_target_pairs={{0,2},{1,3},{2,0},{3,1},{4,6},{5,7},{6,4},{7,5},{8,10},{9,11},{10,... | collective-permute-start | bytes 786440 | tf_op jit(solution)/shard_map/ppermute | solution.py:440
  30.0 11.0 %collective-permute-start.4 = (f32[64,512]{1,0:T(8,128)S(1)}, f32[64,512]{1,0:T(8,128)S(1)}, u32[]{:S(2)}, u32[]{:S(2)}) collective-permute-start(f32[64,512]{1,0:T(8,128)S(1)} %get-tuple-element.91), channel_id=1, source_target_pairs={{0,8},{8,16},{16,24},{24,0},{1,9},{9,17},{17,25},{25,1},{2,10},{10... | collective-permute-start | bytes 393224 | tf_op jit(solution)/shard_map/ppermute | solution.py:443
  30.7 11.1 %collective-permute-start.5 = (f32[64,512]{1,0:T(8,128)S(1)}, f32[64,512]{1,0:T(8,128)S(1)}, u32[]{:S(2)}, u32[]{:S(2)}) collective-permute-start(f32[64,512]{1,0:T(8,128)S(1)} %get-tuple-element.92), channel_id=1, source_target_pairs={{0,16},{8,24},{16,0},{24,8},{1,17},{9,25},{17,1},{25,9},{2,18},{10... | collective-permute-start | bytes 393224 | tf_op jit(solution)/shard_map/ppermute | solution.py:443
  36.6 6.0 %collective-permute-start.6 = (f32[64,512]{1,0:T(8,128)S(1)}, f32[64,512]{1,0:T(8,128)S(1)}, u32[]{:S(2)}, u32[]{:S(2)}) collective-permute-start(f32[64,512]{1,0:T(8,128)S(1)} %get-tuple-element.93), channel_id=1, source_target_pairs={{0,24},{8,0},{16,8},{24,16},{1,25},{9,1},{17,9},{25,17},{2,26},{10... | collective-permute-start | bytes 393224 | tf_op jit(solution)/shard_map/ppermute | solution.py:443
  42.6 9.2 %collective-permute-start.10 = (f32[512,128]{1,0:T(8,128)S(1)}, f32[512,128]{1,0:T(8,128)S(1)}, u32[]{:S(2)}, u32[]{:S(2)}) collective-permute-start(f32[512,128]{1,0:T(8,128)S(1)} %fusion.1.refs_2_), channel_id=1, source_target_pairs={{0,2},{1,3},{2,0},{3,1},{4,6},{5,7},{6,4},{7,5},{8,10},{9,11},{10,... | collective-permute-start | bytes 786440 | tf_op jit(solution)/shard_map/ppermute | solution.py:440
  44.1 12.0 %collective-permute-start.11 = (f32[512,128]{1,0:T(8,128)S(1)}, f32[512,128]{1,0:T(8,128)S(1)}, u32[]{:S(2)}, u32[]{:S(2)}) collective-permute-start(f32[512,128]{1,0:T(8,128)S(1)} %fusion.1.refs_2_), channel_id=1, source_target_pairs={{0,4},{1,5},{2,6},{3,7},{4,0},{5,1},{6,2},{7,3},{8,12},{9,13},{10,... | collective-permute-start | bytes 786440 | tf_op jit(solution)/shard_map/ppermute | solution.py:440
  45.6 10.5 %collective-permute-start.12 = (f32[512,128]{1,0:T(8,128)S(1)}, f32[512,128]{1,0:T(8,128)S(1)}, u32[]{:S(2)}, u32[]{:S(2)}) collective-permute-start(f32[512,128]{1,0:T(8,128)S(1)} %fusion.1.refs_2_), channel_id=1, source_target_pairs={{0,6},{1,7},{2,4},{3,5},{4,2},{5,3},{6,0},{7,1},{8,14},{9,15},{10,... | collective-permute-start | bytes 786440 | tf_op jit(solution)/shard_map/ppermute | solution.py:440
  46.1 11.4 %collective-permute-start.17 = (f32[512,128]{1,0:T(8,128)S(1)}, f32[512,128]{1,0:T(8,128)S(1)}, u32[]{:S(2)}, u32[]{:S(2)}) collective-permute-start(f32[512,128]{1,0:T(8,128)S(1)} %fusion.1.refs_2_), channel_id=1, source_target_pairs={{0,8},{8,16},{16,24},{24,0},{1,9},{9,17},{17,25},{25,1},{2,10},{10... | collective-permute-start | bytes 786440 | tf_op jit(solution)/shard_map/ppermute | solution.py:443
  48.1 9.9 %collective-permute-start.13 = (f32[512,128]{1,0:T(8,128)S(1)}, f32[512,128]{1,0:T(8,128)S(1)}, u32[]{:S(2)}, u32[]{:S(2)}) collective-permute-start(f32[512,128]{1,0:T(8,128)S(1)} %fusion.1.refs_2_), channel_id=1, source_target_pairs={{0,1},{1,0},{2,3},{3,2},{4,5},{5,4},{6,7},{7,6},{8,9},{9,8},{10,11... | collective-permute-start | bytes 786440 | tf_op jit(solution)/shard_map/ppermute | solution.py:440
  51.8 7.8 %collective-permute-start.14 = (f32[512,128]{1,0:T(8,128)S(1)}, f32[512,128]{1,0:T(8,128)S(1)}, u32[]{:S(2)}, u32[]{:S(2)}) collective-permute-start(f32[512,128]{1,0:T(8,128)S(1)} %collective-permute-done.10.refs_3_), channel_id=1, source_target_pairs={{0,1},{1,0},{2,3},{3,2},{4,5},{5,4},{6,7},{7,6},{8,9},{9,8},{10,11... | collective-permute-start | bytes 786440 | tf_op jit(solution)/shard_map/ppermute | solution.py:440
  56.1 5.0 %collective-permute-start.15 = (f32[512,128]{1,0:T(8,128)S(1)}, f32[512,128]{1,0:T(8,128)S(1)}, u32[]{:S(2)}, u32[]{:S(2)}) collective-permute-start(f32[512,128]{1,0:T(8,128)S(1)} %collective-permute-done.11.refs_4_), channel_id=1, source_target_pairs={{0,1},{1,0},{2,3},{3,2},{4,5},{5,4},{6,7},{7,6},{8,9},{9,8},{10,11... | collective-permute-start | bytes 786440 | tf_op jit(solution)/shard_map/ppermute | solution.py:440
  56.1 8.1 %collective-permute-start.16 = (f32[512,128]{1,0:T(8,128)S(1)}, f32[512,128]{1,0:T(8,128)S(1)}, u32[]{:S(2)}, u32[]{:S(2)}) collective-permute-start(f32[512,128]{1,0:T(8,128)S(1)} %collective-permute-done.12.refs_5_), channel_id=1, source_target_pairs={{0,1},{1,0},{2,3},{3,2},{4,5},{5,4},{6,7},{7,6},{8,9},{9,8},{10,11... | collective-permute-start | bytes 786440 | tf_op jit(solution)/shard_map/ppermute | solution.py:440
  57.5 13.3 %collective-permute-start.18 = (f32[512,128]{1,0:T(8,128)S(1)}, f32[512,128]{1,0:T(8,128)S(1)}, u32[]{:S(2)}, u32[]{:S(2)}) collective-permute-start(f32[512,128]{1,0:T(8,128)S(1)} %collective-permute-done.17.refs_2_), channel_id=1, source_target_pairs={{0,2},{1,3},{2,0},{3,1},{4,6},{5,7},{6,4},{7,5},{8,10},{9,11},{10,... | collective-permute-start | bytes 786440 | tf_op jit(solution)/shard_map/ppermute | solution.py:440
  58.0 12.7 %collective-permute-start.19 = (f32[512,128]{1,0:T(8,128)S(1)}, f32[512,128]{1,0:T(8,128)S(1)}, u32[]{:S(2)}, u32[]{:S(2)}) collective-permute-start(f32[512,128]{1,0:T(8,128)S(1)} %collective-permute-done.17.refs_2_), channel_id=1, source_target_pairs={{0,4},{1,5},{2,6},{3,7},{4,0},{5,1},{6,2},{7,3},{8,12},{9,13},{10,... | collective-permute-start | bytes 786440 | tf_op jit(solution)/shard_map/ppermute | solution.py:440
  59.6 12.4 %collective-permute-start.20 = (f32[512,128]{1,0:T(8,128)S(1)}, f32[512,128]{1,0:T(8,128)S(1)}, u32[]{:S(2)}, u32[]{:S(2)}) collective-permute-start(f32[512,128]{1,0:T(8,128)S(1)} %collective-permute-done.17.refs_2_), channel_id=1, source_target_pairs={{0,6},{1,7},{2,4},{3,5},{4,2},{5,3},{6,0},{7,1},{8,14},{9,15},{10,... | collective-permute-start | bytes 786440 | tf_op jit(solution)/shard_map/ppermute | solution.py:440
  61.0 12.0 %collective-permute-start.25 = (f32[512,128]{1,0:T(8,128)S(1)}, f32[512,128]{1,0:T(8,128)S(1)}, u32[]{:S(2)}, u32[]{:S(2)}) collective-permute-start(f32[512,128]{1,0:T(8,128)S(1)} %collective-permute-done.17.refs_2_), channel_id=1, source_target_pairs={{0,8},{8,16},{16,24},{24,0},{1,9},{9,17},{17,25},{25,1},{2,10},{10... | collective-permute-start | bytes 786440 | tf_op jit(solution)/shard_map/ppermute | solution.py:443
  72.1 2.1 collective-permute-start.21
  72.1 3.3 %collective-permute-start.22 = (f32[512,128]{1,0:T(8,128)S(1)}, f32[512,128]{1,0:T(8,128)S(1)}, u32[]{:S(2)}, u32[]{:S(2)}) collective-permute-start(f32[512,128]{1,0:T(8,128)S(1)} %collective-permute-done.18.refs_3_), channel_id=1, source_target_pairs={{0,1},{1,0},{2,3},{3,2},{4,5},{5,4},{6,7},{7,6},{8,9},{9,8},{10,11... | collective-permute-start | bytes 786440 | tf_op jit(solution)/shard_map/ppermute | solution.py:440
  72.6 4.0 %collective-permute-start.23 = (f32[512,128]{1,0:T(8,128)S(1)}, f32[512,128]{1,0:T(8,128)S(1)}, u32[]{:S(2)}, u32[]{:S(2)}) collective-permute-start(f32[512,128]{1,0:T(8,128)S(1)} %collective-permute-done.19.refs_4_), channel_id=1, source_target_pairs={{0,1},{1,0},{2,3},{3,2},{4,5},{5,4},{6,7},{7,6},{8,9},{9,8},{10,11... | collective-permute-start | bytes 786440 | tf_op jit(solution)/shard_map/ppermute | solution.py:440
  72.6 7.4 %collective-permute-start.24 = (f32[512,128]{1,0:T(8,128)S(1)}, f32[512,128]{1,0:T(8,128)S(1)}, u32[]{:S(2)}, u32[]{:S(2)}) collective-permute-start(f32[512,128]{1,0:T(8,128)S(1)} %collective-permute-done.20.refs_5_), channel_id=1, source_target_pairs={{0,1},{1,0},{2,3},{3,2},{4,5},{5,4},{6,7},{7,6},{8,9},{9,8},{10,11... | collective-permute-start | bytes 786440 | tf_op jit(solution)/shard_map/ppermute | solution.py:440
  73.1 13.4 %collective-permute-start.26 = (f32[512,128]{1,0:T(8,128)S(1)}, f32[512,128]{1,0:T(8,128)S(1)}, u32[]{:S(2)}, u32[]{:S(2)}) collective-permute-start(f32[512,128]{1,0:T(8,128)S(1)} %collective-permute-done.25.refs_2_), channel_id=1, source_target_pairs={{0,2},{1,3},{2,0},{3,1},{4,6},{5,7},{6,4},{7,5},{8,10},{9,11},{10,... | collective-permute-start | bytes 786440 | tf_op jit(solution)/shard_map/ppermute | solution.py:440
  74.2 13.6 %collective-permute-start.27 = (f32[512,128]{1,0:T(8,128)S(1)}, f32[512,128]{1,0:T(8,128)S(1)}, u32[]{:S(2)}, u32[]{:S(2)}) collective-permute-start(f32[512,128]{1,0:T(8,128)S(1)} %collective-permute-done.25.refs_2_), channel_id=1, source_target_pairs={{0,4},{1,5},{2,6},{3,7},{4,0},{5,1},{6,2},{7,3},{8,12},{9,13},{10,... | collective-permute-start | bytes 786440 | tf_op jit(solution)/shard_map/ppermute | solution.py:440
  75.4 12.3 %collective-permute-start.28 = (f32[512,128]{1,0:T(8,128)S(1)}, f32[512,128]{1,0:T(8,128)S(1)}, u32[]{:S(2)}, u32[]{:S(2)}) collective-permute-start(f32[512,128]{1,0:T(8,128)S(1)} %collective-permute-done.25.refs_2_), channel_id=1, source_target_pairs={{0,6},{1,7},{2,4},{3,5},{4,2},{5,3},{6,0},{7,1},{8,14},{9,15},{10,... | collective-permute-start | bytes 786440 | tf_op jit(solution)/shard_map/ppermute | solution.py:440
  76.6 12.2 %collective-permute-start.33 = (f32[512,128]{1,0:T(8,128)S(1)}, f32[512,128]{1,0:T(8,128)S(1)}, u32[]{:S(2)}, u32[]{:S(2)}) collective-permute-start(f32[512,128]{1,0:T(8,128)S(1)} %collective-permute-done.25.refs_2_), channel_id=1, source_target_pairs={{0,8},{8,16},{16,24},{24,0},{1,9},{9,17},{17,25},{25,1},{2,10},{10... | collective-permute-start | bytes 786440 | tf_op jit(solution)/shard_map/ppermute | solution.py:443
  87.7 2.0 collective-permute-start.29
  87.7 3.2 %collective-permute-start.30 = (f32[512,128]{1,0:T(8,128)S(1)}, f32[512,128]{1,0:T(8,128)S(1)}, u32[]{:S(2)}, u32[]{:S(2)}) collective-permute-start(f32[512,128]{1,0:T(8,128)S(1)} %collective-permute-done.26.refs_3_), channel_id=1, source_target_pairs={{0,1},{1,0},{2,3},{3,2},{4,5},{5,4},{6,7},{7,6},{8,9},{9,8},{10,11... | collective-permute-start | bytes 786440 | tf_op jit(solution)/shard_map/ppermute | solution.py:440
  88.2 4.0 %collective-permute-start.31 = (f32[512,128]{1,0:T(8,128)S(1)}, f32[512,128]{1,0:T(8,128)S(1)}, u32[]{:S(2)}, u32[]{:S(2)}) collective-permute-start(f32[512,128]{1,0:T(8,128)S(1)} %collective-permute-done.27.refs_4_), channel_id=1, source_target_pairs={{0,1},{1,0},{2,3},{3,2},{4,5},{5,4},{6,7},{7,6},{8,9},{9,8},{10,11... | collective-permute-start | bytes 786440 | tf_op jit(solution)/shard_map/ppermute | solution.py:440
  88.2 4.0 %collective-permute-start.32 = (f32[512,128]{1,0:T(8,128)S(1)}, f32[512,128]{1,0:T(8,128)S(1)}, u32[]{:S(2)}, u32[]{:S(2)}) collective-permute-start(f32[512,128]{1,0:T(8,128)S(1)} %collective-permute-done.28.refs_5_), channel_id=1, source_target_pairs={{0,1},{1,0},{2,3},{3,2},{4,5},{5,4},{6,7},{7,6},{8,9},{9,8},{10,11... | collective-permute-start | bytes 786440 | tf_op jit(solution)/shard_map/ppermute | solution.py:440
  88.7 10.0 %collective-permute-start.34 = (f32[512,128]{1,0:T(8,128)S(1)}, f32[512,128]{1,0:T(8,128)S(1)}, u32[]{:S(2)}, u32[]{:S(2)}) collective-permute-start(f32[512,128]{1,0:T(8,128)S(1)} %collective-permute-done.33.refs_2_), channel_id=1, source_target_pairs={{0,2},{1,3},{2,0},{3,1},{4,6},{5,7},{6,4},{7,5},{8,10},{9,11},{10,... | collective-permute-start | bytes 786440 | tf_op jit(solution)/shard_map/ppermute | solution.py:440
  89.7 12.3 %collective-permute-start.35 = (f32[512,128]{1,0:T(8,128)S(1)}, f32[512,128]{1,0:T(8,128)S(1)}, u32[]{:S(2)}, u32[]{:S(2)}) collective-permute-start(f32[512,128]{1,0:T(8,128)S(1)} %collective-permute-done.33.refs_2_), channel_id=1, source_target_pairs={{0,4},{1,5},{2,6},{3,7},{4,0},{5,1},{6,2},{7,3},{8,12},{9,13},{10,... | collective-permute-start | bytes 786440 | tf_op jit(solution)/shard_map/ppermute | solution.py:440
  90.9 12.3 %collective-permute-start.36 = (f32[512,128]{1,0:T(8,128)S(1)}, f32[512,128]{1,0:T(8,128)S(1)}, u32[]{:S(2)}, u32[]{:S(2)}) collective-permute-start(f32[512,128]{1,0:T(8,128)S(1)} %collective-permute-done.33.refs_2_), channel_id=1, source_target_pairs={{0,6},{1,7},{2,4},{3,5},{4,2},{5,3},{6,0},{7,1},{8,14},{9,15},{10,... | collective-permute-start | bytes 786440 | tf_op jit(solution)/shard_map/ppermute | solution.py:440
  103.3 2.1 collective-permute-start.37
  103.3 3.3 %collective-permute-start.38 = (f32[512,128]{1,0:T(8,128)S(1)}, f32[512,128]{1,0:T(8,128)S(1)}, u32[]{:S(2)}, u32[]{:S(2)}) collective-permute-start(f32[512,128]{1,0:T(8,128)S(1)} %collective-permute-done.34.refs_3_), channel_id=1, source_target_pairs={{0,1},{1,0},{2,3},{3,2},{4,5},{5,4},{6,7},{7,6},{8,9},{9,8},{10,11... | collective-permute-start | bytes 786440 | tf_op jit(solution)/shard_map/ppermute | solution.py:440
  103.8 4.0 %collective-permute-start.39 = (f32[512,128]{1,0:T(8,128)S(1)}, f32[512,128]{1,0:T(8,128)S(1)}, u32[]{:S(2)}, u32[]{:S(2)}) collective-permute-start(f32[512,128]{1,0:T(8,128)S(1)} %collective-permute-done.35.refs_4_), channel_id=1, source_target_pairs={{0,1},{1,0},{2,3},{3,2},{4,5},{5,4},{6,7},{7,6},{8,9},{9,8},{10,11... | collective-permute-start | bytes 786440 | tf_op jit(solution)/shard_map/ppermute | solution.py:440
  103.8 4.0 %collective-permute-start.40 = (f32[512,128]{1,0:T(8,128)S(1)}, f32[512,128]{1,0:T(8,128)S(1)}, u32[]{:S(2)}, u32[]{:S(2)}) collective-permute-start(f32[512,128]{1,0:T(8,128)S(1)} %collective-permute-done.36.refs_5_), channel_id=1, source_target_pairs={{0,1},{1,0},{2,3},{3,2},{4,5},{5,4},{6,7},{7,6},{8,9},{9,8},{10,11... | collective-permute-start | bytes 786440 | tf_op jit(solution)/shard_map/ppermute | solution.py:440
  104.3 10.0 %collective-permute-start.41 = (f32[64,512]{1,0:T(8,128)S(1)}, f32[64,512]{1,0:T(8,128)S(1)}, u32[]{:S(2)}, u32[]{:S(2)}) collective-permute-start(f32[64,512]{1,0:T(8,128)S(1)} %get-tuple-element.147), channel_id=1, source_target_pairs={{0,2},{1,3},{2,0},{3,1},{4,6},{5,7},{6,4},{7,5},{8,10},{9,11},{10,... | collective-permute-start | bytes 393224 | tf_op jit(solution)/shard_map/ppermute | solution.py:440
  105.4 9.0 %collective-permute-start.42 = (f32[64,512]{1,0:T(8,128)S(1)}, f32[64,512]{1,0:T(8,128)S(1)}, u32[]{:S(2)}, u32[]{:S(2)}) collective-permute-start(f32[64,512]{1,0:T(8,128)S(1)} %get-tuple-element.148), channel_id=1, source_target_pairs={{0,4},{1,5},{2,6},{3,7},{4,0},{5,1},{6,2},{7,3},{8,12},{9,13},{10,... | collective-permute-start | bytes 393224 | tf_op jit(solution)/shard_map/ppermute | solution.py:440
  106.6 7.7 %collective-permute-start.43 = (f32[64,512]{1,0:T(8,128)S(1)}, f32[64,512]{1,0:T(8,128)S(1)}, u32[]{:S(2)}, u32[]{:S(2)}) collective-permute-start(f32[64,512]{1,0:T(8,128)S(1)} %get-tuple-element.149), channel_id=1, source_target_pairs={{0,6},{1,7},{2,4},{3,5},{4,2},{5,3},{6,0},{7,1},{8,14},{9,15},{10,... | collective-permute-start | bytes 393224 | tf_op jit(solution)/shard_map/ppermute | solution.py:440
  118.9 2.0 collective-permute-start.44
  130.2 2.0 collective-permute-start.45
  141.7 2.0 collective-permute-start.46
  152.9 0.8 copy-start
  153.7 2.0 collective-permute-start.47
  155.7 1.0 copy-start.1
  157.3 8.6 %collective-permute-start.50 = (f32[64,512]{1,0:T(8,128)S(1)}, f32[64,512]{1,0:T(8,128)S(1)}, u32[]{:S(2)}, u32[]{:S(2)}) collective-permute-start(f32[64,512]{1,0:T(8,128)S(1)} %get-tuple-element.185), channel_id=1, source_target_pairs={{0,6},{1,7},{2,4},{3,5},{4,2},{5,3},{6,0},{7,1},{8,14},{9,15},{10,... | collective-permute-start | bytes 393224 | tf_op jit(solution)/shard_map/ppermute | solution.py:440
  159.1 10.8 %collective-permute-start.49 = (f32[64,512]{1,0:T(8,128)S(1)}, f32[64,512]{1,0:T(8,128)S(1)}, u32[]{:S(2)}, u32[]{:S(2)}) collective-permute-start(f32[64,512]{1,0:T(8,128)S(1)} %get-tuple-element.186), channel_id=1, source_target_pairs={{0,4},{1,5},{2,6},{3,7},{4,0},{5,1},{6,2},{7,3},{8,12},{9,13},{10,... | collective-permute-start | bytes 393224 | tf_op jit(solution)/shard_map/ppermute | solution.py:440
  159.8 10.0 %collective-permute-start.48 = (f32[64,512]{1,0:T(8,128)S(1)}, f32[64,512]{1,0:T(8,128)S(1)}, u32[]{:S(2)}, u32[]{:S(2)}) collective-permute-start(f32[64,512]{1,0:T(8,128)S(1)} %get-tuple-element.187), channel_id=1, source_target_pairs={{0,2},{1,3},{2,0},{3,1},{4,6},{5,7},{6,4},{7,5},{8,10},{9,11},{10,... | collective-permute-start | bytes 393224 | tf_op jit(solution)/shard_map/ppermute | solution.py:440
  160.8 9.2 %collective-permute-start.52 = (f32[64,512]{1,0:T(8,128)S(1)}, f32[64,512]{1,0:T(8,128)S(1)}, u32[]{:S(2)}, u32[]{:S(2)}) collective-permute-start(f32[64,512]{1,0:T(8,128)S(1)} %get-tuple-element.183), channel_id=1, source_target_pairs={{0,24},{2,26},{4,28},{6,30},{8,0},{10,2},{12,4},{14,6},{17,9},{19,... | collective-permute-start | bytes 393224 | tf_op jit(solution)/shard_map/ppermute | solution.py:536
  164.5 5.5 %collective-permute-start.53 = (f32[64,512]{1,0:T(8,128)S(1)}, f32[64,512]{1,0:T(8,128)S(1)}, u32[]{:S(2)}, u32[]{:S(2)}) collective-permute-start(f32[64,512]{1,0:T(8,128)S(1)} %get-tuple-element.182), channel_id=1, source_target_pairs={{0,16},{2,18},{4,20},{6,22},{8,24},{10,26},{12,28},{14,30},{17,1},... | collective-permute-start | bytes 393224 | tf_op jit(solution)/shard_map/ppermute | solution.py:536
  165.9 7.8 %collective-permute-start.54 = (f32[64,512]{1,0:T(8,128)S(1)}, f32[64,512]{1,0:T(8,128)S(1)}, u32[]{:S(2)}, u32[]{:S(2)}) collective-permute-start(f32[64,512]{1,0:T(8,128)S(1)} %get-tuple-element.181), channel_id=1, source_target_pairs={{0,8},{2,10},{4,12},{6,14},{8,16},{10,18},{12,20},{14,22},{17,25},... | collective-permute-start | bytes 393224 | tf_op jit(solution)/shard_map/ppermute | solution.py:536
  169.9 14.4 %collective-permute-start.51 = (f32[256,512]{1,0:T(8,128)S(1)}, f32[256,512]{1,0:T(8,128)S(1)}, u32[]{:S(2)}, u32[]{:S(2)}) collective-permute-start(f32[256,512]{1,0:T(8,128)S(1)} %pad_maximum_fusion.refs_0_), channel_id=1, source_target_pairs={{0,8},{8,16},{16,24},{24,0},{1,9},{9,17},{17,25},{25,1},{2,10},{10... | collective-permute-start | bytes 1572872 | tf_op jit(solution)/shard_map/ppermute | solution.py:443
  184.3 13.6 %collective-permute-start.55 = (f32[256,512]{1,0:T(8,128)S(1)}, f32[256,512]{1,0:T(8,128)S(1)}, u32[]{:S(2)}, u32[]{:S(2)}) collective-permute-start(f32[256,512]{1,0:T(8,128)S(1)} %collective-permute-done.51.refs_1_), channel_id=1, source_target_pairs={{0,8},{8,16},{16,24},{24,0},{1,9},{9,17},{17,25},{25,1},{2,10},{10... | collective-permute-start | bytes 1572872 | tf_op jit(solution)/shard_map/ppermute | solution.py:443
  197.9 13.5 %collective-permute-start.56 = (f32[256,512]{1,0:T(8,128)S(1)}, f32[256,512]{1,0:T(8,128)S(1)}, u32[]{:S(2)}, u32[]{:S(2)}) collective-permute-start(f32[256,512]{1,0:T(8,128)S(1)} %collective-permute-done.55.refs_2_), channel_id=1, source_target_pairs={{0,8},{8,16},{16,24},{24,0},{1,9},{9,17},{17,25},{25,1},{2,10},{10... | collective-permute-start | bytes 1572872 | tf_op jit(solution)/shard_map/ppermute | solution.py:443
